TPU v7x, 32 devices: a whole 2x2x4 slice. The times are simulated.
32 devices in a mesh: frames: 8 (over z, y), heads: 4 (over x, core).
Axes of the slice: x: 2, y: 2, z: 4, core: 2. Of those that a mesh axis runs over, the one named last changes fastest.
Arguments:
- bank_query: bfloat16 [64, 64, 5120], P(None, 'frames', 'heads'), may hold values from -2048 to 2048
- char_bank: bfloat16 [2, 8, 768, 5120], P(None, None, 'frames', 'heads'), may hold values from -8 to 8
- char_slots: int32 [8, 2], replicated, may hold values from 0 to 7, as said below
- slot_live: int32 [8, 2], replicated, may hold values from 0 to 1, as said below
- frame_tokens: bfloat16 [3, 64, 64, 5120], P(None, None, 'frames', 'heads'), may hold values from -2048 to 2048
- out_weight: bfloat16 [5120, 5120], P('heads'), may hold values from -0.078125 to 0.078125
Outputs:
- blended: bfloat16 [64, 64, 5120], P('heads', 'frames')
Inputs may be any that keep to these rules, and one draw needn't show every extreme that they name: `char_slots`: the two ids of a shard differ. `slot_live`: slot 0 of every shard is 1.
All inputs are finite; a program needn't handle non-finite values.
Results may differ from a plain program's by a relative error of at most 0.014.
Values may be sent and summed in bfloat16 or wider, within the bound.
No kernel may reach another device: no remote copies, remote signals or barrier semaphores. Data moves between devices by JAX's collectives and lax.ppermute only.
A program may use at most 128 MiB of HBM per device.

v0:
```python
import functools

import jax
import jax.numpy as jnp
from jax import lax
from jax.experimental import pallas as pl
from jax.experimental.pallas import tpu as pltpu
from jax.sharding import PartitionSpec as P

HEAD_DIM = 128
TILE_ROWS = 16
HEAD_GROUPS = 2
VMEM_BYTES = 24 * 1024 * 1024


def after(block, *before):
    return lax.optimization_barrier((block, *before))[0] if before else block


def wide(block):
    return block.astype(jnp.float32)


def added(*blocks):
    return functools.reduce(jnp.add, [wide(block) for block in blocks]).astype(jnp.bfloat16)


def in_three(block):
    terms = []
    for _ in range(3):
        term = lax.reduce_precision(block, 8, 7)
        terms.append(term.astype(jnp.bfloat16))
        block = block - term
    return terms


def attend_columns(keys, values, queries, allowed):
    scale = HEAD_DIM ** (-0.5)
    scores = lax.dot_general(
        keys, queries, (((1,), (1,)), ((), ())), preferred_element_type=jnp.float32
    )
    scores = jnp.where(allowed, scores, -jnp.inf)
    peak = jnp.max(scores, axis=0, keepdims=True)
    weights = jnp.exp((scores - peak) * scale)
    totals = jnp.sum(weights, axis=0, keepdims=True)
    gathered = lax.dot_general(
        values, weights.astype(jnp.bfloat16), (((0,), (0,)), ((), ())),
        preferred_element_type=jnp.float32,
    )
    return gathered * (1.0 / totals), peak * scale + jnp.log(totals)


def bank_kernel(banks, live_ref, own_ref, far_ref, *refs):
    bank_refs = refs[:banks]
    head = pl.program_id(0)
    tokens = sum(bank.shape[2] for bank in bank_refs)
    second = lax.broadcasted_iota(jnp.int32, (2 * tokens, own_ref.shape[0]), 0) >= tokens
    for side, query_ref in enumerate((own_ref, far_ref)):
        out_ref, level_ref = refs[banks + 2 * side : banks + 2 * side + 2]
        keys, values = (
            jnp.concatenate([bank[which, 2 * side + slot] for slot in range(2) for bank in bank_refs], axis=0)
            for which in range(2)
        )
        allowed = jnp.logical_or(jnp.logical_not(second), live_ref[side, 1] > 0)
        gathered, level = attend_columns(keys, values, query_ref[...], allowed)
        rows = out_ref.shape[2]
        for part in range(out_ref.shape[0]):
            here = slice(part * rows, (part + 1) * rows)
            out_ref[part] = gathered[:, here].astype(out_ref.dtype)
            level_ref[part, pl.ds(head, 1), :] = level[:, here]


def attend_bank(group, parts, rows, live, own, far, banks):
    width = banks[0].shape[3]
    heads = width // HEAD_DIM
    keys_each = 2 * sum(bank.shape[2] for bank in banks)
    query_spec = pl.BlockSpec((parts * rows, HEAD_DIM), lambda h: (0, group * heads + h))
    out = jax.ShapeDtypeStruct((parts, width, rows), jnp.bfloat16)
    level = jax.ShapeDtypeStruct((parts, heads, rows), jnp.float32)
    out_spec = pl.BlockSpec((parts, HEAD_DIM, rows), lambda h: (0, h, 0))
    level_spec = pl.BlockSpec((parts, heads, rows), lambda h: (0, 0, 0))
    return pl.pallas_call(
        functools.partial(bank_kernel, len(banks)),
        grid=(heads,),
        in_specs=[pl.BlockSpec(memory_space=pltpu.SMEM), query_spec, query_spec]
        + [pl.BlockSpec((*bank.shape[:3], HEAD_DIM), lambda h: (0, 0, 0, h)) for bank in banks],
        out_specs=[out_spec, level_spec] * 2,
        out_shape=[out, level] * 2,
        compiler_params=pltpu.CompilerParams(vmem_limit_bytes=VMEM_BYTES),
        cost_estimate=pl.CostEstimate(
            flops=32 * parts * rows * width * keys_each,
            bytes_accessed=2 * (4 * parts * rows * width + sum(bank.size for bank in banks)),
            transcendentals=2 * parts * rows * heads * keys_each,
        ),
    )(live, own, far, *banks)


def frame_kernel(frames_here, token_ref, out_ref):
    scale = HEAD_DIM ** (-0.5)
    pieces, _, parts, rows, _ = token_ref.shape
    size = pieces * rows
    query_spot = lax.broadcasted_iota(jnp.int32, (size, size), 0) % rows // frames_here
    key_spot = lax.broadcasted_iota(jnp.int32, (size, size), 1) % rows // frames_here
    same_spot = query_spot == key_spot
    for part in range(parts):
        queries, keys, values = (
            jnp.concatenate([token_ref[piece, which, part] for piece in range(pieces)], axis=0)
            for which in range(3)
        )
        scores = lax.dot_general(
            queries, keys, (((1,), (1,)), ((), ())), preferred_element_type=jnp.float32
        )
        scores = jnp.where(same_spot, scores, -jnp.inf)
        weights = jnp.exp((scores - jnp.max(scores, axis=1, keepdims=True)) * scale)
        totals = jnp.sum(weights, axis=1, keepdims=True)
        gathered = jnp.dot(weights.astype(jnp.bfloat16), values, preferred_element_type=jnp.float32)
        gathered = (gathered / totals).astype(out_ref.dtype)
        for piece in range(pieces):
            out_ref[piece, part] = gathered[piece * rows : (piece + 1) * rows]


def attend_frames(frames_here, tokens):
    pieces, _, parts, rows, width = tokens.shape
    return pl.pallas_call(
        functools.partial(frame_kernel, frames_here),
        grid=(width // HEAD_DIM,),
        in_specs=[pl.BlockSpec((pieces, 3, parts, rows, HEAD_DIM), lambda h: (0, 0, 0, 0, h))],
        out_specs=pl.BlockSpec((pieces, parts, rows, HEAD_DIM), lambda h: (0, 0, 0, h)),
        out_shape=jax.ShapeDtypeStruct((pieces, parts, rows, width), jnp.bfloat16),
        compiler_params=pltpu.CompilerParams(vmem_limit_bytes=VMEM_BYTES),
        cost_estimate=pl.CostEstimate(
            flops=16 * parts * (pieces * rows) ** 2 * width,
            bytes_accessed=8 * pieces * parts * rows * width,
            transcendentals=parts * (pieces * rows) ** 2 * width // HEAD_DIM,
        ),
    )(tokens)


def listed_kernel(place_ref, slots_ref, *refs):
    count = len(refs) // 2
    for source, target in zip(refs[:count], refs[count:]):
        target[...] = source[...]


def listed_banks(place, char_slots, char_bank, half, group, group_width):
    _, _, tokens, _ = char_bank.shape
    block = (2, 1, tokens, group_width)

    def source(step):
        def index(entry, place_ref, slots_ref):
            shard = place_ref[0] ^ step ^ (entry // 2 * half)
            return 0, slots_ref[shard * 2 + entry % 2], 0, group

        return pl.BlockSpec(block, index)

    return pl.pallas_call(
        listed_kernel,
        grid_spec=pltpu.PrefetchScalarGridSpec(
            num_scalar_prefetch=2,
            grid=(4,),
            in_specs=[source(step) for step in range(half)],
            out_specs=[pl.BlockSpec(block, lambda entry, *_: (0, entry, 0, 0)) for _ in range(half)],
        ),
        out_shape=[jax.ShapeDtypeStruct((2, 4, tokens, group_width), char_bank.dtype) for _ in range(half)],
        compiler_params=pltpu.CompilerParams(vmem_limit_bytes=VMEM_BYTES),
        cost_estimate=pl.CostEstimate(
            flops=0, bytes_accessed=32 * half * tokens * group_width, transcendentals=0
        ),
    )(place.reshape(1), char_slots.reshape(-1), *[char_bank] * half)


def local(bank_query, char_bank, char_slots, slot_live, frame_tokens, out_weight):
    spatial, frames_here, width = bank_query.shape
    heads_here = width // HEAD_DIM
    head_groups = lax.axis_size("heads")
    shards = lax.axis_size("frames")
    half = shards // 2
    place = lax.axis_index("frames")
    parts = max(1, spatial * frames_here // (TILE_ROWS * shards))
    across = shards // head_groups
    spots = spatial // (shards * parts)
    tile = spots * frames_here
    rows = shards * tile

    def swap(block, step):
        return lax.ppermute(block, "frames", [(a, a ^ step) for a in range(shards)])

    def by_part(block):
        cut = block.reshape(head_groups, parts, across, spots, frames_here, width)
        return jnp.moveaxis(cut, 1, 0).reshape(parts * rows, width)

    own = by_part(bank_query)
    far = swap(own, half)

    groups = HEAD_GROUPS if heads_here % HEAD_GROUPS == 0 else 1

    def banks_of(group, *before):
        blocks = listed_banks(
            place, after(char_slots, *before), char_bank, half, group, width // groups
        )
        blocks = [blocks[0]] + [swap(blocks[step], step) for step in range(1, half)]
        return blocks if char_bank.shape[2] % TILE_ROWS == 0 else [jnp.concatenate(blocks, axis=2)]

    banks = [banks_of(0)]
    tokens = frame_tokens.reshape(3, head_groups, parts, across, spots, frames_here, width)
    tokens = tokens.transpose(1, 3, 0, 2, 4, 5, 6).reshape(shards, 3, parts, tile, width)
    tokens = lax.all_to_all(after(tokens, far), "frames", 0, 0, tiled=True)
    live = jnp.stack([slot_live[place], slot_live[place ^ half]])

    place_heads = lax.axis_index("heads")
    chips, core, chip = head_groups // 2, place_heads % 2, place_heads // 2

    def scatter_cores(block):
        block = block.reshape(chips, 2, -1, block.shape[-1])
        give = lax.dynamic_index_in_dim(block, 1 - core, 1, keepdims=False)
        keep = lax.dynamic_index_in_dim(block, core, 1, keepdims=False)
        return added(keep, lax.ppermute(give, "heads", [(h, h ^ 1) for h in range(head_groups)]))

    def scatter_chips(summed):
        parcels = [lax.dynamic_index_in_dim(summed, chip, 0, keepdims=False)]
        for step in range(1, chips):
            give = lax.dynamic_index_in_dim(summed, (chip + step) % chips, 0, keepdims=False)
            parcels.append(
                lax.ppermute(give, "heads", [(h, (h + 2 * step) % head_groups) for h in range(head_groups)])
            )
        return added(*parcels)

    split = (heads_here // groups, HEAD_DIM, rows)
    results = []
    for group in range(groups):
        near_out, near_level, far_out, far_level = attend_bank(group, parts, rows, live, own, far, banks[group])
        if group < groups - 1:
            banks.append(banks_of(group + 1, far_level))
        if group == 0:
            frame_parts = attend_frames(frames_here, after(tokens, far_level))
            back = lax.all_to_all(frame_parts, "frames", 0, 0, tiled=True)
            live = after(live, frame_parts)
        message = jnp.concatenate([far_out, *in_three(far_level)], axis=1)
        message = jnp.pad(message, ((0, 0), (0, -message.shape[1] % TILE_ROWS), (0, 0)))
        if group < groups - 1:
            got = swap(message, half)
        else:
            got = [swap(message[part], half) for part in range(parts)]
        results.append((near_out, near_level, got))

    def share_of(group, part):
        near_out, near_level, got = results[group]
        got = after(got[part], *([results[-1][1]] if group < groups - 1 else []))
        size = heads_here // groups
        got_level = sum(wide(got[low : low + size]) for low in range(width // groups, width // groups + 3 * size, size))
        peak = jnp.maximum(near_level[part], got_level)
        near_share, got_share = jnp.exp(near_level[part] - peak), jnp.exp(got_level - peak)
        total = near_share + got_share
        return (
            wide(near_out[part].reshape(split)) * (near_share / total)[:, None, :]
            + wide(got[: width // groups].reshape(split)) * (got_share / total)[:, None, :]
        )

    summed = []
    for part in range(parts):
        ref_out = jnp.concatenate([share_of(group, part) for group in range(groups)], axis=0).reshape(width, rows)
        frame_out = back[:, part].reshape(rows, width)
        combined = (ref_out + wide(frame_out.T)).astype(jnp.bfloat16)
        combined = after(combined, *summed[max(part - 2, 0) : max(part - 1, 0)])
        projected = lax.dot_general(
            combined, out_weight, (((0,), (0,)), ((), ())), preferred_element_type=jnp.float32
        ).astype(jnp.bfloat16)
        summed.append(scatter_cores(projected))
    pieces = [scatter_chips(block) for block in summed]
    return jnp.concatenate(pieces, axis=0).reshape(spatial // head_groups, frames_here, -1)


def solution(mesh):
    in_specs = (
        P(None, "frames", "heads"),
        P(None, None, "frames", "heads"),
        P(),
        P(),
        P(None, None, "frames", "heads"),
        P("heads", None),
    )
    out_specs = P("heads", "frames", None)
    return jax.shard_map(local, mesh=mesh, in_specs=in_specs, out_specs=out_specs, check_vma=False)
```

profile of v0, /device:TPU:0, one launch (start us, length us, event | category | flops | bytes accessed | tf_op | source)
XLA Modules:
  0.0 368.0 jit_solution(13868643450914635083)
XLA Ops:
  0.0 1.4 copy.22
  1.4 4.1 %collective-permute-start = (bf16[512,1280]{1,0:T(8,128)(2,1)S(1)}, bf16[512,1280]{1,0:T(8,128)(2,1)S(1)}, u32[]{:S(2)}, u32[]{:S(2)}) collective-permute-start(bf16[512,1280]{1,0:T(8,128)(2,1)S(1)} %bitcast.243), channel_id=1, source_target_pairs={{0,16},{4,20},{8,24},{12,28},{16,0},{20,4},{24,8},{28,12},{1,17},{... | collective-permute-start | bytes 3932168 | tf_op jit(solution)/shard_map/ppermute | solution.py:186
  5.5 4.6 %copy.24 = bf16[3,4,4,2,2,8,1280]{6,5,4,2,0,3,1:T(8,128)(2,1)} copy(bf16[3,4,4,2,2,8,1280]{6,5,4,3,2,1,0:T(8,128)(2,1)} %bitcast.257) | data formatting | bytes 7864320 | tf_op jit(solution)/shard_map/reshape | solution.py:205
  10.1 52.3 %collective-permute-done.far_ref = bf16[512,1280]{1,0:T(8,128)(2,1)S(1)} collective-permute-done((bf16[512,1280]{1,0:T(8,128)(2,1)S(1)}, bf16[512,1280]{1,0:T(8,128)(2,1)S(1)}, u32[]{:S(2)}, u32[]{:S(2)}) %collective-permute-start) | collective-permute-done | bytes 1310752 | tf_op jit(solution)/shard_map/ppermute | solution.py:186
  62.4 5.9 %all-to-all-start = ((bf16[8,3,4,16,1280]{4,3,2,1,0:T(8,128)(2,1)}), bf16[8,3,4,16,1280]{4,3,2,1,0:T(8,128)(2,1)}, u32[]{:S(2)}, u32[]{:S(2)}) async-start(bf16[8,3,4,16,1280]{4,3,2,1,0:T(8,128)(2,1)} %bitcast.248), calls=%async_computation | async-start | bytes 7864320 | tf_op jit(solution)/shard_map/all_to_all | solution.py:207
  68.5 2.1 copy-done
  70.6 3.2 shard_map.64
  73.8 0.9 copy-done.4
  74.7 2.0 collective-permute-start.1
  76.7 1.5 collective-permute-start.2
  78.5 55.6 %collective-permute-done.1.refs_1_ = bf16[2,4,96,640]{3,2,1,0:T(8,128)(2,1)} collective-permute-done((bf16[2,4,96,640]{3,2,1,0:T(8,128)(2,1)}, bf16[2,4,96,640]{3,2,1,0:T(8,128)(2,1)}, u32[]{:S(2)}, u32[]{:S(2)}) %collective-permute-start.1) | collective-permute-done | bytes 983072 | tf_op jit(solution)/shard_map/ppermute | solution.py:186
  134.1 22.3 %collective-permute-done.2.refs_2_ = bf16[2,4,96,640]{3,2,1,0:T(8,128)(2,1)} collective-permute-done((bf16[2,4,96,640]{3,2,1,0:T(8,128)(2,1)}, bf16[2,4,96,640]{3,2,1,0:T(8,128)(2,1)}, u32[]{:S(2)}, u32[]{:S(2)}) %collective-permute-start.2) | collective-permute-done | bytes 983072 | tf_op jit(solution)/shard_map/ppermute | solution.py:186
  156.5 20.7 %collective-permute-done.3.refs_3_ = bf16[2,4,96,640]{3,2,1,0:T(8,128)(2,1)} collective-permute-done((bf16[2,4,96,640]{3,2,1,0:T(8,128)(2,1)}, bf16[2,4,96,640]{3,2,1,0:T(8,128)(2,1)}, u32[]{:S(2)}, u32[]{:S(2)}) %collective-permute-start.3) | collective-permute-done | bytes 983072 | tf_op jit(solution)/shard_map/ppermute | solution.py:186
  177.2 1.2 copy-done.5
  178.4 10.1 %shard_map.65 = (bf16[4,640,128]{2,1,0:T(8,128)(2,1)S(1)}, f32[4,5,128]{2,1,0:T(8,128)S(1)}, bf16[4,640,128]{2,1,0:T(8,128)(2,1)S(1)}, f32[4,5,128]{2,1,0:T(8,128)S(1)}) custom-call(s32[2,2]{1,0:T(2,128)S(1)} %pad_add_fusion.live_ref, bf16[512,1280]{1,0:T(8,128)(2,1)S(1)} %bitcast.244, bf16[512,1280]{1,0:T(8,128)(2,1)S(1)} %collective-permute-done.far_ref, ...), custom_call_target="tpu_custom_call" | custom-call | flops 8053063680 | bytes 6553600 | tf_op jit(solution)/shard_map/pallas_call | solution.py:82
  188.5 0.9 fusion.14
  189.4 2.5 collective-permute-start.4
  192.1 2.1 copy-done.1
  194.2 3.3 shard_map.67
  197.5 1.0 copy-done.2
  198.4 0.6 collective-permute-start.5
  199.1 2.8 collective-permute-start.7
  201.9 0.8 fusion.61
  202.7 18.4 %collective-permute-done.4 = bf16[4,656,128]{2,1,0:T(8,128)(2,1)} collective-permute-done((bf16[4,656,128]{2,1,0:T(8,128)(2,1)}, bf16[4,656,128]{2,1,0:T(8,128)(2,1)}, u32[]{:S(2)}, u32[]{:S(2)}) %collective-permute-start.4) | collective-permute-done | bytes 671776 | tf_op jit(solution)/shard_map/ppermute | solution.py:186
  221.1 1.2 slice_bitcast_fusion.7
  222.4 12.6 %shard_map.66 = bf16[8,4,16,1280]{3,2,1,0:T(8,128)(2,1)} custom-call(bf16[8,3,4,16,1280]{4,3,2,1,0:T(8,128)(2,1)} %all-to-all-done.token_ref), custom_call_target="tpu_custom_call" | custom-call | flops 1342177280 | bytes 5242880 | tf_op jit(solution)/shard_map/pallas_call | solution.py:124
  235.0 4.3 %all-to-all-start.1 = ((bf16[8,4,16,1280]{3,2,1,0:T(8,128)(2,1)}), bf16[8,4,16,1280]{3,2,1,0:T(8,128)(2,1)}, u32[]{:S(2)}, u32[]{:S(2)}) async-start(bf16[8,4,16,1280]{3,2,1,0:T(8,128)(2,1)} %shard_map.66), calls=%async_computation.1 | async-start | bytes 2621440 | tf_op jit(solution)/shard_map/all_to_all | solution.py:236
  239.3 33.9 %collective-permute-done.7.refs_3_ = bf16[2,4,96,640]{3,2,1,0:T(8,128)(2,1)} collective-permute-done((bf16[2,4,96,640]{3,2,1,0:T(8,128)(2,1)}, bf16[2,4,96,640]{3,2,1,0:T(8,128)(2,1)}, u32[]{:S(2)}, u32[]{:S(2)}) %collective-permute-start.7) | collective-permute-done | bytes 983072 | tf_op jit(solution)/shard_map/ppermute | solution.py:186
  273.2 1.2 copy-done.3
  274.4 10.2 %shard_map.68 = (bf16[4,640,128]{2,1,0:T(8,128)(2,1)S(1)}, f32[4,5,128]{2,1,0:T(8,128)S(1)}, bf16[4,640,128]{2,1,0:T(8,128)(2,1)S(1)}, f32[4,5,128]{2,1,0:T(8,128)S(1)}) custom-call(s32[2,2]{1,0:T(2,128)S(1)} %pad_add_fusion.live_ref, bf16[512,1280]{1,0:T(8,128)(2,1)S(1)} %bitcast.245, bf16[512,1280]{1,0:T(8,128)(2,1)S(1)} %collective-permute-done.far_ref, ...), custom_call_target="tpu_custom_call" | custom-call | flops 8053063680 | bytes 6553600 | tf_op jit(solution)/shard_map/pallas_call | solution.py:82
  284.7 0.8 slice_bitcast_fusion.6
  285.8 2.9 collective-permute-start.8
  288.7 2.8 collective-permute-start.11
  291.6 0.8 fusion.33
  292.6 7.6 %collective-permute-done.17 = bf16[656,128]{1,0:T(8,128)(2,1)S(1)} collective-permute-done((bf16[656,128]{1,0:T(8,128)(2,1)S(1)}, bf16[656,128]{1,0:T(8,128)(2,1)S(1)}, u32[]{:S(2)}, u32[]{:S(2)}) %collective-permute-start.17) | collective-permute-done | bytes 167968 | tf_op jit(solution)/shard_map/ppermute | solution.py:186
  300.2 3.6 collective-permute-done.8
  303.8 0.8 fusion.32
  304.7 0.2 copy.31
  305.0 2.5 collective-permute-done.14
  307.4 0.9 slice.267
  308.4 0.9 collective-permute-done.11
  309.2 0.9 slice.260
  310.2 0.8 add_divide_fusion.5
  311.1 0.2 copy.27
  311.4 0.2 copy.29
  311.7 1.1 pad_maximum_fusion
  312.8 0.2 copy.26
  313.0 1.4 fusion.60
  314.4 6.8 %convolution_convert_fusion.2 = bf16[128,5120]{1,0:T(8,128)(2,1)S(1)} fusion(bf16[1280,5120]{1,0:T(8,128)(2,1)} %param.11, f32[1280,128]{0,1:T(8,128)S(1)} %copy.27, bf16[128,1280]{1,0:T(8,128)(2,1)S(1)} %bitcast.263), kind=kOutput, calls=%fused_computation.2 | convolution fusion | flops 1678868480 | bytes 15400960 | tf_op jit(solution)/shard_map/dot_general | solution.py:265
  321.4 6.8 %convolution_convert_fusion.3 = bf16[128,5120]{1,0:T(8,128)(2,1)S(1)} fusion(bf16[1280,5120]{1,0:T(8,128)(2,1)} %param.11, f32[1280,128]{0,1:T(8,128)S(1)} %copy.26, bf16[128,1280]{1,0:T(8,128)(2,1)S(1)} %bitcast.262), kind=kOutput, calls=%fused_computation.3 | convolution fusion | flops 1678868480 | bytes 15400960 | tf_op jit(solution)/shard_map/dot_general | solution.py:265
  328.2 0.5 collective-permute-start.9
  328.9 0.2 fusion.10
  329.1 1.9 convolution_convert_fusion
  331.3 1.9 convolution_convert_fusion.1
  333.3 0.5 collective-permute-start.15
  333.9 1.6 collective-permute-start.13
  335.5 0.6 collective-permute-start.10
  336.0 8.5 %collective-permute-done.13 = bf16[32,5120]{1,0:T(8,128)(2,1)S(1)} collective-permute-done((bf16[32,5120]{1,0:T(8,128)(2,1)S(1)}, bf16[32,5120]{1,0:T(8,128)(2,1)S(1)}, u32[]{:S(2)}, u32[]{:S(2)}) %collective-permute-start.13) | collective-permute-done | bytes 327712 | tf_op jit(solution)/shard_map/ppermute | solution.py:224
  344.6 6.0 %collective-permute-done.10 = bf16[32,5120]{1,0:T(8,128)(2,1)S(1)} collective-permute-done((bf16[32,5120]{1,0:T(8,128)(2,1)S(1)}, bf16[32,5120]{1,0:T(8,128)(2,1)S(1)}, u32[]{:S(2)}, u32[]{:S(2)}) %collective-permute-start.10) | collective-permute-done | bytes 327712 | tf_op jit(solution)/shard_map/ppermute | solution.py:224
  350.9 1.6 collective-permute-start.19
  352.7 0.6 collective-permute-start.16
  353.3 8.3 %collective-permute-done.19 = bf16[32,5120]{1,0:T(8,128)(2,1)S(1)} collective-permute-done((bf16[32,5120]{1,0:T(8,128)(2,1)S(1)}, bf16[32,5120]{1,0:T(8,128)(2,1)S(1)}, u32[]{:S(2)}, u32[]{:S(2)}) %collective-permute-start.19) | collective-permute-done | bytes 327712 | tf_op jit(solution)/shard_map/ppermute | solution.py:224
  361.7 5.1 %collective-permute-done.16 = bf16[32,5120]{1,0:T(8,128)(2,1)S(1)} collective-permute-done((bf16[32,5120]{1,0:T(8,128)(2,1)S(1)}, bf16[32,5120]{1,0:T(8,128)(2,1)S(1)}, u32[]{:S(2)}, u32[]{:S(2)}) %collective-permute-start.16) | collective-permute-done | bytes 327712 | tf_op jit(solution)/shard_map/ppermute | solution.py:224
  366.9 1.1 maximum_bitcast_fusion
  (82 shorter events, 3.0 us)
Async XLA Ops:
  1.4 61.0 %collective-permute-start = (bf16[512,1280]{1,0:T(8,128)(2,1)S(1)}, bf16[512,1280]{1,0:T(8,128)(2,1)S(1)}, u32[]{:S(2)}, u32[]{:S(2)}) collective-permute-start(bf16[512,1280]{1,0:T(8,128)(2,1)S(1)} %bitcast.243), channel_id=1, source_target_pairs={{0,16},{4,20},{8,24},{12,28},{16,0},{20,4},{24,8},{28,12},{1,17},{... | collective-permute-start | bytes 3932168 | tf_op jit(solution)/shard_map/ppermute | solution.py:186
  62.4 5.9 %copy-start.9 = (s32[8,2]{0,1:T(2,128)S(1)}, s32[8,2]{0,1:T(2,128)}, u32[]{:S(2)}) copy-start(s32[8,2]{0,1:T(2,128)} %param.8) | copy-start | bytes 196
  62.4 160.0 %all-to-all-start = ((bf16[8,3,4,16,1280]{4,3,2,1,0:T(8,128)(2,1)}), bf16[8,3,4,16,1280]{4,3,2,1,0:T(8,128)(2,1)}, u32[]{:S(2)}, u32[]{:S(2)}) async-start(bf16[8,3,4,16,1280]{4,3,2,1,0:T(8,128)(2,1)} %bitcast.248), calls=%async_computation | async-start | bytes 7864320 | tf_op jit(solution)/shard_map/all_to_all | solution.py:207
  68.5 2.1 copy-start
  70.6 7.6 %copy-start.10 = (s32[8,2]{0,1:T(2,128)S(1)}, s32[8,2]{0,1:T(2,128)}, u32[]{:S(2)}) copy-start(s32[8,2]{0,1:T(2,128)} %param.9) | copy-start | bytes 196
  73.8 1.0 copy-start.4
  74.7 59.4 %collective-permute-start.1 = (bf16[2,4,96,640]{3,2,1,0:T(8,128)(2,1)}, bf16[2,4,96,640]{3,2,1,0:T(8,128)(2,1)}, u32[]{:S(2)}, u32[]{:S(2)}) collective-permute-start(bf16[2,4,96,640]{3,2,1,0:T(8,128)(2,1)} %get-tuple-element.32), channel_id=1, source_target_pairs={{0,4},{4,0},{8,12},{12,8},{16,20},{20,16},{24,28},{28,24},{1,5},{5... | collective-permute-start | bytes 2949128 | tf_op jit(solution)/shard_map/ppermute | solution.py:186
  76.7 79.7 %collective-permute-start.2 = (bf16[2,4,96,640]{3,2,1,0:T(8,128)(2,1)}, bf16[2,4,96,640]{3,2,1,0:T(8,128)(2,1)}, u32[]{:S(2)}, u32[]{:S(2)}) collective-permute-start(bf16[2,4,96,640]{3,2,1,0:T(8,128)(2,1)} %get-tuple-element.33), channel_id=1, source_target_pairs={{0,8},{4,12},{8,0},{12,4},{16,24},{20,28},{24,16},{28,20},{1,9},{5... | collective-permute-start | bytes 2949128 | tf_op jit(solution)/shard_map/ppermute | solution.py:186
  78.2 99.0 %collective-permute-start.3 = (bf16[2,4,96,640]{3,2,1,0:T(8,128)(2,1)}, bf16[2,4,96,640]{3,2,1,0:T(8,128)(2,1)}, u32[]{:S(2)}, u32[]{:S(2)}) collective-permute-start(bf16[2,4,96,640]{3,2,1,0:T(8,128)(2,1)} %get-tuple-element.34), channel_id=1, source_target_pairs={{0,12},{4,8},{8,4},{12,0},{16,28},{20,24},{24,20},{28,16},{1,13},{... | collective-permute-start | bytes 2949128 | tf_op jit(solution)/shard_map/ppermute | solution.py:186
  177.2 1.2 copy-start.5
  189.4 31.7 %collective-permute-start.4 = (bf16[4,656,128]{2,1,0:T(8,128)(2,1)}, bf16[4,656,128]{2,1,0:T(8,128)(2,1)}, u32[]{:S(2)}, u32[]{:S(2)}) collective-permute-start(bf16[4,656,128]{2,1,0:T(8,128)(2,1)} %fusion.14), channel_id=1, source_target_pairs={{0,16},{4,20},{8,24},{12,28},{16,0},{20,4},{24,8},{28,12},{1,17},{... | collective-permute-start | bytes 2015240 | tf_op jit(solution)/shard_map/ppermute | solution.py:186
  192.1 2.1 copy-start.1
  197.5 1.0 copy-start.2
  198.4 40.9 %collective-permute-start.5 = (bf16[2,4,96,640]{3,2,1,0:T(8,128)(2,1)}, bf16[2,4,96,640]{3,2,1,0:T(8,128)(2,1)}, u32[]{:S(2)}, u32[]{:S(2)}) collective-permute-start(bf16[2,4,96,640]{3,2,1,0:T(8,128)(2,1)} %get-tuple-element.44), channel_id=1, source_target_pairs={{0,4},{4,0},{8,12},{12,8},{16,20},{20,16},{24,28},{28,24},{1,5},{5... | collective-permute-start | bytes 2949128 | tf_op jit(solution)/shard_map/ppermute | solution.py:186
  199.0 40.3 %collective-permute-start.6 = (bf16[2,4,96,640]{3,2,1,0:T(8,128)(2,1)}, bf16[2,4,96,640]{3,2,1,0:T(8,128)(2,1)}, u32[]{:S(2)}, u32[]{:S(2)}) collective-permute-start(bf16[2,4,96,640]{3,2,1,0:T(8,128)(2,1)} %get-tuple-element.45), channel_id=1, source_target_pairs={{0,8},{4,12},{8,0},{12,4},{16,24},{20,28},{24,16},{28,20},{1,9},{5... | collective-permute-start | bytes 2949128 | tf_op jit(solution)/shard_map/ppermute | solution.py:186
  199.1 74.1 %collective-permute-start.7 = (bf16[2,4,96,640]{3,2,1,0:T(8,128)(2,1)}, bf16[2,4,96,640]{3,2,1,0:T(8,128)(2,1)}, u32[]{:S(2)}, u32[]{:S(2)}) collective-permute-start(bf16[2,4,96,640]{3,2,1,0:T(8,128)(2,1)} %get-tuple-element.46), channel_id=1, source_target_pairs={{0,12},{4,8},{8,4},{12,0},{16,28},{20,24},{24,20},{28,16},{1,13},{... | collective-permute-start | bytes 2949128 | tf_op jit(solution)/shard_map/ppermute | solution.py:186
  235.0 78.1 %all-to-all-start.1 = ((bf16[8,4,16,1280]{3,2,1,0:T(8,128)(2,1)}), bf16[8,4,16,1280]{3,2,1,0:T(8,128)(2,1)}, u32[]{:S(2)}, u32[]{:S(2)}) async-start(bf16[8,4,16,1280]{3,2,1,0:T(8,128)(2,1)} %shard_map.66), calls=%async_computation.1 | async-start | bytes 2621440 | tf_op jit(solution)/shard_map/all_to_all | solution.py:236
  273.2 1.2 copy-start.3
  284.7 6.9 %copy-start.7 = (bf16[1,640,128]{2,1,0:T(8,128)(2,1)S(1)}, bf16[1,640,128]{2,1,0:T(8,128)(2,1)}, u32[]{:S(2)}) copy-start(bf16[1,640,128]{2,1,0:T(8,128)(2,1)} %get-tuple-element.69) | copy-start | bytes 491524
  284.7 6.9 %copy-start.8 = (bf16[1,640,128]{2,1,0:T(8,128)(2,1)S(1)}, bf16[1,640,128]{2,1,0:T(8,128)(2,1)}, u32[]{:S(2)}) copy-start(bf16[1,640,128]{2,1,0:T(8,128)(2,1)} %get-tuple-element.70) | copy-start | bytes 491524
  285.6 6.9 %copy-start.6 = (bf16[1,640,128]{2,1,0:T(8,128)(2,1)S(1)}, bf16[1,640,128]{2,1,0:T(8,128)(2,1)}, u32[]{:S(2)}) copy-start(bf16[1,640,128]{2,1,0:T(8,128)(2,1)} %get-tuple-element.72) | copy-start | bytes 491524
  285.7 14.5 %collective-permute-start.17 = (bf16[656,128]{1,0:T(8,128)(2,1)S(1)}, bf16[656,128]{1,0:T(8,128)(2,1)S(1)}, u32[]{:S(2)}, u32[]{:S(2)}) collective-permute-start(bf16[656,128]{1,0:T(8,128)(2,1)S(1)} %get-tuple-element.68), channel_id=1, source_target_pairs={{0,16},{4,20},{8,24},{12,28},{16,0},{20,4},{24,8},{28,12},{1,17},{... | collective-permute-start | bytes 503816 | tf_op jit(solution)/shard_map/ppermute | solution.py:186
  285.8 18.0 %collective-permute-start.8 = (bf16[656,128]{1,0:T(8,128)(2,1)S(1)}, bf16[656,128]{1,0:T(8,128)(2,1)S(1)}, u32[]{:S(2)}, u32[]{:S(2)}) collective-permute-start(bf16[656,128]{1,0:T(8,128)(2,1)S(1)} %get-tuple-element.65), channel_id=1, source_target_pairs={{0,16},{4,20},{8,24},{12,28},{16,0},{20,4},{24,8},{28,12},{1,17},{... | collective-permute-start | bytes 503816 | tf_op jit(solution)/shard_map/ppermute | solution.py:186
  288.7 18.8 %collective-permute-start.14 = (bf16[656,128]{1,0:T(8,128)(2,1)}, bf16[656,128]{1,0:T(8,128)(2,1)}, u32[]{:S(2)}, u32[]{:S(2)}) collective-permute-start(bf16[656,128]{1,0:T(8,128)(2,1)} %get-tuple-element.66), channel_id=1, source_target_pairs={{0,16},{4,20},{8,24},{12,28},{16,0},{20,4},{24,8},{28,12},{1,17},{... | collective-permute-start | bytes 503816 | tf_op jit(solution)/shard_map/ppermute | solution.py:186
  288.7 20.5 %collective-permute-start.11 = (bf16[656,128]{1,0:T(8,128)(2,1)}, bf16[656,128]{1,0:T(8,128)(2,1)}, u32[]{:S(2)}, u32[]{:S(2)}) collective-permute-start(bf16[656,128]{1,0:T(8,128)(2,1)} %get-tuple-element.67), channel_id=1, source_target_pairs={{0,16},{4,20},{8,24},{12,28},{16,0},{20,4},{24,8},{28,12},{1,17},{... | collective-permute-start | bytes 503816 | tf_op jit(solution)/shard_map/ppermute | solution.py:186
  314.4 14.7 %slice-start = ((s8[13107200]{0:T(1024)(128)(4,1)}), s8[4194304]{0:T(1024)(128)(4,1)S(1)}, s32[]{:S(2)}) async-start(s8[13107200]{0:T(1024)(128)(4,1)} %bitcast.246), calls=%async_computation.2 | async-start | bytes 8388608
  314.4 14.7 %slice-start.1 = ((s8[13107200]{0:T(1024)(128)(4,1)}), s8[4194304]{0:T(1024)(128)(4,1)S(1)}, s32[]{:S(2)}) async-start(s8[13107200]{0:T(1024)(128)(4,1)} %bitcast.246), calls=%async_computation.3 | async-start | bytes 8388608
  321.3 7.7 %collective-permute-start.12 = (bf16[2,32,5120]{2,1,0:T(8,128)(2,1)S(1)}, bf16[2,32,5120]{2,1,0:T(8,128)(2,1)S(1)}, u32[]{:S(2)}, u32[]{:S(2)}) collective-permute-start(bf16[2,32,5120]{2,1,0:T(8,128)(2,1)S(1)} %dynamic-slice_bitcast_fusion.2), channel_id=1, source_target_pairs={{0,1},{1,0},{2,3},{3,2},{4,5},{5,4},{6,7},{7,6},{8,9},{9,8},{10,11... | collective-permute-start | bytes 1966088 | tf_op jit(solution)/shard_map/ppermute | solution.py:217
  321.4 7.8 %slice-start.2 = ((s8[13107200]{0:T(1024)(128)(4,1)}), s8[4194304]{0:T(1024)(128)(4,1)S(1)}, s32[]{:S(2)}) async-start(s8[13107200]{0:T(1024)(128)(4,1)} %bitcast.246), calls=%async_computation.4 | async-start | bytes 8388608
  321.4 7.8 %slice-start.3 = ((s8[13107200]{0:T(1024)(128)(4,1)}), s8[524288]{0:T(1024)(128)(4,1)S(1)}, s32[]{:S(2)}) async-start(s8[13107200]{0:T(1024)(128)(4,1)} %bitcast.246), calls=%async_computation.5 | async-start | bytes 1048576
  328.2 3.0 collective-permute-start.9
  331.1 19.6 %collective-permute-start.18 = (bf16[2,32,5120]{2,1,0:T(8,128)(2,1)S(1)}, bf16[2,32,5120]{2,1,0:T(8,128)(2,1)S(1)}, u32[]{:S(2)}, u32[]{:S(2)}) collective-permute-start(bf16[2,32,5120]{2,1,0:T(8,128)(2,1)S(1)} %dynamic-slice_bitcast_fusion), channel_id=1, source_target_pairs={{0,1},{1,0},{2,3},{3,2},{4,5},{5,4},{6,7},{7,6},{8,9},{9,8},{10,11... | collective-permute-start | bytes 1966088 | tf_op jit(solution)/shard_map/ppermute | solution.py:217
  333.3 19.2 %collective-permute-start.15 = (bf16[2,32,5120]{2,1,0:T(8,128)(2,1)S(1)}, bf16[2,32,5120]{2,1,0:T(8,128)(2,1)S(1)}, u32[]{:S(2)}, u32[]{:S(2)}) collective-permute-start(bf16[2,32,5120]{2,1,0:T(8,128)(2,1)S(1)} %dynamic-slice_bitcast_fusion.1), channel_id=1, source_target_pairs={{0,1},{1,0},{2,3},{3,2},{4,5},{5,4},{6,7},{7,6},{8,9},{9,8},{10,11... | collective-permute-start | bytes 1966088 | tf_op jit(solution)/shard_map/ppermute | solution.py:217
  333.9 10.6 %collective-permute-start.13 = (bf16[32,5120]{1,0:T(8,128)(2,1)S(1)}, bf16[32,5120]{1,0:T(8,128)(2,1)S(1)}, u32[]{:S(2)}, u32[]{:S(2)}) collective-permute-start(bf16[32,5120]{1,0:T(8,128)(2,1)S(1)} %dynamic-slice_bitcast_fusion.6), channel_id=1, source_target_pairs={{0,2},{1,3},{2,0},{3,1},{4,6},{5,7},{6,4},{7,5},{8,10},{9,11},{10,... | collective-permute-start | bytes 983048 | tf_op jit(solution)/shard_map/ppermute | solution.py:224
  335.5 15.1 %collective-permute-start.10 = (bf16[32,5120]{1,0:T(8,128)(2,1)S(1)}, bf16[32,5120]{1,0:T(8,128)(2,1)S(1)}, u32[]{:S(2)}, u32[]{:S(2)}) collective-permute-start(bf16[32,5120]{1,0:T(8,128)(2,1)S(1)} %dynamic-slice_bitcast_fusion.7), channel_id=1, source_target_pairs={{0,2},{1,3},{2,0},{3,1},{4,6},{5,7},{6,4},{7,5},{8,10},{9,11},{10,... | collective-permute-start | bytes 983048 | tf_op jit(solution)/shard_map/ppermute | solution.py:224
  350.9 10.7 %collective-permute-start.19 = (bf16[32,5120]{1,0:T(8,128)(2,1)S(1)}, bf16[32,5120]{1,0:T(8,128)(2,1)S(1)}, u32[]{:S(2)}, u32[]{:S(2)}) collective-permute-start(bf16[32,5120]{1,0:T(8,128)(2,1)S(1)} %dynamic-slice_bitcast_fusion.4), channel_id=1, source_target_pairs={{0,2},{1,3},{2,0},{3,1},{4,6},{5,7},{6,4},{7,5},{8,10},{9,11},{10,... | collective-permute-start | bytes 983048 | tf_op jit(solution)/shard_map/ppermute | solution.py:224
  352.7 14.1 %collective-permute-start.16 = (bf16[32,5120]{1,0:T(8,128)(2,1)S(1)}, bf16[32,5120]{1,0:T(8,128)(2,1)S(1)}, u32[]{:S(2)}, u32[]{:S(2)}) collective-permute-start(bf16[32,5120]{1,0:T(8,128)(2,1)S(1)} %dynamic-slice_bitcast_fusion.5), channel_id=1, source_target_pairs={{0,2},{1,3},{2,0},{3,1},{4,6},{5,7},{6,4},{7,5},{8,10},{9,11},{10,... | collective-permute-start | bytes 983048 | tf_op jit(solution)/shard_map/ppermute | solution.py:224
where the time goes:
time: 369 us; the launch traced here: 368 us
  waiting for transfers between devices  246 us (67%)
  Pallas kernels  39.4 us (11%)
  starting transfers between devices  35.3 us (10%)
  local copies, waits for them, and re-layouts  22.6 us (6%)
  matrix products  17.3 us (5%)
  other arithmetic  7.24 us (2%)
    ppermute x12, waiting for transfers between devices, swap(): return lax.ppermute(block, 'frames', [(a, a ^ step) for a in range(shards)])  218 us
    ppermute x4, waiting for transfers between devices, scatter_chips(): lax.ppermute(give, 'heads', [(h, (h + 2 * step) % head_groups) for h in r...  27.9 us
    pallas_call x2, Pallas kernels, attend_bank(): pl.pallas_call(functools.partial(bank_kernel, len(banks)), grid=(heads,),...  20.3 us
    ppermute x12, starting transfers between devices, swap(): return lax.ppermute(block, 'frames', [(a, a ^ step) for a in range(shards)])  19.5 us
    dot_general x4, matrix products, local(): lax.dot_general(combined, out_weight, (((0,), (0,)), ((), ())), preferred...  17.3 us
    pallas_call x1, Pallas kernels, attend_frames(): pl.pallas_call(functools.partial(frame_kernel, frames_here), grid=(width...  12.6 us
    unnamed x33, local copies, waits for them, and re-layouts  8.88 us
  transfers between devices with their start and end apart: 22, of which 14 were waited for; matrix products, arithmetic and copies ran while one was open for 8% of the time, Pallas kernels for 11%

commit v1 on v0

--- a/solution.py
+++ b/solution.py
@@ -204,7 +204,7 @@
     banks = [banks_of(0)]
     tokens = frame_tokens.reshape(3, head_groups, parts, across, spots, frames_here, width)
     tokens = tokens.transpose(1, 3, 0, 2, 4, 5, 6).reshape(shards, 3, parts, tile, width)
-    tokens = lax.all_to_all(after(tokens, far), "frames", 0, 0, tiled=True)
+    tokens = lax.all_to_all(after(tokens, far, *banks[0]), "frames", 0, 0, tiled=True)
     live = jnp.stack([slot_live[place], slot_live[place ^ half]])
 
     place_heads = lax.axis_index("heads")
@@ -242,10 +242,14 @@
         else:
             got = [swap(message[part], half) for part in range(parts)]
         results.append((near_out, near_level, got))
-
-    def share_of(group, part):
+    results = [
+        (near_out, near_level, after(got, results[-1][1]) if group < groups - 1 else got)
+        for group, (near_out, near_level, got) in enumerate(results)
+    ]
+
+    def share_of(group, part, *before):
         near_out, near_level, got = results[group]
-        got = after(got[part], *([results[-1][1]] if group < groups - 1 else []))
+        got = after(got[part], *(before if group == groups - 1 else ()))
         size = heads_here // groups
         got_level = sum(wide(got[low : low + size]) for low in range(width // groups, width // groups + 3 * size, size))
         peak = jnp.maximum(near_level[part], got_level)
@@ -256,16 +260,19 @@
             + wide(got[: width // groups].reshape(split)) * (got_share / total)[:, None, :]
         )
 
-    summed = []
+    projected, summed = [], []
     for part in range(parts):
-        ref_out = jnp.concatenate([share_of(group, part) for group in range(groups)], axis=0).reshape(width, rows)
+        shares = [share_of(group, part, *projected[-1:]) for group in range(groups)]
+        ref_out = jnp.concatenate(shares, axis=0).reshape(width, rows)
         frame_out = back[:, part].reshape(rows, width)
         combined = (ref_out + wide(frame_out.T)).astype(jnp.bfloat16)
-        combined = after(combined, *summed[max(part - 2, 0) : max(part - 1, 0)])
-        projected = lax.dot_general(
-            combined, out_weight, (((0,), (0,)), ((), ())), preferred_element_type=jnp.float32
-        ).astype(jnp.bfloat16)
-        summed.append(scatter_cores(projected))
+        projected.append(
+            lax.dot_general(
+                after(combined, *summed[-1:]), out_weight, (((0,), (0,)), ((), ())),
+                preferred_element_type=jnp.float32,
+            ).astype(jnp.bfloat16)
+        )
+        summed.append(scatter_cores(projected[-1]))
     pieces = [scatter_chips(block) for block in summed]
     return jnp.concatenate(pieces, axis=0).reshape(spatial // head_groups, frames_here, -1)
 

time: 369 us -> 339 us (0.919)
  waiting for transfers between devices: 246 us -> 189 us
  local copies, waits for them, and re-layouts: 22.6 us -> 35.4 us
  matrix products: 17.3 us -> 26.6 us
  other arithmetic: 7.24 us -> 14.9 us
    ppermute x12, waiting for transfers between devices: 218 us -> 106 us  [swap(): return lax.ppermute(block, 'frames', [(a, a ^ step) for a in range(shards)])]
    all_to_all x1, waiting for transfers between devices: 0.01 us -> 58.4 us  [local(): lax.all_to_all(after(tokens, far, *banks[0]), 'frames', 0, 0, tiled=True)]
    unnamed x33 -> x51, local copies, waits for them, and re-layouts: 8.88 us -> 18.6 us
    dot_general x4, matrix products: 17.3 us -> 26.6 us  [local(): lax.dot_general(after(combined, *summed[-1:]), out_weight, (((0,), (0,)),...]
    ppermute x4, waiting for transfers between devices: 27.9 us -> 20.9 us  [scatter_chips(): lax.ppermute(give, 'heads', [(h, (h + 2 * step) % head_groups) for h in r...]
    convert_element_type x8, other arithmetic: 0.96 us -> 6.88 us  [added(): functools.reduce(jnp.add, [wide(block) for block in blocks])]
  transfers between devices with their start and end apart: 22 -> 22, of which waited for: 14 -> 12; matrix products, arithmetic and copies ran while one was open for 8% -> 16% of each run, Pallas kernels for 11% -> 11%
where the time goes in v1:
time: 339 us; the launch traced here: 338 us
  waiting for transfers between devices  189 us (56%)
  Pallas kernels  37.9 us (11%)
  local copies, waits for them, and re-layouts  35.4 us (10%)
  starting transfers between devices  34 us (10%)
  matrix products  26.6 us (8%)
  other arithmetic  14.9 us (4%)
    ppermute x12, waiting for transfers between devices, swap(): return lax.ppermute(block, 'frames', [(a, a ^ step) for a in range(shards)])  106 us
    all_to_all x1, waiting for transfers between devices, local(): lax.all_to_all(after(tokens, far, *banks[0]), 'frames', 0, 0, tiled=True)  58.4 us
    dot_general x4, matrix products, local(): lax.dot_general(after(combined, *summed[-1:]), out_weight, (((0,), (0,)),...  26.6 us
    ppermute x4, waiting for transfers between devices, scatter_chips(): lax.ppermute(give, 'heads', [(h, (h + 2 * step) % head_groups) for h in r...  20.9 us
    pallas_call x2, Pallas kernels, attend_bank(): pl.pallas_call(functools.partial(bank_kernel, len(banks)), grid=(heads,),...  20 us
    ppermute x12, starting transfers between devices, swap(): return lax.ppermute(block, 'frames', [(a, a ^ step) for a in range(shards)])  19.8 us
    unnamed x51, local copies, waits for them, and re-layouts  18.6 us
    pallas_call x1, Pallas kernels, attend_frames(): pl.pallas_call(functools.partial(frame_kernel, frames_here), grid=(width...  12.6 us
  transfers between devices with their start and end apart: 22, of which 12 were waited for; matrix products, arithmetic and copies ran while one was open for 16% of the time, Pallas kernels for 11%

profile of v1, /device:TPU:0, one launch (start us, length us, event | category | flops | bytes accessed | tf_op | source)
XLA Modules:
  0.0 338.0 jit_solution(8484010276473185409)
XLA Ops:
  0.0 1.4 copy.22
  1.4 4.1 %collective-permute-start = (bf16[512,1280]{1,0:T(8,128)(2,1)S(1)}, bf16[512,1280]{1,0:T(8,128)(2,1)S(1)}, u32[]{:S(2)}, u32[]{:S(2)}) collective-permute-start(bf16[512,1280]{1,0:T(8,128)(2,1)S(1)} %bitcast.280), channel_id=1, source_target_pairs={{0,16},{4,20},{8,24},{12,28},{16,0},{20,4},{24,8},{28,12},{1,17},{... | collective-permute-start | bytes 3932168 | tf_op jit(solution)/shard_map/ppermute | solution.py:186
  5.7 2.1 copy-done
  7.8 2.0 shard_map.64
  9.8 1.0 copy-done.7
  10.8 1.5 collective-permute-start.1
  12.3 1.6 collective-permute-start.2
  14.3 2.4 copy.24
  16.7 17.9 %collective-permute-done.1.refs_1_ = bf16[2,4,96,640]{3,2,1,0:T(8,128)(2,1)S(1)} collective-permute-done((bf16[2,4,96,640]{3,2,1,0:T(8,128)(2,1)S(1)}, bf16[2,4,96,640]{3,2,1,0:T(8,128)(2,1)S(1)}, u32[]{:S(2)}, u32[]{:S(2)}) %collective-permute-start.1) | collective-permute-done | bytes 983072 | tf_op jit(solution)/shard_map/ppermute | solution.py:186
  34.6 1.0 copy-done.9
  35.6 28.4 %collective-permute-done.2.refs_2_ = bf16[2,4,96,640]{3,2,1,0:T(8,128)(2,1)S(1)} collective-permute-done((bf16[2,4,96,640]{3,2,1,0:T(8,128)(2,1)S(1)}, bf16[2,4,96,640]{3,2,1,0:T(8,128)(2,1)S(1)}, u32[]{:S(2)}, u32[]{:S(2)}) %collective-permute-start.2) | collective-permute-done | bytes 983072 | tf_op jit(solution)/shard_map/ppermute | solution.py:186
  64.0 1.0 copy-done.11
  64.9 18.3 %collective-permute-done.3.refs_3_ = bf16[2,4,96,640]{3,2,1,0:T(8,128)(2,1)S(1)} collective-permute-done((bf16[2,4,96,640]{3,2,1,0:T(8,128)(2,1)S(1)}, bf16[2,4,96,640]{3,2,1,0:T(8,128)(2,1)S(1)}, u32[]{:S(2)}, u32[]{:S(2)}) %collective-permute-start.3) | collective-permute-done | bytes 983072 | tf_op jit(solution)/shard_map/ppermute | solution.py:186
  83.3 1.0 copy-done.13
  84.2 1.1 copy-done.2
  85.3 4.6 %all-to-all-start = ((bf16[8,3,4,16,1280]{4,3,2,1,0:T(8,128)(2,1)}), bf16[8,3,4,16,1280]{4,3,2,1,0:T(8,128)(2,1)}, u32[]{:S(2)}, u32[]{:S(2)}) async-start(bf16[8,3,4,16,1280]{4,3,2,1,0:T(8,128)(2,1)} %bitcast.283), calls=%async_computation | async-start | bytes 7864320 | tf_op jit(solution)/shard_map/all_to_all | solution.py:207
  90.2 1.3 copy-done.3
  91.5 1.2 copy-done.8
  92.7 1.2 copy-done.10
  93.9 1.2 copy-done.12
  95.1 1.2 copy-done.14
  96.3 9.8 %shard_map.65 = (bf16[4,640,128]{2,1,0:T(8,128)(2,1)S(1)}, f32[4,5,128]{2,1,0:T(8,128)S(1)}, bf16[4,640,128]{2,1,0:T(8,128)(2,1)S(1)}, f32[4,5,128]{2,1,0:T(8,128)S(1)}) custom-call(s32[2,2]{1,0:T(2,128)S(1)} %pad_add_fusion.live_ref, bf16[512,1280]{1,0:T(8,128)(2,1)S(1)} %bitcast.281, bf16[512,1280]{1,0:T(8,128)(2,1)S(1)} %copy-done.3, ...), custom_call_target="tpu_custom_call" | custom-call | flops 8053063680 | bytes 6553600 | tf_op jit(solution)/shard_map/pallas_call | solution.py:82
  106.3 2.1 copy-done.1
  108.4 3.2 shard_map.67
  111.6 1.0 copy-done.5
  112.6 2.0 collective-permute-start.5
  114.6 1.5 collective-permute-start.6
  116.1 0.9 fusion.14
  117.0 2.9 collective-permute-start.4
  120.7 58.4 %all-to-all-done.token_ref = bf16[8,3,4,16,1280]{4,3,2,1,0:T(8,128)(2,1)} async-done(((bf16[8,3,4,16,1280]{4,3,2,1,0:T(8,128)(2,1)}), bf16[8,3,4,16,1280]{4,3,2,1,0:T(8,128)(2,1)}, u32[]{:S(2)}, u32[]{:S(2)}) %all-to-all-start) | async-done | bytes 3932192 | tf_op jit(solution)/shard_map/all_to_all | solution.py:207
  179.1 12.6 %shard_map.66 = bf16[8,4,16,1280]{3,2,1,0:T(8,128)(2,1)} custom-call(bf16[8,3,4,16,1280]{4,3,2,1,0:T(8,128)(2,1)} %all-to-all-done.token_ref), custom_call_target="tpu_custom_call" | custom-call | flops 1342177280 | bytes 5242880 | tf_op jit(solution)/shard_map/pallas_call | solution.py:124
  191.7 4.4 %all-to-all-start.1 = ((bf16[8,4,16,1280]{3,2,1,0:T(8,128)(2,1)}), bf16[8,4,16,1280]{3,2,1,0:T(8,128)(2,1)}, u32[]{:S(2)}, u32[]{:S(2)}) async-start(bf16[8,4,16,1280]{3,2,1,0:T(8,128)(2,1)} %shard_map.66), calls=%async_computation.1 | async-start | bytes 2621440 | tf_op jit(solution)/shard_map/all_to_all | solution.py:236
  196.1 19.5 %collective-permute-done.7.refs_3_ = bf16[2,4,96,640]{3,2,1,0:T(8,128)(2,1)} collective-permute-done((bf16[2,4,96,640]{3,2,1,0:T(8,128)(2,1)}, bf16[2,4,96,640]{3,2,1,0:T(8,128)(2,1)}, u32[]{:S(2)}, u32[]{:S(2)}) %collective-permute-start.7) | collective-permute-done | bytes 983072 | tf_op jit(solution)/shard_map/ppermute | solution.py:186
  215.7 1.3 copy-done.4
  217.0 10.3 %shard_map.68 = (bf16[4,640,128]{2,1,0:T(8,128)(2,1)S(1)}, f32[4,5,128]{2,1,0:T(8,128)S(1)}, bf16[4,640,128]{2,1,0:T(8,128)(2,1)S(1)}, f32[4,5,128]{2,1,0:T(8,128)S(1)}) custom-call(s32[2,2]{1,0:T(2,128)S(1)} %pad_add_fusion.live_ref, bf16[512,1280]{1,0:T(8,128)(2,1)S(1)} %bitcast.282, bf16[512,1280]{1,0:T(8,128)(2,1)S(1)} %copy-done.4, ...), custom_call_target="tpu_custom_call" | custom-call | flops 8053063680 | bytes 6553600 | tf_op jit(solution)/shard_map/pallas_call | solution.py:82
  228.2 2.9 collective-permute-start.11
  231.1 2.9 collective-permute-start.17
  236.6 22.0 %collective-permute-done.8 = bf16[656,128]{1,0:T(8,128)(2,1)S(1)} collective-permute-done((bf16[656,128]{1,0:T(8,128)(2,1)S(1)}, bf16[656,128]{1,0:T(8,128)(2,1)S(1)}, u32[]{:S(2)}, u32[]{:S(2)}) %collective-permute-start.8) | collective-permute-done | bytes 167968 | tf_op jit(solution)/shard_map/ppermute | solution.py:186
  259.0 2.2 fusion.59
  261.2 6.6 %convolution_convert_fusion.3 = bf16[128,5120]{1,0:T(8,128)(2,1)S(1)} fusion(bf16[1280,5120]{1,0:T(8,128)(2,1)} %param.11, f32[1280,128]{0,1:T(8,128)S(1)} %copy.26, bf16[128,1280]{1,0:T(8,128)(2,1)S(1)} %bitcast.297), kind=kOutput, calls=%fused_computation.3 | convolution fusion | flops 1678868480 | bytes 15400960 | tf_op jit(solution)/shard_map/dot_general | solution.py:270
  268.6 0.9 slice.238
  269.6 0.9 dynamic-slice_bitcast_fusion.3
  270.9 2.0 collective-permute-done.9
  272.9 1.2 fusion.11
  274.1 6.7 %convolution_convert_fusion.2 = bf16[128,5120]{1,0:T(8,128)(2,1)S(1)} fusion(bf16[1280,128]{0,1:T(8,128)(2,1)S(1)} %fusion.26, bf16[1280,5120]{1,0:T(8,128)(2,1)} %param.11), kind=kOutput, calls=%fused_computation.2 | convolution fusion | flops 1678376960 | bytes 14745600 | tf_op jit(solution)/shard_map/dot_general | solution.py:270
  281.6 0.9 slice.252
  283.3 1.5 collective-permute-start.10
  284.8 0.9 dynamic-slice_bitcast_fusion.2
  286.0 1.0 fusion.23
  287.0 6.3 %collective-permute-done.10 = bf16[32,5120]{1,0:T(8,128)(2,1)} collective-permute-done((bf16[32,5120]{1,0:T(8,128)(2,1)}, bf16[32,5120]{1,0:T(8,128)(2,1)}, u32[]{:S(2)}, u32[]{:S(2)}) %collective-permute-start.10) | collective-permute-done | bytes 327712 | tf_op jit(solution)/shard_map/ppermute | solution.py:224
  293.4 1.8 fusion.27
  295.1 1.2 fusion.10
  296.4 6.7 %convolution_convert_fusion.1 = bf16[128,5120]{1,0:T(8,128)(2,1)S(1)} fusion(bf16[1280,128]{0,1:T(8,128)(2,1)S(1)} %fusion.23, bf16[1280,5120]{1,0:T(8,128)(2,1)} %param.11), kind=kOutput, calls=%fused_computation.1 | convolution fusion | flops 1678376960 | bytes 14745600 | tf_op jit(solution)/shard_map/dot_general | solution.py:270
  304.6 0.9 slice.266
  305.6 1.6 collective-permute-start.13
  308.4 1.0 fusion.20
  309.4 1.0 collective-permute-done.15
  310.4 1.2 fusion.9
  311.7 6.6 %convolution_convert_fusion = bf16[128,5120]{1,0:T(8,128)(2,1)S(1)} fusion(bf16[1280,128]{0,1:T(8,128)(2,1)S(1)} %fusion.20, bf16[1280,5120]{1,0:T(8,128)(2,1)} %param.11), kind=kOutput, calls=%fused_computation | convolution fusion | flops 1678376960 | bytes 14745600 | tf_op jit(solution)/shard_map/dot_general | solution.py:270
  318.6 1.1 fusion.24
  320.8 1.3 collective-permute-start.19
  322.1 8.2 %collective-permute-done.16 = bf16[32,5120]{1,0:T(8,128)(2,1)S(1)} collective-permute-done((bf16[32,5120]{1,0:T(8,128)(2,1)S(1)}, bf16[32,5120]{1,0:T(8,128)(2,1)S(1)}, u32[]{:S(2)}, u32[]{:S(2)}) %collective-permute-start.16) | collective-permute-done | bytes 327712 | tf_op jit(solution)/shard_map/ppermute | solution.py:224
  330.4 6.4 %collective-permute-done.19 = bf16[32,5120]{1,0:T(8,128)(2,1)S(1)} collective-permute-done((bf16[32,5120]{1,0:T(8,128)(2,1)S(1)}, bf16[32,5120]{1,0:T(8,128)(2,1)S(1)}, u32[]{:S(2)}, u32[]{:S(2)}) %collective-permute-start.19) | collective-permute-done | bytes 327712 | tf_op jit(solution)/shard_map/ppermute | solution.py:224
  336.9 1.1 maximum_bitcast_fusion
  (100 shorter events, 13.0 us)
Async XLA Ops:
  0.0 5.5 %copy-start.22 = (s32[8,2]{0,1:T(2,128)S(1)}, s32[8,2]{0,1:T(2,128)}, u32[]{:S(2)}) copy-start(s32[8,2]{0,1:T(2,128)} %param.8) | copy-start | bytes 196
  1.4 82.8 %collective-permute-start = (bf16[512,1280]{1,0:T(8,128)(2,1)S(1)}, bf16[512,1280]{1,0:T(8,128)(2,1)S(1)}, u32[]{:S(2)}, u32[]{:S(2)}) collective-permute-start(bf16[512,1280]{1,0:T(8,128)(2,1)S(1)} %bitcast.280), channel_id=1, source_target_pairs={{0,16},{4,20},{8,24},{12,28},{16,0},{20,4},{24,8},{28,12},{1,17},{... | collective-permute-start | bytes 3932168 | tf_op jit(solution)/shard_map/ppermute | solution.py:186
  5.7 2.1 copy-start
  7.8 6.5 %copy-start.15 = (bf16[3,64,8,1280]{3,2,1,0:T(8,128)(2,1)S(1)}, bf16[3,64,8,1280]{3,2,1,0:T(8,128)(2,1)}, u32[]{:S(2)}) copy-start(bf16[3,64,8,1280]{3,2,1,0:T(8,128)(2,1)} %param.10) | copy-start | bytes 11796484
  9.8 1.0 copy-start.7
  10.8 23.8 %collective-permute-start.1 = (bf16[2,4,96,640]{3,2,1,0:T(8,128)(2,1)S(1)}, bf16[2,4,96,640]{3,2,1,0:T(8,128)(2,1)S(1)}, u32[]{:S(2)}, u32[]{:S(2)}) collective-permute-start(bf16[2,4,96,640]{3,2,1,0:T(8,128)(2,1)S(1)} %get-tuple-element.33), channel_id=1, source_target_pairs={{0,4},{4,0},{8,12},{12,8},{16,20},{20,16},{24,28},{28,24},{1,5},{5... | collective-permute-start | bytes 2949128 | tf_op jit(solution)/shard_map/ppermute | solution.py:186
  12.3 51.6 %collective-permute-start.2 = (bf16[2,4,96,640]{3,2,1,0:T(8,128)(2,1)S(1)}, bf16[2,4,96,640]{3,2,1,0:T(8,128)(2,1)S(1)}, u32[]{:S(2)}, u32[]{:S(2)}) collective-permute-start(bf16[2,4,96,640]{3,2,1,0:T(8,128)(2,1)S(1)} %get-tuple-element.34), channel_id=1, source_target_pairs={{0,8},{4,12},{8,0},{12,4},{16,24},{20,28},{24,16},{28,20},{1,9},{5... | collective-permute-start | bytes 2949128 | tf_op jit(solution)/shard_map/ppermute | solution.py:186
  13.9 69.3 %collective-permute-start.3 = (bf16[2,4,96,640]{3,2,1,0:T(8,128)(2,1)S(1)}, bf16[2,4,96,640]{3,2,1,0:T(8,128)(2,1)S(1)}, u32[]{:S(2)}, u32[]{:S(2)}) collective-permute-start(bf16[2,4,96,640]{3,2,1,0:T(8,128)(2,1)S(1)} %get-tuple-element.35), channel_id=1, source_target_pairs={{0,12},{4,8},{8,4},{12,0},{16,28},{20,24},{24,20},{28,16},{1,13},{... | collective-permute-start | bytes 2949128 | tf_op jit(solution)/shard_map/ppermute | solution.py:186
  34.6 1.0 copy-start.9
  64.0 1.0 copy-start.11
  83.3 1.0 copy-start.13
  84.2 1.1 copy-start.2
  84.2 5.7 %copy-start.23 = (s32[8,2]{0,1:T(2,128)S(1)}, s32[8,2]{0,1:T(2,128)}, u32[]{:S(2)}) copy-start(s32[8,2]{0,1:T(2,128)} %param.9) | copy-start | bytes 196
  85.3 93.8 %all-to-all-start = ((bf16[8,3,4,16,1280]{4,3,2,1,0:T(8,128)(2,1)}), bf16[8,3,4,16,1280]{4,3,2,1,0:T(8,128)(2,1)}, u32[]{:S(2)}, u32[]{:S(2)}) async-start(bf16[8,3,4,16,1280]{4,3,2,1,0:T(8,128)(2,1)} %bitcast.283), calls=%async_computation | async-start | bytes 7864320 | tf_op jit(solution)/shard_map/all_to_all | solution.py:207
  90.2 1.3 copy-start.3
  91.5 1.2 copy-start.8
  92.7 1.2 copy-start.10
  93.9 1.2 copy-start.12
  95.1 1.2 copy-start.14
  106.3 2.1 copy-start.1
  111.6 1.0 copy-start.5
  112.6 83.6 %collective-permute-start.5 = (bf16[2,4,96,640]{3,2,1,0:T(8,128)(2,1)}, bf16[2,4,96,640]{3,2,1,0:T(8,128)(2,1)}, u32[]{:S(2)}, u32[]{:S(2)}) collective-permute-start(bf16[2,4,96,640]{3,2,1,0:T(8,128)(2,1)} %get-tuple-element.45), channel_id=1, source_target_pairs={{0,4},{4,0},{8,12},{12,8},{16,20},{20,16},{24,28},{28,24},{1,5},{5... | collective-permute-start | bytes 2949128 | tf_op jit(solution)/shard_map/ppermute | solution.py:186
  114.6 81.6 %collective-permute-start.6 = (bf16[2,4,96,640]{3,2,1,0:T(8,128)(2,1)}, bf16[2,4,96,640]{3,2,1,0:T(8,128)(2,1)}, u32[]{:S(2)}, u32[]{:S(2)}) collective-permute-start(bf16[2,4,96,640]{3,2,1,0:T(8,128)(2,1)} %get-tuple-element.46), channel_id=1, source_target_pairs={{0,8},{4,12},{8,0},{12,4},{16,24},{20,28},{24,16},{28,20},{1,9},{5... | collective-permute-start | bytes 2949128 | tf_op jit(solution)/shard_map/ppermute | solution.py:186
  116.0 99.7 %collective-permute-start.7 = (bf16[2,4,96,640]{3,2,1,0:T(8,128)(2,1)}, bf16[2,4,96,640]{3,2,1,0:T(8,128)(2,1)}, u32[]{:S(2)}, u32[]{:S(2)}) collective-permute-start(bf16[2,4,96,640]{3,2,1,0:T(8,128)(2,1)} %get-tuple-element.47), channel_id=1, source_target_pairs={{0,12},{4,8},{8,4},{12,0},{16,28},{20,24},{24,20},{28,16},{1,13},{... | collective-permute-start | bytes 2949128 | tf_op jit(solution)/shard_map/ppermute | solution.py:186
  117.0 110.3 %collective-permute-start.4 = (bf16[4,656,128]{2,1,0:T(8,128)(2,1)}, bf16[4,656,128]{2,1,0:T(8,128)(2,1)S(1)}, u32[]{:S(2)}, u32[]{:S(2)}) collective-permute-start(bf16[4,656,128]{2,1,0:T(8,128)(2,1)} %fusion.14), channel_id=1, source_target_pairs={{0,16},{4,20},{8,24},{12,28},{16,0},{20,4},{24,8},{28,12},{1,17},{... | collective-permute-start | bytes 2015240 | tf_op jit(solution)/shard_map/ppermute | solution.py:186
  191.7 24.0 %copy-start.6 = (bf16[2,4,96,640]{3,2,1,0:T(8,128)(2,1)S(1)}, bf16[2,4,96,640]{3,2,1,0:T(8,128)(2,1)}, u32[]{:S(2)}) copy-start(bf16[2,4,96,640]{3,2,1,0:T(8,128)(2,1)} %copy-done.5) | copy-start | bytes 2949124
  191.7 67.3 %all-to-all-start.1 = ((bf16[8,4,16,1280]{3,2,1,0:T(8,128)(2,1)}), bf16[8,4,16,1280]{3,2,1,0:T(8,128)(2,1)}, u32[]{:S(2)}, u32[]{:S(2)}) async-start(bf16[8,4,16,1280]{3,2,1,0:T(8,128)(2,1)} %shard_map.66), calls=%async_computation.1 | async-start | bytes 2621440 | tf_op jit(solution)/shard_map/all_to_all | solution.py:236
  215.7 1.3 copy-start.4
  227.4 6.8 %copy-start.21 = (bf16[1,640,128]{2,1,0:T(8,128)(2,1)S(1)}, bf16[1,640,128]{2,1,0:T(8,128)(2,1)}, u32[]{:S(2)}) copy-start(bf16[1,640,128]{2,1,0:T(8,128)(2,1)} %get-tuple-element.82) | copy-start | bytes 491524
  228.2 30.4 %collective-permute-start.8 = (bf16[656,128]{1,0:T(8,128)(2,1)S(1)}, bf16[656,128]{1,0:T(8,128)(2,1)S(1)}, u32[]{:S(2)}, u32[]{:S(2)}) collective-permute-start(bf16[656,128]{1,0:T(8,128)(2,1)S(1)} %get-tuple-element.75), channel_id=1, source_target_pairs={{0,16},{4,20},{8,24},{12,28},{16,0},{20,4},{24,8},{28,12},{1,17},{... | collective-permute-start | bytes 503816 | tf_op jit(solution)/shard_map/ppermute | solution.py:186
  228.2 39.7 %collective-permute-start.11 = (bf16[656,128]{1,0:T(8,128)(2,1)}, bf16[656,128]{1,0:T(8,128)(2,1)}, u32[]{:S(2)}, u32[]{:S(2)}) collective-permute-start(bf16[656,128]{1,0:T(8,128)(2,1)} %get-tuple-element.77), channel_id=1, source_target_pairs={{0,16},{4,20},{8,24},{12,28},{16,0},{20,4},{24,8},{28,12},{1,17},{... | collective-permute-start | bytes 503816 | tf_op jit(solution)/shard_map/ppermute | solution.py:186
  231.1 49.7 %collective-permute-start.14 = (bf16[656,128]{1,0:T(8,128)(2,1)}, bf16[656,128]{1,0:T(8,128)(2,1)}, u32[]{:S(2)}, u32[]{:S(2)}) collective-permute-start(bf16[656,128]{1,0:T(8,128)(2,1)} %get-tuple-element.76), channel_id=1, source_target_pairs={{0,16},{4,20},{8,24},{12,28},{16,0},{20,4},{24,8},{28,12},{1,17},{... | collective-permute-start | bytes 503816 | tf_op jit(solution)/shard_map/ppermute | solution.py:186
  231.1 72.7 %collective-permute-start.17 = (bf16[656,128]{1,0:T(8,128)(2,1)}, bf16[656,128]{1,0:T(8,128)(2,1)}, u32[]{:S(2)}, u32[]{:S(2)}) collective-permute-start(bf16[656,128]{1,0:T(8,128)(2,1)} %get-tuple-element.78), channel_id=1, source_target_pairs={{0,16},{4,20},{8,24},{12,28},{16,0},{20,4},{24,8},{28,12},{1,17},{... | collective-permute-start | bytes 503816 | tf_op jit(solution)/shard_map/ppermute | solution.py:186
  234.1 0.9 copy-start.20
  267.8 2.6 copy-start.19
  270.4 2.4 collective-permute-start.9
  280.8 4.9 %copy-start.18 = (bf16[1,640,128]{2,1,0:T(8,128)(2,1)S(1)}, bf16[1,640,128]{2,1,0:T(8,128)(2,1)}, u32[]{:S(2)}) copy-start(bf16[1,640,128]{2,1,0:T(8,128)(2,1)} %get-tuple-element.84) | copy-start | bytes 491524
  283.3 10.1 %collective-permute-start.10 = (bf16[32,5120]{1,0:T(8,128)(2,1)}, bf16[32,5120]{1,0:T(8,128)(2,1)}, u32[]{:S(2)}, u32[]{:S(2)}) collective-permute-start(bf16[32,5120]{1,0:T(8,128)(2,1)} %dynamic-slice_bitcast_fusion.7), channel_id=1, source_target_pairs={{0,2},{1,3},{2,0},{3,1},{4,6},{5,7},{6,4},{7,5},{8,10},{9,11},{10,... | collective-permute-start | bytes 983048 | tf_op jit(solution)/shard_map/ppermute | solution.py:224
  285.7 9.5 %collective-permute-start.12 = (bf16[2,32,5120]{2,1,0:T(8,128)(2,1)}, bf16[2,32,5120]{2,1,0:T(8,128)(2,1)}, u32[]{:S(2)}, u32[]{:S(2)}) collective-permute-start(bf16[2,32,5120]{2,1,0:T(8,128)(2,1)} %dynamic-slice_bitcast_fusion.2), channel_id=1, source_target_pairs={{0,1},{1,0},{2,3},{3,2},{4,5},{5,4},{6,7},{7,6},{8,9},{9,8},{10,11... | collective-permute-start | bytes 1966088 | tf_op jit(solution)/shard_map/ppermute | solution.py:217
  303.0 5.0 %copy-start.17 = (f32[5,128,128]{2,1,0:T(8,128)S(1)}, f32[5,128,128]{2,1,0:T(8,128)}, u32[]{:S(2)}) copy-start(f32[5,128,128]{2,1,0:T(8,128)} %get-tuple-element.103) | copy-start | bytes 983044
  305.6 13.0 %collective-permute-start.13 = (bf16[32,5120]{1,0:T(8,128)(2,1)}, bf16[32,5120]{1,0:T(8,128)(2,1)}, u32[]{:S(2)}, u32[]{:S(2)}) collective-permute-start(bf16[32,5120]{1,0:T(8,128)(2,1)} %dynamic-slice_bitcast_fusion.6), channel_id=1, source_target_pairs={{0,2},{1,3},{2,0},{3,1},{4,6},{5,7},{6,4},{7,5},{8,10},{9,11},{10,... | collective-permute-start | bytes 983048 | tf_op jit(solution)/shard_map/ppermute | solution.py:224
  308.0 2.4 collective-permute-start.15
  318.4 2.2 collective-permute-start.18
  319.7 10.6 %collective-permute-start.16 = (bf16[32,5120]{1,0:T(8,128)(2,1)S(1)}, bf16[32,5120]{1,0:T(8,128)(2,1)S(1)}, u32[]{:S(2)}, u32[]{:S(2)}) collective-permute-start(bf16[32,5120]{1,0:T(8,128)(2,1)S(1)} %dynamic-slice_bitcast_fusion.5), channel_id=1, source_target_pairs={{0,2},{1,3},{2,0},{3,1},{4,6},{5,7},{6,4},{7,5},{8,10},{9,11},{10,... | collective-permute-start | bytes 983048 | tf_op jit(solution)/shard_map/ppermute | solution.py:224
  320.7 16.1 %copy-start.16 = (bf16[32,5120]{1,0:T(8,128)(2,1)S(1)}, bf16[32,5120]{1,0:T(8,128)(2,1)}, u32[]{:S(2)}) copy-start(bf16[32,5120]{1,0:T(8,128)(2,1)} %fusion.27) | copy-start | bytes 983044
  320.8 16.0 %collective-permute-start.19 = (bf16[32,5120]{1,0:T(8,128)(2,1)S(1)}, bf16[32,5120]{1,0:T(8,128)(2,1)S(1)}, u32[]{:S(2)}, u32[]{:S(2)}) collective-permute-start(bf16[32,5120]{1,0:T(8,128)(2,1)S(1)} %dynamic-slice_bitcast_fusion.4), channel_id=1, source_target_pairs={{0,2},{1,3},{2,0},{3,1},{4,6},{5,7},{6,4},{7,5},{8,10},{9,11},{10,... | collective-permute-start | bytes 983048 | tf_op jit(solution)/shard_map/ppermute | solution.py:224

commit v2 on v1

--- a/solution.py
+++ b/solution.py
@@ -10,7 +10,7 @@
 HEAD_DIM = 128
 TILE_ROWS = 16
 HEAD_GROUPS = 2
-VMEM_BYTES = 24 * 1024 * 1024
+VMEM_BYTES = 48 * 1024 * 1024
 
 
 def after(block, *before):
@@ -95,7 +95,7 @@
     )(live, own, far, *banks)
 
 
-def frame_kernel(frames_here, token_ref, out_ref):
+def frame_kernel(frames_here, query_ref, token_ref, out_ref):
     scale = HEAD_DIM ** (-0.5)
     pieces, _, parts, rows, _ = token_ref.shape
     size = pieces * rows
@@ -104,8 +104,8 @@
     same_spot = query_spot == key_spot
     for part in range(parts):
         queries, keys, values = (
-            jnp.concatenate([token_ref[piece, which, part] for piece in range(pieces)], axis=0)
-            for which in range(3)
+            jnp.concatenate([source[piece, which, part] for piece in range(pieces)], axis=0)
+            for source, which in ((query_ref, 0), (token_ref, 0), (token_ref, 1))
         )
         scores = lax.dot_general(
             queries, keys, (((1,), (1,)), ((), ())), preferred_element_type=jnp.float32
@@ -119,12 +119,12 @@
             out_ref[piece, part] = gathered[piece * rows : (piece + 1) * rows]
 
 
-def attend_frames(frames_here, tokens):
-    pieces, _, parts, rows, width = tokens.shape
+def attend_frames(frames_here, *tokens):
+    pieces, _, parts, rows, width = tokens[0].shape
     return pl.pallas_call(
         functools.partial(frame_kernel, frames_here),
         grid=(width // HEAD_DIM,),
-        in_specs=[pl.BlockSpec((pieces, 3, parts, rows, HEAD_DIM), lambda h: (0, 0, 0, 0, h))],
+        in_specs=[pl.BlockSpec((*block.shape[:4], HEAD_DIM), lambda h: (0, 0, 0, 0, h)) for block in tokens],
         out_specs=pl.BlockSpec((pieces, parts, rows, HEAD_DIM), lambda h: (0, 0, 0, h)),
         out_shape=jax.ShapeDtypeStruct((pieces, parts, rows, width), jnp.bfloat16),
         compiler_params=pltpu.CompilerParams(vmem_limit_bytes=VMEM_BYTES),
@@ -133,7 +133,7 @@
             bytes_accessed=8 * pieces * parts * rows * width,
             transcendentals=parts * (pieces * rows) ** 2 * width // HEAD_DIM,
         ),
-    )(tokens)
+    )(*tokens)
 
 
 def listed_kernel(place_ref, slots_ref, *refs):
@@ -204,7 +204,10 @@
     banks = [banks_of(0)]
     tokens = frame_tokens.reshape(3, head_groups, parts, across, spots, frames_here, width)
     tokens = tokens.transpose(1, 3, 0, 2, 4, 5, 6).reshape(shards, 3, parts, tile, width)
-    tokens = lax.all_to_all(after(tokens, far, *banks[0]), "frames", 0, 0, tiled=True)
+    tokens = [
+        lax.all_to_all(after(tokens[:, :1], far, *banks[0][:-1]), "frames", 0, 0, tiled=True),
+        lax.all_to_all(after(tokens[:, 1:], far, *banks[0]), "frames", 0, 0, tiled=True),
+    ]
     live = jnp.stack([slot_live[place], slot_live[place ^ half]])
 
     place_heads = lax.axis_index("heads")
@@ -232,7 +235,7 @@
         if group < groups - 1:
             banks.append(banks_of(group + 1, far_level))
         if group == 0:
-            frame_parts = attend_frames(frames_here, after(tokens, far_level))
+            frame_parts = attend_frames(frames_here, after(tokens[0], far_level), tokens[1])
             back = lax.all_to_all(frame_parts, "frames", 0, 0, tiled=True)
             live = after(live, frame_parts)
         message = jnp.concatenate([far_out, *in_three(far_level)], axis=1)

time: 339 us -> 353 us (1.041)
  starting transfers between devices: 34 us -> 43.9 us
  waiting for transfers between devices: 189 us -> 194 us
    ppermute x12, waiting for transfers between devices: 106 us -> 139 us  [swap(): return lax.ppermute(block, 'frames', [(a, a ^ step) for a in range(shards)])]
    all_to_all x1 -> x2, waiting for transfers between devices: 58.4 us -> 29.6 us  [the longest x1 29.6 us: local(): lax.all_to_all(after(tokens[:, 1:], far, *banks[0]), 'frames', 0, 0, tile...]
    all_to_all x1 -> x2, starting transfers between devices: 4.6 us -> 11.3 us  [the longest x1 5.77 us: local(): lax.all_to_all(after(tokens[:, :1], far, *banks[0][:-1]), 'frames', 0, 0,...]
    unnamed x51 -> x55, local copies, waits for them, and re-layouts: 18.6 us -> 13.3 us
    slice x0 -> x2, local copies, waits for them, and re-layouts: none -> 4.82 us  [the longest x1 3.5 us: local(): tokens[:, 1:]]
    pallas_call x2, Pallas kernels: 5.19 us -> 9.46 us  [listed_banks(): pl.pallas_call(listed_kernel, grid_spec=pltpu.PrefetchScalarGridSpec(num_...]
  transfers between devices with their start and end apart: 22 -> 23, of which waited for: 12 -> 12; matrix products, arithmetic and copies ran while one was open for 16% -> 15% of each run, Pallas kernels for 11% -> 12%
where the time goes in v2:
time: 353 us; the launch traced here: 352 us
  waiting for transfers between devices  194 us (55%)
  starting transfers between devices  43.9 us (12%)
  Pallas kernels  41.3 us (12%)
  local copies, waits for them, and re-layouts  31.9 us (9%)
  matrix products  26.6 us (8%)
  other arithmetic  13.7 us (4%)
    ppermute x12, waiting for transfers between devices, swap(): return lax.ppermute(block, 'frames', [(a, a ^ step) for a in range(shards)])  139 us
    all_to_all x1, waiting for transfers between devices, local(): lax.all_to_all(after(tokens[:, 1:], far, *banks[0]), 'frames', 0, 0, tile...  29.6 us
    dot_general x4, matrix products, local(): lax.dot_general(after(combined, *summed[-1:]), out_weight, (((0,), (0,)),...  26.6 us
    ppermute x12, starting transfers between devices, swap(): return lax.ppermute(block, 'frames', [(a, a ^ step) for a in range(shards)])  22.5 us
    ppermute x4, waiting for transfers between devices, scatter_chips(): lax.ppermute(give, 'heads', [(h, (h + 2 * step) % head_groups) for h in r...  22.3 us
    pallas_call x2, Pallas kernels, attend_bank(): pl.pallas_call(functools.partial(bank_kernel, len(banks)), grid=(heads,),...  20.1 us
    unnamed x55, local copies, waits for them, and re-layouts  13.3 us
    pallas_call x1, Pallas kernels, attend_frames(): pl.pallas_call(functools.partial(frame_kernel, frames_here), grid=(width...  11.7 us
  transfers between devices with their start and end apart: 23, of which 12 were waited for; matrix products, arithmetic and copies ran while one was open for 15% of the time, Pallas kernels for 12%

profile of v2, /device:TPU:0, one launch (start us, length us, event | category | flops | bytes accessed | tf_op | source)
XLA Modules:
  0.0 351.5 jit_solution(9656291106538164473)
XLA Ops:
  0.0 1.4 copy.22
  1.4 4.1 %collective-permute-start = (bf16[512,1280]{1,0:T(8,128)(2,1)S(1)}, bf16[512,1280]{1,0:T(8,128)(2,1)}, u32[]{:S(2)}, u32[]{:S(2)}) collective-permute-start(bf16[512,1280]{1,0:T(8,128)(2,1)S(1)} %bitcast.297), channel_id=1, source_target_pairs={{0,16},{4,20},{8,24},{12,28},{16,0},{20,4},{24,8},{28,12},{1,17},{... | collective-permute-start | bytes 3932168 | tf_op jit(solution)/shard_map/ppermute | solution.py:186
  5.7 4.3 %shard_map.64 = (bf16[2,4,96,640]{3,2,1,0:T(8,128)(2,1)S(1)}, bf16[2,4,96,640]{3,2,1,0:T(8,128)(2,1)S(1)}, bf16[2,4,96,640]{3,2,1,0:T(8,128)(2,1)S(1)}, bf16[2,4,96,640]{3,2,1,0:T(8,128)(2,1)S(1)}) custom-call(s32[1]{0:T(128)} %bitcast.4.place_ref, s32[16]{0:T(128)S(1)} %reshape.348.slots_ref, bf16[2,8,96,1280]{3,2,1,0:T(8,128)(2,1)} %refs_3_.3, ...), custom_call_target="tpu_custom_call" | custom-call | bytes 7864320 | tf_op jit(solution)/shard_map/pallas_call | solution.py:156
  10.0 1.6 collective-permute-start.1
  11.6 1.6 collective-permute-start.2
  13.7 1.3 slice.276
  15.0 18.3 %collective-permute-done.1.refs_1_ = bf16[2,4,96,640]{3,2,1,0:T(8,128)(2,1)S(1)} collective-permute-done((bf16[2,4,96,640]{3,2,1,0:T(8,128)(2,1)S(1)}, bf16[2,4,96,640]{3,2,1,0:T(8,128)(2,1)S(1)}, u32[]{:S(2)}, u32[]{:S(2)}) %collective-permute-start.1) | collective-permute-done | bytes 983072 | tf_op jit(solution)/shard_map/ppermute | solution.py:186
  33.3 1.0 copy-done.8
  34.3 20.4 %collective-permute-done.2.refs_2_ = bf16[2,4,96,640]{3,2,1,0:T(8,128)(2,1)S(1)} collective-permute-done((bf16[2,4,96,640]{3,2,1,0:T(8,128)(2,1)S(1)}, bf16[2,4,96,640]{3,2,1,0:T(8,128)(2,1)S(1)}, u32[]{:S(2)}, u32[]{:S(2)}) %collective-permute-start.2) | collective-permute-done | bytes 983072 | tf_op jit(solution)/shard_map/ppermute | solution.py:186
  54.7 0.9 copy-done.10
  55.6 6.9 %collective-permute-done.far_ref = bf16[512,1280]{1,0:T(8,128)(2,1)} collective-permute-done((bf16[512,1280]{1,0:T(8,128)(2,1)S(1)}, bf16[512,1280]{1,0:T(8,128)(2,1)}, u32[]{:S(2)}, u32[]{:S(2)}) %collective-permute-start) | collective-permute-done | bytes 1310752 | tf_op jit(solution)/shard_map/ppermute | solution.py:186
  62.5 5.8 %all-to-all-start = ((bf16[8,1,4,16,1280]{4,3,2,1,0:T(8,128)(2,1)}), bf16[8,1,4,16,1280]{4,3,2,1,0:T(8,128)(2,1)S(1)}, u32[]{:S(2)}, u32[]{:S(2)}) async-start(bf16[8,1,4,16,1280]{4,3,2,1,0:T(8,128)(2,1)} %slice.276), calls=%async_computation | async-start | bytes 2621440 | tf_op jit(solution)/shard_map/all_to_all | solution.py:208
  68.3 2.9 collective-permute-start.3
  71.2 3.5 slice.277
  74.7 39.1 %collective-permute-done.3.refs_3_ = bf16[2,4,96,640]{3,2,1,0:T(8,128)(2,1)S(1)} collective-permute-done((bf16[2,4,96,640]{3,2,1,0:T(8,128)(2,1)S(1)}, bf16[2,4,96,640]{3,2,1,0:T(8,128)(2,1)S(1)}, u32[]{:S(2)}, u32[]{:S(2)}) %collective-permute-start.3) | collective-permute-done | bytes 983072 | tf_op jit(solution)/shard_map/ppermute | solution.py:186
  113.8 1.0 copy-done.12
  114.8 1.1 copy-done
  115.9 5.5 %all-to-all-start.1 = ((bf16[8,2,4,16,1280]{4,3,2,1,0:T(8,128)(2,1)}), bf16[8,2,4,16,1280]{4,3,2,1,0:T(8,128)(2,1)S(1)}, u32[]{:S(2)}, u32[]{:S(2)}) async-start(bf16[8,2,4,16,1280]{4,3,2,1,0:T(8,128)(2,1)} %slice.277), calls=%async_computation.1 | async-start | bytes 5242880 | tf_op jit(solution)/shard_map/all_to_all | solution.py:209
  121.6 1.2 copy-done.7
  122.8 1.2 copy-done.9
  124.1 1.2 copy-done.11
  125.3 1.2 copy-done.13
  126.5 9.9 %shard_map.65 = (bf16[4,640,128]{2,1,0:T(8,128)(2,1)S(1)}, f32[4,5,128]{2,1,0:T(8,128)S(1)}, bf16[4,640,128]{2,1,0:T(8,128)(2,1)S(1)}, f32[4,5,128]{2,1,0:T(8,128)S(1)}) custom-call(s32[2,2]{1,0:T(2,128)S(1)} %pad_add_fusion.live_ref, bf16[512,1280]{1,0:T(8,128)(2,1)} %bitcast.298, bf16[512,1280]{1,0:T(8,128)(2,1)} %collective-permute-done.far_ref, ...), custom_call_target="tpu_custom_call" | custom-call | flops 8053063680 | bytes 6553600 | tf_op jit(solution)/shard_map/pallas_call | solution.py:82
  137.4 5.2 %shard_map.67 = (bf16[2,4,96,640]{3,2,1,0:T(8,128)(2,1)S(1)}, bf16[2,4,96,640]{3,2,1,0:T(8,128)(2,1)}, bf16[2,4,96,640]{3,2,1,0:T(8,128)(2,1)}, bf16[2,4,96,640]{3,2,1,0:T(8,128)(2,1)}) custom-call(s32[1]{0:T(128)} %bitcast.4.place_ref, s32[16]{0:T(128)S(1)} %reshape.351.slots_ref, bf16[2,8,96,1280]{3,2,1,0:T(8,128)(2,1)} %refs_3_.3, ...), custom_call_target="tpu_custom_call" | custom-call | bytes 7864320 | tf_op jit(solution)/shard_map/pallas_call | solution.py:156
  142.6 1.0 copy-done.4
  143.5 2.0 collective-permute-start.5
  145.5 1.5 collective-permute-start.6
  147.0 2.0 fusion.14
  149.0 2.9 collective-permute-start.4
  152.8 29.6 %all-to-all-done.1.token_ref = bf16[8,2,4,16,1280]{4,3,2,1,0:T(8,128)(2,1)S(1)} async-done(((bf16[8,2,4,16,1280]{4,3,2,1,0:T(8,128)(2,1)}), bf16[8,2,4,16,1280]{4,3,2,1,0:T(8,128)(2,1)S(1)}, u32[]{:S(2)}, u32[]{:S(2)}) %all-to-all-start.1) | async-done | bytes 2621472 | tf_op jit(solution)/shard_map/all_to_all | solution.py:209
  182.4 1.3 copy-done.1
  183.7 11.7 %shard_map.66 = bf16[8,4,16,1280]{3,2,1,0:T(8,128)(2,1)S(1)} custom-call(bf16[8,1,4,16,1280]{4,3,2,1,0:T(8,128)(2,1)S(1)} %copy-done.1, bf16[8,2,4,16,1280]{4,3,2,1,0:T(8,128)(2,1)S(1)} %all-to-all-done.1.token_ref), custom_call_target="tpu_custom_call" | custom-call | flops 1342177280 | bytes 5242880 | tf_op jit(solution)/shard_map/pallas_call | solution.py:124
  195.4 1.1 copy-done.2
  196.5 4.4 %all-to-all-start.2 = ((bf16[8,4,16,1280]{3,2,1,0:T(8,128)(2,1)}), bf16[8,4,16,1280]{3,2,1,0:T(8,128)(2,1)}, u32[]{:S(2)}, u32[]{:S(2)}) async-start(bf16[8,4,16,1280]{3,2,1,0:T(8,128)(2,1)} %copy-done.2), calls=%async_computation.2 | async-start | bytes 2621440 | tf_op jit(solution)/shard_map/all_to_all | solution.py:239
  200.9 28.2 %collective-permute-done.7.refs_3_ = bf16[2,4,96,640]{3,2,1,0:T(8,128)(2,1)} collective-permute-done((bf16[2,4,96,640]{3,2,1,0:T(8,128)(2,1)}, bf16[2,4,96,640]{3,2,1,0:T(8,128)(2,1)}, u32[]{:S(2)}, u32[]{:S(2)}) %collective-permute-start.7) | collective-permute-done | bytes 983072 | tf_op jit(solution)/shard_map/ppermute | solution.py:186
  229.2 10.2 %shard_map.68 = (bf16[4,640,128]{2,1,0:T(8,128)(2,1)S(1)}, f32[4,5,128]{2,1,0:T(8,128)S(1)}, bf16[4,640,128]{2,1,0:T(8,128)(2,1)S(1)}, f32[4,5,128]{2,1,0:T(8,128)S(1)}) custom-call(s32[2,2]{1,0:T(2,128)S(1)} %pad_add_fusion.live_ref, bf16[512,1280]{1,0:T(8,128)(2,1)} %bitcast.299, bf16[512,1280]{1,0:T(8,128)(2,1)} %collective-permute-done.far_ref, ...), custom_call_target="tpu_custom_call" | custom-call | flops 8053063680 | bytes 6553600 | tf_op jit(solution)/shard_map/pallas_call | solution.py:82
  240.2 2.9 collective-permute-start.14
  243.2 2.9 collective-permute-start.8
  247.7 1.2 fusion.60
  249.1 0.9 fusion.32
  250.1 26.2 %collective-permute-done.8 = bf16[656,128]{1,0:T(8,128)(2,1)S(1)} collective-permute-done((bf16[656,128]{1,0:T(8,128)(2,1)S(1)}, bf16[656,128]{1,0:T(8,128)(2,1)S(1)}, u32[]{:S(2)}, u32[]{:S(2)}) %collective-permute-start.8) | collective-permute-done | bytes 167968 | tf_op jit(solution)/shard_map/ppermute | solution.py:186
  276.6 2.2 fusion.59
  278.8 6.6 %convolution_convert_fusion.3 = bf16[128,5120]{1,0:T(8,128)(2,1)S(1)} fusion(bf16[1280,5120]{1,0:T(8,128)(2,1)} %param.11, f32[1280,128]{0,1:T(8,128)S(1)} %copy.26, bf16[128,1280]{1,0:T(8,128)(2,1)S(1)} %bitcast.295), kind=kOutput, calls=%fused_computation.3 | convolution fusion | flops 1678868480 | bytes 15400960 | tf_op jit(solution)/shard_map/dot_general | solution.py:273
  285.5 0.9 slice.246
  287.2 0.9 dynamic-slice_bitcast_fusion.3
  288.5 2.0 collective-permute-done.9
  290.5 1.2 fusion.11
  291.8 6.7 %convolution_convert_fusion.2 = bf16[128,5120]{1,0:T(8,128)(2,1)S(1)} fusion(bf16[1280,128]{0,1:T(8,128)(2,1)S(1)} %fusion.26, bf16[1280,5120]{1,0:T(8,128)(2,1)} %param.11), kind=kOutput, calls=%fused_computation.2 | convolution fusion | flops 1678376960 | bytes 14745600 | tf_op jit(solution)/shard_map/dot_general | solution.py:273
  298.5 0.9 slice.260
  300.8 1.6 collective-permute-start.10
  302.5 8.4 %collective-permute-done.10 = bf16[32,5120]{1,0:T(8,128)(2,1)S(1)} collective-permute-done((bf16[32,5120]{1,0:T(8,128)(2,1)S(1)}, bf16[32,5120]{1,0:T(8,128)(2,1)S(1)}, u32[]{:S(2)}, u32[]{:S(2)}) %collective-permute-start.10) | collective-permute-done | bytes 327712 | tf_op jit(solution)/shard_map/ppermute | solution.py:227
  310.9 0.8 fusion.27
  311.9 6.7 %convolution_convert_fusion.1 = bf16[128,5120]{1,0:T(8,128)(2,1)S(1)} fusion(bf16[1280,128]{0,1:T(8,128)(2,1)S(1)} %fusion.23, bf16[1280,5120]{1,0:T(8,128)(2,1)} %param.11), kind=kOutput, calls=%fused_computation.1 | convolution fusion | flops 1678376960 | bytes 14745600 | tf_op jit(solution)/shard_map/dot_general | solution.py:273
  318.6 0.9 slice.274
  321.0 0.9 dynamic-slice_bitcast_fusion.1
  322.3 1.5 collective-permute-start.13
  323.8 1.0 fusion.20
  324.9 1.2 fusion.9
  326.1 6.7 %convolution_convert_fusion = bf16[128,5120]{1,0:T(8,128)(2,1)S(1)} fusion(bf16[1280,128]{0,1:T(8,128)(2,1)S(1)} %fusion.20, bf16[1280,5120]{1,0:T(8,128)(2,1)} %param.11), kind=kOutput, calls=%fused_computation | convolution fusion | flops 1678376960 | bytes 14745600 | tf_op jit(solution)/shard_map/dot_general | solution.py:273
  333.3 1.1 collective-permute-start.16
  335.2 1.0 collective-permute-start.19
  336.3 7.6 %collective-permute-done.16 = bf16[32,5120]{1,0:T(8,128)(2,1)S(1)} collective-permute-done((bf16[32,5120]{1,0:T(8,128)(2,1)S(1)}, bf16[32,5120]{1,0:T(8,128)(2,1)S(1)}, u32[]{:S(2)}, u32[]{:S(2)}) %collective-permute-start.16) | collective-permute-done | bytes 327712 | tf_op jit(solution)/shard_map/ppermute | solution.py:227
  344.0 6.3 %collective-permute-done.19 = bf16[32,5120]{1,0:T(8,128)(2,1)S(1)} collective-permute-done((bf16[32,5120]{1,0:T(8,128)(2,1)S(1)}, bf16[32,5120]{1,0:T(8,128)(2,1)S(1)}, u32[]{:S(2)}, u32[]{:S(2)}) %collective-permute-start.19) | collective-permute-done | bytes 327712 | tf_op jit(solution)/shard_map/ppermute | solution.py:227
  350.4 1.1 maximum_bitcast_fusion
  (108 shorter events, 12.1 us)
Async XLA Ops:
  0.0 5.5 %copy-start.24 = (s32[8,2]{0,1:T(2,128)S(1)}, s32[8,2]{0,1:T(2,128)}, u32[]{:S(2)}) copy-start(s32[8,2]{0,1:T(2,128)} %param.8) | copy-start | bytes 196
  1.4 8.6 %copy-start.18 = (bf16[4,4,2,2,8,1280]{5,4,3,2,0,1:T(8,128)(2,1)}, bf16[4,4,2,2,8,1280]{5,4,3,2,0,1:T(8,128)(2,1)S(1)}, u32[]{:S(2)}) copy-start(bf16[4,4,2,2,8,1280]{5,4,3,2,0,1:T(8,128)(2,1)S(1)} %copy.22) | copy-start | bytes 3932164
  1.4 61.1 %collective-permute-start = (bf16[512,1280]{1,0:T(8,128)(2,1)S(1)}, bf16[512,1280]{1,0:T(8,128)(2,1)}, u32[]{:S(2)}, u32[]{:S(2)}) collective-permute-start(bf16[512,1280]{1,0:T(8,128)(2,1)S(1)} %bitcast.297), channel_id=1, source_target_pairs={{0,16},{4,20},{8,24},{12,28},{16,0},{20,4},{24,8},{28,12},{1,17},{... | collective-permute-start | bytes 3932168 | tf_op jit(solution)/shard_map/ppermute | solution.py:186
  5.7 7.5 %copy-start.15 = (bf16[3,64,8,1280]{3,2,1,0:T(8,128)(2,1)S(1)}, bf16[3,64,8,1280]{3,2,1,0:T(8,128)(2,1)}, u32[]{:S(2)}) copy-start(bf16[3,64,8,1280]{3,2,1,0:T(8,128)(2,1)} %param.10) | copy-start | bytes 11796484
  10.0 3.7 %copy-start.6 = (bf16[2,4,96,640]{3,2,1,0:T(8,128)(2,1)}, bf16[2,4,96,640]{3,2,1,0:T(8,128)(2,1)S(1)}, u32[]{:S(2)}) copy-start(bf16[2,4,96,640]{3,2,1,0:T(8,128)(2,1)S(1)} %get-tuple-element.33.refs_0_) | copy-start | bytes 2949124
  10.0 23.3 %collective-permute-start.1 = (bf16[2,4,96,640]{3,2,1,0:T(8,128)(2,1)S(1)}, bf16[2,4,96,640]{3,2,1,0:T(8,128)(2,1)S(1)}, u32[]{:S(2)}, u32[]{:S(2)}) collective-permute-start(bf16[2,4,96,640]{3,2,1,0:T(8,128)(2,1)S(1)} %get-tuple-element.34), channel_id=1, source_target_pairs={{0,4},{4,0},{8,12},{12,8},{16,20},{20,16},{24,28},{28,24},{1,5},{5... | collective-permute-start | bytes 2949128 | tf_op jit(solution)/shard_map/ppermute | solution.py:186
  11.6 43.1 %collective-permute-start.2 = (bf16[2,4,96,640]{3,2,1,0:T(8,128)(2,1)S(1)}, bf16[2,4,96,640]{3,2,1,0:T(8,128)(2,1)S(1)}, u32[]{:S(2)}, u32[]{:S(2)}) collective-permute-start(bf16[2,4,96,640]{3,2,1,0:T(8,128)(2,1)S(1)} %get-tuple-element.35), channel_id=1, source_target_pairs={{0,8},{4,12},{8,0},{12,4},{16,24},{20,28},{24,16},{28,20},{1,9},{5... | collective-permute-start | bytes 2949128 | tf_op jit(solution)/shard_map/ppermute | solution.py:186
  13.7 41.0 %copy-start.14 = (bf16[3,4,4,2,2,8,1280]{6,5,4,2,0,3,1:T(8,128)(2,1)}, bf16[3,4,4,2,2,8,1280]{6,5,4,2,0,3,1:T(8,128)(2,1)S(1)}, u32[]{:S(2)}) copy-start(bf16[3,4,4,2,2,8,1280]{6,5,4,2,0,3,1:T(8,128)(2,1)S(1)} %copy.24) | copy-start | bytes 11796484
  33.3 1.0 copy-start.8
  54.7 0.9 copy-start.10
  62.5 52.3 %all-to-all-start = ((bf16[8,1,4,16,1280]{4,3,2,1,0:T(8,128)(2,1)}), bf16[8,1,4,16,1280]{4,3,2,1,0:T(8,128)(2,1)S(1)}, u32[]{:S(2)}, u32[]{:S(2)}) async-start(bf16[8,1,4,16,1280]{4,3,2,1,0:T(8,128)(2,1)} %slice.276), calls=%async_computation | async-start | bytes 2621440 | tf_op jit(solution)/shard_map/all_to_all | solution.py:208
  68.3 45.6 %collective-permute-start.3 = (bf16[2,4,96,640]{3,2,1,0:T(8,128)(2,1)S(1)}, bf16[2,4,96,640]{3,2,1,0:T(8,128)(2,1)S(1)}, u32[]{:S(2)}, u32[]{:S(2)}) collective-permute-start(bf16[2,4,96,640]{3,2,1,0:T(8,128)(2,1)S(1)} %get-tuple-element.36), channel_id=1, source_target_pairs={{0,12},{4,8},{8,4},{12,0},{16,28},{20,24},{24,20},{28,16},{1,13},{... | collective-permute-start | bytes 2949128 | tf_op jit(solution)/shard_map/ppermute | solution.py:186
  74.7 46.7 %copy-start.25 = (s32[8,2]{0,1:T(2,128)S(1)}, s32[8,2]{0,1:T(2,128)}, u32[]{:S(2)}) copy-start(s32[8,2]{0,1:T(2,128)} %param.9) | copy-start | bytes 196
  113.8 1.0 copy-start.12
  114.8 1.1 copy-start
  115.9 66.5 %all-to-all-start.1 = ((bf16[8,2,4,16,1280]{4,3,2,1,0:T(8,128)(2,1)}), bf16[8,2,4,16,1280]{4,3,2,1,0:T(8,128)(2,1)S(1)}, u32[]{:S(2)}, u32[]{:S(2)}) async-start(bf16[8,2,4,16,1280]{4,3,2,1,0:T(8,128)(2,1)} %slice.277), calls=%async_computation.1 | async-start | bytes 5242880 | tf_op jit(solution)/shard_map/all_to_all | solution.py:209
  121.6 1.2 copy-start.7
  122.8 1.2 copy-start.9
  124.0 1.2 copy-start.11
  125.3 1.2 copy-start.13
  136.4 0.9 copy-start.3
  142.6 1.0 copy-start.4
  143.5 57.4 %collective-permute-start.5 = (bf16[2,4,96,640]{3,2,1,0:T(8,128)(2,1)}, bf16[2,4,96,640]{3,2,1,0:T(8,128)(2,1)}, u32[]{:S(2)}, u32[]{:S(2)}) collective-permute-start(bf16[2,4,96,640]{3,2,1,0:T(8,128)(2,1)} %get-tuple-element.47), channel_id=1, source_target_pairs={{0,4},{4,0},{8,12},{12,8},{16,20},{20,16},{24,28},{28,24},{1,5},{5... | collective-permute-start | bytes 2949128 | tf_op jit(solution)/shard_map/ppermute | solution.py:186
  145.5 55.4 %collective-permute-start.6 = (bf16[2,4,96,640]{3,2,1,0:T(8,128)(2,1)}, bf16[2,4,96,640]{3,2,1,0:T(8,128)(2,1)}, u32[]{:S(2)}, u32[]{:S(2)}) collective-permute-start(bf16[2,4,96,640]{3,2,1,0:T(8,128)(2,1)} %get-tuple-element.48), channel_id=1, source_target_pairs={{0,8},{4,12},{8,0},{12,4},{16,24},{20,28},{24,16},{28,20},{1,9},{5... | collective-permute-start | bytes 2949128 | tf_op jit(solution)/shard_map/ppermute | solution.py:186
  147.0 82.2 %collective-permute-start.7 = (bf16[2,4,96,640]{3,2,1,0:T(8,128)(2,1)}, bf16[2,4,96,640]{3,2,1,0:T(8,128)(2,1)}, u32[]{:S(2)}, u32[]{:S(2)}) collective-permute-start(bf16[2,4,96,640]{3,2,1,0:T(8,128)(2,1)} %get-tuple-element.49), channel_id=1, source_target_pairs={{0,12},{4,8},{8,4},{12,0},{16,28},{20,24},{24,20},{28,16},{1,13},{... | collective-permute-start | bytes 2949128 | tf_op jit(solution)/shard_map/ppermute | solution.py:186
  149.0 97.1 %collective-permute-start.4 = (bf16[4,656,128]{2,1,0:T(8,128)(2,1)}, bf16[4,656,128]{2,1,0:T(8,128)(2,1)}, u32[]{:S(2)}, u32[]{:S(2)}) collective-permute-start(bf16[4,656,128]{2,1,0:T(8,128)(2,1)} %fusion.14), channel_id=1, source_target_pairs={{0,16},{4,20},{8,24},{12,28},{16,0},{20,4},{24,8},{28,12},{1,17},{... | collective-permute-start | bytes 2015240 | tf_op jit(solution)/shard_map/ppermute | solution.py:186
  182.4 1.3 copy-start.1
  195.4 1.1 copy-start.2
  196.5 32.7 %copy-start.5 = (bf16[2,4,96,640]{3,2,1,0:T(8,128)(2,1)S(1)}, bf16[2,4,96,640]{3,2,1,0:T(8,128)(2,1)}, u32[]{:S(2)}) copy-start(bf16[2,4,96,640]{3,2,1,0:T(8,128)(2,1)} %copy-done.4) | copy-start | bytes 2949124
  196.5 80.1 %all-to-all-start.2 = ((bf16[8,4,16,1280]{3,2,1,0:T(8,128)(2,1)}), bf16[8,4,16,1280]{3,2,1,0:T(8,128)(2,1)}, u32[]{:S(2)}, u32[]{:S(2)}) async-start(bf16[8,4,16,1280]{3,2,1,0:T(8,128)(2,1)} %copy-done.2), calls=%async_computation.2 | async-start | bytes 2621440 | tf_op jit(solution)/shard_map/all_to_all | solution.py:239
  239.4 9.5 %copy-start.22 = (bf16[1,640,128]{2,1,0:T(8,128)(2,1)S(1)}, bf16[1,640,128]{2,1,0:T(8,128)(2,1)}, u32[]{:S(2)}) copy-start(bf16[1,640,128]{2,1,0:T(8,128)(2,1)} %get-tuple-element.83) | copy-start | bytes 491524
  239.4 9.5 %copy-start.23 = (bf16[1,640,128]{2,1,0:T(8,128)(2,1)S(1)}, bf16[1,640,128]{2,1,0:T(8,128)(2,1)}, u32[]{:S(2)}) copy-start(bf16[1,640,128]{2,1,0:T(8,128)(2,1)} %get-tuple-element.84) | copy-start | bytes 491524
  240.2 78.3 %collective-permute-start.17 = (bf16[656,128]{1,0:T(8,128)(2,1)}, bf16[656,128]{1,0:T(8,128)(2,1)}, u32[]{:S(2)}, u32[]{:S(2)}) collective-permute-start(bf16[656,128]{1,0:T(8,128)(2,1)} %get-tuple-element.80), channel_id=1, source_target_pairs={{0,16},{4,20},{8,24},{12,28},{16,0},{20,4},{24,8},{28,12},{1,17},{... | collective-permute-start | bytes 503816 | tf_op jit(solution)/shard_map/ppermute | solution.py:186
  240.2 58.2 %collective-permute-start.14 = (bf16[656,128]{1,0:T(8,128)(2,1)}, bf16[656,128]{1,0:T(8,128)(2,1)}, u32[]{:S(2)}, u32[]{:S(2)}) collective-permute-start(bf16[656,128]{1,0:T(8,128)(2,1)} %get-tuple-element.78), channel_id=1, source_target_pairs={{0,16},{4,20},{8,24},{12,28},{16,0},{20,4},{24,8},{28,12},{1,17},{... | collective-permute-start | bytes 503816 | tf_op jit(solution)/shard_map/ppermute | solution.py:186
  243.2 42.3 %collective-permute-start.11 = (bf16[656,128]{1,0:T(8,128)(2,1)}, bf16[656,128]{1,0:T(8,128)(2,1)}, u32[]{:S(2)}, u32[]{:S(2)}) collective-permute-start(bf16[656,128]{1,0:T(8,128)(2,1)} %get-tuple-element.79), channel_id=1, source_target_pairs={{0,16},{4,20},{8,24},{12,28},{16,0},{20,4},{24,8},{28,12},{1,17},{... | collective-permute-start | bytes 503816 | tf_op jit(solution)/shard_map/ppermute | solution.py:186
  243.2 33.0 %collective-permute-start.8 = (bf16[656,128]{1,0:T(8,128)(2,1)S(1)}, bf16[656,128]{1,0:T(8,128)(2,1)S(1)}, u32[]{:S(2)}, u32[]{:S(2)}) collective-permute-start(bf16[656,128]{1,0:T(8,128)(2,1)S(1)} %get-tuple-element.77), channel_id=1, source_target_pairs={{0,16},{4,20},{8,24},{12,28},{16,0},{20,4},{24,8},{28,12},{1,17},{... | collective-permute-start | bytes 503816 | tf_op jit(solution)/shard_map/ppermute | solution.py:186
  247.7 1.4 copy-start.21
  288.1 2.4 collective-permute-start.9
  291.8 8.5 %copy-start.20 = (f32[5,128,128]{2,1,0:T(8,128)S(1)}, f32[5,128,128]{2,1,0:T(8,128)}, u32[]{:S(2)}) copy-start(f32[5,128,128]{2,1,0:T(8,128)} %get-tuple-element.106) | copy-start | bytes 983044
  300.5 1.9 copy-start.17
  300.6 11.1 %collective-permute-start.12 = (bf16[2,32,5120]{2,1,0:T(8,128)(2,1)S(1)}, bf16[2,32,5120]{2,1,0:T(8,128)(2,1)S(1)}, u32[]{:S(2)}, u32[]{:S(2)}) collective-permute-start(bf16[2,32,5120]{2,1,0:T(8,128)(2,1)S(1)} %dynamic-slice_bitcast_fusion.2), channel_id=1, source_target_pairs={{0,1},{1,0},{2,3},{3,2},{4,5},{5,4},{6,7},{7,6},{8,9},{9,8},{10,11... | collective-permute-start | bytes 1966088 | tf_op jit(solution)/shard_map/ppermute | solution.py:220
  300.8 10.1 %collective-permute-start.10 = (bf16[32,5120]{1,0:T(8,128)(2,1)S(1)}, bf16[32,5120]{1,0:T(8,128)(2,1)S(1)}, u32[]{:S(2)}, u32[]{:S(2)}) collective-permute-start(bf16[32,5120]{1,0:T(8,128)(2,1)S(1)} %dynamic-slice_bitcast_fusion.7), channel_id=1, source_target_pairs={{0,2},{1,3},{2,0},{3,1},{4,6},{5,7},{6,4},{7,5},{8,10},{9,11},{10,... | collective-permute-start | bytes 983048 | tf_op jit(solution)/shard_map/ppermute | solution.py:227
  319.5 2.5 copy-start.19
  321.9 2.9 collective-permute-start.15
  322.3 10.9 %collective-permute-start.13 = (bf16[32,5120]{1,0:T(8,128)(2,1)}, bf16[32,5120]{1,0:T(8,128)(2,1)S(1)}, u32[]{:S(2)}, u32[]{:S(2)}) collective-permute-start(bf16[32,5120]{1,0:T(8,128)(2,1)} %dynamic-slice_bitcast_fusion.6), channel_id=1, source_target_pairs={{0,2},{1,3},{2,0},{3,1},{4,6},{5,7},{6,4},{7,5},{8,10},{9,11},{10,... | collective-permute-start | bytes 983048 | tf_op jit(solution)/shard_map/ppermute | solution.py:227
  332.8 2.2 collective-permute-start.18
  333.3 10.6 %collective-permute-start.16 = (bf16[32,5120]{1,0:T(8,128)(2,1)S(1)}, bf16[32,5120]{1,0:T(8,128)(2,1)S(1)}, u32[]{:S(2)}, u32[]{:S(2)}) collective-permute-start(bf16[32,5120]{1,0:T(8,128)(2,1)S(1)} %dynamic-slice_bitcast_fusion.5), channel_id=1, source_target_pairs={{0,2},{1,3},{2,0},{3,1},{4,6},{5,7},{6,4},{7,5},{8,10},{9,11},{10,... | collective-permute-start | bytes 983048 | tf_op jit(solution)/shard_map/ppermute | solution.py:227
  335.2 15.2 %copy-start.16 = (bf16[32,5120]{1,0:T(8,128)(2,1)S(1)}, bf16[32,5120]{1,0:T(8,128)(2,1)}, u32[]{:S(2)}) copy-start(bf16[32,5120]{1,0:T(8,128)(2,1)} %fusion.27) | copy-start | bytes 983044
  335.2 15.0 %collective-permute-start.19 = (bf16[32,5120]{1,0:T(8,128)(2,1)S(1)}, bf16[32,5120]{1,0:T(8,128)(2,1)S(1)}, u32[]{:S(2)}, u32[]{:S(2)}) collective-permute-start(bf16[32,5120]{1,0:T(8,128)(2,1)S(1)} %dynamic-slice_bitcast_fusion.4), channel_id=1, source_target_pairs={{0,2},{1,3},{2,0},{3,1},{4,6},{5,7},{6,4},{7,5},{8,10},{9,11},{10,... | collective-permute-start | bytes 983048 | tf_op jit(solution)/shard_map/ppermute | solution.py:227

commit v3 on v1

--- a/solution.py
+++ b/solution.py
@@ -9,6 +9,7 @@
 
 HEAD_DIM = 128
 TILE_ROWS = 16
+PART_TILE = 32
 HEAD_GROUPS = 2
 VMEM_BYTES = 24 * 1024 * 1024
 
@@ -176,7 +177,7 @@
     shards = lax.axis_size("frames")
     half = shards // 2
     place = lax.axis_index("frames")
-    parts = max(1, spatial * frames_here // (TILE_ROWS * shards))
+    parts = max(1, spatial * frames_here // (PART_TILE * shards))
     across = shards // head_groups
     spots = spatial // (shards * parts)
     tile = spots * frames_here

time: 339 us -> 324 us (0.956)
  matrix products: 26.6 us -> 17.4 us
  waiting for transfers between devices: 189 us -> 198 us
  other arithmetic: 14.9 us -> 8.9 us
  starting transfers between devices: 34 us -> 29.7 us
    dot_general x4 -> x2, matrix products: 26.6 us -> 17.4 us  [local(): lax.dot_general(after(combined, *summed[-1:]), out_weight, (((0,), (0,)),...]
    ppermute x12 -> x10, waiting for transfers between devices: 106 us -> 113 us  [swap(): return lax.ppermute(block, 'frames', [(a, a ^ step) for a in range(shards)])]
    ppermute x4 -> x2, waiting for transfers between devices: 20.9 us -> 24.6 us  [scatter_chips(): lax.ppermute(give, 'heads', [(h, (h + 2 * step) % head_groups) for h in r...]
    convert_element_type x8 -> x4, other arithmetic: 6.88 us -> 3.55 us  [added(): functools.reduce(jnp.add, [wide(block) for block in blocks])]
    ppermute x12 -> x10, starting transfers between devices: 19.8 us -> 16.9 us  [swap(): return lax.ppermute(block, 'frames', [(a, a ^ step) for a in range(shards)])]
    unnamed x51 -> x49, local copies, waits for them, and re-layouts: 18.6 us -> 19.9 us
  transfers between devices with their start and end apart: 22 -> 16, of which waited for: 12 -> 10; matrix products, arithmetic and copies ran while one was open for 16% -> 8% of each run, Pallas kernels for 11% -> 11%
where the time goes in v3:
time: 324 us; the launch traced here: 322 us
  waiting for transfers between devices  198 us (61%)
  Pallas kernels  35.1 us (11%)
  local copies, waits for them, and re-layouts  32.5 us (10%)
  starting transfers between devices  29.7 us (9%)
  matrix products  17.4 us (5%)
  other arithmetic  8.9 us (3%)
    ppermute x10, waiting for transfers between devices, swap(): return lax.ppermute(block, 'frames', [(a, a ^ step) for a in range(shards)])  113 us
    all_to_all x1, waiting for transfers between devices, local(): lax.all_to_all(after(tokens, far, *banks[0]), 'frames', 0, 0, tiled=True)  58.5 us
    ppermute x2, waiting for transfers between devices, scatter_chips(): lax.ppermute(give, 'heads', [(h, (h + 2 * step) % head_groups) for h in r...  24.6 us
    unnamed x49, local copies, waits for them, and re-layouts  19.9 us
    pallas_call x2, Pallas kernels, attend_bank(): pl.pallas_call(functools.partial(bank_kernel, len(banks)), grid=(heads,),...  19.7 us
    dot_general x2, matrix products, local(): lax.dot_general(after(combined, *summed[-1:]), out_weight, (((0,), (0,)),...  17.4 us
    ppermute x10, starting transfers between devices, swap(): return lax.ppermute(block, 'frames', [(a, a ^ step) for a in range(shards)])  16.9 us
    pallas_call x1, Pallas kernels, attend_frames(): pl.pallas_call(functools.partial(frame_kernel, frames_here), grid=(width...  10.2 us
  transfers between devices with their start and end apart: 16, of which 10 were waited for; matrix products, arithmetic and copies ran while one was open for 8% of the time, Pallas kernels for 11%

profile of v3, /device:TPU:0, one launch (start us, length us, event | category | flops | bytes accessed | tf_op | source)
XLA Modules:
  0.0 322.4 jit_solution(4115843881344888044)
XLA Ops:
  0.0 1.4 copy.18
  1.5 4.1 %collective-permute-start = (bf16[512,1280]{1,0:T(8,128)(2,1)S(1)}, bf16[512,1280]{1,0:T(8,128)(2,1)S(1)}, u32[]{:S(2)}, u32[]{:S(2)}) collective-permute-start(bf16[512,1280]{1,0:T(8,128)(2,1)S(1)} %bitcast.144), channel_id=1, source_target_pairs={{0,16},{4,20},{8,24},{12,28},{16,0},{20,4},{24,8},{28,12},{1,17},{... | collective-permute-start | bytes 3932168 | tf_op jit(solution)/shard_map/ppermute | solution.py:187
  5.7 2.1 copy-done
  7.8 1.9 shard_map.64
  9.8 1.0 copy-done.7
  10.8 1.5 collective-permute-start.1
  12.4 1.6 collective-permute-start.2
  14.3 2.1 copy.20
  16.5 18.2 %collective-permute-done.1.refs_1_ = bf16[2,4,96,640]{3,2,1,0:T(8,128)(2,1)S(1)} collective-permute-done((bf16[2,4,96,640]{3,2,1,0:T(8,128)(2,1)S(1)}, bf16[2,4,96,640]{3,2,1,0:T(8,128)(2,1)S(1)}, u32[]{:S(2)}, u32[]{:S(2)}) %collective-permute-start.1) | collective-permute-done | bytes 983072 | tf_op jit(solution)/shard_map/ppermute | solution.py:187
  34.6 1.0 copy-done.9
  35.6 28.4 %collective-permute-done.2.refs_2_ = bf16[2,4,96,640]{3,2,1,0:T(8,128)(2,1)S(1)} collective-permute-done((bf16[2,4,96,640]{3,2,1,0:T(8,128)(2,1)S(1)}, bf16[2,4,96,640]{3,2,1,0:T(8,128)(2,1)S(1)}, u32[]{:S(2)}, u32[]{:S(2)}) %collective-permute-start.2) | collective-permute-done | bytes 983072 | tf_op jit(solution)/shard_map/ppermute | solution.py:187
  64.0 1.0 copy-done.11
  64.9 18.3 %collective-permute-done.3.refs_3_ = bf16[2,4,96,640]{3,2,1,0:T(8,128)(2,1)S(1)} collective-permute-done((bf16[2,4,96,640]{3,2,1,0:T(8,128)(2,1)S(1)}, bf16[2,4,96,640]{3,2,1,0:T(8,128)(2,1)S(1)}, u32[]{:S(2)}, u32[]{:S(2)}) %collective-permute-start.3) | collective-permute-done | bytes 983072 | tf_op jit(solution)/shard_map/ppermute | solution.py:187
  83.3 1.0 copy-done.13
  84.3 1.1 copy-done.2
  85.3 4.7 %all-to-all-start = ((bf16[8,3,2,32,1280]{4,3,2,1,0:T(8,128)(2,1)}), bf16[8,3,2,32,1280]{4,3,2,1,0:T(8,128)(2,1)}, u32[]{:S(2)}, u32[]{:S(2)}) async-start(bf16[8,3,2,32,1280]{4,3,2,1,0:T(8,128)(2,1)} %bitcast.147), calls=%async_computation | async-start | bytes 7864320 | tf_op jit(solution)/shard_map/all_to_all | solution.py:208
  90.3 1.3 copy-done.3
  91.6 1.2 copy-done.8
  92.8 1.2 copy-done.10
  94.0 1.2 copy-done.12
  95.2 1.2 copy-done.14
  96.4 9.7 %shard_map.65 = (bf16[2,640,256]{2,1,0:T(8,128)(2,1)S(1)}, f32[2,5,256]{2,1,0:T(8,128)S(1)}, bf16[2,640,256]{2,1,0:T(8,128)(2,1)S(1)}, f32[2,5,256]{2,1,0:T(8,128)S(1)}) custom-call(s32[2,2]{1,0:T(2,128)S(1)} %pad_add_fusion.live_ref, bf16[512,1280]{1,0:T(8,128)(2,1)S(1)} %bitcast.145, bf16[512,1280]{1,0:T(8,128)(2,1)S(1)} %copy-done.3, ...), custom_call_target="tpu_custom_call" | custom-call | flops 8053063680 | bytes 6553600 | tf_op jit(solution)/shard_map/pallas_call | solution.py:83
  106.2 2.1 copy-done.1
  108.4 3.3 %shard_map.67 = (bf16[2,4,96,640]{3,2,1,0:T(8,128)(2,1)S(1)}, bf16[2,4,96,640]{3,2,1,0:T(8,128)(2,1)}, bf16[2,4,96,640]{3,2,1,0:T(8,128)(2,1)}, bf16[2,4,96,640]{3,2,1,0:T(8,128)(2,1)}) custom-call(s32[1]{0:T(128)} %bitcast.4.place_ref, s32[16]{0:T(128)S(1)} %reshape.191.slots_ref, bf16[2,8,96,1280]{3,2,1,0:T(8,128)(2,1)S(1)} %copy-done.1, ...), custom_call_target="tpu_custom_call" | custom-call | bytes 7864320 | tf_op jit(solution)/shard_map/pallas_call | solution.py:157
  111.6 1.0 copy-done.5
  112.6 2.0 collective-permute-start.5
  114.6 1.5 collective-permute-start.6
  116.1 0.9 fusion.18
  117.0 2.9 collective-permute-start.4
  119.9 0.8 fusion.41
  120.7 58.5 %all-to-all-done.token_ref = bf16[8,3,2,32,1280]{4,3,2,1,0:T(8,128)(2,1)} async-done(((bf16[8,3,2,32,1280]{4,3,2,1,0:T(8,128)(2,1)}), bf16[8,3,2,32,1280]{4,3,2,1,0:T(8,128)(2,1)}, u32[]{:S(2)}, u32[]{:S(2)}) %all-to-all-start) | async-done | bytes 3932192 | tf_op jit(solution)/shard_map/all_to_all | solution.py:208
  179.2 10.2 %shard_map.66 = bf16[8,2,32,1280]{3,2,1,0:T(8,128)(2,1)} custom-call(bf16[8,3,2,32,1280]{4,3,2,1,0:T(8,128)(2,1)} %all-to-all-done.token_ref), custom_call_target="tpu_custom_call" | custom-call | flops 2684354560 | bytes 5242880 | tf_op jit(solution)/shard_map/pallas_call | solution.py:125
  189.3 4.6 %all-to-all-start.1 = ((bf16[8,2,32,1280]{3,2,1,0:T(8,128)(2,1)}), bf16[8,2,32,1280]{3,2,1,0:T(8,128)(2,1)}, u32[]{:S(2)}, u32[]{:S(2)}) async-start(bf16[8,2,32,1280]{3,2,1,0:T(8,128)(2,1)} %shard_map.66), calls=%async_computation.1 | async-start | bytes 2621440 | tf_op jit(solution)/shard_map/all_to_all | solution.py:237
  194.0 22.7 %collective-permute-done.7.refs_3_ = bf16[2,4,96,640]{3,2,1,0:T(8,128)(2,1)} collective-permute-done((bf16[2,4,96,640]{3,2,1,0:T(8,128)(2,1)}, bf16[2,4,96,640]{3,2,1,0:T(8,128)(2,1)}, u32[]{:S(2)}, u32[]{:S(2)}) %collective-permute-start.7) | collective-permute-done | bytes 983072 | tf_op jit(solution)/shard_map/ppermute | solution.py:187
  216.6 1.2 copy-done.6
  217.8 10.0 %shard_map.68 = (bf16[2,640,256]{2,1,0:T(8,128)(2,1)S(1)}, f32[2,5,256]{2,1,0:T(8,128)S(1)}, bf16[2,640,256]{2,1,0:T(8,128)(2,1)S(1)}, f32[2,5,256]{2,1,0:T(8,128)S(1)}) custom-call(s32[2,2]{1,0:T(2,128)S(1)} %pad_add_fusion.live_ref, bf16[512,1280]{1,0:T(8,128)(2,1)S(1)} %bitcast.146, bf16[512,1280]{1,0:T(8,128)(2,1)S(1)} %copy-done.4, ...), custom_call_target="tpu_custom_call" | custom-call | flops 8053063680 | bytes 6553600 | tf_op jit(solution)/shard_map/pallas_call | solution.py:83
  227.9 0.8 slice_bitcast_fusion.1
  228.7 1.2 fusion.40
  230.0 0.8 add_divide_fusion.3
  230.8 2.9 collective-permute-start.11
  233.7 1.1 fusion.24
  234.8 25.8 %collective-permute-done.8 = bf16[656,256]{1,0:T(8,128)(2,1)S(1)} collective-permute-done((bf16[656,256]{1,0:T(8,128)(2,1)S(1)}, bf16[656,256]{1,0:T(8,128)(2,1)S(1)}, u32[]{:S(2)}, u32[]{:S(2)}) %collective-permute-start.8) | collective-permute-done | bytes 335904 | tf_op jit(solution)/shard_map/ppermute | solution.py:187
  260.9 0.4 copy.22
  261.3 1.4 fusion.39
  262.7 8.5 %convolution_convert_fusion.1 = bf16[256,5120]{1,0:T(8,128)(2,1)S(1)} fusion(bf16[1280,5120]{1,0:T(8,128)(2,1)} %param.11, f32[1280,256]{0,1:T(8,128)S(1)} %copy.22, bf16[256,1280]{1,0:T(8,128)(2,1)S(1)} %bitcast.164), kind=kOutput, calls=%fused_computation.1 | convolution fusion | flops 3357736960 | bytes 17694720 | tf_op jit(solution)/shard_map/dot_general | solution.py:271
  271.2 1.3 dynamic-slice_bitcast_fusion.1
  272.5 0.6 copy-done.17
  273.1 1.1 slice.132
  274.2 0.8 add_divide_fusion.1
  275.2 0.4 copy.23
  275.8 0.7 collective-permute-done.9
  276.5 0.8 copy-done.18
  277.3 1.6 fusion.1
  279.0 8.9 %convolution_convert_fusion = bf16[256,5120]{1,0:T(8,128)(2,1)S(1)} fusion(bf16[1280,256]{0,1:T(8,128)(2,1)S(1)} %fusion.12, bf16[1280,5120]{1,0:T(8,128)(2,1)} %param.11), kind=kOutput, calls=%fused_computation | convolution fusion | flops 3356753920 | bytes 16384000 | tf_op jit(solution)/shard_map/dot_general | solution.py:271
  287.9 1.3 dynamic-slice_bitcast_fusion
  289.1 0.6 copy-done.16
  289.8 0.4 collective-permute-start.12
  290.2 1.6 collective-permute-start.10
  291.8 1.3 collective-permute-done.12
  293.1 1.6 fusion
  294.8 1.6 collective-permute-start.13
  296.3 11.6 %collective-permute-done.10 = bf16[64,5120]{1,0:T(8,128)(2,1)S(1)} collective-permute-done((bf16[64,5120]{1,0:T(8,128)(2,1)S(1)}, bf16[64,5120]{1,0:T(8,128)(2,1)S(1)}, u32[]{:S(2)}, u32[]{:S(2)}) %collective-permute-start.10) | collective-permute-done | bytes 655392 | tf_op jit(solution)/shard_map/ppermute | solution.py:225
  308.1 13.0 %collective-permute-done.13 = bf16[64,5120]{1,0:T(8,128)(2,1)S(1)} collective-permute-done((bf16[64,5120]{1,0:T(8,128)(2,1)S(1)}, bf16[64,5120]{1,0:T(8,128)(2,1)S(1)}, u32[]{:S(2)}, u32[]{:S(2)}) %collective-permute-start.13) | collective-permute-done | bytes 655392 | tf_op jit(solution)/shard_map/ppermute | solution.py:225
  321.2 1.1 maximum_bitcast_fusion
  (62 shorter events, 2.2 us)
Async XLA Ops:
  0.0 5.6 %copy-start.21 = (s32[8,2]{0,1:T(2,128)S(1)}, s32[8,2]{0,1:T(2,128)}, u32[]{:S(2)}) copy-start(s32[8,2]{0,1:T(2,128)} %param.8) | copy-start | bytes 196
  1.5 82.8 %collective-permute-start = (bf16[512,1280]{1,0:T(8,128)(2,1)S(1)}, bf16[512,1280]{1,0:T(8,128)(2,1)S(1)}, u32[]{:S(2)}, u32[]{:S(2)}) collective-permute-start(bf16[512,1280]{1,0:T(8,128)(2,1)S(1)} %bitcast.144), channel_id=1, source_target_pairs={{0,16},{4,20},{8,24},{12,28},{16,0},{20,4},{24,8},{28,12},{1,17},{... | collective-permute-start | bytes 3932168 | tf_op jit(solution)/shard_map/ppermute | solution.py:187
  5.7 2.1 copy-start
  7.8 6.5 %copy-start.15 = (bf16[3,64,8,1280]{3,2,1,0:T(8,128)(2,1)S(1)}, bf16[3,64,8,1280]{3,2,1,0:T(8,128)(2,1)}, u32[]{:S(2)}) copy-start(bf16[3,64,8,1280]{3,2,1,0:T(8,128)(2,1)} %param.10) | copy-start | bytes 11796484
  9.8 1.0 copy-start.7
  10.8 23.8 %collective-permute-start.1 = (bf16[2,4,96,640]{3,2,1,0:T(8,128)(2,1)S(1)}, bf16[2,4,96,640]{3,2,1,0:T(8,128)(2,1)S(1)}, u32[]{:S(2)}, u32[]{:S(2)}) collective-permute-start(bf16[2,4,96,640]{3,2,1,0:T(8,128)(2,1)S(1)} %get-tuple-element.29), channel_id=1, source_target_pairs={{0,4},{4,0},{8,12},{12,8},{16,20},{20,16},{24,28},{28,24},{1,5},{5... | collective-permute-start | bytes 2949128 | tf_op jit(solution)/shard_map/ppermute | solution.py:187
  12.4 51.6 %collective-permute-start.2 = (bf16[2,4,96,640]{3,2,1,0:T(8,128)(2,1)S(1)}, bf16[2,4,96,640]{3,2,1,0:T(8,128)(2,1)S(1)}, u32[]{:S(2)}, u32[]{:S(2)}) collective-permute-start(bf16[2,4,96,640]{3,2,1,0:T(8,128)(2,1)S(1)} %get-tuple-element.30), channel_id=1, source_target_pairs={{0,8},{4,12},{8,0},{12,4},{16,24},{20,28},{24,16},{28,20},{1,9},{5... | collective-permute-start | bytes 2949128 | tf_op jit(solution)/shard_map/ppermute | solution.py:187
  13.9 69.3 %collective-permute-start.3 = (bf16[2,4,96,640]{3,2,1,0:T(8,128)(2,1)S(1)}, bf16[2,4,96,640]{3,2,1,0:T(8,128)(2,1)S(1)}, u32[]{:S(2)}, u32[]{:S(2)}) collective-permute-start(bf16[2,4,96,640]{3,2,1,0:T(8,128)(2,1)S(1)} %get-tuple-element.31), channel_id=1, source_target_pairs={{0,12},{4,8},{8,4},{12,0},{16,28},{20,24},{24,20},{28,16},{1,13},{... | collective-permute-start | bytes 2949128 | tf_op jit(solution)/shard_map/ppermute | solution.py:187
  34.6 1.0 copy-start.9
  64.0 1.0 copy-start.11
  83.3 1.0 copy-start.13
  84.3 1.1 copy-start.2
  84.3 5.7 %copy-start.22 = (s32[8,2]{0,1:T(2,128)S(1)}, s32[8,2]{0,1:T(2,128)}, u32[]{:S(2)}) copy-start(s32[8,2]{0,1:T(2,128)} %param.9) | copy-start | bytes 196
  85.3 93.9 %all-to-all-start = ((bf16[8,3,2,32,1280]{4,3,2,1,0:T(8,128)(2,1)}), bf16[8,3,2,32,1280]{4,3,2,1,0:T(8,128)(2,1)}, u32[]{:S(2)}, u32[]{:S(2)}) async-start(bf16[8,3,2,32,1280]{4,3,2,1,0:T(8,128)(2,1)} %bitcast.147), calls=%async_computation | async-start | bytes 7864320 | tf_op jit(solution)/shard_map/all_to_all | solution.py:208
  90.3 1.3 copy-start.3
  91.6 1.2 copy-start.8
  92.8 1.2 copy-start.10
  94.0 1.2 copy-start.12
  95.2 1.2 copy-start.14
  106.2 2.1 copy-start.1
  111.6 1.0 copy-start.5
  112.6 81.3 %collective-permute-start.5 = (bf16[2,4,96,640]{3,2,1,0:T(8,128)(2,1)}, bf16[2,4,96,640]{3,2,1,0:T(8,128)(2,1)}, u32[]{:S(2)}, u32[]{:S(2)}) collective-permute-start(bf16[2,4,96,640]{3,2,1,0:T(8,128)(2,1)} %get-tuple-element.41), channel_id=1, source_target_pairs={{0,4},{4,0},{8,12},{12,8},{16,20},{20,16},{24,28},{28,24},{1,5},{5... | collective-permute-start | bytes 2949128 | tf_op jit(solution)/shard_map/ppermute | solution.py:187
  114.6 79.3 %collective-permute-start.6 = (bf16[2,4,96,640]{3,2,1,0:T(8,128)(2,1)}, bf16[2,4,96,640]{3,2,1,0:T(8,128)(2,1)}, u32[]{:S(2)}, u32[]{:S(2)}) collective-permute-start(bf16[2,4,96,640]{3,2,1,0:T(8,128)(2,1)} %get-tuple-element.42), channel_id=1, source_target_pairs={{0,8},{4,12},{8,0},{12,4},{16,24},{20,28},{24,16},{28,20},{1,9},{5... | collective-permute-start | bytes 2949128 | tf_op jit(solution)/shard_map/ppermute | solution.py:187
  116.1 100.6 %collective-permute-start.7 = (bf16[2,4,96,640]{3,2,1,0:T(8,128)(2,1)}, bf16[2,4,96,640]{3,2,1,0:T(8,128)(2,1)}, u32[]{:S(2)}, u32[]{:S(2)}) collective-permute-start(bf16[2,4,96,640]{3,2,1,0:T(8,128)(2,1)} %get-tuple-element.43), channel_id=1, source_target_pairs={{0,12},{4,8},{8,4},{12,0},{16,28},{20,24},{24,20},{28,16},{1,13},{... | collective-permute-start | bytes 2949128 | tf_op jit(solution)/shard_map/ppermute | solution.py:187
  117.0 110.9 %collective-permute-start.4 = (bf16[2,656,256]{2,1,0:T(8,128)(2,1)}, bf16[2,656,256]{2,1,0:T(8,128)(2,1)}, u32[]{:S(2)}, u32[]{:S(2)}) collective-permute-start(bf16[2,656,256]{2,1,0:T(8,128)(2,1)} %fusion.18), channel_id=1, source_target_pairs={{0,16},{4,20},{8,24},{12,28},{16,0},{20,4},{24,8},{28,12},{1,17},{... | collective-permute-start | bytes 2015240 | tf_op jit(solution)/shard_map/ppermute | solution.py:187
  189.3 27.3 %copy-start.4 = (bf16[512,1280]{1,0:T(8,128)(2,1)S(1)}, bf16[512,1280]{1,0:T(8,128)(2,1)}, u32[]{:S(2)}) copy-start(bf16[512,1280]{1,0:T(8,128)(2,1)} %copy-done.2) | copy-start | bytes 3932164
  189.3 71.9 %all-to-all-start.1 = ((bf16[8,2,32,1280]{3,2,1,0:T(8,128)(2,1)}), bf16[8,2,32,1280]{3,2,1,0:T(8,128)(2,1)}, u32[]{:S(2)}, u32[]{:S(2)}) async-start(bf16[8,2,32,1280]{3,2,1,0:T(8,128)(2,1)} %shard_map.66), calls=%async_computation.1 | async-start | bytes 2621440 | tf_op jit(solution)/shard_map/all_to_all | solution.py:237
  216.6 1.2 copy-start.6
  228.7 5.0 %copy-start.20 = (bf16[1,640,256]{2,1,0:T(8,128)(2,1)S(1)}, bf16[1,640,256]{2,1,0:T(8,128)(2,1)}, u32[]{:S(2)}) copy-start(bf16[1,640,256]{2,1,0:T(8,128)(2,1)} %get-tuple-element.62) | copy-start | bytes 983044
  228.7 31.9 %collective-permute-start.8 = (bf16[656,256]{1,0:T(8,128)(2,1)S(1)}, bf16[656,256]{1,0:T(8,128)(2,1)S(1)}, u32[]{:S(2)}, u32[]{:S(2)}) collective-permute-start(bf16[656,256]{1,0:T(8,128)(2,1)S(1)} %get-tuple-element.59), channel_id=1, source_target_pairs={{0,16},{4,20},{8,24},{12,28},{16,0},{20,4},{24,8},{28,12},{1,17},{... | collective-permute-start | bytes 1007624 | tf_op jit(solution)/shard_map/ppermute | solution.py:187
  230.8 42.3 %collective-permute-start.11 = (bf16[656,256]{1,0:T(8,128)(2,1)}, bf16[656,256]{1,0:T(8,128)(2,1)}, u32[]{:S(2)}, u32[]{:S(2)}) collective-permute-start(bf16[656,256]{1,0:T(8,128)(2,1)} %get-tuple-element.60), channel_id=1, source_target_pairs={{0,16},{4,20},{8,24},{12,28},{16,0},{20,4},{24,8},{28,12},{1,17},{... | collective-permute-start | bytes 1007624 | tf_op jit(solution)/shard_map/ppermute | solution.py:187
  271.2 1.9 copy-start.17
  273.1 2.0 copy-start.19
  273.1 3.4 %collective-permute-start.9 = (bf16[2,64,5120]{2,1,0:T(8,128)(2,1)}, bf16[2,64,5120]{2,1,0:T(8,128)(2,1)}, u32[]{:S(2)}, u32[]{:S(2)}) collective-permute-start(bf16[2,64,5120]{2,1,0:T(8,128)(2,1)} %dynamic-slice_bitcast_fusion.1), channel_id=1, source_target_pairs={{0,1},{1,0},{2,3},{3,2},{4,5},{5,4},{6,7},{7,6},{8,9},{9,8},{10,11... | collective-permute-start | bytes 3932168 | tf_op jit(solution)/shard_map/ppermute | solution.py:218
  275.6 1.7 copy-start.18
  287.8 1.9 copy-start.16
  289.8 3.3 %collective-permute-start.12 = (bf16[2,64,5120]{2,1,0:T(8,128)(2,1)}, bf16[2,64,5120]{2,1,0:T(8,128)(2,1)S(1)}, u32[]{:S(2)}, u32[]{:S(2)}) collective-permute-start(bf16[2,64,5120]{2,1,0:T(8,128)(2,1)} %dynamic-slice_bitcast_fusion), channel_id=1, source_target_pairs={{0,1},{1,0},{2,3},{3,2},{4,5},{5,4},{6,7},{7,6},{8,9},{9,8},{10,11... | collective-permute-start | bytes 3932168 | tf_op jit(solution)/shard_map/ppermute | solution.py:218
  290.2 17.7 %collective-permute-start.10 = (bf16[64,5120]{1,0:T(8,128)(2,1)S(1)}, bf16[64,5120]{1,0:T(8,128)(2,1)S(1)}, u32[]{:S(2)}, u32[]{:S(2)}) collective-permute-start(bf16[64,5120]{1,0:T(8,128)(2,1)S(1)} %dynamic-slice_bitcast_fusion.3), channel_id=1, source_target_pairs={{0,2},{1,3},{2,0},{3,1},{4,6},{5,7},{6,4},{7,5},{8,10},{9,11},{10,... | collective-permute-start | bytes 1966088 | tf_op jit(solution)/shard_map/ppermute | solution.py:225
  294.8 26.3 %collective-permute-start.13 = (bf16[64,5120]{1,0:T(8,128)(2,1)S(1)}, bf16[64,5120]{1,0:T(8,128)(2,1)S(1)}, u32[]{:S(2)}, u32[]{:S(2)}) collective-permute-start(bf16[64,5120]{1,0:T(8,128)(2,1)S(1)} %dynamic-slice_bitcast_fusion.2), channel_id=1, source_target_pairs={{0,2},{1,3},{2,0},{3,1},{4,6},{5,7},{6,4},{7,5},{8,10},{9,11},{10,... | collective-permute-start | bytes 1966088 | tf_op jit(solution)/shard_map/ppermute | solution.py:225

commit v4 on v3

--- a/solution.py
+++ b/solution.py
@@ -261,20 +261,21 @@
             + wide(got[: width // groups].reshape(split)) * (got_share / total)[:, None, :]
         )
 
-    projected, summed = [], []
+    def project(group, part, *before):
+        low, high = group * width // groups, (group + 1) * width // groups
+        frame_out = back[:, part].reshape(rows, width)[:, low:high]
+        combined = share_of(group, part, *before).reshape(width // groups, rows) + wide(frame_out.T)
+        return lax.dot_general(
+            combined.astype(jnp.bfloat16), out_weight[low:high], (((0,), (0,)), ((), ())),
+            preferred_element_type=jnp.float32,
+        )
+
+    early = [[project(group, part) for group in range(groups - 1)] for part in range(parts)]
+    projected, pieces = [], []
     for part in range(parts):
-        shares = [share_of(group, part, *projected[-1:]) for group in range(groups)]
-        ref_out = jnp.concatenate(shares, axis=0).reshape(width, rows)
-        frame_out = back[:, part].reshape(rows, width)
-        combined = (ref_out + wide(frame_out.T)).astype(jnp.bfloat16)
-        projected.append(
-            lax.dot_general(
-                after(combined, *summed[-1:]), out_weight, (((0,), (0,)), ((), ())),
-                preferred_element_type=jnp.float32,
-            ).astype(jnp.bfloat16)
-        )
-        summed.append(scatter_cores(projected[-1]))
-    pieces = [scatter_chips(block) for block in summed]
+        total = project(groups - 1, part, *early[-1], *early[0], *projected[-1:])
+        projected.append(functools.reduce(jnp.add, [*early[part], total]).astype(jnp.bfloat16))
+        pieces.append(scatter_chips(after(scatter_cores(projected[-1]), *pieces[-1:])))
     return jnp.concatenate(pieces, axis=0).reshape(spatial // head_groups, frames_here, -1)
 
 

time: 324 us -> 337 us (1.040)
  waiting for transfers between devices: 198 us -> 210 us
  matrix products: 17.4 us -> 23.6 us
  local copies, waits for them, and re-layouts: 32.5 us -> 29 us
    ppermute x10, waiting for transfers between devices: 113 us -> 120 us  [swap(): return lax.ppermute(block, 'frames', [(a, a ^ step) for a in range(shards)])]
    dot_general x2 -> x4, matrix products: 17.4 us -> 23.6 us  [project(): lax.dot_general(combined.astype(jnp.bfloat16), out_weight[low:high], (((0...]
    ppermute x2, waiting for transfers between devices: 24.6 us -> 30.2 us  [scatter_chips(): lax.ppermute(give, 'heads', [(h, (h + 2 * step) % head_groups) for h in r...]
    convert_element_type x1 -> x3, other arithmetic: 0.16 us -> 3.8 us  [project(): combined.astype(jnp.bfloat16)]
    unnamed x49 -> x57, local copies, waits for them, and re-layouts: 19.9 us -> 21 us
  transfers between devices with their start and end apart: 16 -> 16, of which waited for: 10 -> 9; matrix products, arithmetic and copies ran while one was open for 8% -> 11% of each run, Pallas kernels for 11% -> 11%
where the time goes in v4:
time: 337 us; the launch traced here: 335 us
  waiting for transfers between devices  210 us (62%)
  Pallas kernels  35.3 us (10%)
  starting transfers between devices  29.4 us (9%)
  local copies, waits for them, and re-layouts  29 us (9%)
  matrix products  23.6 us (7%)
  other arithmetic  7.59 us (2%)
    ppermute x10, waiting for transfers between devices, swap(): return lax.ppermute(block, 'frames', [(a, a ^ step) for a in range(shards)])  120 us
    all_to_all x1, waiting for transfers between devices, local(): lax.all_to_all(after(tokens, far, *banks[0]), 'frames', 0, 0, tiled=True)  60.2 us
    ppermute x2, waiting for transfers between devices, scatter_chips(): lax.ppermute(give, 'heads', [(h, (h + 2 * step) % head_groups) for h in r...  30.2 us
    dot_general x4, matrix products, project(): lax.dot_general(combined.astype(jnp.bfloat16), out_weight[low:high], (((0...  23.6 us
    unnamed x57, local copies, waits for them, and re-layouts  21 us
    pallas_call x2, Pallas kernels, attend_bank(): pl.pallas_call(functools.partial(bank_kernel, len(banks)), grid=(heads,),...  19.9 us
    ppermute x10, starting transfers between devices, swap(): return lax.ppermute(block, 'frames', [(a, a ^ step) for a in range(shards)])  16.8 us
    pallas_call x1, Pallas kernels, attend_frames(): pl.pallas_call(functools.partial(frame_kernel, frames_here), grid=(width...  10.2 us
  transfers between devices with their start and end apart: 16, of which 9 were waited for; matrix products, arithmetic and copies ran while one was open for 11% of the time, Pallas kernels for 11%

profile of v4, /device:TPU:0, one launch (start us, length us, event | category | flops | bytes accessed | tf_op | source)
XLA Modules:
  0.0 335.4 jit_solution(10449936499359300785)
XLA Ops:
  0.0 1.4 copy.18
  1.4 4.1 %collective-permute-start = (bf16[512,1280]{1,0:T(8,128)(2,1)S(1)}, bf16[512,1280]{1,0:T(8,128)(2,1)S(1)}, u32[]{:S(2)}, u32[]{:S(2)}) collective-permute-start(bf16[512,1280]{1,0:T(8,128)(2,1)S(1)} %bitcast.157), channel_id=1, source_target_pairs={{0,16},{4,20},{8,24},{12,28},{16,0},{20,4},{24,8},{28,12},{1,17},{... | collective-permute-start | bytes 3932168 | tf_op jit(solution)/shard_map/ppermute | solution.py:187
  5.7 2.1 copy-done
  7.8 2.0 shard_map.64
  9.8 0.9 copy-done.7
  10.8 1.5 collective-permute-start.1
  12.3 1.6 collective-permute-start.2
  13.9 0.4 collective-permute-start.3
  14.3 2.1 copy.20
  16.4 18.2 %collective-permute-done.1.refs_1_ = bf16[2,4,96,640]{3,2,1,0:T(8,128)(2,1)S(1)} collective-permute-done((bf16[2,4,96,640]{3,2,1,0:T(8,128)(2,1)S(1)}, bf16[2,4,96,640]{3,2,1,0:T(8,128)(2,1)S(1)}, u32[]{:S(2)}, u32[]{:S(2)}) %collective-permute-start.1) | collective-permute-done | bytes 983072 | tf_op jit(solution)/shard_map/ppermute | solution.py:187
  34.6 1.0 copy-done.9
  35.5 28.4 %collective-permute-done.2.refs_2_ = bf16[2,4,96,640]{3,2,1,0:T(8,128)(2,1)S(1)} collective-permute-done((bf16[2,4,96,640]{3,2,1,0:T(8,128)(2,1)S(1)}, bf16[2,4,96,640]{3,2,1,0:T(8,128)(2,1)S(1)}, u32[]{:S(2)}, u32[]{:S(2)}) %collective-permute-start.2) | collective-permute-done | bytes 983072 | tf_op jit(solution)/shard_map/ppermute | solution.py:187
  63.9 0.9 copy-done.11
  64.8 18.4 %collective-permute-done.3.refs_3_ = bf16[2,4,96,640]{3,2,1,0:T(8,128)(2,1)S(1)} collective-permute-done((bf16[2,4,96,640]{3,2,1,0:T(8,128)(2,1)S(1)}, bf16[2,4,96,640]{3,2,1,0:T(8,128)(2,1)S(1)}, u32[]{:S(2)}, u32[]{:S(2)}) %collective-permute-start.3) | collective-permute-done | bytes 983072 | tf_op jit(solution)/shard_map/ppermute | solution.py:187
  83.2 1.0 copy-done.13
  84.2 1.1 copy-done.2
  85.3 4.6 %all-to-all-start = ((bf16[8,3,2,32,1280]{4,3,2,1,0:T(8,128)(2,1)}), bf16[8,3,2,32,1280]{4,3,2,1,0:T(8,128)(2,1)}, u32[]{:S(2)}, u32[]{:S(2)}) async-start(bf16[8,3,2,32,1280]{4,3,2,1,0:T(8,128)(2,1)} %bitcast.162), calls=%async_computation | async-start | bytes 7864320 | tf_op jit(solution)/shard_map/all_to_all | solution.py:208
  90.2 1.3 copy-done.3
  91.5 1.2 copy-done.8
  92.7 1.2 copy-done.10
  93.9 1.2 copy-done.12
  95.1 1.2 copy-done.14
  96.3 9.7 %shard_map.65 = (bf16[2,640,256]{2,1,0:T(8,128)(2,1)S(1)}, f32[2,5,256]{2,1,0:T(8,128)S(1)}, bf16[2,640,256]{2,1,0:T(8,128)(2,1)S(1)}, f32[2,5,256]{2,1,0:T(8,128)S(1)}) custom-call(s32[2,2]{1,0:T(2,128)S(1)} %pad_add_fusion.live_ref, bf16[512,1280]{1,0:T(8,128)(2,1)S(1)} %bitcast.158, bf16[512,1280]{1,0:T(8,128)(2,1)S(1)} %copy-done.3, ...), custom_call_target="tpu_custom_call" | custom-call | flops 8053063680 | bytes 6553600 | tf_op jit(solution)/shard_map/pallas_call | solution.py:83
  106.2 2.1 copy-done.1
  108.3 3.3 shard_map.67
  111.6 1.0 copy-done.5
  112.6 2.0 collective-permute-start.5
  114.6 1.5 collective-permute-start.6
  116.1 60.2 %all-to-all-done.token_ref = bf16[8,3,2,32,1280]{4,3,2,1,0:T(8,128)(2,1)} async-done(((bf16[8,3,2,32,1280]{4,3,2,1,0:T(8,128)(2,1)}), bf16[8,3,2,32,1280]{4,3,2,1,0:T(8,128)(2,1)}, u32[]{:S(2)}, u32[]{:S(2)}) %all-to-all-start) | async-done | bytes 3932192 | tf_op jit(solution)/shard_map/all_to_all | solution.py:208
  176.3 10.2 %shard_map.66 = bf16[8,2,32,1280]{3,2,1,0:T(8,128)(2,1)} custom-call(bf16[8,3,2,32,1280]{4,3,2,1,0:T(8,128)(2,1)} %all-to-all-done.token_ref), custom_call_target="tpu_custom_call" | custom-call | flops 2684354560 | bytes 5242880 | tf_op jit(solution)/shard_map/pallas_call | solution.py:125
  186.4 4.3 %all-to-all-start.1 = ((bf16[8,2,32,1280]{3,2,1,0:T(8,128)(2,1)}), bf16[8,2,32,1280]{3,2,1,0:T(8,128)(2,1)}, u32[]{:S(2)}, u32[]{:S(2)}) async-start(bf16[8,2,32,1280]{3,2,1,0:T(8,128)(2,1)} %shard_map.66), calls=%async_computation.1 | async-start | bytes 2621440 | tf_op jit(solution)/shard_map/all_to_all | solution.py:237
  190.8 2.8 collective-permute-start.4
  193.7 9.0 %collective-permute-done.7.refs_3_ = bf16[2,4,96,640]{3,2,1,0:T(8,128)(2,1)} collective-permute-done((bf16[2,4,96,640]{3,2,1,0:T(8,128)(2,1)}, bf16[2,4,96,640]{3,2,1,0:T(8,128)(2,1)}, u32[]{:S(2)}, u32[]{:S(2)}) %collective-permute-start.7) | collective-permute-done | bytes 983072 | tf_op jit(solution)/shard_map/ppermute | solution.py:187
  202.7 1.2 copy-done.6
  203.9 10.2 %shard_map.68 = (bf16[2,640,256]{2,1,0:T(8,128)(2,1)S(1)}, f32[2,5,256]{2,1,0:T(8,128)S(1)}, bf16[2,640,256]{2,1,0:T(8,128)(2,1)S(1)}, f32[2,5,256]{2,1,0:T(8,128)S(1)}) custom-call(s32[2,2]{1,0:T(2,128)S(1)} %pad_add_fusion.live_ref, bf16[512,1280]{1,0:T(8,128)(2,1)S(1)} %bitcast.159, bf16[512,1280]{1,0:T(8,128)(2,1)S(1)} %copy-done.4, ...), custom_call_target="tpu_custom_call" | custom-call | flops 8053063680 | bytes 6553600 | tf_op jit(solution)/shard_map/pallas_call | solution.py:83
  214.1 37.4 %collective-permute-done.4 = bf16[2,656,256]{2,1,0:T(8,128)(2,1)S(1)} collective-permute-done((bf16[2,656,256]{2,1,0:T(8,128)(2,1)S(1)}, bf16[2,656,256]{2,1,0:T(8,128)(2,1)S(1)}, u32[]{:S(2)}, u32[]{:S(2)}) %collective-permute-start.4) | collective-permute-done | bytes 671776 | tf_op jit(solution)/shard_map/ppermute | solution.py:187
  251.5 1.0 slice_bitcast_fusion.1
  252.5 2.9 collective-permute-start.8
  255.5 1.4 fusion.50
  256.9 0.9 copy.29
  257.9 0.9 copy.30
  258.8 0.2 copy.31
  259.0 1.5 fusion.37
  260.6 7.6 %fusion.4 = f32[256,5120]{1,0:T(8,128)} fusion(bf16[640,256]{1,0:T(8,128)(2,1)S(1)} %get-tuple-element.54, bf16[1280,5120]{1,0:T(8,128)(2,1)} %param.11), kind=kOutput, calls=%fused_computation.6 | convolution fusion | flops 1677721600 | bytes 12124160 | tf_op jit(solution)/shard_map/dot_general | solution.py:268
  268.1 5.3 %fusion.6 = f32[256,5120]{1,0:T(8,128)S(1)} fusion(bf16[640,256]{1,0:T(8,128)(2,1)S(1)} %get-tuple-element.53, bf16[1280,5120]{1,0:T(8,128)(2,1)} %param.11), kind=kOutput, calls=%fused_computation.8 | convolution fusion | flops 1677721600 | bytes 12124160 | tf_op jit(solution)/shard_map/dot_general | solution.py:268
  273.5 8.4 %collective-permute-done.8 = bf16[656,256]{1,0:T(8,128)(2,1)} collective-permute-done((bf16[656,256]{1,0:T(8,128)(2,1)}, bf16[656,256]{1,0:T(8,128)(2,1)}, u32[]{:S(2)}, u32[]{:S(2)}) %collective-permute-start.8) | collective-permute-done | bytes 335904 | tf_op jit(solution)/shard_map/ppermute | solution.py:187
  281.9 0.8 add_divide_fusion.3
  282.7 1.2 fusion.34
  283.9 4.0 %fusion = bf16[256,5120]{1,0:T(8,128)(2,1)} fusion(f32[256,5120]{1,0:T(8,128)S(1)} %fusion.6, bf16[640,256]{1,0:T(8,128)(2,1)S(1)} %fusion.34, bf16[1280,5120]{1,0:T(8,128)(2,1)S(1)} %bitcast.161), kind=kOutput, calls=%fused_computation.2 | convolution fusion | flops 1680343040 | bytes 14745600 | tf_op jit(solution)/shard_map/dot_general | solution.py:268
  287.9 0.2 copy.32
  288.1 0.8 add_divide_fusion.1
  288.9 1.4 dynamic-slice_bitcast_fusion.1
  290.4 1.1 fusion.28
  291.5 6.6 %fusion.1 = bf16[256,5120]{1,0:T(8,128)(2,1)S(1)} fusion(f32[256,5120]{1,0:T(8,128)} %fusion.4, bf16[640,256]{1,0:T(8,128)(2,1)S(1)} %fusion.28, bf16[1280,5120]{1,0:T(8,128)(2,1)} %param.11), kind=kOutput, calls=%fused_computation.3 | convolution fusion | flops 1680343040 | bytes 14745600 | tf_op jit(solution)/shard_map/dot_general | solution.py:268
  298.3 0.6 collective-permute-start.12
  298.8 1.1 copy-done.15
  299.9 0.3 fusion.9
  300.3 1.6 collective-permute-start.10
  301.8 0.3 fusion.8
  302.2 15.3 %collective-permute-done.10 = bf16[64,5120]{1,0:T(8,128)(2,1)S(1)} collective-permute-done((bf16[64,5120]{1,0:T(8,128)(2,1)S(1)}, bf16[64,5120]{1,0:T(8,128)(2,1)S(1)}, u32[]{:S(2)}, u32[]{:S(2)}) %collective-permute-start.10) | collective-permute-done | bytes 655392 | tf_op jit(solution)/shard_map/ppermute | solution.py:225
  317.7 1.6 collective-permute-start.13
  319.3 14.9 %collective-permute-done.13 = bf16[64,5120]{1,0:T(8,128)(2,1)S(1)} collective-permute-done((bf16[64,5120]{1,0:T(8,128)(2,1)S(1)}, bf16[64,5120]{1,0:T(8,128)(2,1)S(1)}, u32[]{:S(2)}, u32[]{:S(2)}) %collective-permute-start.13) | collective-permute-done | bytes 655392 | tf_op jit(solution)/shard_map/ppermute | solution.py:225
  334.1 0.2 fusion.18
  334.3 1.1 maximum_bitcast_fusion
  (65 shorter events, 1.4 us)
Async XLA Ops:
  0.0 5.5 %copy-start.19 = (s32[8,2]{0,1:T(2,128)S(1)}, s32[8,2]{0,1:T(2,128)}, u32[]{:S(2)}) copy-start(s32[8,2]{0,1:T(2,128)} %param.8) | copy-start | bytes 196
  1.4 82.8 %collective-permute-start = (bf16[512,1280]{1,0:T(8,128)(2,1)S(1)}, bf16[512,1280]{1,0:T(8,128)(2,1)S(1)}, u32[]{:S(2)}, u32[]{:S(2)}) collective-permute-start(bf16[512,1280]{1,0:T(8,128)(2,1)S(1)} %bitcast.157), channel_id=1, source_target_pairs={{0,16},{4,20},{8,24},{12,28},{16,0},{20,4},{24,8},{28,12},{1,17},{... | collective-permute-start | bytes 3932168 | tf_op jit(solution)/shard_map/ppermute | solution.py:187
  5.7 2.1 copy-start
  7.8 6.4 %copy-start.16 = (bf16[3,64,8,1280]{3,2,1,0:T(8,128)(2,1)S(1)}, bf16[3,64,8,1280]{3,2,1,0:T(8,128)(2,1)}, u32[]{:S(2)}) copy-start(bf16[3,64,8,1280]{3,2,1,0:T(8,128)(2,1)} %param.10) | copy-start | bytes 11796484
  9.8 0.9 copy-start.7
  10.8 23.8 %collective-permute-start.1 = (bf16[2,4,96,640]{3,2,1,0:T(8,128)(2,1)S(1)}, bf16[2,4,96,640]{3,2,1,0:T(8,128)(2,1)S(1)}, u32[]{:S(2)}, u32[]{:S(2)}) collective-permute-start(bf16[2,4,96,640]{3,2,1,0:T(8,128)(2,1)S(1)} %get-tuple-element.30), channel_id=1, source_target_pairs={{0,4},{4,0},{8,12},{12,8},{16,20},{20,16},{24,28},{28,24},{1,5},{5... | collective-permute-start | bytes 2949128 | tf_op jit(solution)/shard_map/ppermute | solution.py:187
  12.3 51.6 %collective-permute-start.2 = (bf16[2,4,96,640]{3,2,1,0:T(8,128)(2,1)S(1)}, bf16[2,4,96,640]{3,2,1,0:T(8,128)(2,1)S(1)}, u32[]{:S(2)}, u32[]{:S(2)}) collective-permute-start(bf16[2,4,96,640]{3,2,1,0:T(8,128)(2,1)S(1)} %get-tuple-element.31), channel_id=1, source_target_pairs={{0,8},{4,12},{8,0},{12,4},{16,24},{20,28},{24,16},{28,20},{1,9},{5... | collective-permute-start | bytes 2949128 | tf_op jit(solution)/shard_map/ppermute | solution.py:187
  13.9 69.3 %collective-permute-start.3 = (bf16[2,4,96,640]{3,2,1,0:T(8,128)(2,1)S(1)}, bf16[2,4,96,640]{3,2,1,0:T(8,128)(2,1)S(1)}, u32[]{:S(2)}, u32[]{:S(2)}) collective-permute-start(bf16[2,4,96,640]{3,2,1,0:T(8,128)(2,1)S(1)} %get-tuple-element.32), channel_id=1, source_target_pairs={{0,12},{4,8},{8,4},{12,0},{16,28},{20,24},{24,20},{28,16},{1,13},{... | collective-permute-start | bytes 2949128 | tf_op jit(solution)/shard_map/ppermute | solution.py:187
  34.6 1.0 copy-start.9
  63.9 0.9 copy-start.11
  83.2 1.0 copy-start.13
  84.2 1.1 copy-start.2
  84.2 5.7 %copy-start.20 = (s32[8,2]{0,1:T(2,128)S(1)}, s32[8,2]{0,1:T(2,128)}, u32[]{:S(2)}) copy-start(s32[8,2]{0,1:T(2,128)} %param.9) | copy-start | bytes 196
  85.3 91.0 %all-to-all-start = ((bf16[8,3,2,32,1280]{4,3,2,1,0:T(8,128)(2,1)}), bf16[8,3,2,32,1280]{4,3,2,1,0:T(8,128)(2,1)}, u32[]{:S(2)}, u32[]{:S(2)}) async-start(bf16[8,3,2,32,1280]{4,3,2,1,0:T(8,128)(2,1)} %bitcast.162), calls=%async_computation | async-start | bytes 7864320 | tf_op jit(solution)/shard_map/all_to_all | solution.py:208
  90.2 1.3 copy-start.3
  91.5 1.2 copy-start.8
  92.7 1.2 copy-start.10
  93.9 1.2 copy-start.12
  95.1 1.2 copy-start.14
  106.2 2.1 copy-start.1
  111.6 1.0 copy-start.5
  112.6 81.1 %collective-permute-start.5 = (bf16[2,4,96,640]{3,2,1,0:T(8,128)(2,1)}, bf16[2,4,96,640]{3,2,1,0:T(8,128)(2,1)}, u32[]{:S(2)}, u32[]{:S(2)}) collective-permute-start(bf16[2,4,96,640]{3,2,1,0:T(8,128)(2,1)} %get-tuple-element.42), channel_id=1, source_target_pairs={{0,4},{4,0},{8,12},{12,8},{16,20},{20,16},{24,28},{28,24},{1,5},{5... | collective-permute-start | bytes 2949128 | tf_op jit(solution)/shard_map/ppermute | solution.py:187
  114.6 79.1 %collective-permute-start.6 = (bf16[2,4,96,640]{3,2,1,0:T(8,128)(2,1)}, bf16[2,4,96,640]{3,2,1,0:T(8,128)(2,1)}, u32[]{:S(2)}, u32[]{:S(2)}) collective-permute-start(bf16[2,4,96,640]{3,2,1,0:T(8,128)(2,1)} %get-tuple-element.43), channel_id=1, source_target_pairs={{0,8},{4,12},{8,0},{12,4},{16,24},{20,28},{24,16},{28,20},{1,9},{5... | collective-permute-start | bytes 2949128 | tf_op jit(solution)/shard_map/ppermute | solution.py:187
  116.1 86.6 %collective-permute-start.7 = (bf16[2,4,96,640]{3,2,1,0:T(8,128)(2,1)}, bf16[2,4,96,640]{3,2,1,0:T(8,128)(2,1)}, u32[]{:S(2)}, u32[]{:S(2)}) collective-permute-start(bf16[2,4,96,640]{3,2,1,0:T(8,128)(2,1)} %get-tuple-element.44), channel_id=1, source_target_pairs={{0,12},{4,8},{8,4},{12,0},{16,28},{20,24},{24,20},{28,16},{1,13},{... | collective-permute-start | bytes 2949128 | tf_op jit(solution)/shard_map/ppermute | solution.py:187
  186.4 69.0 %all-to-all-start.1 = ((bf16[8,2,32,1280]{3,2,1,0:T(8,128)(2,1)}), bf16[8,2,32,1280]{3,2,1,0:T(8,128)(2,1)}, u32[]{:S(2)}, u32[]{:S(2)}) async-start(bf16[8,2,32,1280]{3,2,1,0:T(8,128)(2,1)} %shard_map.66), calls=%async_computation.1 | async-start | bytes 2621440 | tf_op jit(solution)/shard_map/all_to_all | solution.py:237
  190.8 11.9 %copy-start.4 = (bf16[512,1280]{1,0:T(8,128)(2,1)S(1)}, bf16[512,1280]{1,0:T(8,128)(2,1)}, u32[]{:S(2)}) copy-start(bf16[512,1280]{1,0:T(8,128)(2,1)} %copy-done.2) | copy-start | bytes 3932164
  190.8 60.6 %collective-permute-start.4 = (bf16[2,656,256]{2,1,0:T(8,128)(2,1)S(1)}, bf16[2,656,256]{2,1,0:T(8,128)(2,1)S(1)}, u32[]{:S(2)}, u32[]{:S(2)}) collective-permute-start(bf16[2,656,256]{2,1,0:T(8,128)(2,1)S(1)} %fusion.22), channel_id=1, source_target_pairs={{0,16},{4,20},{8,24},{12,28},{16,0},{20,4},{24,8},{28,12},{1,17},{... | collective-permute-start | bytes 2015240 | tf_op jit(solution)/shard_map/ppermute | solution.py:187
  202.7 1.2 copy-start.6
  251.4 4.0 %copy-start.18 = (bf16[2,656,256]{2,1,0:T(8,128)(2,1)}, bf16[2,656,256]{2,1,0:T(8,128)(2,1)S(1)}, u32[]{:S(2)}) copy-start(bf16[2,656,256]{2,1,0:T(8,128)(2,1)S(1)} %collective-permute-done.4) | copy-start | bytes 2015236
  252.5 35.6 %collective-permute-start.11 = (bf16[656,256]{1,0:T(8,128)(2,1)}, bf16[656,256]{1,0:T(8,128)(2,1)}, u32[]{:S(2)}, u32[]{:S(2)}) collective-permute-start(bf16[656,256]{1,0:T(8,128)(2,1)} %get-tuple-element.62), channel_id=1, source_target_pairs={{0,16},{4,20},{8,24},{12,28},{16,0},{20,4},{24,8},{28,12},{1,17},{... | collective-permute-start | bytes 1007624 | tf_op jit(solution)/shard_map/ppermute | solution.py:187
  252.5 29.4 %collective-permute-start.8 = (bf16[656,256]{1,0:T(8,128)(2,1)}, bf16[656,256]{1,0:T(8,128)(2,1)}, u32[]{:S(2)}, u32[]{:S(2)}) collective-permute-start(bf16[656,256]{1,0:T(8,128)(2,1)} %get-tuple-element.61), channel_id=1, source_target_pairs={{0,16},{4,20},{8,24},{12,28},{16,0},{20,4},{24,8},{28,12},{1,17},{... | collective-permute-start | bytes 1007624 | tf_op jit(solution)/shard_map/ppermute | solution.py:187
  257.8 1.2 copy-start.17
  260.5 23.3 %slice-start = ((s8[13107200]{0:T(1024)(128)(4,1)}), s8[4194304]{0:T(1024)(128)(4,1)S(1)}, s32[]{:S(2)}) async-start(s8[13107200]{0:T(1024)(128)(4,1)} %bitcast.160), calls=%async_computation.2 | async-start | bytes 8388608
  260.5 23.3 %slice-start.1 = ((s8[13107200]{0:T(1024)(128)(4,1)}), s8[4194304]{0:T(1024)(128)(4,1)S(1)}, s32[]{:S(2)}) async-start(s8[13107200]{0:T(1024)(128)(4,1)} %bitcast.160), calls=%async_computation.3 | async-start | bytes 8388608
  268.1 15.7 %slice-start.2 = ((s8[13107200]{0:T(1024)(128)(4,1)}), s8[4194304]{0:T(1024)(128)(4,1)S(1)}, s32[]{:S(2)}) async-start(s8[13107200]{0:T(1024)(128)(4,1)} %bitcast.160), calls=%async_computation.4 | async-start | bytes 8388608
  268.1 15.7 %slice-start.3 = ((s8[13107200]{0:T(1024)(128)(4,1)}), s8[524288]{0:T(1024)(128)(4,1)S(1)}, s32[]{:S(2)}) async-start(s8[13107200]{0:T(1024)(128)(4,1)} %bitcast.160), calls=%async_computation.5 | async-start | bytes 1048576
  290.3 8.5 %collective-permute-start.9 = (bf16[2,64,5120]{2,1,0:T(8,128)(2,1)S(1)}, bf16[2,64,5120]{2,1,0:T(8,128)(2,1)S(1)}, u32[]{:S(2)}, u32[]{:S(2)}) collective-permute-start(bf16[2,64,5120]{2,1,0:T(8,128)(2,1)S(1)} %dynamic-slice_bitcast_fusion.1), channel_id=1, source_target_pairs={{0,1},{1,0},{2,3},{3,2},{4,5},{5,4},{6,7},{7,6},{8,9},{9,8},{10,11... | collective-permute-start | bytes 3932168 | tf_op jit(solution)/shard_map/ppermute | solution.py:218
  298.2 1.7 copy-start.15
  298.3 3.6 %collective-permute-start.12 = (bf16[2,64,5120]{2,1,0:T(8,128)(2,1)S(1)}, bf16[2,64,5120]{2,1,0:T(8,128)(2,1)S(1)}, u32[]{:S(2)}, u32[]{:S(2)}) collective-permute-start(bf16[2,64,5120]{2,1,0:T(8,128)(2,1)S(1)} %dynamic-slice_bitcast_fusion), channel_id=1, source_target_pairs={{0,1},{1,0},{2,3},{3,2},{4,5},{5,4},{6,7},{7,6},{8,9},{9,8},{10,11... | collective-permute-start | bytes 3932168 | tf_op jit(solution)/shard_map/ppermute | solution.py:218
  300.3 17.2 %collective-permute-start.10 = (bf16[64,5120]{1,0:T(8,128)(2,1)S(1)}, bf16[64,5120]{1,0:T(8,128)(2,1)S(1)}, u32[]{:S(2)}, u32[]{:S(2)}) collective-permute-start(bf16[64,5120]{1,0:T(8,128)(2,1)S(1)} %dynamic-slice_bitcast_fusion.3), channel_id=1, source_target_pairs={{0,2},{1,3},{2,0},{3,1},{4,6},{5,7},{6,4},{7,5},{8,10},{9,11},{10,... | collective-permute-start | bytes 1966088 | tf_op jit(solution)/shard_map/ppermute | solution.py:225
  317.7 16.4 %collective-permute-start.13 = (bf16[64,5120]{1,0:T(8,128)(2,1)S(1)}, bf16[64,5120]{1,0:T(8,128)(2,1)S(1)}, u32[]{:S(2)}, u32[]{:S(2)}) collective-permute-start(bf16[64,5120]{1,0:T(8,128)(2,1)S(1)} %dynamic-slice_bitcast_fusion.2), channel_id=1, source_target_pairs={{0,2},{1,3},{2,0},{3,1},{4,6},{5,7},{6,4},{7,5},{8,10},{9,11},{10,... | collective-permute-start | bytes 1966088 | tf_op jit(solution)/shard_map/ppermute | solution.py:225

commit v5 on v3

--- a/solution.py
+++ b/solution.py
@@ -11,7 +11,7 @@
 TILE_ROWS = 16
 PART_TILE = 32
 HEAD_GROUPS = 2
-VMEM_BYTES = 24 * 1024 * 1024
+VMEM_BYTES = 60 * 1024 * 1024
 
 
 def after(block, *before):
@@ -274,7 +274,9 @@
             ).astype(jnp.bfloat16)
         )
         summed.append(scatter_cores(projected[-1]))
-    pieces = [scatter_chips(block) for block in summed]
+    pieces = []
+    for block in summed:
+        pieces.append(scatter_chips(after(block, *pieces[-1:])))
     return jnp.concatenate(pieces, axis=0).reshape(spatial // head_groups, frames_here, -1)
 
 

time: 324 us -> 320 us (0.988)
  local copies, waits for them, and re-layouts: 32.5 us -> 19.3 us
  Pallas kernels: 35.1 us -> 42.8 us
    unnamed x49 -> x39, local copies, waits for them, and re-layouts: 19.9 us -> 5.13 us
    all_to_all x1, waiting for transfers between devices: 58.5 us -> 64.9 us  [local(): lax.all_to_all(after(tokens, far, *banks[0]), 'frames', 0, 0, tiled=True)]
    pallas_call x2, Pallas kernels: 5.2 us -> 11.5 us  [listed_banks(): pl.pallas_call(listed_kernel, grid_spec=pltpu.PrefetchScalarGridSpec(num_...]
    ppermute x2, waiting for transfers between devices: 24.6 us -> 19.7 us  [scatter_chips(): lax.ppermute(give, 'heads', [(h, (h + 2 * step) % head_groups) for h in r...]
  transfers between devices with their start and end apart: 16 -> 16, of which waited for: 10 -> 9; matrix products, arithmetic and copies ran while one was open for 8% -> 10% of each run, Pallas kernels for 11% -> 13%
where the time goes in v5:
time: 320 us; the launch traced here: 319 us
  waiting for transfers between devices  201 us (63%)
  Pallas kernels  42.8 us (13%)
  starting transfers between devices  28.4 us (9%)
  local copies, waits for them, and re-layouts  19.3 us (6%)
  matrix products  17.4 us (5%)
  other arithmetic  9.67 us (3%)
    ppermute x10, waiting for transfers between devices, swap(): return lax.ppermute(block, 'frames', [(a, a ^ step) for a in range(shards)])  116 us
    all_to_all x1, waiting for transfers between devices, local(): lax.all_to_all(after(tokens, far, *banks[0]), 'frames', 0, 0, tiled=True)  64.9 us
    pallas_call x2, Pallas kernels, attend_bank(): pl.pallas_call(functools.partial(bank_kernel, len(banks)), grid=(heads,),...  21.1 us
    ppermute x2, waiting for transfers between devices, scatter_chips(): lax.ppermute(give, 'heads', [(h, (h + 2 * step) % head_groups) for h in r...  19.7 us
    dot_general x2, matrix products, local(): lax.dot_general(after(combined, *summed[-1:]), out_weight, (((0,), (0,)),...  17.4 us
    ppermute x10, starting transfers between devices, swap(): return lax.ppermute(block, 'frames', [(a, a ^ step) for a in range(shards)])  16.7 us
    pallas_call x2, Pallas kernels, listed_banks(): pl.pallas_call(listed_kernel, grid_spec=pltpu.PrefetchScalarGridSpec(num_...  11.5 us
    pallas_call x1, Pallas kernels, attend_frames(): pl.pallas_call(functools.partial(frame_kernel, frames_here), grid=(width...  10.2 us
  transfers between devices with their start and end apart: 16, of which 9 were waited for; matrix products, arithmetic and copies ran while one was open for 10% of the time, Pallas kernels for 13%

profile of v5, /device:TPU:0, one launch (start us, length us, event | category | flops | bytes accessed | tf_op | source)
XLA Modules:
  0.0 319.1 jit_solution(3050204450385715061)
XLA Ops:
  0.0 2.5 copy.18
  2.5 4.0 %collective-permute-start = (bf16[512,1280]{1,0:T(8,128)(2,1)}, bf16[512,1280]{1,0:T(8,128)(2,1)}, u32[]{:S(2)}, u32[]{:S(2)}) collective-permute-start(bf16[512,1280]{1,0:T(8,128)(2,1)} %bitcast.2.own_ref), channel_id=1, source_target_pairs={{0,16},{4,20},{8,24},{12,28},{16,0},{20,4},{24,8},{28,12},{1,17},{... | collective-permute-start | bytes 3932168 | tf_op jit(solution)/shard_map/ppermute | solution.py:187
  6.6 0.7 reshape.188.slots_ref
  7.3 6.0 %shard_map.64 = (bf16[2,4,96,640]{3,2,1,0:T(8,128)(2,1)}, bf16[2,4,96,640]{3,2,1,0:T(8,128)(2,1)}, bf16[2,4,96,640]{3,2,1,0:T(8,128)(2,1)}, bf16[2,4,96,640]{3,2,1,0:T(8,128)(2,1)}) custom-call(s32[1]{0:T(128)} %bitcast.4.place_ref, s32[16]{0:T(128)} %reshape.188.slots_ref, bf16[2,8,96,1280]{3,2,1,0:T(8,128)(2,1)} %refs_3_.3, ...), custom_call_target="tpu_custom_call" | custom-call | bytes 7864320 | tf_op jit(solution)/shard_map/pallas_call | solution.py:157
  13.3 1.5 collective-permute-start.1
  14.8 1.6 collective-permute-start.2
  16.4 0.4 collective-permute-start.3
  16.8 2.3 copy.20
  19.0 18.0 %collective-permute-done.1.refs_1_ = bf16[2,4,96,640]{3,2,1,0:T(8,128)(2,1)S(1)} collective-permute-done((bf16[2,4,96,640]{3,2,1,0:T(8,128)(2,1)}, bf16[2,4,96,640]{3,2,1,0:T(8,128)(2,1)S(1)}, u32[]{:S(2)}, u32[]{:S(2)}) %collective-permute-start.1) | collective-permute-done | bytes 983072 | tf_op jit(solution)/shard_map/ppermute | solution.py:187
  37.0 29.6 %collective-permute-done.2.refs_2_ = bf16[2,4,96,640]{3,2,1,0:T(8,128)(2,1)S(1)} collective-permute-done((bf16[2,4,96,640]{3,2,1,0:T(8,128)(2,1)}, bf16[2,4,96,640]{3,2,1,0:T(8,128)(2,1)S(1)}, u32[]{:S(2)}, u32[]{:S(2)}) %collective-permute-start.2) | collective-permute-done | bytes 983072 | tf_op jit(solution)/shard_map/ppermute | solution.py:187
  66.6 19.3 %collective-permute-done.3.refs_3_ = bf16[2,4,96,640]{3,2,1,0:T(8,128)(2,1)S(1)} collective-permute-done((bf16[2,4,96,640]{3,2,1,0:T(8,128)(2,1)}, bf16[2,4,96,640]{3,2,1,0:T(8,128)(2,1)S(1)}, u32[]{:S(2)}, u32[]{:S(2)}) %collective-permute-start.3) | collective-permute-done | bytes 983072 | tf_op jit(solution)/shard_map/ppermute | solution.py:187
  85.9 1.0 copy-done.17
  86.9 4.7 %all-to-all-start = ((bf16[8,3,2,32,1280]{4,3,2,1,0:T(8,128)(2,1)}), bf16[8,3,2,32,1280]{4,3,2,1,0:T(8,128)(2,1)}, u32[]{:S(2)}, u32[]{:S(2)}) async-start(bf16[8,3,2,32,1280]{4,3,2,1,0:T(8,128)(2,1)} %bitcast.144), calls=%async_computation | async-start | bytes 7864320 | tf_op jit(solution)/shard_map/all_to_all | solution.py:208
  91.7 0.1 copy.25
  91.8 0.1 copy.26
  91.9 0.6 pad_add_fusion.live_ref
  92.5 10.6 %shard_map.65 = (bf16[2,640,256]{2,1,0:T(8,128)(2,1)}, f32[2,5,256]{2,1,0:T(8,128)}, bf16[2,640,256]{2,1,0:T(8,128)(2,1)}, f32[2,5,256]{2,1,0:T(8,128)}) custom-call(s32[2,2]{1,0:T(2,128)} %pad_add_fusion.live_ref, bf16[512,1280]{1,0:T(8,128)(2,1)} %bitcast.2.own_ref, bf16[512,1280]{1,0:T(8,128)(2,1)} %collective-permute-done.far_ref, ...), custom_call_target="tpu_custom_call" | custom-call | flops 8053063680 | bytes 6553600 | tf_op jit(solution)/shard_map/pallas_call | solution.py:83
  103.1 0.6 reshape.191.slots_ref
  103.7 5.5 %shard_map.67 = (bf16[2,4,96,640]{3,2,1,0:T(8,128)(2,1)}, bf16[2,4,96,640]{3,2,1,0:T(8,128)(2,1)}, bf16[2,4,96,640]{3,2,1,0:T(8,128)(2,1)}, bf16[2,4,96,640]{3,2,1,0:T(8,128)(2,1)}) custom-call(s32[1]{0:T(128)} %bitcast.4.place_ref, s32[16]{0:T(128)} %reshape.191.slots_ref, bf16[2,8,96,1280]{3,2,1,0:T(8,128)(2,1)} %refs_3_.3, ...), custom_call_target="tpu_custom_call" | custom-call | bytes 7864320 | tf_op jit(solution)/shard_map/pallas_call | solution.py:157
  109.2 2.1 collective-permute-start.5
  111.3 1.5 collective-permute-start.6
  112.9 2.9 collective-permute-start.4
  115.9 64.9 %all-to-all-done.token_ref = bf16[8,3,2,32,1280]{4,3,2,1,0:T(8,128)(2,1)} async-done(((bf16[8,3,2,32,1280]{4,3,2,1,0:T(8,128)(2,1)}), bf16[8,3,2,32,1280]{4,3,2,1,0:T(8,128)(2,1)}, u32[]{:S(2)}, u32[]{:S(2)}) %all-to-all-start) | async-done | bytes 3932192 | tf_op jit(solution)/shard_map/all_to_all | solution.py:208
  180.8 10.2 %shard_map.66 = bf16[8,2,32,1280]{3,2,1,0:T(8,128)(2,1)} custom-call(bf16[8,3,2,32,1280]{4,3,2,1,0:T(8,128)(2,1)} %all-to-all-done.token_ref), custom_call_target="tpu_custom_call" | custom-call | flops 2684354560 | bytes 5242880 | tf_op jit(solution)/shard_map/pallas_call | solution.py:125
  191.0 3.7 %all-to-all-start.1 = ((bf16[8,2,32,1280]{3,2,1,0:T(8,128)(2,1)}), bf16[8,2,32,1280]{3,2,1,0:T(8,128)(2,1)S(1)}, u32[]{:S(2)}, u32[]{:S(2)}) async-start(bf16[8,2,32,1280]{3,2,1,0:T(8,128)(2,1)} %shard_map.66), calls=%async_computation.1 | async-start | bytes 2621440 | tf_op jit(solution)/shard_map/all_to_all | solution.py:237
  194.8 23.7 %collective-permute-done.7.refs_3_ = bf16[2,4,96,640]{3,2,1,0:T(8,128)(2,1)} collective-permute-done((bf16[2,4,96,640]{3,2,1,0:T(8,128)(2,1)}, bf16[2,4,96,640]{3,2,1,0:T(8,128)(2,1)}, u32[]{:S(2)}, u32[]{:S(2)}) %collective-permute-start.7) | collective-permute-done | bytes 983072 | tf_op jit(solution)/shard_map/ppermute | solution.py:187
  218.5 10.6 %shard_map.68 = (bf16[2,640,256]{2,1,0:T(8,128)(2,1)}, f32[2,5,256]{2,1,0:T(8,128)}, bf16[2,640,256]{2,1,0:T(8,128)(2,1)}, f32[2,5,256]{2,1,0:T(8,128)}) custom-call(s32[2,2]{1,0:T(2,128)} %pad_add_fusion.live_ref, bf16[512,1280]{1,0:T(8,128)(2,1)} %bitcast.2.own_ref, bf16[512,1280]{1,0:T(8,128)(2,1)} %collective-permute-done.far_ref, ...), custom_call_target="tpu_custom_call" | custom-call | flops 8053063680 | bytes 6553600 | tf_op jit(solution)/shard_map/pallas_call | solution.py:83
  229.1 0.7 reduce-precision_convert_fusion.1
  229.8 1.1 fusion.21
  231.0 0.8 slice_bitcast_fusion.1
  231.8 0.4 copy-done.9
  232.2 0.8 fusion.42
  233.0 2.6 collective-permute-start.11
  235.6 1.1 fusion.24
  236.7 25.4 %collective-permute-done.8 = bf16[656,256]{1,0:T(8,128)(2,1)S(1)} collective-permute-done((bf16[656,256]{1,0:T(8,128)(2,1)S(1)}, bf16[656,256]{1,0:T(8,128)(2,1)S(1)}, u32[]{:S(2)}, u32[]{:S(2)}) %collective-permute-start.8) | collective-permute-done | bytes 335904 | tf_op jit(solution)/shard_map/ppermute | solution.py:187
  262.1 0.1 fusion.25
  262.2 0.1 pad_maximum_fusion
  262.3 1.5 copy.22
  263.9 1.2 copy-done.5
  265.1 8.5 %convolution_convert_fusion.1 = bf16[256,5120]{1,0:T(8,128)(2,1)S(1)} fusion(bf16[1280,5120]{1,0:T(8,128)(2,1)} %param.11, f32[1280,256]{0,1:T(8,128)S(1)} %copy-done.5, bf16[256,1280]{1,0:T(8,128)(2,1)S(1)} %bitcast.161), kind=kOutput, calls=%fused_computation.1 | convolution fusion | flops 3357736960 | bytes 17694720 | tf_op jit(solution)/shard_map/dot_general | solution.py:271
  273.7 1.2 dynamic-slice_bitcast_fusion.1
  274.8 0.7 copy-done.1
  275.6 1.1 slice.132
  276.6 0.8 add_divide_fusion.1
  277.4 0.1 fusion.23
  277.5 0.1 pad_maximum_fusion.1
  277.6 0.4 copy.23
  278.1 0.2 fusion.12
  278.2 0.7 collective-permute-done.9
  278.9 0.9 copy-done.2
  279.8 1.6 fusion.1
  281.4 0.9 dynamic-slice_bitcast_fusion.3
  282.3 1.5 collective-permute-start.10
  283.8 8.9 %convolution_convert_fusion = bf16[256,5120]{1,0:T(8,128)(2,1)S(1)} fusion(bf16[1280,256]{0,1:T(8,128)(2,1)S(1)} %fusion.12, bf16[1280,5120]{1,0:T(8,128)(2,1)} %param.11), kind=kOutput, calls=%fused_computation | convolution fusion | flops 3356753920 | bytes 16384000 | tf_op jit(solution)/shard_map/dot_general | solution.py:271
  292.7 1.3 dynamic-slice_bitcast_fusion
  293.9 0.6 copy-done.3
  294.6 0.2 collective-permute-start.12
  294.7 4.9 %collective-permute-done.10 = bf16[64,5120]{1,0:T(8,128)(2,1)S(1)} collective-permute-done((bf16[64,5120]{1,0:T(8,128)(2,1)}, bf16[64,5120]{1,0:T(8,128)(2,1)S(1)}, u32[]{:S(2)}, u32[]{:S(2)}) %collective-permute-start.10) | collective-permute-done | bytes 655392 | tf_op jit(solution)/shard_map/ppermute | solution.py:225
  299.6 0.2 fusion.13
  299.8 1.6 fusion
  301.5 1.5 collective-permute-start.13
  303.0 14.8 %collective-permute-done.13 = bf16[64,5120]{1,0:T(8,128)(2,1)S(1)} collective-permute-done((bf16[64,5120]{1,0:T(8,128)(2,1)S(1)}, bf16[64,5120]{1,0:T(8,128)(2,1)S(1)}, u32[]{:S(2)}, u32[]{:S(2)}) %collective-permute-start.13) | collective-permute-done | bytes 655392 | tf_op jit(solution)/shard_map/ppermute | solution.py:225
  317.8 0.2 fusion.10
  318.0 1.2 maximum_bitcast_fusion
  (52 shorter events, 0.7 us)
Async XLA Ops:
  0.0 6.5 %copy-start.13 = (s32[8,2]{0,1:T(2,128)S(1)}, s32[8,2]{0,1:T(2,128)}, u32[]{:S(2)}) copy-start(s32[8,2]{0,1:T(2,128)} %param.8) | copy-start | bytes 196
  2.5 83.4 %collective-permute-start = (bf16[512,1280]{1,0:T(8,128)(2,1)}, bf16[512,1280]{1,0:T(8,128)(2,1)}, u32[]{:S(2)}, u32[]{:S(2)}) collective-permute-start(bf16[512,1280]{1,0:T(8,128)(2,1)} %bitcast.2.own_ref), channel_id=1, source_target_pairs={{0,16},{4,20},{8,24},{12,28},{16,0},{20,4},{24,8},{28,12},{1,17},{... | collective-permute-start | bytes 3932168 | tf_op jit(solution)/shard_map/ppermute | solution.py:187
  7.3 9.5 %copy-start = (bf16[3,64,8,1280]{3,2,1,0:T(8,128)(2,1)S(1)}, bf16[3,64,8,1280]{3,2,1,0:T(8,128)(2,1)}, u32[]{:S(2)}) copy-start(bf16[3,64,8,1280]{3,2,1,0:T(8,128)(2,1)} %param.10) | copy-start | bytes 11796484
  13.3 23.8 %collective-permute-start.1 = (bf16[2,4,96,640]{3,2,1,0:T(8,128)(2,1)}, bf16[2,4,96,640]{3,2,1,0:T(8,128)(2,1)S(1)}, u32[]{:S(2)}, u32[]{:S(2)}) collective-permute-start(bf16[2,4,96,640]{3,2,1,0:T(8,128)(2,1)} %get-tuple-element.30), channel_id=1, source_target_pairs={{0,4},{4,0},{8,12},{12,8},{16,20},{20,16},{24,28},{28,24},{1,5},{5... | collective-permute-start | bytes 2949128 | tf_op jit(solution)/shard_map/ppermute | solution.py:187
  14.8 51.8 %collective-permute-start.2 = (bf16[2,4,96,640]{3,2,1,0:T(8,128)(2,1)}, bf16[2,4,96,640]{3,2,1,0:T(8,128)(2,1)S(1)}, u32[]{:S(2)}, u32[]{:S(2)}) collective-permute-start(bf16[2,4,96,640]{3,2,1,0:T(8,128)(2,1)} %get-tuple-element.31), channel_id=1, source_target_pairs={{0,8},{4,12},{8,0},{12,4},{16,24},{20,28},{24,16},{28,20},{1,9},{5... | collective-permute-start | bytes 2949128 | tf_op jit(solution)/shard_map/ppermute | solution.py:187
  16.4 69.6 %collective-permute-start.3 = (bf16[2,4,96,640]{3,2,1,0:T(8,128)(2,1)}, bf16[2,4,96,640]{3,2,1,0:T(8,128)(2,1)S(1)}, u32[]{:S(2)}, u32[]{:S(2)}) collective-permute-start(bf16[2,4,96,640]{3,2,1,0:T(8,128)(2,1)} %get-tuple-element.32), channel_id=1, source_target_pairs={{0,12},{4,8},{8,4},{12,0},{16,28},{20,24},{24,20},{28,16},{1,13},{... | collective-permute-start | bytes 2949128 | tf_op jit(solution)/shard_map/ppermute | solution.py:187
  37.0 48.9 %copy-start.15 = (bf16[2,4,96,640]{3,2,1,0:T(8,128)(2,1)}, bf16[2,4,96,640]{3,2,1,0:T(8,128)(2,1)S(1)}, u32[]{:S(2)}) copy-start(bf16[2,4,96,640]{3,2,1,0:T(8,128)(2,1)S(1)} %collective-permute-done.1.refs_1_) | copy-start | bytes 2949124
  66.6 19.3 %copy-start.16 = (bf16[2,4,96,640]{3,2,1,0:T(8,128)(2,1)}, bf16[2,4,96,640]{3,2,1,0:T(8,128)(2,1)S(1)}, u32[]{:S(2)}) copy-start(bf16[2,4,96,640]{3,2,1,0:T(8,128)(2,1)S(1)} %collective-permute-done.2.refs_2_) | copy-start | bytes 2949124
  85.9 1.0 copy-start.17
  86.9 4.7 %copy-start.14 = (s32[8,2]{0,1:T(2,128)S(1)}, s32[8,2]{0,1:T(2,128)}, u32[]{:S(2)}) copy-start(s32[8,2]{0,1:T(2,128)} %param.9) | copy-start | bytes 196
  86.9 93.9 %all-to-all-start = ((bf16[8,3,2,32,1280]{4,3,2,1,0:T(8,128)(2,1)}), bf16[8,3,2,32,1280]{4,3,2,1,0:T(8,128)(2,1)}, u32[]{:S(2)}, u32[]{:S(2)}) async-start(bf16[8,3,2,32,1280]{4,3,2,1,0:T(8,128)(2,1)} %bitcast.144), calls=%async_computation | async-start | bytes 7864320 | tf_op jit(solution)/shard_map/all_to_all | solution.py:208
  103.7 9.2 %copy-start.10 = (f32[2,5,256]{2,1,0:T(8,128)S(1)}, f32[2,5,256]{2,1,0:T(8,128)}, u32[]{:S(2)}) copy-start(f32[2,5,256]{2,1,0:T(8,128)} %get-tuple-element.36) | copy-start | bytes 30724
  103.7 9.2 %copy-start.8 = (bf16[2,640,256]{2,1,0:T(8,128)(2,1)S(1)}, bf16[2,640,256]{2,1,0:T(8,128)(2,1)}, u32[]{:S(2)}) copy-start(bf16[2,640,256]{2,1,0:T(8,128)(2,1)} %get-tuple-element.35) | copy-start | bytes 1966084
  109.2 6.6 %copy-start.7 = (bf16[2,640,256]{2,1,0:T(8,128)(2,1)S(1)}, bf16[2,640,256]{2,1,0:T(8,128)(2,1)}, u32[]{:S(2)}) copy-start(bf16[2,640,256]{2,1,0:T(8,128)(2,1)} %get-tuple-element.33) | copy-start | bytes 1966084
  109.2 85.5 %collective-permute-start.5 = (bf16[2,4,96,640]{3,2,1,0:T(8,128)(2,1)}, bf16[2,4,96,640]{3,2,1,0:T(8,128)(2,1)}, u32[]{:S(2)}, u32[]{:S(2)}) collective-permute-start(bf16[2,4,96,640]{3,2,1,0:T(8,128)(2,1)} %get-tuple-element.42), channel_id=1, source_target_pairs={{0,4},{4,0},{8,12},{12,8},{16,20},{20,16},{24,28},{28,24},{1,5},{5... | collective-permute-start | bytes 2949128 | tf_op jit(solution)/shard_map/ppermute | solution.py:187
  111.3 83.5 %collective-permute-start.6 = (bf16[2,4,96,640]{3,2,1,0:T(8,128)(2,1)}, bf16[2,4,96,640]{3,2,1,0:T(8,128)(2,1)}, u32[]{:S(2)}, u32[]{:S(2)}) collective-permute-start(bf16[2,4,96,640]{3,2,1,0:T(8,128)(2,1)} %get-tuple-element.43), channel_id=1, source_target_pairs={{0,8},{4,12},{8,0},{12,4},{16,24},{20,28},{24,16},{28,20},{1,9},{5... | collective-permute-start | bytes 2949128 | tf_op jit(solution)/shard_map/ppermute | solution.py:187
  112.8 105.7 %collective-permute-start.7 = (bf16[2,4,96,640]{3,2,1,0:T(8,128)(2,1)}, bf16[2,4,96,640]{3,2,1,0:T(8,128)(2,1)}, u32[]{:S(2)}, u32[]{:S(2)}) collective-permute-start(bf16[2,4,96,640]{3,2,1,0:T(8,128)(2,1)} %get-tuple-element.44), channel_id=1, source_target_pairs={{0,12},{4,8},{8,4},{12,0},{16,28},{20,24},{24,20},{28,16},{1,13},{... | collective-permute-start | bytes 2949128 | tf_op jit(solution)/shard_map/ppermute | solution.py:187
  112.9 116.2 %collective-permute-start.4 = (bf16[2,656,256]{2,1,0:T(8,128)(2,1)S(1)}, bf16[2,656,256]{2,1,0:T(8,128)(2,1)S(1)}, u32[]{:S(2)}, u32[]{:S(2)}) collective-permute-start(bf16[2,656,256]{2,1,0:T(8,128)(2,1)S(1)} %fusion.18), channel_id=1, source_target_pairs={{0,16},{4,20},{8,24},{12,28},{16,0},{20,4},{24,8},{28,12},{1,17},{... | collective-permute-start | bytes 2015240 | tf_op jit(solution)/shard_map/ppermute | solution.py:187
  191.0 72.8 %all-to-all-start.1 = ((bf16[8,2,32,1280]{3,2,1,0:T(8,128)(2,1)}), bf16[8,2,32,1280]{3,2,1,0:T(8,128)(2,1)S(1)}, u32[]{:S(2)}, u32[]{:S(2)}) async-start(bf16[8,2,32,1280]{3,2,1,0:T(8,128)(2,1)} %shard_map.66), calls=%async_computation.1 | async-start | bytes 2621440 | tf_op jit(solution)/shard_map/all_to_all | solution.py:237
  231.0 1.2 copy-start.9
  231.8 1.2 copy-start.12
  231.8 30.3 %collective-permute-start.8 = (bf16[656,256]{1,0:T(8,128)(2,1)S(1)}, bf16[656,256]{1,0:T(8,128)(2,1)S(1)}, u32[]{:S(2)}, u32[]{:S(2)}) collective-permute-start(bf16[656,256]{1,0:T(8,128)(2,1)S(1)} %get-tuple-element.61), channel_id=1, source_target_pairs={{0,16},{4,20},{8,24},{12,28},{16,0},{20,4},{24,8},{28,12},{1,17},{... | collective-permute-start | bytes 1007624 | tf_op jit(solution)/shard_map/ppermute | solution.py:187
  233.0 42.6 %collective-permute-start.11 = (bf16[656,256]{1,0:T(8,128)(2,1)}, bf16[656,256]{1,0:T(8,128)(2,1)}, u32[]{:S(2)}, u32[]{:S(2)}) collective-permute-start(bf16[656,256]{1,0:T(8,128)(2,1)} %get-tuple-element.62), channel_id=1, source_target_pairs={{0,16},{4,20},{8,24},{12,28},{16,0},{20,4},{24,8},{28,12},{1,17},{... | collective-permute-start | bytes 1007624 | tf_op jit(solution)/shard_map/ppermute | solution.py:187
  235.6 26.5 %copy-start.11 = (f32[2,5,256]{2,1,0:T(8,128)S(1)}, f32[2,5,256]{2,1,0:T(8,128)}, u32[]{:S(2)}) copy-start(f32[2,5,256]{2,1,0:T(8,128)} %get-tuple-element.45) | copy-start | bytes 30724
  263.8 1.3 copy-start.5
  273.6 1.9 copy-start.1
  273.6 3.8 %copy-start.6 = (bf16[1,640,256]{2,1,0:T(8,128)(2,1)S(1)}, bf16[1,640,256]{2,1,0:T(8,128)(2,1)}, u32[]{:S(2)}) copy-start(bf16[1,640,256]{2,1,0:T(8,128)(2,1)} %get-tuple-element.65) | copy-start | bytes 983044
  275.5 2.0 copy-start.4
  275.5 3.4 %collective-permute-start.9 = (bf16[2,64,5120]{2,1,0:T(8,128)(2,1)}, bf16[2,64,5120]{2,1,0:T(8,128)(2,1)}, u32[]{:S(2)}, u32[]{:S(2)}) collective-permute-start(bf16[2,64,5120]{2,1,0:T(8,128)(2,1)} %dynamic-slice_bitcast_fusion.1), channel_id=1, source_target_pairs={{0,1},{1,0},{2,3},{3,2},{4,5},{5,4},{6,7},{7,6},{8,9},{9,8},{10,11... | collective-permute-start | bytes 3932168 | tf_op jit(solution)/shard_map/ppermute | solution.py:218
  278.0 1.7 copy-start.2
  282.3 17.3 %collective-permute-start.10 = (bf16[64,5120]{1,0:T(8,128)(2,1)}, bf16[64,5120]{1,0:T(8,128)(2,1)S(1)}, u32[]{:S(2)}, u32[]{:S(2)}) collective-permute-start(bf16[64,5120]{1,0:T(8,128)(2,1)} %dynamic-slice_bitcast_fusion.3), channel_id=1, source_target_pairs={{0,2},{1,3},{2,0},{3,1},{4,6},{5,7},{6,4},{7,5},{8,10},{9,11},{10,... | collective-permute-start | bytes 1966088 | tf_op jit(solution)/shard_map/ppermute | solution.py:225
  292.6 1.9 copy-start.3
  294.6 5.2 %collective-permute-start.12 = (bf16[2,64,5120]{2,1,0:T(8,128)(2,1)}, bf16[2,64,5120]{2,1,0:T(8,128)(2,1)S(1)}, u32[]{:S(2)}, u32[]{:S(2)}) collective-permute-start(bf16[2,64,5120]{2,1,0:T(8,128)(2,1)} %dynamic-slice_bitcast_fusion), channel_id=1, source_target_pairs={{0,1},{1,0},{2,3},{3,2},{4,5},{5,4},{6,7},{7,6},{8,9},{9,8},{10,11... | collective-permute-start | bytes 3932168 | tf_op jit(solution)/shard_map/ppermute | solution.py:218
  301.5 16.4 %collective-permute-start.13 = (bf16[64,5120]{1,0:T(8,128)(2,1)S(1)}, bf16[64,5120]{1,0:T(8,128)(2,1)S(1)}, u32[]{:S(2)}, u32[]{:S(2)}) collective-permute-start(bf16[64,5120]{1,0:T(8,128)(2,1)S(1)} %dynamic-slice_bitcast_fusion.2), channel_id=1, source_target_pairs={{0,2},{1,3},{2,0},{3,1},{4,6},{5,7},{6,4},{7,5},{8,10},{9,11},{10,... | collective-permute-start | bytes 1966088 | tf_op jit(solution)/shard_map/ppermute | solution.py:225

commit v6 on v5

--- a/solution.py
+++ b/solution.py
@@ -10,7 +10,7 @@
 HEAD_DIM = 128
 TILE_ROWS = 16
 PART_TILE = 32
-HEAD_GROUPS = 2
+HEAD_FIFTHS = ((4, 1), (2, 2), (0, 2))
 VMEM_BYTES = 60 * 1024 * 1024
 
 
@@ -71,11 +71,11 @@
             level_ref[part, pl.ds(head, 1), :] = level[:, here]
 
 
-def attend_bank(group, parts, rows, live, own, far, banks):
+def attend_bank(first, parts, rows, live, own, far, banks):
     width = banks[0].shape[3]
     heads = width // HEAD_DIM
     keys_each = 2 * sum(bank.shape[2] for bank in banks)
-    query_spec = pl.BlockSpec((parts * rows, HEAD_DIM), lambda h: (0, group * heads + h))
+    query_spec = pl.BlockSpec((parts * rows, HEAD_DIM), lambda h: (0, first + h))
     out = jax.ShapeDtypeStruct((parts, width, rows), jnp.bfloat16)
     level = jax.ShapeDtypeStruct((parts, heads, rows), jnp.float32)
     out_spec = pl.BlockSpec((parts, HEAD_DIM, rows), lambda h: (0, h, 0))
@@ -143,14 +143,14 @@
         target[...] = source[...]
 
 
-def listed_banks(place, char_slots, char_bank, half, group, group_width):
+def listed_banks(place, char_slots, char_bank, half, column, group_width):
     _, _, tokens, _ = char_bank.shape
     block = (2, 1, tokens, group_width)
 
     def source(step):
         def index(entry, place_ref, slots_ref):
             shard = place_ref[0] ^ step ^ (entry // 2 * half)
-            return 0, slots_ref[shard * 2 + entry % 2], 0, group
+            return 0, slots_ref[shard * 2 + entry % 2], 0, column
 
         return pl.BlockSpec(block, index)
 
@@ -193,11 +193,16 @@
     own = by_part(bank_query)
     far = swap(own, half)
 
-    groups = HEAD_GROUPS if heads_here % HEAD_GROUPS == 0 else 1
+    fifth = heads_here // 5
+    spans = [(low * fifth, size * fifth) for low, size in HEAD_FIFTHS]
+    if heads_here % 5:
+        spans = [(0, heads_here)]
+    groups = len(spans)
 
     def banks_of(group, *before):
+        first, size = spans[group]
         blocks = listed_banks(
-            place, after(char_slots, *before), char_bank, half, group, width // groups
+            place, after(char_slots, *before), char_bank, half, first // size, size * HEAD_DIM
         )
         blocks = [blocks[0]] + [swap(blocks[step], step) for step in range(1, half)]
         return blocks if char_bank.shape[2] % TILE_ROWS == 0 else [jnp.concatenate(blocks, axis=2)]
@@ -226,16 +231,16 @@
             )
         return added(*parcels)
 
-    split = (heads_here // groups, HEAD_DIM, rows)
     results = []
-    for group in range(groups):
-        near_out, near_level, far_out, far_level = attend_bank(group, parts, rows, live, own, far, banks[group])
-        if group < groups - 1:
-            banks.append(banks_of(group + 1, far_level))
+    for group, (first, _) in enumerate(spans):
+        near_out, near_level, far_out, far_level = attend_bank(first, parts, rows, live, own, far, banks[group])
         if group == 0:
+            if groups > 1:
+                banks.append(banks_of(1, far_level))
             frame_parts = attend_frames(frames_here, after(tokens, far_level))
             back = lax.all_to_all(frame_parts, "frames", 0, 0, tiled=True)
             live = after(live, frame_parts)
+            banks += [banks_of(later, tokens) for later in range(2, groups)]
         message = jnp.concatenate([far_out, *in_three(far_level)], axis=1)
         message = jnp.pad(message, ((0, 0), (0, -message.shape[1] % TILE_ROWS), (0, 0)))
         if group < groups - 1:
@@ -251,19 +256,21 @@
     def share_of(group, part, *before):
         near_out, near_level, got = results[group]
         got = after(got[part], *(before if group == groups - 1 else ()))
-        size = heads_here // groups
-        got_level = sum(wide(got[low : low + size]) for low in range(width // groups, width // groups + 3 * size, size))
+        size = spans[group][1]
+        deep, split = size * HEAD_DIM, (size, HEAD_DIM, rows)
+        got_level = sum(wide(got[low : low + size]) for low in range(deep, deep + 3 * size, size))
         peak = jnp.maximum(near_level[part], got_level)
         near_share, got_share = jnp.exp(near_level[part] - peak), jnp.exp(got_level - peak)
         total = near_share + got_share
         return (
             wide(near_out[part].reshape(split)) * (near_share / total)[:, None, :]
-            + wide(got[: width // groups].reshape(split)) * (got_share / total)[:, None, :]
-        )
-
+            + wide(got[:deep].reshape(split)) * (got_share / total)[:, None, :]
+        )
+
+    in_order = sorted(range(groups), key=lambda group: spans[group][0])
     projected, summed = [], []
     for part in range(parts):
-        shares = [share_of(group, part, *projected[-1:]) for group in range(groups)]
+        shares = [share_of(group, part, *projected[-1:]) for group in in_order]
         ref_out = jnp.concatenate(shares, axis=0).reshape(width, rows)
         frame_out = back[:, part].reshape(rows, width)
         combined = (ref_out + wide(frame_out.T)).astype(jnp.bfloat16)

time: 320 us -> 339 us (1.059)
  starting transfers between devices: 28.4 us -> 42.4 us
  Pallas kernels: 42.8 us -> 48.6 us
    ppermute x10 -> x14, waiting for transfers between devices: 116 us -> 108 us  [swap(): return lax.ppermute(block, 'frames', [(a, a ^ step) for a in range(shards)])]
    ppermute x10 -> x14, starting transfers between devices: 16.7 us -> 23.4 us  [swap(): return lax.ppermute(block, 'frames', [(a, a ^ step) for a in range(shards)])]
    all_to_all x1, starting transfers between devices: 3.75 us -> 9.99 us  [local(): back = lax.all_to_all(frame_parts, 'frames', 0, 0, tiled=True)]
    all_to_all x1, waiting for transfers between devices: 64.9 us -> 70.4 us  [local(): lax.all_to_all(after(tokens, far, *banks[0]), 'frames', 0, 0, tiled=True)]
    pallas_call x2 -> x3, Pallas kernels: 11.5 us -> 15.2 us  [listed_banks(): pl.pallas_call(listed_kernel, grid_spec=pltpu.PrefetchScalarGridSpec(num_...]
    pallas_call x2 -> x3, Pallas kernels: 21.1 us -> 23.2 us  [attend_bank(): pl.pallas_call(functools.partial(bank_kernel, len(banks)), grid=(heads,),...]
  transfers between devices with their start and end apart: 16 -> 20, of which waited for: 9 -> 12; matrix products, arithmetic and copies ran while one was open for 10% -> 10% of each run, Pallas kernels for 13% -> 14%
where the time goes in v6:
time: 339 us; the launch traced here: 337 us
  waiting for transfers between devices  199 us (59%)
  Pallas kernels  48.6 us (14%)
  starting transfers between devices  42.4 us (13%)
  local copies, waits for them, and re-layouts  18.4 us (5%)
  matrix products  17.4 us (5%)
  other arithmetic  10.6 us (3%)
    ppermute x14, waiting for transfers between devices, swap(): return lax.ppermute(block, 'frames', [(a, a ^ step) for a in range(shards)])  108 us
    all_to_all x1, waiting for transfers between devices, local(): lax.all_to_all(after(tokens, far, *banks[0]), 'frames', 0, 0, tiled=True)  70.4 us
    ppermute x14, starting transfers between devices, swap(): return lax.ppermute(block, 'frames', [(a, a ^ step) for a in range(shards)])  23.4 us
    pallas_call x3, Pallas kernels, attend_bank(): pl.pallas_call(functools.partial(bank_kernel, len(banks)), grid=(heads,),...  23.2 us
    ppermute x2, waiting for transfers between devices, scatter_chips(): lax.ppermute(give, 'heads', [(h, (h + 2 * step) % head_groups) for h in r...  19.7 us
    dot_general x2, matrix products, local(): lax.dot_general(after(combined, *summed[-1:]), out_weight, (((0,), (0,)),...  17.4 us
    pallas_call x3, Pallas kernels, listed_banks(): pl.pallas_call(listed_kernel, grid_spec=pltpu.PrefetchScalarGridSpec(num_...  15.2 us
    pallas_call x1, Pallas kernels, attend_frames(): pl.pallas_call(functools.partial(frame_kernel, frames_here), grid=(width...  10.2 us
  transfers between devices with their start and end apart: 20, of which 12 were waited for; matrix products, arithmetic and copies ran while one was open for 10% of the time, Pallas kernels for 14%

profile of v6, /device:TPU:0, one launch (start us, length us, event | category | flops | bytes accessed | tf_op | source)
XLA Modules:
  0.0 337.3 jit_solution(8723310873067145933)
XLA Ops:
  0.0 2.5 copy.20
  2.5 4.0 %collective-permute-start = (bf16[512,1280]{1,0:T(8,128)(2,1)}, bf16[512,1280]{1,0:T(8,128)(2,1)}, u32[]{:S(2)}, u32[]{:S(2)}) collective-permute-start(bf16[512,1280]{1,0:T(8,128)(2,1)} %bitcast.5.own_ref), channel_id=1, source_target_pairs={{0,16},{4,20},{8,24},{12,28},{16,0},{20,4},{24,8},{28,12},{1,17},{... | collective-permute-start | bytes 3932168 | tf_op jit(solution)/shard_map/ppermute | solution.py:187
  6.6 0.6 reshape.316.slots_ref
  7.2 4.9 %shard_map.64 = (bf16[2,4,96,256]{3,2,1,0:T(8,128)(2,1)}, bf16[2,4,96,256]{3,2,1,0:T(8,128)(2,1)}, bf16[2,4,96,256]{3,2,1,0:T(8,128)(2,1)}, bf16[2,4,96,256]{3,2,1,0:T(8,128)(2,1)}) custom-call(s32[1]{0:T(128)} %bitcast.6.place_ref, s32[16]{0:T(128)} %reshape.316.slots_ref, bf16[2,8,96,1280]{3,2,1,0:T(8,128)(2,1)} %refs_3_.5, ...), custom_call_target="tpu_custom_call" | custom-call | bytes 3145728 | tf_op jit(solution)/shard_map/pallas_call | solution.py:157
  12.1 1.5 collective-permute-start.1
  13.7 1.6 collective-permute-start.2
  15.2 0.4 collective-permute-start.3
  15.6 2.3 copy.19
  17.9 5.6 %collective-permute-done.1.refs_1_ = bf16[2,4,96,256]{3,2,1,0:T(8,128)(2,1)S(1)} collective-permute-done((bf16[2,4,96,256]{3,2,1,0:T(8,128)(2,1)}, bf16[2,4,96,256]{3,2,1,0:T(8,128)(2,1)S(1)}, u32[]{:S(2)}, u32[]{:S(2)}) %collective-permute-start.1) | collective-permute-done | bytes 393248 | tf_op jit(solution)/shard_map/ppermute | solution.py:187
  23.5 21.0 %collective-permute-done.2.refs_2_ = bf16[2,4,96,256]{3,2,1,0:T(8,128)(2,1)S(1)} collective-permute-done((bf16[2,4,96,256]{3,2,1,0:T(8,128)(2,1)}, bf16[2,4,96,256]{3,2,1,0:T(8,128)(2,1)S(1)}, u32[]{:S(2)}, u32[]{:S(2)}) %collective-permute-start.2) | collective-permute-done | bytes 393248 | tf_op jit(solution)/shard_map/ppermute | solution.py:187
  44.5 7.3 %collective-permute-done.3.refs_3_ = bf16[2,4,96,256]{3,2,1,0:T(8,128)(2,1)S(1)} collective-permute-done((bf16[2,4,96,256]{3,2,1,0:T(8,128)(2,1)}, bf16[2,4,96,256]{3,2,1,0:T(8,128)(2,1)S(1)}, u32[]{:S(2)}, u32[]{:S(2)}) %collective-permute-start.3) | collective-permute-done | bytes 393248 | tf_op jit(solution)/shard_map/ppermute | solution.py:187
  51.8 11.9 %collective-permute-done.far_ref = bf16[512,1280]{1,0:T(8,128)(2,1)} collective-permute-done((bf16[512,1280]{1,0:T(8,128)(2,1)}, bf16[512,1280]{1,0:T(8,128)(2,1)}, u32[]{:S(2)}, u32[]{:S(2)}) %collective-permute-start) | collective-permute-done | bytes 1310752 | tf_op jit(solution)/shard_map/ppermute | solution.py:187
  63.7 5.8 %all-to-all-start = ((bf16[8,3,2,32,1280]{4,3,2,1,0:T(8,128)(2,1)}), bf16[8,3,2,32,1280]{4,3,2,1,0:T(8,128)(2,1)}, u32[]{:S(2)}, u32[]{:S(2)}) async-start(bf16[8,3,2,32,1280]{4,3,2,1,0:T(8,128)(2,1)} %bitcast.172), calls=%async_computation | async-start | bytes 7864320 | tf_op jit(solution)/shard_map/all_to_all | solution.py:213
  69.8 0.6 pad_add_fusion.live_ref
  70.4 5.4 %shard_map.65 = (bf16[2,256,256]{2,1,0:T(8,128)(2,1)}, f32[2,2,256]{2,1,0:T(2,128)}, bf16[2,256,256]{2,1,0:T(8,128)(2,1)}, f32[2,2,256]{2,1,0:T(2,128)}) custom-call(s32[2,2]{1,0:T(2,128)} %pad_add_fusion.live_ref, bf16[512,1280]{1,0:T(8,128)(2,1)} %bitcast.5.own_ref, bf16[512,1280]{1,0:T(8,128)(2,1)} %collective-permute-done.far_ref, ...), custom_call_target="tpu_custom_call" | custom-call | flops 3221225472 | bytes 2621440 | tf_op jit(solution)/shard_map/pallas_call | solution.py:83
  75.9 0.6 reshape.318.slots_ref
  76.5 5.2 %shard_map.69 = (bf16[2,4,96,512]{3,2,1,0:T(8,128)(2,1)}, bf16[2,4,96,512]{3,2,1,0:T(8,128)(2,1)}, bf16[2,4,96,512]{3,2,1,0:T(8,128)(2,1)}, bf16[2,4,96,512]{3,2,1,0:T(8,128)(2,1)}) custom-call(s32[1]{0:T(128)} %bitcast.6.place_ref, s32[16]{0:T(128)} %reshape.318.slots_ref, bf16[2,8,96,1280]{3,2,1,0:T(8,128)(2,1)} %refs_3_.5, ...), custom_call_target="tpu_custom_call" | custom-call | bytes 6291456 | tf_op jit(solution)/shard_map/pallas_call | solution.py:157
  81.7 2.9 collective-permute-start.10
  84.6 0.6 collective-permute-start.8
  85.3 2.9 collective-permute-start.12
  88.2 70.4 %all-to-all-done.token_ref = bf16[8,3,2,32,1280]{4,3,2,1,0:T(8,128)(2,1)} async-done(((bf16[8,3,2,32,1280]{4,3,2,1,0:T(8,128)(2,1)}), bf16[8,3,2,32,1280]{4,3,2,1,0:T(8,128)(2,1)}, u32[]{:S(2)}, u32[]{:S(2)}) %all-to-all-start) | async-done | bytes 3932192 | tf_op jit(solution)/shard_map/all_to_all | solution.py:213
  158.7 10.2 %shard_map.66 = bf16[8,2,32,1280]{3,2,1,0:T(8,128)(2,1)} custom-call(bf16[8,3,2,32,1280]{4,3,2,1,0:T(8,128)(2,1)} %all-to-all-done.token_ref), custom_call_target="tpu_custom_call" | custom-call | flops 2684354560 | bytes 5242880 | tf_op jit(solution)/shard_map/pallas_call | solution.py:125
  168.8 10.0 %all-to-all-start.1 = ((bf16[8,2,32,1280]{3,2,1,0:T(8,128)(2,1)}), bf16[8,2,32,1280]{3,2,1,0:T(8,128)(2,1)S(1)}, u32[]{:S(2)}, u32[]{:S(2)}) async-start(bf16[8,2,32,1280]{3,2,1,0:T(8,128)(2,1)} %shard_map.66), calls=%async_computation.1 | async-start | bytes 2621440 | tf_op jit(solution)/shard_map/all_to_all | solution.py:241
  178.9 0.7 reshape.317.slots_ref
  179.6 5.1 %shard_map.67 = (bf16[2,4,96,512]{3,2,1,0:T(8,128)(2,1)}, bf16[2,4,96,512]{3,2,1,0:T(8,128)(2,1)}, bf16[2,4,96,512]{3,2,1,0:T(8,128)(2,1)}, bf16[2,4,96,512]{3,2,1,0:T(8,128)(2,1)}) custom-call(s32[1]{0:T(128)} %bitcast.6.place_ref, s32[16]{0:T(128)} %reshape.317.slots_ref, bf16[2,8,96,1280]{3,2,1,0:T(8,128)(2,1)} %refs_3_.5, ...), custom_call_target="tpu_custom_call" | custom-call | bytes 6291456 | tf_op jit(solution)/shard_map/pallas_call | solution.py:157
  184.7 2.0 collective-permute-start.4
  186.7 1.5 collective-permute-start.5
  188.3 8.9 %shard_map.70 = (bf16[2,512,256]{2,1,0:T(8,128)(2,1)}, f32[2,4,256]{2,1,0:T(4,128)}, bf16[2,512,256]{2,1,0:T(8,128)(2,1)}, f32[2,4,256]{2,1,0:T(4,128)}) custom-call(s32[2,2]{1,0:T(2,128)} %pad_add_fusion.live_ref, bf16[512,1280]{1,0:T(8,128)(2,1)} %bitcast.5.own_ref, bf16[512,1280]{1,0:T(8,128)(2,1)} %collective-permute-done.far_ref, ...), custom_call_target="tpu_custom_call" | custom-call | flops 6442450944 | bytes 5242880 | tf_op jit(solution)/shard_map/pallas_call | solution.py:83
  197.2 0.8 reduce-precision_convert_fusion.1
  198.0 1.1 fusion.26
  199.0 2.9 collective-permute-start.11
  202.0 11.1 %collective-permute-done.4.refs_1_ = bf16[2,4,96,512]{3,2,1,0:T(8,128)(2,1)} collective-permute-done((bf16[2,4,96,512]{3,2,1,0:T(8,128)(2,1)}, bf16[2,4,96,512]{3,2,1,0:T(8,128)(2,1)}, u32[]{:S(2)}, u32[]{:S(2)}) %collective-permute-start.4) | collective-permute-done | bytes 786464 | tf_op jit(solution)/shard_map/ppermute | solution.py:187
  213.1 19.2 %collective-permute-done.5.refs_2_ = bf16[2,4,96,512]{3,2,1,0:T(8,128)(2,1)} collective-permute-done((bf16[2,4,96,512]{3,2,1,0:T(8,128)(2,1)}, bf16[2,4,96,512]{3,2,1,0:T(8,128)(2,1)}, u32[]{:S(2)}, u32[]{:S(2)}) %collective-permute-start.5) | collective-permute-done | bytes 786464 | tf_op jit(solution)/shard_map/ppermute | solution.py:187
  232.3 16.4 %collective-permute-done.6.refs_3_ = bf16[2,4,96,512]{3,2,1,0:T(8,128)(2,1)} collective-permute-done((bf16[2,4,96,512]{3,2,1,0:T(8,128)(2,1)}, bf16[2,4,96,512]{3,2,1,0:T(8,128)(2,1)}, u32[]{:S(2)}, u32[]{:S(2)}) %collective-permute-start.6) | collective-permute-done | bytes 786464 | tf_op jit(solution)/shard_map/ppermute | solution.py:187
  248.6 8.8 %shard_map.68 = (bf16[2,512,256]{2,1,0:T(8,128)(2,1)}, f32[2,4,256]{2,1,0:T(4,128)}, bf16[2,512,256]{2,1,0:T(8,128)(2,1)}, f32[2,4,256]{2,1,0:T(4,128)}) custom-call(s32[2,2]{1,0:T(2,128)} %pad_add_fusion.live_ref, bf16[512,1280]{1,0:T(8,128)(2,1)} %bitcast.5.own_ref, bf16[512,1280]{1,0:T(8,128)(2,1)} %collective-permute-done.far_ref, ...), custom_call_target="tpu_custom_call" | custom-call | flops 6442450944 | bytes 5242880 | tf_op jit(solution)/shard_map/pallas_call | solution.py:83
  257.5 0.7 reduce-precision_convert_fusion.3
  258.2 1.1 fusion.23
  259.3 0.7 slice_bitcast_fusion.1
  260.1 2.9 collective-permute-start.15
  263.2 0.7 fusion.60
  264.0 0.2 fusion.27
  264.2 16.0 %collective-permute-done.7 = bf16[528,256]{1,0:T(8,128)(2,1)S(1)} collective-permute-done((bf16[528,256]{1,0:T(8,128)(2,1)S(1)}, bf16[528,256]{1,0:T(8,128)(2,1)S(1)}, u32[]{:S(2)}, u32[]{:S(2)}) %collective-permute-start.7) | collective-permute-done | bytes 270368 | tf_op jit(solution)/shard_map/ppermute | solution.py:187
  280.5 1.5 copy.24
  282.0 1.2 copy-done.4
  283.2 8.6 %convolution_convert_fusion.1 = bf16[256,5120]{1,0:T(8,128)(2,1)S(1)} fusion(bf16[1280,5120]{1,0:T(8,128)(2,1)} %param.11, f32[1280,256]{0,1:T(8,128)S(1)} %copy-done.4, bf16[256,1280]{1,0:T(8,128)(2,1)S(1)} %bitcast.189), kind=kOutput, calls=%fused_computation.1 | convolution fusion | flops 3357736960 | bytes 17694720 | tf_op jit(solution)/shard_map/dot_general | solution.py:278
  291.8 1.2 dynamic-slice_bitcast_fusion.1
  293.0 0.7 copy-done.1
  293.7 1.0 slice.188
  294.7 0.8 add_divide_fusion.3
  295.7 0.4 copy.25
  296.2 0.8 collective-permute-done.13
  297.1 0.7 copy-done.2
  297.8 1.6 fusion.1
  299.4 0.9 dynamic-slice_bitcast_fusion.3
  300.3 1.5 collective-permute-start.14
  301.8 8.9 %convolution_convert_fusion = bf16[256,5120]{1,0:T(8,128)(2,1)S(1)} fusion(bf16[1280,256]{0,1:T(8,128)(2,1)S(1)} %fusion.4, bf16[1280,5120]{1,0:T(8,128)(2,1)} %param.11), kind=kOutput, calls=%fused_computation | convolution fusion | flops 3356753920 | bytes 16384000 | tf_op jit(solution)/shard_map/dot_general | solution.py:278
  310.7 1.3 dynamic-slice_bitcast_fusion
  312.0 0.6 copy-done.3
  312.6 0.2 collective-permute-start.16
  312.8 4.9 %collective-permute-done.14 = bf16[64,5120]{1,0:T(8,128)(2,1)S(1)} collective-permute-done((bf16[64,5120]{1,0:T(8,128)(2,1)}, bf16[64,5120]{1,0:T(8,128)(2,1)S(1)}, u32[]{:S(2)}, u32[]{:S(2)}) %collective-permute-start.14) | collective-permute-done | bytes 655392 | tf_op jit(solution)/shard_map/ppermute | solution.py:230
  317.8 1.6 fusion
  319.5 1.6 collective-permute-start.17
  321.1 14.9 %collective-permute-done.17 = bf16[64,5120]{1,0:T(8,128)(2,1)S(1)} collective-permute-done((bf16[64,5120]{1,0:T(8,128)(2,1)S(1)}, bf16[64,5120]{1,0:T(8,128)(2,1)S(1)}, u32[]{:S(2)}, u32[]{:S(2)}) %collective-permute-start.17) | collective-permute-done | bytes 655392 | tf_op jit(solution)/shard_map/ppermute | solution.py:230
  336.1 1.2 maximum_bitcast_fusion
  (76 shorter events, 2.1 us)
Async XLA Ops:
  0.0 6.5 %copy-start.10 = (s32[8,2]{0,1:T(2,128)S(1)}, s32[8,2]{0,1:T(2,128)}, u32[]{:S(2)}) copy-start(s32[8,2]{0,1:T(2,128)} %param.8) | copy-start | bytes 196
  2.5 61.2 %collective-permute-start = (bf16[512,1280]{1,0:T(8,128)(2,1)}, bf16[512,1280]{1,0:T(8,128)(2,1)}, u32[]{:S(2)}, u32[]{:S(2)}) collective-permute-start(bf16[512,1280]{1,0:T(8,128)(2,1)} %bitcast.5.own_ref), channel_id=1, source_target_pairs={{0,16},{4,20},{8,24},{12,28},{16,0},{20,4},{24,8},{28,12},{1,17},{... | collective-permute-start | bytes 3932168 | tf_op jit(solution)/shard_map/ppermute | solution.py:187
  7.2 8.4 %copy-start = (bf16[3,64,8,1280]{3,2,1,0:T(8,128)(2,1)S(1)}, bf16[3,64,8,1280]{3,2,1,0:T(8,128)(2,1)}, u32[]{:S(2)}) copy-start(bf16[3,64,8,1280]{3,2,1,0:T(8,128)(2,1)} %param.10) | copy-start | bytes 11796484
  12.1 11.4 %collective-permute-start.1 = (bf16[2,4,96,256]{3,2,1,0:T(8,128)(2,1)}, bf16[2,4,96,256]{3,2,1,0:T(8,128)(2,1)S(1)}, u32[]{:S(2)}, u32[]{:S(2)}) collective-permute-start(bf16[2,4,96,256]{3,2,1,0:T(8,128)(2,1)} %get-tuple-element.40), channel_id=1, source_target_pairs={{0,4},{4,0},{8,12},{12,8},{16,20},{20,16},{24,28},{28,24},{1,5},{5... | collective-permute-start | bytes 1179656 | tf_op jit(solution)/shard_map/ppermute | solution.py:187
  13.7 30.8 %collective-permute-start.2 = (bf16[2,4,96,256]{3,2,1,0:T(8,128)(2,1)}, bf16[2,4,96,256]{3,2,1,0:T(8,128)(2,1)S(1)}, u32[]{:S(2)}, u32[]{:S(2)}) collective-permute-start(bf16[2,4,96,256]{3,2,1,0:T(8,128)(2,1)} %get-tuple-element.41), channel_id=1, source_target_pairs={{0,8},{4,12},{8,0},{12,4},{16,24},{20,28},{24,16},{28,20},{1,9},{5... | collective-permute-start | bytes 1179656 | tf_op jit(solution)/shard_map/ppermute | solution.py:187
  15.2 36.5 %collective-permute-start.3 = (bf16[2,4,96,256]{3,2,1,0:T(8,128)(2,1)}, bf16[2,4,96,256]{3,2,1,0:T(8,128)(2,1)S(1)}, u32[]{:S(2)}, u32[]{:S(2)}) collective-permute-start(bf16[2,4,96,256]{3,2,1,0:T(8,128)(2,1)} %get-tuple-element.42), channel_id=1, source_target_pairs={{0,12},{4,8},{8,4},{12,0},{16,28},{20,24},{24,20},{28,16},{1,13},{... | collective-permute-start | bytes 1179656 | tf_op jit(solution)/shard_map/ppermute | solution.py:187
  23.5 40.2 %copy-start.17 = (bf16[2,4,96,256]{3,2,1,0:T(8,128)(2,1)}, bf16[2,4,96,256]{3,2,1,0:T(8,128)(2,1)S(1)}, u32[]{:S(2)}) copy-start(bf16[2,4,96,256]{3,2,1,0:T(8,128)(2,1)S(1)} %collective-permute-done.1.refs_1_) | copy-start | bytes 1179652
  44.5 19.2 %copy-start.18 = (bf16[2,4,96,256]{3,2,1,0:T(8,128)(2,1)}, bf16[2,4,96,256]{3,2,1,0:T(8,128)(2,1)S(1)}, u32[]{:S(2)}) copy-start(bf16[2,4,96,256]{3,2,1,0:T(8,128)(2,1)S(1)} %collective-permute-done.2.refs_2_) | copy-start | bytes 1179652
  51.8 11.9 %copy-start.19 = (bf16[2,4,96,256]{3,2,1,0:T(8,128)(2,1)}, bf16[2,4,96,256]{3,2,1,0:T(8,128)(2,1)S(1)}, u32[]{:S(2)}) copy-start(bf16[2,4,96,256]{3,2,1,0:T(8,128)(2,1)S(1)} %collective-permute-done.3.refs_3_) | copy-start | bytes 1179652
  63.7 5.8 %copy-start.14 = (s32[8,2]{0,1:T(2,128)S(1)}, s32[8,2]{0,1:T(2,128)}, u32[]{:S(2)}) copy-start(s32[8,2]{0,1:T(2,128)} %param.9) | copy-start | bytes 196
  63.7 95.0 %all-to-all-start = ((bf16[8,3,2,32,1280]{4,3,2,1,0:T(8,128)(2,1)}), bf16[8,3,2,32,1280]{4,3,2,1,0:T(8,128)(2,1)}, u32[]{:S(2)}, u32[]{:S(2)}) async-start(bf16[8,3,2,32,1280]{4,3,2,1,0:T(8,128)(2,1)} %bitcast.172), calls=%async_computation | async-start | bytes 7864320 | tf_op jit(solution)/shard_map/all_to_all | solution.py:213
  76.5 8.8 %copy-start.13 = (f32[2,2,256]{2,1,0:T(2,128)S(1)}, f32[2,2,256]{2,1,0:T(2,128)}, u32[]{:S(2)}) copy-start(f32[2,2,256]{2,1,0:T(2,128)} %get-tuple-element.44) | copy-start | bytes 12292
  76.5 8.8 %copy-start.9 = (bf16[2,256,256]{2,1,0:T(8,128)(2,1)S(1)}, bf16[2,256,256]{2,1,0:T(8,128)(2,1)}, u32[]{:S(2)}) copy-start(bf16[2,256,256]{2,1,0:T(8,128)(2,1)} %get-tuple-element.68) | copy-start | bytes 786436
  76.5 11.7 %copy-start.8 = (bf16[2,256,256]{2,1,0:T(8,128)(2,1)S(1)}, bf16[2,256,256]{2,1,0:T(8,128)(2,1)}, u32[]{:S(2)}) copy-start(bf16[2,256,256]{2,1,0:T(8,128)(2,1)} %get-tuple-element.66) | copy-start | bytes 786436
  81.7 105.0 %collective-permute-start.10 = (bf16[2,4,96,512]{3,2,1,0:T(8,128)(2,1)}, bf16[2,4,96,512]{3,2,1,0:T(8,128)(2,1)S(1)}, u32[]{:S(2)}, u32[]{:S(2)}) collective-permute-start(bf16[2,4,96,512]{3,2,1,0:T(8,128)(2,1)} %get-tuple-element.60), channel_id=1, source_target_pairs={{0,12},{4,8},{8,4},{12,0},{16,28},{20,24},{24,20},{28,16},{1,13},{... | collective-permute-start | bytes 2359304 | tf_op jit(solution)/shard_map/ppermute | solution.py:187
  84.6 103.6 %collective-permute-start.8 = (bf16[2,4,96,512]{3,2,1,0:T(8,128)(2,1)}, bf16[2,4,96,512]{3,2,1,0:T(8,128)(2,1)}, u32[]{:S(2)}, u32[]{:S(2)}) collective-permute-start(bf16[2,4,96,512]{3,2,1,0:T(8,128)(2,1)} %get-tuple-element.58), channel_id=1, source_target_pairs={{0,4},{4,0},{8,12},{12,8},{16,20},{20,16},{24,28},{28,24},{1,5},{5... | collective-permute-start | bytes 2359304 | tf_op jit(solution)/shard_map/ppermute | solution.py:187
  85.2 103.1 %collective-permute-start.9 = (bf16[2,4,96,512]{3,2,1,0:T(8,128)(2,1)}, bf16[2,4,96,512]{3,2,1,0:T(8,128)(2,1)}, u32[]{:S(2)}, u32[]{:S(2)}) collective-permute-start(bf16[2,4,96,512]{3,2,1,0:T(8,128)(2,1)} %get-tuple-element.59), channel_id=1, source_target_pairs={{0,8},{4,12},{8,0},{12,4},{16,24},{20,28},{24,16},{28,20},{1,9},{5... | collective-permute-start | bytes 2359304 | tf_op jit(solution)/shard_map/ppermute | solution.py:187
  85.3 174.8 %collective-permute-start.12 = (bf16[2,272,256]{2,1,0:T(8,128)(2,1)S(1)}, bf16[2,272,256]{2,1,0:T(8,128)(2,1)S(1)}, u32[]{:S(2)}, u32[]{:S(2)}) collective-permute-start(bf16[2,272,256]{2,1,0:T(8,128)(2,1)S(1)} %fusion.33), channel_id=1, source_target_pairs={{0,16},{4,20},{8,24},{12,28},{16,0},{20,4},{24,8},{28,12},{1,17},{... | collective-permute-start | bytes 835592 | tf_op jit(solution)/shard_map/ppermute | solution.py:187
  168.8 113.1 %all-to-all-start.1 = ((bf16[8,2,32,1280]{3,2,1,0:T(8,128)(2,1)}), bf16[8,2,32,1280]{3,2,1,0:T(8,128)(2,1)S(1)}, u32[]{:S(2)}, u32[]{:S(2)}) async-start(bf16[8,2,32,1280]{3,2,1,0:T(8,128)(2,1)} %shard_map.66), calls=%async_computation.1 | async-start | bytes 2621440 | tf_op jit(solution)/shard_map/all_to_all | solution.py:241
  184.7 28.4 %collective-permute-start.4 = (bf16[2,4,96,512]{3,2,1,0:T(8,128)(2,1)}, bf16[2,4,96,512]{3,2,1,0:T(8,128)(2,1)}, u32[]{:S(2)}, u32[]{:S(2)}) collective-permute-start(bf16[2,4,96,512]{3,2,1,0:T(8,128)(2,1)} %get-tuple-element.49), channel_id=1, source_target_pairs={{0,4},{4,0},{8,12},{12,8},{16,20},{20,16},{24,28},{28,24},{1,5},{5... | collective-permute-start | bytes 2359304 | tf_op jit(solution)/shard_map/ppermute | solution.py:187
  186.7 1.6 copy-start.16
  186.7 45.6 %collective-permute-start.5 = (bf16[2,4,96,512]{3,2,1,0:T(8,128)(2,1)}, bf16[2,4,96,512]{3,2,1,0:T(8,128)(2,1)}, u32[]{:S(2)}, u32[]{:S(2)}) collective-permute-start(bf16[2,4,96,512]{3,2,1,0:T(8,128)(2,1)} %get-tuple-element.50), channel_id=1, source_target_pairs={{0,8},{4,12},{8,0},{12,4},{16,24},{20,28},{24,16},{28,20},{1,9},{5... | collective-permute-start | bytes 2359304 | tf_op jit(solution)/shard_map/ppermute | solution.py:187
  188.2 60.5 %collective-permute-start.6 = (bf16[2,4,96,512]{3,2,1,0:T(8,128)(2,1)}, bf16[2,4,96,512]{3,2,1,0:T(8,128)(2,1)}, u32[]{:S(2)}, u32[]{:S(2)}) collective-permute-start(bf16[2,4,96,512]{3,2,1,0:T(8,128)(2,1)} %get-tuple-element.51), channel_id=1, source_target_pairs={{0,12},{4,8},{8,4},{12,0},{16,28},{20,24},{24,20},{28,16},{1,13},{... | collective-permute-start | bytes 2359304 | tf_op jit(solution)/shard_map/ppermute | solution.py:187
  197.2 4.8 %copy-start.7 = (bf16[2,512,256]{2,1,0:T(8,128)(2,1)S(1)}, bf16[2,512,256]{2,1,0:T(8,128)(2,1)}, u32[]{:S(2)}) copy-start(bf16[2,512,256]{2,1,0:T(8,128)(2,1)} %get-tuple-element.61) | copy-start | bytes 1572868
  199.0 61.0 %collective-permute-start.11 = (bf16[2,528,256]{2,1,0:T(8,128)(2,1)S(1)}, bf16[2,528,256]{2,1,0:T(8,128)(2,1)S(1)}, u32[]{:S(2)}, u32[]{:S(2)}) collective-permute-start(bf16[2,528,256]{2,1,0:T(8,128)(2,1)S(1)} %fusion.26), channel_id=1, source_target_pairs={{0,16},{4,20},{8,24},{12,28},{16,0},{20,4},{24,8},{28,12},{1,17},{... | collective-permute-start | bytes 1622024 | tf_op jit(solution)/shard_map/ppermute | solution.py:187
  257.5 5.5 %copy-start.15 = (f32[2,2,256]{2,1,0:T(2,128)S(1)}, f32[2,2,256]{2,1,0:T(2,128)}, u32[]{:S(2)}) copy-start(f32[2,2,256]{2,1,0:T(2,128)} %get-tuple-element.67) | copy-start | bytes 12292
  257.5 5.6 %copy-start.12 = (f32[2,4,256]{2,1,0:T(4,128)S(1)}, f32[2,4,256]{2,1,0:T(4,128)}, u32[]{:S(2)}) copy-start(f32[2,4,256]{2,1,0:T(4,128)} %get-tuple-element.62) | copy-start | bytes 24580
  259.3 3.9 %copy-start.6 = (bf16[2,512,256]{2,1,0:T(8,128)(2,1)S(1)}, bf16[2,512,256]{2,1,0:T(8,128)(2,1)}, u32[]{:S(2)}) copy-start(bf16[2,512,256]{2,1,0:T(8,128)(2,1)} %get-tuple-element.52) | copy-start | bytes 1572868
  260.0 20.2 %collective-permute-start.7 = (bf16[528,256]{1,0:T(8,128)(2,1)S(1)}, bf16[528,256]{1,0:T(8,128)(2,1)S(1)}, u32[]{:S(2)}, u32[]{:S(2)}) collective-permute-start(bf16[528,256]{1,0:T(8,128)(2,1)S(1)} %get-tuple-element.85), channel_id=1, source_target_pairs={{0,16},{4,20},{8,24},{12,28},{16,0},{20,4},{24,8},{28,12},{1,17},{... | collective-permute-start | bytes 811016 | tf_op jit(solution)/shard_map/ppermute | solution.py:187
  260.1 33.7 %collective-permute-start.15 = (bf16[528,256]{1,0:T(8,128)(2,1)}, bf16[528,256]{1,0:T(8,128)(2,1)}, u32[]{:S(2)}, u32[]{:S(2)}) collective-permute-start(bf16[528,256]{1,0:T(8,128)(2,1)} %get-tuple-element.86), channel_id=1, source_target_pairs={{0,16},{4,20},{8,24},{12,28},{16,0},{20,4},{24,8},{28,12},{1,17},{... | collective-permute-start | bytes 811016 | tf_op jit(solution)/shard_map/ppermute | solution.py:187
  264.0 16.2 %copy-start.11 = (f32[2,4,256]{2,1,0:T(4,128)S(1)}, f32[2,4,256]{2,1,0:T(4,128)}, u32[]{:S(2)}) copy-start(f32[2,4,256]{2,1,0:T(4,128)} %get-tuple-element.53) | copy-start | bytes 24580
  281.9 1.3 copy-start.4
  291.8 1.9 copy-start.1
  291.8 3.6 %copy-start.5 = (bf16[1,512,256]{2,1,0:T(8,128)(2,1)S(1)}, bf16[1,512,256]{2,1,0:T(8,128)(2,1)}, u32[]{:S(2)}) copy-start(bf16[1,512,256]{2,1,0:T(8,128)(2,1)} %get-tuple-element.89) | copy-start | bytes 786436
  293.7 3.4 %collective-permute-start.13 = (bf16[2,64,5120]{2,1,0:T(8,128)(2,1)}, bf16[2,64,5120]{2,1,0:T(8,128)(2,1)}, u32[]{:S(2)}, u32[]{:S(2)}) collective-permute-start(bf16[2,64,5120]{2,1,0:T(8,128)(2,1)} %dynamic-slice_bitcast_fusion.1), channel_id=1, source_target_pairs={{0,1},{1,0},{2,3},{3,2},{4,5},{5,4},{6,7},{7,6},{8,9},{9,8},{10,11... | collective-permute-start | bytes 3932168 | tf_op jit(solution)/shard_map/ppermute | solution.py:223
  296.1 1.7 copy-start.2
  300.3 17.4 %collective-permute-start.14 = (bf16[64,5120]{1,0:T(8,128)(2,1)}, bf16[64,5120]{1,0:T(8,128)(2,1)S(1)}, u32[]{:S(2)}, u32[]{:S(2)}) collective-permute-start(bf16[64,5120]{1,0:T(8,128)(2,1)} %dynamic-slice_bitcast_fusion.3), channel_id=1, source_target_pairs={{0,2},{1,3},{2,0},{3,1},{4,6},{5,7},{6,4},{7,5},{8,10},{9,11},{10,... | collective-permute-start | bytes 1966088 | tf_op jit(solution)/shard_map/ppermute | solution.py:230
  310.7 1.9 copy-start.3
  312.6 5.2 %collective-permute-start.16 = (bf16[2,64,5120]{2,1,0:T(8,128)(2,1)}, bf16[2,64,5120]{2,1,0:T(8,128)(2,1)S(1)}, u32[]{:S(2)}, u32[]{:S(2)}) collective-permute-start(bf16[2,64,5120]{2,1,0:T(8,128)(2,1)} %dynamic-slice_bitcast_fusion), channel_id=1, source_target_pairs={{0,1},{1,0},{2,3},{3,2},{4,5},{5,4},{6,7},{7,6},{8,9},{9,8},{10,11... | collective-permute-start | bytes 3932168 | tf_op jit(solution)/shard_map/ppermute | solution.py:223
  319.5 16.4 %collective-permute-start.17 = (bf16[64,5120]{1,0:T(8,128)(2,1)S(1)}, bf16[64,5120]{1,0:T(8,128)(2,1)S(1)}, u32[]{:S(2)}, u32[]{:S(2)}) collective-permute-start(bf16[64,5120]{1,0:T(8,128)(2,1)S(1)} %dynamic-slice_bitcast_fusion.2), channel_id=1, source_target_pairs={{0,2},{1,3},{2,0},{3,1},{4,6},{5,7},{6,4},{7,5},{8,10},{9,11},{10,... | collective-permute-start | bytes 1966088 | tf_op jit(solution)/shard_map/ppermute | solution.py:230

commit v7 on v6

--- a/solution.py
+++ b/solution.py
@@ -199,12 +199,14 @@
         spans = [(0, heads_here)]
     groups = len(spans)
 
-    def banks_of(group, *before):
+    def banks_of(group, before=(), before_near=()):
         first, size = spans[group]
         blocks = listed_banks(
             place, after(char_slots, *before), char_bank, half, first // size, size * HEAD_DIM
         )
-        blocks = [blocks[0]] + [swap(blocks[step], step) for step in range(1, half)]
+        blocks = [blocks[0]] + [
+            swap(after(blocks[step], *(before_near if step == 1 else ())), step) for step in range(1, half)
+        ]
         return blocks if char_bank.shape[2] % TILE_ROWS == 0 else [jnp.concatenate(blocks, axis=2)]
 
     banks = [banks_of(0)]
@@ -236,11 +238,11 @@
         near_out, near_level, far_out, far_level = attend_bank(first, parts, rows, live, own, far, banks[group])
         if group == 0:
             if groups > 1:
-                banks.append(banks_of(1, far_level))
+                banks.append(banks_of(1, [far_level]))
+                banks += [banks_of(later, [far_level], [tokens]) for later in range(2, groups)]
             frame_parts = attend_frames(frames_here, after(tokens, far_level))
             back = lax.all_to_all(frame_parts, "frames", 0, 0, tiled=True)
             live = after(live, frame_parts)
-            banks += [banks_of(later, tokens) for later in range(2, groups)]
         message = jnp.concatenate([far_out, *in_three(far_level)], axis=1)
         message = jnp.pad(message, ((0, 0), (0, -message.shape[1] % TILE_ROWS), (0, 0)))
         if group < groups - 1:

time: 339 us -> 336 us (level)
  starting transfers between devices: 42.4 us -> 31.5 us
  waiting for transfers between devices: 199 us -> 208 us
    ppermute x14, waiting for transfers between devices: 108 us -> 124 us  [swap(): return lax.ppermute(block, 'frames', [(a, a ^ step) for a in range(shards)])]
    all_to_all x1, waiting for transfers between devices: 70.4 us -> 63.5 us  [local(): lax.all_to_all(after(tokens, far, *banks[0]), 'frames', 0, 0, tiled=True)]
    all_to_all x1, starting transfers between devices: 9.99 us -> 3.75 us  [local(): back = lax.all_to_all(frame_parts, 'frames', 0, 0, tiled=True)]
    ppermute x14, starting transfers between devices: 23.4 us -> 18.7 us  [swap(): return lax.ppermute(block, 'frames', [(a, a ^ step) for a in range(shards)])]
  transfers between devices with their start and end apart: 20 -> 20, of which waited for: 12 -> 12; matrix products, arithmetic and copies ran while one was open for 10% -> 10% of each run, Pallas kernels for 14% -> 15%
where the time goes in v7:
time: 336 us; the launch traced here: 334 us
  waiting for transfers between devices  208 us (62%)
  Pallas kernels  48.6 us (14%)
  starting transfers between devices  31.5 us (9%)
  local copies, waits for them, and re-layouts  17.7 us (5%)
  matrix products  17.4 us (5%)
  other arithmetic  10.6 us (3%)
    ppermute x14, waiting for transfers between devices, swap(): return lax.ppermute(block, 'frames', [(a, a ^ step) for a in range(shards)])  124 us
    all_to_all x1, waiting for transfers between devices, local(): lax.all_to_all(after(tokens, far, *banks[0]), 'frames', 0, 0, tiled=True)  63.5 us
    pallas_call x3, Pallas kernels, attend_bank(): pl.pallas_call(functools.partial(bank_kernel, len(banks)), grid=(heads,),...  23.2 us
    ppermute x2, waiting for transfers between devices, scatter_chips(): lax.ppermute(give, 'heads', [(h, (h + 2 * step) % head_groups) for h in r...  19.7 us
    ppermute x14, starting transfers between devices, swap(): return lax.ppermute(block, 'frames', [(a, a ^ step) for a in range(shards)])  18.7 us
    dot_general x2, matrix products, local(): lax.dot_general(after(combined, *summed[-1:]), out_weight, (((0,), (0,)),...  17.4 us
    pallas_call x3, Pallas kernels, listed_banks(): pl.pallas_call(listed_kernel, grid_spec=pltpu.PrefetchScalarGridSpec(num_...  15.2 us
    pallas_call x1, Pallas kernels, attend_frames(): pl.pallas_call(functools.partial(frame_kernel, frames_here), grid=(width...  10.2 us
  transfers between devices with their start and end apart: 20, of which 12 were waited for; matrix products, arithmetic and copies ran while one was open for 10% of the time, Pallas kernels for 15%

profile of v7, /device:TPU:0, one launch (start us, length us, event | category | flops | bytes accessed | tf_op | source)
XLA Modules:
  0.0 334.4 jit_solution(18035054900731040314)
XLA Ops:
  0.0 2.5 copy.19
  2.5 4.0 %collective-permute-start = (bf16[512,1280]{1,0:T(8,128)(2,1)}, bf16[512,1280]{1,0:T(8,128)(2,1)}, u32[]{:S(2)}, u32[]{:S(2)}) collective-permute-start(bf16[512,1280]{1,0:T(8,128)(2,1)} %bitcast.5.own_ref), channel_id=1, source_target_pairs={{0,16},{4,20},{8,24},{12,28},{16,0},{20,4},{24,8},{28,12},{1,17},{... | collective-permute-start | bytes 3932168 | tf_op jit(solution)/shard_map/ppermute | solution.py:187
  6.6 0.6 reshape.314.slots_ref
  7.2 4.9 %shard_map.64 = (bf16[2,4,96,256]{3,2,1,0:T(8,128)(2,1)}, bf16[2,4,96,256]{3,2,1,0:T(8,128)(2,1)}, bf16[2,4,96,256]{3,2,1,0:T(8,128)(2,1)}, bf16[2,4,96,256]{3,2,1,0:T(8,128)(2,1)}) custom-call(s32[1]{0:T(128)} %bitcast.6.place_ref, s32[16]{0:T(128)} %reshape.314.slots_ref, bf16[2,8,96,1280]{3,2,1,0:T(8,128)(2,1)} %refs_3_.5, ...), custom_call_target="tpu_custom_call" | custom-call | bytes 3145728 | tf_op jit(solution)/shard_map/pallas_call | solution.py:157
  12.1 1.5 collective-permute-start.1
  13.7 1.6 collective-permute-start.2
  15.2 0.4 collective-permute-start.3
  15.6 2.3 copy.18
  17.9 5.6 %collective-permute-done.1.refs_1_ = bf16[2,4,96,256]{3,2,1,0:T(8,128)(2,1)S(1)} collective-permute-done((bf16[2,4,96,256]{3,2,1,0:T(8,128)(2,1)}, bf16[2,4,96,256]{3,2,1,0:T(8,128)(2,1)S(1)}, u32[]{:S(2)}, u32[]{:S(2)}) %collective-permute-start.1) | collective-permute-done | bytes 393248 | tf_op jit(solution)/shard_map/ppermute | solution.py:187
  23.5 21.0 %collective-permute-done.2.refs_2_ = bf16[2,4,96,256]{3,2,1,0:T(8,128)(2,1)S(1)} collective-permute-done((bf16[2,4,96,256]{3,2,1,0:T(8,128)(2,1)}, bf16[2,4,96,256]{3,2,1,0:T(8,128)(2,1)S(1)}, u32[]{:S(2)}, u32[]{:S(2)}) %collective-permute-start.2) | collective-permute-done | bytes 393248 | tf_op jit(solution)/shard_map/ppermute | solution.py:187
  44.5 7.3 %collective-permute-done.3.refs_3_ = bf16[2,4,96,256]{3,2,1,0:T(8,128)(2,1)S(1)} collective-permute-done((bf16[2,4,96,256]{3,2,1,0:T(8,128)(2,1)}, bf16[2,4,96,256]{3,2,1,0:T(8,128)(2,1)S(1)}, u32[]{:S(2)}, u32[]{:S(2)}) %collective-permute-start.3) | collective-permute-done | bytes 393248 | tf_op jit(solution)/shard_map/ppermute | solution.py:187
  51.8 11.9 %collective-permute-done.far_ref = bf16[512,1280]{1,0:T(8,128)(2,1)} collective-permute-done((bf16[512,1280]{1,0:T(8,128)(2,1)}, bf16[512,1280]{1,0:T(8,128)(2,1)}, u32[]{:S(2)}, u32[]{:S(2)}) %collective-permute-start) | collective-permute-done | bytes 1310752 | tf_op jit(solution)/shard_map/ppermute | solution.py:187
  63.7 5.8 %all-to-all-start = ((bf16[8,3,2,32,1280]{4,3,2,1,0:T(8,128)(2,1)}), bf16[8,3,2,32,1280]{4,3,2,1,0:T(8,128)(2,1)}, u32[]{:S(2)}, u32[]{:S(2)}) async-start(bf16[8,3,2,32,1280]{4,3,2,1,0:T(8,128)(2,1)} %bitcast.172), calls=%async_computation | async-start | bytes 7864320 | tf_op jit(solution)/shard_map/all_to_all | solution.py:215
  69.8 0.6 pad_add_fusion.live_ref
  70.4 5.4 %shard_map.65 = (bf16[2,256,256]{2,1,0:T(8,128)(2,1)}, f32[2,2,256]{2,1,0:T(2,128)}, bf16[2,256,256]{2,1,0:T(8,128)(2,1)}, f32[2,2,256]{2,1,0:T(2,128)}) custom-call(s32[2,2]{1,0:T(2,128)} %pad_add_fusion.live_ref, bf16[512,1280]{1,0:T(8,128)(2,1)} %bitcast.5.own_ref, bf16[512,1280]{1,0:T(8,128)(2,1)} %collective-permute-done.far_ref, ...), custom_call_target="tpu_custom_call" | custom-call | flops 3221225472 | bytes 2621440 | tf_op jit(solution)/shard_map/pallas_call | solution.py:83
  75.9 0.6 reshape.315.slots_ref
  76.5 5.1 %shard_map.67 = (bf16[2,4,96,512]{3,2,1,0:T(8,128)(2,1)}, bf16[2,4,96,512]{3,2,1,0:T(8,128)(2,1)}, bf16[2,4,96,512]{3,2,1,0:T(8,128)(2,1)}, bf16[2,4,96,512]{3,2,1,0:T(8,128)(2,1)}) custom-call(s32[1]{0:T(128)} %bitcast.6.place_ref, s32[16]{0:T(128)} %reshape.315.slots_ref, bf16[2,8,96,1280]{3,2,1,0:T(8,128)(2,1)} %refs_3_.5, ...), custom_call_target="tpu_custom_call" | custom-call | bytes 6291456 | tf_op jit(solution)/shard_map/pallas_call | solution.py:157
  81.6 5.2 %shard_map.69 = (bf16[2,4,96,512]{3,2,1,0:T(8,128)(2,1)}, bf16[2,4,96,512]{3,2,1,0:T(8,128)(2,1)}, bf16[2,4,96,512]{3,2,1,0:T(8,128)(2,1)}, bf16[2,4,96,512]{3,2,1,0:T(8,128)(2,1)}) custom-call(s32[1]{0:T(128)} %bitcast.6.place_ref, s32[16]{0:T(128)} %reshape.315.slots_ref, bf16[2,8,96,1280]{3,2,1,0:T(8,128)(2,1)} %refs_3_.5, ...), custom_call_target="tpu_custom_call" | custom-call | bytes 6291456 | tf_op jit(solution)/shard_map/pallas_call | solution.py:157
  86.9 2.0 collective-permute-start.5
  88.9 1.5 collective-permute-start.6
  90.4 1.5 collective-permute-start.10
  91.8 1.5 collective-permute-start.8
  93.3 0.6 collective-permute-start.9
  93.9 63.5 %all-to-all-done.token_ref = bf16[8,3,2,32,1280]{4,3,2,1,0:T(8,128)(2,1)} async-done(((bf16[8,3,2,32,1280]{4,3,2,1,0:T(8,128)(2,1)}), bf16[8,3,2,32,1280]{4,3,2,1,0:T(8,128)(2,1)}, u32[]{:S(2)}, u32[]{:S(2)}) %all-to-all-start) | async-done | bytes 3932192 | tf_op jit(solution)/shard_map/all_to_all | solution.py:215
  157.5 10.2 %shard_map.66 = bf16[8,2,32,1280]{3,2,1,0:T(8,128)(2,1)} custom-call(bf16[8,3,2,32,1280]{4,3,2,1,0:T(8,128)(2,1)} %all-to-all-done.token_ref), custom_call_target="tpu_custom_call" | custom-call | flops 2684354560 | bytes 5242880 | tf_op jit(solution)/shard_map/pallas_call | solution.py:125
  167.6 3.7 %all-to-all-start.1 = ((bf16[8,2,32,1280]{3,2,1,0:T(8,128)(2,1)}), bf16[8,2,32,1280]{3,2,1,0:T(8,128)(2,1)S(1)}, u32[]{:S(2)}, u32[]{:S(2)}) async-start(bf16[8,2,32,1280]{3,2,1,0:T(8,128)(2,1)} %shard_map.66), calls=%async_computation.1 | async-start | bytes 2621440 | tf_op jit(solution)/shard_map/all_to_all | solution.py:244
  171.4 23.4 %collective-permute-done.10.refs_3_ = bf16[2,4,96,512]{3,2,1,0:T(8,128)(2,1)S(1)} collective-permute-done((bf16[2,4,96,512]{3,2,1,0:T(8,128)(2,1)}, bf16[2,4,96,512]{3,2,1,0:T(8,128)(2,1)S(1)}, u32[]{:S(2)}, u32[]{:S(2)}) %collective-permute-start.10) | collective-permute-done | bytes 786464 | tf_op jit(solution)/shard_map/ppermute | solution.py:187
  194.8 1.2 collective-permute-start.4
  196.1 28.0 %collective-permute-done.9.refs_2_ = bf16[2,4,96,512]{3,2,1,0:T(8,128)(2,1)} collective-permute-done((bf16[2,4,96,512]{3,2,1,0:T(8,128)(2,1)}, bf16[2,4,96,512]{3,2,1,0:T(8,128)(2,1)}, u32[]{:S(2)}, u32[]{:S(2)}) %collective-permute-start.9) | collective-permute-done | bytes 786464 | tf_op jit(solution)/shard_map/ppermute | solution.py:187
  224.1 8.9 %shard_map.70 = (bf16[2,512,256]{2,1,0:T(8,128)(2,1)}, f32[2,4,256]{2,1,0:T(4,128)}, bf16[2,512,256]{2,1,0:T(8,128)(2,1)}, f32[2,4,256]{2,1,0:T(4,128)}) custom-call(s32[2,2]{1,0:T(2,128)} %pad_add_fusion.live_ref, bf16[512,1280]{1,0:T(8,128)(2,1)} %bitcast.5.own_ref, bf16[512,1280]{1,0:T(8,128)(2,1)} %collective-permute-done.far_ref, ...), custom_call_target="tpu_custom_call" | custom-call | flops 6442450944 | bytes 5242880 | tf_op jit(solution)/shard_map/pallas_call | solution.py:83
  233.0 0.8 reduce-precision_convert_fusion.1
  233.8 1.1 fusion.26
  235.0 8.9 %shard_map.68 = (bf16[2,512,256]{2,1,0:T(8,128)(2,1)}, f32[2,4,256]{2,1,0:T(4,128)}, bf16[2,512,256]{2,1,0:T(8,128)(2,1)}, f32[2,4,256]{2,1,0:T(4,128)}) custom-call(s32[2,2]{1,0:T(2,128)} %pad_add_fusion.live_ref, bf16[512,1280]{1,0:T(8,128)(2,1)} %bitcast.5.own_ref, bf16[512,1280]{1,0:T(8,128)(2,1)} %collective-permute-done.far_ref, ...), custom_call_target="tpu_custom_call" | custom-call | flops 6442450944 | bytes 5242880 | tf_op jit(solution)/shard_map/pallas_call | solution.py:83
  243.9 0.7 reduce-precision_convert_fusion.3
  244.6 1.1 fusion.23
  245.7 0.7 slice_bitcast_fusion.1
  246.4 2.9 collective-permute-start.7
  249.4 16.4 %collective-permute-done.11 = bf16[2,528,256]{2,1,0:T(8,128)(2,1)S(1)} collective-permute-done((bf16[2,528,256]{2,1,0:T(8,128)(2,1)S(1)}, bf16[2,528,256]{2,1,0:T(8,128)(2,1)S(1)}, u32[]{:S(2)}, u32[]{:S(2)}) %collective-permute-start.11) | collective-permute-done | bytes 540704 | tf_op jit(solution)/shard_map/ppermute | solution.py:187
  266.0 0.8 fusion.60
  266.8 0.2 fusion.27
  267.0 10.3 %collective-permute-done.7 = bf16[528,256]{1,0:T(8,128)(2,1)S(1)} collective-permute-done((bf16[528,256]{1,0:T(8,128)(2,1)S(1)}, bf16[528,256]{1,0:T(8,128)(2,1)S(1)}, u32[]{:S(2)}, u32[]{:S(2)}) %collective-permute-start.7) | collective-permute-done | bytes 270368 | tf_op jit(solution)/shard_map/ppermute | solution.py:187
  277.6 1.5 copy.22
  279.2 1.2 copy-done.4
  280.4 8.6 %convolution_convert_fusion.1 = bf16[256,5120]{1,0:T(8,128)(2,1)S(1)} fusion(bf16[1280,5120]{1,0:T(8,128)(2,1)} %param.11, f32[1280,256]{0,1:T(8,128)S(1)} %copy-done.4, bf16[256,1280]{1,0:T(8,128)(2,1)S(1)} %bitcast.189), kind=kOutput, calls=%fused_computation.1 | convolution fusion | flops 3357736960 | bytes 17694720 | tf_op jit(solution)/shard_map/dot_general | solution.py:280
  289.0 1.2 dynamic-slice_bitcast_fusion.1
  290.1 0.7 copy-done.1
  290.9 1.0 slice.188
  291.8 0.8 add_divide_fusion.3
  292.8 0.4 copy.23
  293.4 0.8 collective-permute-done.13
  294.2 0.7 copy-done.2
  294.9 1.6 fusion.1
  296.6 0.9 dynamic-slice_bitcast_fusion.3
  297.5 1.5 collective-permute-start.14
  299.0 8.9 %convolution_convert_fusion = bf16[256,5120]{1,0:T(8,128)(2,1)S(1)} fusion(bf16[1280,256]{0,1:T(8,128)(2,1)S(1)} %fusion.4, bf16[1280,5120]{1,0:T(8,128)(2,1)} %param.11), kind=kOutput, calls=%fused_computation | convolution fusion | flops 3356753920 | bytes 16384000 | tf_op jit(solution)/shard_map/dot_general | solution.py:280
  307.8 1.3 dynamic-slice_bitcast_fusion
  309.1 0.6 copy-done.3
  309.7 0.2 collective-permute-start.16
  310.0 4.8 %collective-permute-done.14 = bf16[64,5120]{1,0:T(8,128)(2,1)S(1)} collective-permute-done((bf16[64,5120]{1,0:T(8,128)(2,1)}, bf16[64,5120]{1,0:T(8,128)(2,1)S(1)}, u32[]{:S(2)}, u32[]{:S(2)}) %collective-permute-start.14) | collective-permute-done | bytes 655392 | tf_op jit(solution)/shard_map/ppermute | solution.py:232
  315.0 1.6 fusion
  316.7 1.6 collective-permute-start.17
  318.2 14.9 %collective-permute-done.17 = bf16[64,5120]{1,0:T(8,128)(2,1)S(1)} collective-permute-done((bf16[64,5120]{1,0:T(8,128)(2,1)S(1)}, bf16[64,5120]{1,0:T(8,128)(2,1)S(1)}, u32[]{:S(2)}, u32[]{:S(2)}) %collective-permute-start.17) | collective-permute-done | bytes 655392 | tf_op jit(solution)/shard_map/ppermute | solution.py:232
  333.1 0.2 fusion.2
  333.3 1.2 maximum_bitcast_fusion
  (74 shorter events, 1.7 us)
Async XLA Ops:
  0.0 6.5 %copy-start.12 = (s32[8,2]{0,1:T(2,128)S(1)}, s32[8,2]{0,1:T(2,128)}, u32[]{:S(2)}) copy-start(s32[8,2]{0,1:T(2,128)} %param.8) | copy-start | bytes 196
  2.5 61.2 %collective-permute-start = (bf16[512,1280]{1,0:T(8,128)(2,1)}, bf16[512,1280]{1,0:T(8,128)(2,1)}, u32[]{:S(2)}, u32[]{:S(2)}) collective-permute-start(bf16[512,1280]{1,0:T(8,128)(2,1)} %bitcast.5.own_ref), channel_id=1, source_target_pairs={{0,16},{4,20},{8,24},{12,28},{16,0},{20,4},{24,8},{28,12},{1,17},{... | collective-permute-start | bytes 3932168 | tf_op jit(solution)/shard_map/ppermute | solution.py:187
  7.2 8.4 %copy-start = (bf16[3,64,8,1280]{3,2,1,0:T(8,128)(2,1)S(1)}, bf16[3,64,8,1280]{3,2,1,0:T(8,128)(2,1)}, u32[]{:S(2)}) copy-start(bf16[3,64,8,1280]{3,2,1,0:T(8,128)(2,1)} %param.10) | copy-start | bytes 11796484
  12.1 11.4 %collective-permute-start.1 = (bf16[2,4,96,256]{3,2,1,0:T(8,128)(2,1)}, bf16[2,4,96,256]{3,2,1,0:T(8,128)(2,1)S(1)}, u32[]{:S(2)}, u32[]{:S(2)}) collective-permute-start(bf16[2,4,96,256]{3,2,1,0:T(8,128)(2,1)} %get-tuple-element.40), channel_id=1, source_target_pairs={{0,4},{4,0},{8,12},{12,8},{16,20},{20,16},{24,28},{28,24},{1,5},{5... | collective-permute-start | bytes 1179656 | tf_op jit(solution)/shard_map/ppermute | solution.py:187
  13.7 30.8 %collective-permute-start.2 = (bf16[2,4,96,256]{3,2,1,0:T(8,128)(2,1)}, bf16[2,4,96,256]{3,2,1,0:T(8,128)(2,1)S(1)}, u32[]{:S(2)}, u32[]{:S(2)}) collective-permute-start(bf16[2,4,96,256]{3,2,1,0:T(8,128)(2,1)} %get-tuple-element.41), channel_id=1, source_target_pairs={{0,8},{4,12},{8,0},{12,4},{16,24},{20,28},{24,16},{28,20},{1,9},{5... | collective-permute-start | bytes 1179656 | tf_op jit(solution)/shard_map/ppermute | solution.py:187
  15.2 36.5 %collective-permute-start.3 = (bf16[2,4,96,256]{3,2,1,0:T(8,128)(2,1)}, bf16[2,4,96,256]{3,2,1,0:T(8,128)(2,1)S(1)}, u32[]{:S(2)}, u32[]{:S(2)}) collective-permute-start(bf16[2,4,96,256]{3,2,1,0:T(8,128)(2,1)} %get-tuple-element.42), channel_id=1, source_target_pairs={{0,12},{4,8},{8,4},{12,0},{16,28},{20,24},{24,20},{28,16},{1,13},{... | collective-permute-start | bytes 1179656 | tf_op jit(solution)/shard_map/ppermute | solution.py:187
  23.5 40.2 %copy-start.17 = (bf16[2,4,96,256]{3,2,1,0:T(8,128)(2,1)}, bf16[2,4,96,256]{3,2,1,0:T(8,128)(2,1)S(1)}, u32[]{:S(2)}) copy-start(bf16[2,4,96,256]{3,2,1,0:T(8,128)(2,1)S(1)} %collective-permute-done.1.refs_1_) | copy-start | bytes 1179652
  44.5 19.2 %copy-start.18 = (bf16[2,4,96,256]{3,2,1,0:T(8,128)(2,1)}, bf16[2,4,96,256]{3,2,1,0:T(8,128)(2,1)S(1)}, u32[]{:S(2)}) copy-start(bf16[2,4,96,256]{3,2,1,0:T(8,128)(2,1)S(1)} %collective-permute-done.2.refs_2_) | copy-start | bytes 1179652
  51.8 11.9 %copy-start.19 = (bf16[2,4,96,256]{3,2,1,0:T(8,128)(2,1)}, bf16[2,4,96,256]{3,2,1,0:T(8,128)(2,1)S(1)}, u32[]{:S(2)}) copy-start(bf16[2,4,96,256]{3,2,1,0:T(8,128)(2,1)S(1)} %collective-permute-done.3.refs_3_) | copy-start | bytes 1179652
  63.7 5.8 %copy-start.14 = (s32[8,2]{0,1:T(2,128)S(1)}, s32[8,2]{0,1:T(2,128)}, u32[]{:S(2)}) copy-start(s32[8,2]{0,1:T(2,128)} %param.9) | copy-start | bytes 196
  63.7 93.7 %all-to-all-start = ((bf16[8,3,2,32,1280]{4,3,2,1,0:T(8,128)(2,1)}), bf16[8,3,2,32,1280]{4,3,2,1,0:T(8,128)(2,1)}, u32[]{:S(2)}, u32[]{:S(2)}) async-start(bf16[8,3,2,32,1280]{4,3,2,1,0:T(8,128)(2,1)} %bitcast.172), calls=%async_computation | async-start | bytes 7864320 | tf_op jit(solution)/shard_map/all_to_all | solution.py:215
  81.6 12.2 %copy-start.13 = (f32[2,2,256]{2,1,0:T(2,128)S(1)}, f32[2,2,256]{2,1,0:T(2,128)}, u32[]{:S(2)}) copy-start(f32[2,2,256]{2,1,0:T(2,128)} %get-tuple-element.44) | copy-start | bytes 12292
  81.6 12.2 %copy-start.9 = (bf16[2,256,256]{2,1,0:T(8,128)(2,1)S(1)}, bf16[2,256,256]{2,1,0:T(8,128)(2,1)}, u32[]{:S(2)}) copy-start(bf16[2,256,256]{2,1,0:T(8,128)(2,1)} %get-tuple-element.68) | copy-start | bytes 786436
  81.6 12.3 %copy-start.8 = (bf16[2,256,256]{2,1,0:T(8,128)(2,1)S(1)}, bf16[2,256,256]{2,1,0:T(8,128)(2,1)}, u32[]{:S(2)}) copy-start(bf16[2,256,256]{2,1,0:T(8,128)(2,1)} %get-tuple-element.66) | copy-start | bytes 786436
  86.9 148.1 %collective-permute-start.5 = (bf16[2,4,96,512]{3,2,1,0:T(8,128)(2,1)}, bf16[2,4,96,512]{3,2,1,0:T(8,128)(2,1)}, u32[]{:S(2)}, u32[]{:S(2)}) collective-permute-start(bf16[2,4,96,512]{3,2,1,0:T(8,128)(2,1)} %get-tuple-element.51), channel_id=1, source_target_pairs={{0,8},{4,12},{8,0},{12,4},{16,24},{20,28},{24,16},{28,20},{1,9},{5... | collective-permute-start | bytes 2359304 | tf_op jit(solution)/shard_map/ppermute | solution.py:187
  88.9 146.1 %collective-permute-start.6 = (bf16[2,4,96,512]{3,2,1,0:T(8,128)(2,1)}, bf16[2,4,96,512]{3,2,1,0:T(8,128)(2,1)}, u32[]{:S(2)}, u32[]{:S(2)}) collective-permute-start(bf16[2,4,96,512]{3,2,1,0:T(8,128)(2,1)} %get-tuple-element.52), channel_id=1, source_target_pairs={{0,12},{4,8},{8,4},{12,0},{16,28},{20,24},{24,20},{28,16},{1,13},{... | collective-permute-start | bytes 2359304 | tf_op jit(solution)/shard_map/ppermute | solution.py:187
  90.4 104.5 %collective-permute-start.10 = (bf16[2,4,96,512]{3,2,1,0:T(8,128)(2,1)}, bf16[2,4,96,512]{3,2,1,0:T(8,128)(2,1)S(1)}, u32[]{:S(2)}, u32[]{:S(2)}) collective-permute-start(bf16[2,4,96,512]{3,2,1,0:T(8,128)(2,1)} %get-tuple-element.60), channel_id=1, source_target_pairs={{0,12},{4,8},{8,4},{12,0},{16,28},{20,24},{24,20},{28,16},{1,13},{... | collective-permute-start | bytes 2359304 | tf_op jit(solution)/shard_map/ppermute | solution.py:187
  91.8 103.0 %collective-permute-start.8 = (bf16[2,4,96,512]{3,2,1,0:T(8,128)(2,1)}, bf16[2,4,96,512]{3,2,1,0:T(8,128)(2,1)}, u32[]{:S(2)}, u32[]{:S(2)}) collective-permute-start(bf16[2,4,96,512]{3,2,1,0:T(8,128)(2,1)} %get-tuple-element.58), channel_id=1, source_target_pairs={{0,4},{4,0},{8,12},{12,8},{16,20},{20,16},{24,28},{28,24},{1,5},{5... | collective-permute-start | bytes 2359304 | tf_op jit(solution)/shard_map/ppermute | solution.py:187
  93.3 130.8 %collective-permute-start.9 = (bf16[2,4,96,512]{3,2,1,0:T(8,128)(2,1)}, bf16[2,4,96,512]{3,2,1,0:T(8,128)(2,1)}, u32[]{:S(2)}, u32[]{:S(2)}) collective-permute-start(bf16[2,4,96,512]{3,2,1,0:T(8,128)(2,1)} %get-tuple-element.59), channel_id=1, source_target_pairs={{0,8},{4,12},{8,0},{12,4},{16,24},{20,28},{24,16},{28,20},{1,9},{5... | collective-permute-start | bytes 2359304 | tf_op jit(solution)/shard_map/ppermute | solution.py:187
  167.6 111.4 %all-to-all-start.1 = ((bf16[8,2,32,1280]{3,2,1,0:T(8,128)(2,1)}), bf16[8,2,32,1280]{3,2,1,0:T(8,128)(2,1)S(1)}, u32[]{:S(2)}, u32[]{:S(2)}) async-start(bf16[8,2,32,1280]{3,2,1,0:T(8,128)(2,1)} %shard_map.66), calls=%async_computation.1 | async-start | bytes 2621440 | tf_op jit(solution)/shard_map/all_to_all | solution.py:244
  194.8 29.2 %copy-start.16 = (bf16[2,4,96,512]{3,2,1,0:T(8,128)(2,1)}, bf16[2,4,96,512]{3,2,1,0:T(8,128)(2,1)S(1)}, u32[]{:S(2)}) copy-start(bf16[2,4,96,512]{3,2,1,0:T(8,128)(2,1)S(1)} %collective-permute-done.10.refs_3_) | copy-start | bytes 2359300
  194.8 70.9 %collective-permute-start.12 = (bf16[2,272,256]{2,1,0:T(8,128)(2,1)S(1)}, bf16[2,272,256]{2,1,0:T(8,128)(2,1)S(1)}, u32[]{:S(2)}, u32[]{:S(2)}) collective-permute-start(bf16[2,272,256]{2,1,0:T(8,128)(2,1)S(1)} %fusion.33), channel_id=1, source_target_pairs={{0,16},{4,20},{8,24},{12,28},{16,0},{20,4},{24,8},{28,12},{1,17},{... | collective-permute-start | bytes 835592 | tf_op jit(solution)/shard_map/ppermute | solution.py:187
  194.8 40.1 %collective-permute-start.4 = (bf16[2,4,96,512]{3,2,1,0:T(8,128)(2,1)}, bf16[2,4,96,512]{3,2,1,0:T(8,128)(2,1)}, u32[]{:S(2)}, u32[]{:S(2)}) collective-permute-start(bf16[2,4,96,512]{3,2,1,0:T(8,128)(2,1)} %get-tuple-element.50), channel_id=1, source_target_pairs={{0,4},{4,0},{8,12},{12,8},{16,20},{20,16},{24,28},{28,24},{1,5},{5... | collective-permute-start | bytes 2359304 | tf_op jit(solution)/shard_map/ppermute | solution.py:187
  233.0 1.9 copy-start.7
  234.8 30.9 %collective-permute-start.11 = (bf16[2,528,256]{2,1,0:T(8,128)(2,1)S(1)}, bf16[2,528,256]{2,1,0:T(8,128)(2,1)S(1)}, u32[]{:S(2)}, u32[]{:S(2)}) collective-permute-start(bf16[2,528,256]{2,1,0:T(8,128)(2,1)S(1)} %fusion.26), channel_id=1, source_target_pairs={{0,16},{4,20},{8,24},{12,28},{16,0},{20,4},{24,8},{28,12},{1,17},{... | collective-permute-start | bytes 1622024 | tf_op jit(solution)/shard_map/ppermute | solution.py:187
  243.9 21.9 %copy-start.15 = (f32[2,2,256]{2,1,0:T(2,128)S(1)}, f32[2,2,256]{2,1,0:T(2,128)}, u32[]{:S(2)}) copy-start(f32[2,2,256]{2,1,0:T(2,128)} %get-tuple-element.67) | copy-start | bytes 12292
  243.9 22.0 %copy-start.11 = (f32[2,4,256]{2,1,0:T(4,128)S(1)}, f32[2,4,256]{2,1,0:T(4,128)}, u32[]{:S(2)}) copy-start(f32[2,4,256]{2,1,0:T(4,128)} %get-tuple-element.62) | copy-start | bytes 24580
  245.7 20.3 %copy-start.6 = (bf16[2,512,256]{2,1,0:T(8,128)(2,1)S(1)}, bf16[2,512,256]{2,1,0:T(8,128)(2,1)}, u32[]{:S(2)}) copy-start(bf16[2,512,256]{2,1,0:T(8,128)(2,1)} %get-tuple-element.53) | copy-start | bytes 1572868
  246.4 30.9 %collective-permute-start.7 = (bf16[528,256]{1,0:T(8,128)(2,1)S(1)}, bf16[528,256]{1,0:T(8,128)(2,1)S(1)}, u32[]{:S(2)}, u32[]{:S(2)}) collective-permute-start(bf16[528,256]{1,0:T(8,128)(2,1)S(1)} %get-tuple-element.85), channel_id=1, source_target_pairs={{0,16},{4,20},{8,24},{12,28},{16,0},{20,4},{24,8},{28,12},{1,17},{... | collective-permute-start | bytes 811016 | tf_op jit(solution)/shard_map/ppermute | solution.py:187
  265.8 25.1 %collective-permute-start.15 = (bf16[528,256]{1,0:T(8,128)(2,1)}, bf16[528,256]{1,0:T(8,128)(2,1)}, u32[]{:S(2)}, u32[]{:S(2)}) collective-permute-start(bf16[528,256]{1,0:T(8,128)(2,1)} %get-tuple-element.86), channel_id=1, source_target_pairs={{0,16},{4,20},{8,24},{12,28},{16,0},{20,4},{24,8},{28,12},{1,17},{... | collective-permute-start | bytes 811016 | tf_op jit(solution)/shard_map/ppermute | solution.py:187
  266.8 10.5 %copy-start.10 = (f32[2,4,256]{2,1,0:T(4,128)S(1)}, f32[2,4,256]{2,1,0:T(4,128)}, u32[]{:S(2)}) copy-start(f32[2,4,256]{2,1,0:T(4,128)} %get-tuple-element.54) | copy-start | bytes 24580
  279.1 1.3 copy-start.4
  288.9 1.9 copy-start.1
  288.9 3.7 %copy-start.5 = (bf16[1,512,256]{2,1,0:T(8,128)(2,1)S(1)}, bf16[1,512,256]{2,1,0:T(8,128)(2,1)}, u32[]{:S(2)}) copy-start(bf16[1,512,256]{2,1,0:T(8,128)(2,1)} %get-tuple-element.89) | copy-start | bytes 786436
  290.8 3.4 %collective-permute-start.13 = (bf16[2,64,5120]{2,1,0:T(8,128)(2,1)}, bf16[2,64,5120]{2,1,0:T(8,128)(2,1)}, u32[]{:S(2)}, u32[]{:S(2)}) collective-permute-start(bf16[2,64,5120]{2,1,0:T(8,128)(2,1)} %dynamic-slice_bitcast_fusion.1), channel_id=1, source_target_pairs={{0,1},{1,0},{2,3},{3,2},{4,5},{5,4},{6,7},{7,6},{8,9},{9,8},{10,11... | collective-permute-start | bytes 3932168 | tf_op jit(solution)/shard_map/ppermute | solution.py:225
  293.2 1.7 copy-start.2
  297.5 17.4 %collective-permute-start.14 = (bf16[64,5120]{1,0:T(8,128)(2,1)}, bf16[64,5120]{1,0:T(8,128)(2,1)S(1)}, u32[]{:S(2)}, u32[]{:S(2)}) collective-permute-start(bf16[64,5120]{1,0:T(8,128)(2,1)} %dynamic-slice_bitcast_fusion.3), channel_id=1, source_target_pairs={{0,2},{1,3},{2,0},{3,1},{4,6},{5,7},{6,4},{7,5},{8,10},{9,11},{10,... | collective-permute-start | bytes 1966088 | tf_op jit(solution)/shard_map/ppermute | solution.py:232
  307.8 1.9 copy-start.3
  309.7 5.2 %collective-permute-start.16 = (bf16[2,64,5120]{2,1,0:T(8,128)(2,1)}, bf16[2,64,5120]{2,1,0:T(8,128)(2,1)S(1)}, u32[]{:S(2)}, u32[]{:S(2)}) collective-permute-start(bf16[2,64,5120]{2,1,0:T(8,128)(2,1)} %dynamic-slice_bitcast_fusion), channel_id=1, source_target_pairs={{0,1},{1,0},{2,3},{3,2},{4,5},{5,4},{6,7},{7,6},{8,9},{9,8},{10,11... | collective-permute-start | bytes 3932168 | tf_op jit(solution)/shard_map/ppermute | solution.py:225
  316.7 16.4 %collective-permute-start.17 = (bf16[64,5120]{1,0:T(8,128)(2,1)S(1)}, bf16[64,5120]{1,0:T(8,128)(2,1)S(1)}, u32[]{:S(2)}, u32[]{:S(2)}) collective-permute-start(bf16[64,5120]{1,0:T(8,128)(2,1)S(1)} %dynamic-slice_bitcast_fusion.2), channel_id=1, source_target_pairs={{0,2},{1,3},{2,0},{3,1},{4,6},{5,7},{6,4},{7,5},{8,10},{9,11},{10,... | collective-permute-start | bytes 1966088 | tf_op jit(solution)/shard_map/ppermute | solution.py:232

commit v8 on v5

--- a/solution.py
+++ b/solution.py
@@ -205,7 +205,7 @@
     banks = [banks_of(0)]
     tokens = frame_tokens.reshape(3, head_groups, parts, across, spots, frames_here, width)
     tokens = tokens.transpose(1, 3, 0, 2, 4, 5, 6).reshape(shards, 3, parts, tile, width)
-    tokens = lax.all_to_all(after(tokens, far, *banks[0]), "frames", 0, 0, tiled=True)
+    tokens = lax.all_to_all(after(tokens, far, *banks[0][:-1]), "frames", 0, 0, tiled=True)
     live = jnp.stack([slot_live[place], slot_live[place ^ half]])
 
     place_heads = lax.axis_index("heads")
@@ -231,7 +231,7 @@
     for group in range(groups):
         near_out, near_level, far_out, far_level = attend_bank(group, parts, rows, live, own, far, banks[group])
         if group < groups - 1:
-            banks.append(banks_of(group + 1, far_level))
+            banks.append(banks_of(group + 1, *banks[0][-2:-1]))
         if group == 0:
             frame_parts = attend_frames(frames_here, after(tokens, far_level))
             back = lax.all_to_all(frame_parts, "frames", 0, 0, tiled=True)

time: 320 us -> 323 us (level)
  starting transfers between devices: 28.4 us -> 42.3 us
  waiting for transfers between devices: 201 us -> 188 us
    all_to_all x1, waiting for transfers between devices: 64.9 us -> 0.01 us  [local(): lax.all_to_all(after(tokens, far, *banks[0][:-1]), 'frames', 0, 0, tiled=...]
    ppermute x10, waiting for transfers between devices: 116 us -> 168 us  [swap(): return lax.ppermute(block, 'frames', [(a, a ^ step) for a in range(shards)])]
    ppermute x10, starting transfers between devices: 16.7 us -> 29.4 us  [swap(): return lax.ppermute(block, 'frames', [(a, a ^ step) for a in range(shards)])]
  transfers between devices with their start and end apart: 16 -> 16, of which waited for: 9 -> 8; matrix products, arithmetic and copies ran while one was open for 10% -> 11% of each run, Pallas kernels for 13% -> 13%
where the time goes in v8:
time: 323 us; the launch traced here: 322 us
  waiting for transfers between devices  188 us (58%)
  Pallas kernels  42.7 us (13%)
  starting transfers between devices  42.3 us (13%)
  local copies, waits for them, and re-layouts  19.3 us (6%)
  matrix products  17.4 us (5%)
  other arithmetic  11.5 us (4%)
    ppermute x10, waiting for transfers between devices, swap(): return lax.ppermute(block, 'frames', [(a, a ^ step) for a in range(shards)])  168 us
    ppermute x10, starting transfers between devices, swap(): return lax.ppermute(block, 'frames', [(a, a ^ step) for a in range(shards)])  29.4 us
    pallas_call x2, Pallas kernels, attend_bank(): pl.pallas_call(functools.partial(bank_kernel, len(banks)), grid=(heads,),...  21.2 us
    ppermute x2, waiting for transfers between devices, scatter_chips(): lax.ppermute(give, 'heads', [(h, (h + 2 * step) % head_groups) for h in r...  19.6 us
    dot_general x2, matrix products, local(): lax.dot_general(after(combined, *summed[-1:]), out_weight, (((0,), (0,)),...  17.4 us
    pallas_call x2, Pallas kernels, listed_banks(): pl.pallas_call(listed_kernel, grid_spec=pltpu.PrefetchScalarGridSpec(num_...  11.4 us
    pallas_call x1, Pallas kernels, attend_frames(): pl.pallas_call(functools.partial(frame_kernel, frames_here), grid=(width...  10.2 us
  transfers between devices with their start and end apart: 16, of which 8 were waited for; matrix products, arithmetic and copies ran while one was open for 11% of the time, Pallas kernels for 13%

profile of v8, /device:TPU:0, one launch (start us, length us, event | category | flops | bytes accessed | tf_op | source)
XLA Modules:
  0.0 321.9 jit_solution(14674058285995349256)
XLA Ops:
  0.0 2.5 copy.18
  2.5 4.0 %collective-permute-start = (bf16[512,1280]{1,0:T(8,128)(2,1)}, bf16[512,1280]{1,0:T(8,128)(2,1)}, u32[]{:S(2)}, u32[]{:S(2)}) collective-permute-start(bf16[512,1280]{1,0:T(8,128)(2,1)} %bitcast.2.own_ref), channel_id=1, source_target_pairs={{0,16},{4,20},{8,24},{12,28},{16,0},{20,4},{24,8},{28,12},{1,17},{... | collective-permute-start | bytes 3932168 | tf_op jit(solution)/shard_map/ppermute | solution.py:187
  6.6 0.6 reshape.188.slots_ref
  7.2 5.9 %shard_map.64 = (bf16[2,4,96,640]{3,2,1,0:T(8,128)(2,1)}, bf16[2,4,96,640]{3,2,1,0:T(8,128)(2,1)}, bf16[2,4,96,640]{3,2,1,0:T(8,128)(2,1)}, bf16[2,4,96,640]{3,2,1,0:T(8,128)(2,1)}) custom-call(s32[1]{0:T(128)} %bitcast.4.place_ref, s32[16]{0:T(128)} %reshape.188.slots_ref, bf16[2,8,96,1280]{3,2,1,0:T(8,128)(2,1)} %refs_3_.3, ...), custom_call_target="tpu_custom_call" | custom-call | bytes 7864320 | tf_op jit(solution)/shard_map/pallas_call | solution.py:157
  13.1 1.6 collective-permute-start.2
  14.7 1.5 collective-permute-start.1
  16.2 2.3 copy.20
  18.5 37.5 %collective-permute-done.2.refs_2_ = bf16[2,4,96,640]{3,2,1,0:T(8,128)(2,1)S(1)} collective-permute-done((bf16[2,4,96,640]{3,2,1,0:T(8,128)(2,1)}, bf16[2,4,96,640]{3,2,1,0:T(8,128)(2,1)S(1)}, u32[]{:S(2)}, u32[]{:S(2)}) %collective-permute-start.2) | collective-permute-done | bytes 983072 | tf_op jit(solution)/shard_map/ppermute | solution.py:187
  56.0 7.7 %collective-permute-done.far_ref = bf16[512,1280]{1,0:T(8,128)(2,1)} collective-permute-done((bf16[512,1280]{1,0:T(8,128)(2,1)}, bf16[512,1280]{1,0:T(8,128)(2,1)}, u32[]{:S(2)}, u32[]{:S(2)}) %collective-permute-start) | collective-permute-done | bytes 1310752 | tf_op jit(solution)/shard_map/ppermute | solution.py:187
  63.7 5.9 %all-to-all-start = ((bf16[8,3,2,32,1280]{4,3,2,1,0:T(8,128)(2,1)}), bf16[8,3,2,32,1280]{4,3,2,1,0:T(8,128)(2,1)}, u32[]{:S(2)}, u32[]{:S(2)}) async-start(bf16[8,3,2,32,1280]{4,3,2,1,0:T(8,128)(2,1)} %bitcast.144), calls=%async_computation | async-start | bytes 7864320 | tf_op jit(solution)/shard_map/all_to_all | solution.py:208
  69.6 2.9 collective-permute-start.3
  72.6 0.1 copy.25
  72.7 0.1 copy.26
  72.8 0.6 pad_add_fusion.live_ref
  73.5 0.6 reshape.191.slots_ref
  74.1 5.5 %shard_map.67 = (bf16[2,4,96,640]{3,2,1,0:T(8,128)(2,1)}, bf16[2,4,96,640]{3,2,1,0:T(8,128)(2,1)}, bf16[2,4,96,640]{3,2,1,0:T(8,128)(2,1)}, bf16[2,4,96,640]{3,2,1,0:T(8,128)(2,1)}) custom-call(s32[1]{0:T(128)} %bitcast.4.place_ref, s32[16]{0:T(128)} %reshape.191.slots_ref, bf16[2,8,96,1280]{3,2,1,0:T(8,128)(2,1)} %refs_3_.3, ...), custom_call_target="tpu_custom_call" | custom-call | bytes 7864320 | tf_op jit(solution)/shard_map/pallas_call | solution.py:157
  79.6 0.6 collective-permute-start.5
  80.2 2.9 collective-permute-start.7
  83.1 73.3 %collective-permute-done.3.refs_3_ = bf16[2,4,96,640]{3,2,1,0:T(8,128)(2,1)S(1)} collective-permute-done((bf16[2,4,96,640]{3,2,1,0:T(8,128)(2,1)S(1)}, bf16[2,4,96,640]{3,2,1,0:T(8,128)(2,1)S(1)}, u32[]{:S(2)}, u32[]{:S(2)}) %collective-permute-start.3) | collective-permute-done | bytes 983072 | tf_op jit(solution)/shard_map/ppermute | solution.py:187
  156.4 0.9 copy-done.16
  157.3 10.6 %shard_map.65 = (bf16[2,640,256]{2,1,0:T(8,128)(2,1)}, f32[2,5,256]{2,1,0:T(8,128)}, bf16[2,640,256]{2,1,0:T(8,128)(2,1)}, f32[2,5,256]{2,1,0:T(8,128)}) custom-call(s32[2,2]{1,0:T(2,128)} %pad_add_fusion.live_ref, bf16[512,1280]{1,0:T(8,128)(2,1)} %bitcast.2.own_ref, bf16[512,1280]{1,0:T(8,128)(2,1)} %collective-permute-done.far_ref, ...), custom_call_target="tpu_custom_call" | custom-call | flops 8053063680 | bytes 6553600 | tf_op jit(solution)/shard_map/pallas_call | solution.py:83
  167.9 0.8 reduce-precision_convert_fusion.3
  168.7 1.1 fusion.18
  169.8 13.2 %collective-permute-start.4 = (bf16[2,656,256]{2,1,0:T(8,128)(2,1)S(1)}, bf16[2,656,256]{2,1,0:T(8,128)(2,1)S(1)}, u32[]{:S(2)}, u32[]{:S(2)}) collective-permute-start(bf16[2,656,256]{2,1,0:T(8,128)(2,1)S(1)} %fusion.18), channel_id=1, source_target_pairs={{0,16},{4,20},{8,24},{12,28},{16,0},{20,4},{24,8},{28,12},{1,17},{... | collective-permute-start | bytes 2015240 | tf_op jit(solution)/shard_map/ppermute | solution.py:187
  183.1 10.2 %shard_map.66 = bf16[8,2,32,1280]{3,2,1,0:T(8,128)(2,1)} custom-call(bf16[8,3,2,32,1280]{4,3,2,1,0:T(8,128)(2,1)} %all-to-all-done.token_ref), custom_call_target="tpu_custom_call" | custom-call | flops 2684354560 | bytes 5242880 | tf_op jit(solution)/shard_map/pallas_call | solution.py:125
  193.3 3.7 %all-to-all-start.1 = ((bf16[8,2,32,1280]{3,2,1,0:T(8,128)(2,1)}), bf16[8,2,32,1280]{3,2,1,0:T(8,128)(2,1)S(1)}, u32[]{:S(2)}, u32[]{:S(2)}) async-start(bf16[8,2,32,1280]{3,2,1,0:T(8,128)(2,1)} %shard_map.66), calls=%async_computation.1 | async-start | bytes 2621440 | tf_op jit(solution)/shard_map/all_to_all | solution.py:237
  197.1 24.0 %collective-permute-done.7.refs_3_ = bf16[2,4,96,640]{3,2,1,0:T(8,128)(2,1)} collective-permute-done((bf16[2,4,96,640]{3,2,1,0:T(8,128)(2,1)}, bf16[2,4,96,640]{3,2,1,0:T(8,128)(2,1)}, u32[]{:S(2)}, u32[]{:S(2)}) %collective-permute-start.7) | collective-permute-done | bytes 983072 | tf_op jit(solution)/shard_map/ppermute | solution.py:187
  221.0 10.6 %shard_map.68 = (bf16[2,640,256]{2,1,0:T(8,128)(2,1)}, f32[2,5,256]{2,1,0:T(8,128)}, bf16[2,640,256]{2,1,0:T(8,128)(2,1)}, f32[2,5,256]{2,1,0:T(8,128)}) custom-call(s32[2,2]{1,0:T(2,128)} %pad_add_fusion.live_ref, bf16[512,1280]{1,0:T(8,128)(2,1)} %bitcast.2.own_ref, bf16[512,1280]{1,0:T(8,128)(2,1)} %collective-permute-done.far_ref, ...), custom_call_target="tpu_custom_call" | custom-call | flops 8053063680 | bytes 6553600 | tf_op jit(solution)/shard_map/pallas_call | solution.py:83
  231.7 0.7 reduce-precision_convert_fusion.1
  232.4 1.1 fusion.21
  233.6 0.8 slice_bitcast_fusion.1
  234.4 0.4 copy-done.7
  234.8 0.8 fusion.42
  235.5 2.6 collective-permute-start.11
  238.2 1.1 fusion.24
  239.2 25.6 %collective-permute-done.8 = bf16[656,256]{1,0:T(8,128)(2,1)S(1)} collective-permute-done((bf16[656,256]{1,0:T(8,128)(2,1)S(1)}, bf16[656,256]{1,0:T(8,128)(2,1)S(1)}, u32[]{:S(2)}, u32[]{:S(2)}) %collective-permute-start.8) | collective-permute-done | bytes 335904 | tf_op jit(solution)/shard_map/ppermute | solution.py:187
  264.9 0.1 fusion.25
  265.0 0.1 pad_maximum_fusion
  265.1 1.5 copy.22
  266.7 1.2 copy-done.5
  267.9 8.5 %convolution_convert_fusion.1 = bf16[256,5120]{1,0:T(8,128)(2,1)S(1)} fusion(bf16[1280,5120]{1,0:T(8,128)(2,1)} %param.11, f32[1280,256]{0,1:T(8,128)S(1)} %copy-done.5, bf16[256,1280]{1,0:T(8,128)(2,1)S(1)} %bitcast.161), kind=kOutput, calls=%fused_computation.1 | convolution fusion | flops 3357736960 | bytes 17694720 | tf_op jit(solution)/shard_map/dot_general | solution.py:271
  276.4 1.2 dynamic-slice_bitcast_fusion.1
  277.6 0.7 copy-done.1
  278.3 1.1 slice.132
  279.4 0.8 add_divide_fusion.1
  280.2 0.1 fusion.23
  280.4 0.4 copy.23
  280.8 0.2 fusion.12
  281.0 0.7 collective-permute-done.9
  281.7 0.9 copy-done.2
  282.6 1.6 fusion.1
  284.2 0.9 dynamic-slice_bitcast_fusion.3
  285.1 1.5 collective-permute-start.10
  286.6 8.9 %convolution_convert_fusion = bf16[256,5120]{1,0:T(8,128)(2,1)S(1)} fusion(bf16[1280,256]{0,1:T(8,128)(2,1)S(1)} %fusion.12, bf16[1280,5120]{1,0:T(8,128)(2,1)} %param.11), kind=kOutput, calls=%fused_computation | convolution fusion | flops 3356753920 | bytes 16384000 | tf_op jit(solution)/shard_map/dot_general | solution.py:271
  295.5 1.3 dynamic-slice_bitcast_fusion
  296.7 0.7 copy-done.3
  297.4 0.1 collective-permute-start.12
  297.6 4.8 %collective-permute-done.10 = bf16[64,5120]{1,0:T(8,128)(2,1)S(1)} collective-permute-done((bf16[64,5120]{1,0:T(8,128)(2,1)}, bf16[64,5120]{1,0:T(8,128)(2,1)S(1)}, u32[]{:S(2)}, u32[]{:S(2)}) %collective-permute-start.10) | collective-permute-done | bytes 655392 | tf_op jit(solution)/shard_map/ppermute | solution.py:225
  302.4 0.2 fusion.13
  302.6 1.6 fusion
  304.3 1.6 collective-permute-start.13
  305.8 14.8 %collective-permute-done.13 = bf16[64,5120]{1,0:T(8,128)(2,1)S(1)} collective-permute-done((bf16[64,5120]{1,0:T(8,128)(2,1)S(1)}, bf16[64,5120]{1,0:T(8,128)(2,1)S(1)}, u32[]{:S(2)}, u32[]{:S(2)}) %collective-permute-start.13) | collective-permute-done | bytes 655392 | tf_op jit(solution)/shard_map/ppermute | solution.py:225
  320.6 0.2 fusion.10
  320.8 1.2 maximum_bitcast_fusion
  (50 shorter events, 0.8 us)
Async XLA Ops:
  0.0 6.5 %copy-start.11 = (s32[8,2]{0,1:T(2,128)S(1)}, s32[8,2]{0,1:T(2,128)}, u32[]{:S(2)}) copy-start(s32[8,2]{0,1:T(2,128)} %param.8) | copy-start | bytes 196
  2.5 61.2 %collective-permute-start = (bf16[512,1280]{1,0:T(8,128)(2,1)}, bf16[512,1280]{1,0:T(8,128)(2,1)}, u32[]{:S(2)}, u32[]{:S(2)}) collective-permute-start(bf16[512,1280]{1,0:T(8,128)(2,1)} %bitcast.2.own_ref), channel_id=1, source_target_pairs={{0,16},{4,20},{8,24},{12,28},{16,0},{20,4},{24,8},{28,12},{1,17},{... | collective-permute-start | bytes 3932168 | tf_op jit(solution)/shard_map/ppermute | solution.py:187
  7.2 9.0 %copy-start = (bf16[3,64,8,1280]{3,2,1,0:T(8,128)(2,1)S(1)}, bf16[3,64,8,1280]{3,2,1,0:T(8,128)(2,1)}, u32[]{:S(2)}) copy-start(bf16[3,64,8,1280]{3,2,1,0:T(8,128)(2,1)} %param.10) | copy-start | bytes 11796484
  13.1 42.9 %collective-permute-start.2 = (bf16[2,4,96,640]{3,2,1,0:T(8,128)(2,1)}, bf16[2,4,96,640]{3,2,1,0:T(8,128)(2,1)S(1)}, u32[]{:S(2)}, u32[]{:S(2)}) collective-permute-start(bf16[2,4,96,640]{3,2,1,0:T(8,128)(2,1)} %get-tuple-element.31), channel_id=1, source_target_pairs={{0,8},{4,12},{8,0},{12,4},{16,24},{20,28},{24,16},{28,20},{1,9},{5... | collective-permute-start | bytes 2949128 | tf_op jit(solution)/shard_map/ppermute | solution.py:187
  14.7 41.3 %collective-permute-start.1 = (bf16[2,4,96,640]{3,2,1,0:T(8,128)(2,1)}, bf16[2,4,96,640]{3,2,1,0:T(8,128)(2,1)S(1)}, u32[]{:S(2)}, u32[]{:S(2)}) collective-permute-start(bf16[2,4,96,640]{3,2,1,0:T(8,128)(2,1)} %get-tuple-element.30), channel_id=1, source_target_pairs={{0,4},{4,0},{8,12},{12,8},{16,20},{20,16},{24,28},{28,24},{1,5},{5... | collective-permute-start | bytes 2949128 | tf_op jit(solution)/shard_map/ppermute | solution.py:187
  56.0 7.7 %copy-start.13 = (bf16[2,4,96,640]{3,2,1,0:T(8,128)(2,1)}, bf16[2,4,96,640]{3,2,1,0:T(8,128)(2,1)S(1)}, u32[]{:S(2)}) copy-start(bf16[2,4,96,640]{3,2,1,0:T(8,128)(2,1)S(1)} %collective-permute-done.2.refs_2_) | copy-start | bytes 2949124
  56.0 7.7 %copy-start.14 = (bf16[2,4,96,640]{3,2,1,0:T(8,128)(2,1)}, bf16[2,4,96,640]{3,2,1,0:T(8,128)(2,1)S(1)}, u32[]{:S(2)}) copy-start(bf16[2,4,96,640]{3,2,1,0:T(8,128)(2,1)S(1)} %collective-permute-done.1.refs_1_) | copy-start | bytes 2949124
  63.7 5.9 %copy-start.15 = (bf16[2,4,96,640]{3,2,1,0:T(8,128)(2,1)S(1)}, bf16[2,4,96,640]{3,2,1,0:T(8,128)(2,1)}, u32[]{:S(2)}) copy-start(bf16[2,4,96,640]{3,2,1,0:T(8,128)(2,1)} %get-tuple-element.32) | copy-start | bytes 2949124
  63.7 8.9 %copy-start.12 = (s32[8,2]{0,1:T(2,128)S(1)}, s32[8,2]{0,1:T(2,128)}, u32[]{:S(2)}) copy-start(s32[8,2]{0,1:T(2,128)} %param.9) | copy-start | bytes 196
  63.7 119.4 %all-to-all-start = ((bf16[8,3,2,32,1280]{4,3,2,1,0:T(8,128)(2,1)}), bf16[8,3,2,32,1280]{4,3,2,1,0:T(8,128)(2,1)}, u32[]{:S(2)}, u32[]{:S(2)}) async-start(bf16[8,3,2,32,1280]{4,3,2,1,0:T(8,128)(2,1)} %bitcast.144), calls=%async_computation | async-start | bytes 7864320 | tf_op jit(solution)/shard_map/all_to_all | solution.py:208
  69.6 86.7 %collective-permute-start.3 = (bf16[2,4,96,640]{3,2,1,0:T(8,128)(2,1)S(1)}, bf16[2,4,96,640]{3,2,1,0:T(8,128)(2,1)S(1)}, u32[]{:S(2)}, u32[]{:S(2)}) collective-permute-start(bf16[2,4,96,640]{3,2,1,0:T(8,128)(2,1)S(1)} %copy-done.15), channel_id=1, source_target_pairs={{0,12},{4,8},{8,4},{12,0},{16,28},{20,24},{24,20},{28,16},{1,13},{... | collective-permute-start | bytes 2949128 | tf_op jit(solution)/shard_map/ppermute | solution.py:187
  79.6 117.5 %collective-permute-start.5 = (bf16[2,4,96,640]{3,2,1,0:T(8,128)(2,1)}, bf16[2,4,96,640]{3,2,1,0:T(8,128)(2,1)}, u32[]{:S(2)}, u32[]{:S(2)}) collective-permute-start(bf16[2,4,96,640]{3,2,1,0:T(8,128)(2,1)} %get-tuple-element.42), channel_id=1, source_target_pairs={{0,4},{4,0},{8,12},{12,8},{16,20},{20,16},{24,28},{28,24},{1,5},{5... | collective-permute-start | bytes 2949128 | tf_op jit(solution)/shard_map/ppermute | solution.py:187
  80.1 116.9 %collective-permute-start.6 = (bf16[2,4,96,640]{3,2,1,0:T(8,128)(2,1)}, bf16[2,4,96,640]{3,2,1,0:T(8,128)(2,1)}, u32[]{:S(2)}, u32[]{:S(2)}) collective-permute-start(bf16[2,4,96,640]{3,2,1,0:T(8,128)(2,1)} %get-tuple-element.43), channel_id=1, source_target_pairs={{0,8},{4,12},{8,0},{12,4},{16,24},{20,28},{24,16},{28,20},{1,9},{5... | collective-permute-start | bytes 2949128 | tf_op jit(solution)/shard_map/ppermute | solution.py:187
  80.2 140.8 %collective-permute-start.7 = (bf16[2,4,96,640]{3,2,1,0:T(8,128)(2,1)}, bf16[2,4,96,640]{3,2,1,0:T(8,128)(2,1)}, u32[]{:S(2)}, u32[]{:S(2)}) collective-permute-start(bf16[2,4,96,640]{3,2,1,0:T(8,128)(2,1)} %get-tuple-element.44), channel_id=1, source_target_pairs={{0,12},{4,8},{8,4},{12,0},{16,28},{20,24},{24,20},{28,16},{1,13},{... | collective-permute-start | bytes 2949128 | tf_op jit(solution)/shard_map/ppermute | solution.py:187
  156.4 0.9 copy-start.16
  167.9 15.2 %copy-start.8 = (bf16[2,640,256]{2,1,0:T(8,128)(2,1)S(1)}, bf16[2,640,256]{2,1,0:T(8,128)(2,1)}, u32[]{:S(2)}) copy-start(bf16[2,640,256]{2,1,0:T(8,128)(2,1)} %get-tuple-element.33) | copy-start | bytes 1966084
  169.8 61.9 %collective-permute-start.4 = (bf16[2,656,256]{2,1,0:T(8,128)(2,1)S(1)}, bf16[2,656,256]{2,1,0:T(8,128)(2,1)S(1)}, u32[]{:S(2)}, u32[]{:S(2)}) collective-permute-start(bf16[2,656,256]{2,1,0:T(8,128)(2,1)S(1)} %fusion.18), channel_id=1, source_target_pairs={{0,16},{4,20},{8,24},{12,28},{16,0},{20,4},{24,8},{28,12},{1,17},{... | collective-permute-start | bytes 2015240 | tf_op jit(solution)/shard_map/ppermute | solution.py:187
  193.3 73.3 %all-to-all-start.1 = ((bf16[8,2,32,1280]{3,2,1,0:T(8,128)(2,1)}), bf16[8,2,32,1280]{3,2,1,0:T(8,128)(2,1)S(1)}, u32[]{:S(2)}, u32[]{:S(2)}) async-start(bf16[8,2,32,1280]{3,2,1,0:T(8,128)(2,1)} %shard_map.66), calls=%async_computation.1 | async-start | bytes 2621440 | tf_op jit(solution)/shard_map/all_to_all | solution.py:237
  233.5 1.2 copy-start.7
  234.3 1.2 copy-start.10
  234.3 30.5 %collective-permute-start.8 = (bf16[656,256]{1,0:T(8,128)(2,1)S(1)}, bf16[656,256]{1,0:T(8,128)(2,1)S(1)}, u32[]{:S(2)}, u32[]{:S(2)}) collective-permute-start(bf16[656,256]{1,0:T(8,128)(2,1)S(1)} %get-tuple-element.61), channel_id=1, source_target_pairs={{0,16},{4,20},{8,24},{12,28},{16,0},{20,4},{24,8},{28,12},{1,17},{... | collective-permute-start | bytes 1007624 | tf_op jit(solution)/shard_map/ppermute | solution.py:187
  235.5 42.8 %collective-permute-start.11 = (bf16[656,256]{1,0:T(8,128)(2,1)}, bf16[656,256]{1,0:T(8,128)(2,1)}, u32[]{:S(2)}, u32[]{:S(2)}) collective-permute-start(bf16[656,256]{1,0:T(8,128)(2,1)} %get-tuple-element.62), channel_id=1, source_target_pairs={{0,16},{4,20},{8,24},{12,28},{16,0},{20,4},{24,8},{28,12},{1,17},{... | collective-permute-start | bytes 1007624 | tf_op jit(solution)/shard_map/ppermute | solution.py:187
  238.2 26.7 %copy-start.9 = (f32[2,5,256]{2,1,0:T(8,128)S(1)}, f32[2,5,256]{2,1,0:T(8,128)}, u32[]{:S(2)}) copy-start(f32[2,5,256]{2,1,0:T(8,128)} %get-tuple-element.45) | copy-start | bytes 30724
  266.6 1.3 copy-start.5
  276.4 1.9 copy-start.1
  276.4 3.8 %copy-start.6 = (bf16[1,640,256]{2,1,0:T(8,128)(2,1)S(1)}, bf16[1,640,256]{2,1,0:T(8,128)(2,1)}, u32[]{:S(2)}) copy-start(bf16[1,640,256]{2,1,0:T(8,128)(2,1)} %get-tuple-element.65) | copy-start | bytes 983044
  278.3 2.0 copy-start.4
  278.3 3.4 %collective-permute-start.9 = (bf16[2,64,5120]{2,1,0:T(8,128)(2,1)}, bf16[2,64,5120]{2,1,0:T(8,128)(2,1)}, u32[]{:S(2)}, u32[]{:S(2)}) collective-permute-start(bf16[2,64,5120]{2,1,0:T(8,128)(2,1)} %dynamic-slice_bitcast_fusion.1), channel_id=1, source_target_pairs={{0,1},{1,0},{2,3},{3,2},{4,5},{5,4},{6,7},{7,6},{8,9},{9,8},{10,11... | collective-permute-start | bytes 3932168 | tf_op jit(solution)/shard_map/ppermute | solution.py:218
  280.8 1.7 copy-start.2
  285.1 17.3 %collective-permute-start.10 = (bf16[64,5120]{1,0:T(8,128)(2,1)}, bf16[64,5120]{1,0:T(8,128)(2,1)S(1)}, u32[]{:S(2)}, u32[]{:S(2)}) collective-permute-start(bf16[64,5120]{1,0:T(8,128)(2,1)} %dynamic-slice_bitcast_fusion.3), channel_id=1, source_target_pairs={{0,2},{1,3},{2,0},{3,1},{4,6},{5,7},{6,4},{7,5},{8,10},{9,11},{10,... | collective-permute-start | bytes 1966088 | tf_op jit(solution)/shard_map/ppermute | solution.py:225
  295.5 1.9 copy-start.3
  297.4 5.2 %collective-permute-start.12 = (bf16[2,64,5120]{2,1,0:T(8,128)(2,1)}, bf16[2,64,5120]{2,1,0:T(8,128)(2,1)S(1)}, u32[]{:S(2)}, u32[]{:S(2)}) collective-permute-start(bf16[2,64,5120]{2,1,0:T(8,128)(2,1)} %dynamic-slice_bitcast_fusion), channel_id=1, source_target_pairs={{0,1},{1,0},{2,3},{3,2},{4,5},{5,4},{6,7},{7,6},{8,9},{9,8},{10,11... | collective-permute-start | bytes 3932168 | tf_op jit(solution)/shard_map/ppermute | solution.py:218
  304.3 16.4 %collective-permute-start.13 = (bf16[64,5120]{1,0:T(8,128)(2,1)S(1)}, bf16[64,5120]{1,0:T(8,128)(2,1)S(1)}, u32[]{:S(2)}, u32[]{:S(2)}) collective-permute-start(bf16[64,5120]{1,0:T(8,128)(2,1)S(1)} %dynamic-slice_bitcast_fusion.2), channel_id=1, source_target_pairs={{0,2},{1,3},{2,0},{3,1},{4,6},{5,7},{6,4},{7,5},{8,10},{9,11},{10,... | collective-permute-start | bytes 1966088 | tf_op jit(solution)/shard_map/ppermute | solution.py:225

commit v9 on v4

--- a/solution.py
+++ b/solution.py
@@ -11,7 +11,7 @@
 TILE_ROWS = 16
 PART_TILE = 32
 HEAD_GROUPS = 2
-VMEM_BYTES = 24 * 1024 * 1024
+VMEM_BYTES = 60 * 1024 * 1024
 
 
 def after(block, *before):
@@ -240,6 +240,7 @@
         message = jnp.pad(message, ((0, 0), (0, -message.shape[1] % TILE_ROWS), (0, 0)))
         if group < groups - 1:
             got = swap(message, half)
+            live = after(live, got)
         else:
             got = [swap(message[part], half) for part in range(parts)]
         results.append((near_out, near_level, got))
@@ -261,21 +262,24 @@
             + wide(got[: width // groups].reshape(split)) * (got_share / total)[:, None, :]
         )
 
-    def project(group, part, *before):
+    def project(group, part, before, before_dot):
         low, high = group * width // groups, (group + 1) * width // groups
         frame_out = back[:, part].reshape(rows, width)[:, low:high]
         combined = share_of(group, part, *before).reshape(width // groups, rows) + wide(frame_out.T)
         return lax.dot_general(
-            combined.astype(jnp.bfloat16), out_weight[low:high], (((0,), (0,)), ((), ())),
-            preferred_element_type=jnp.float32,
-        )
-
-    early = [[project(group, part) for group in range(groups - 1)] for part in range(parts)]
-    projected, pieces = [], []
+            after(combined.astype(jnp.bfloat16), *before_dot), out_weight[low:high],
+            (((0,), (0,)), ((), ())), preferred_element_type=jnp.float32,
+        )
+
+    early = [[project(group, part, (), ()) for group in range(groups - 1)] for part in range(parts)]
+    projected, summed, pieces = [], [], []
     for part in range(parts):
-        total = project(groups - 1, part, *early[-1], *early[0], *projected[-1:])
+        before = [term for terms in early for term in terms] if part == 0 else projected[-1:]
+        total = project(groups - 1, part, before, summed[-1:])
         projected.append(functools.reduce(jnp.add, [*early[part], total]).astype(jnp.bfloat16))
-        pieces.append(scatter_chips(after(scatter_cores(projected[-1]), *pieces[-1:])))
+        summed.append(scatter_cores(projected[-1]))
+    for block in summed:
+        pieces.append(scatter_chips(after(block, *pieces[-1:])))
     return jnp.concatenate(pieces, axis=0).reshape(spatial // head_groups, frames_here, -1)
 
 

time: 337 us -> 355 us (1.053)
  waiting for transfers between devices: 210 us -> 235 us
  local copies, waits for them, and re-layouts: 29 us -> 13.2 us
  Pallas kernels: 35.3 us -> 42.9 us
  other arithmetic: 7.59 us -> 12 us
    ppermute x10, waiting for transfers between devices: 120 us -> 141 us  [swap(): return lax.ppermute(block, 'frames', [(a, a ^ step) for a in range(shards)])]
    unnamed x57 -> x43, local copies, waits for them, and re-layouts: 21 us -> 2.63 us
    pallas_call x2, Pallas kernels: 5.3 us -> 11.4 us  [listed_banks(): pl.pallas_call(listed_kernel, grid_spec=pltpu.PrefetchScalarGridSpec(num_...]
    all_to_all x1, waiting for transfers between devices: 60.2 us -> 65.1 us  [local(): lax.all_to_all(after(tokens, far, *banks[0]), 'frames', 0, 0, tiled=True)]
    convert_element_type x4, other arithmetic: 0.94 us -> 4.68 us  [added(): functools.reduce(jnp.add, [wide(block) for block in blocks])]
  transfers between devices with their start and end apart: 16 -> 16, of which waited for: 9 -> 8; matrix products, arithmetic and copies ran while one was open for 11% -> 8% of each run, Pallas kernels for 11% -> 12%
where the time goes in v9:
time: 355 us; the launch traced here: 354 us
  waiting for transfers between devices  235 us (66%)
  Pallas kernels  42.9 us (12%)
  starting transfers between devices  28.7 us (8%)
  matrix products  22.5 us (6%)
  local copies, waits for them, and re-layouts  13.2 us (4%)
  other arithmetic  12 us (3%)
    ppermute x10, waiting for transfers between devices, swap(): return lax.ppermute(block, 'frames', [(a, a ^ step) for a in range(shards)])  141 us
    all_to_all x1, waiting for transfers between devices, local(): lax.all_to_all(after(tokens, far, *banks[0]), 'frames', 0, 0, tiled=True)  65.1 us
    ppermute x2, waiting for transfers between devices, scatter_chips(): lax.ppermute(give, 'heads', [(h, (h + 2 * step) % head_groups) for h in r...  28.3 us
    dot_general x4, matrix products, project(): lax.dot_general(after(combined.astype(jnp.bfloat16), *before_dot), out_we...  22.5 us
    pallas_call x2, Pallas kernels, attend_bank(): pl.pallas_call(functools.partial(bank_kernel, len(banks)), grid=(heads,),...  21.4 us
    ppermute x10, starting transfers between devices, swap(): return lax.ppermute(block, 'frames', [(a, a ^ step) for a in range(shards)])  17 us
    pallas_call x2, Pallas kernels, listed_banks(): pl.pallas_call(listed_kernel, grid_spec=pltpu.PrefetchScalarGridSpec(num_...  11.4 us
    pallas_call x1, Pallas kernels, attend_frames(): pl.pallas_call(functools.partial(frame_kernel, frames_here), grid=(width...  10.2 us
  transfers between devices with their start and end apart: 16, of which 8 were waited for; matrix products, arithmetic and copies ran while one was open for 8% of the time, Pallas kernels for 12%

profile of v9, /device:TPU:0, one launch (start us, length us, event | category | flops | bytes accessed | tf_op | source)
XLA Modules:
  0.0 354.3 jit_solution(7354052437294770298)
XLA Ops:
  0.0 2.6 copy.18
  2.6 4.0 %collective-permute-start = (bf16[512,1280]{1,0:T(8,128)(2,1)}, bf16[512,1280]{1,0:T(8,128)(2,1)}, u32[]{:S(2)}, u32[]{:S(2)}) collective-permute-start(bf16[512,1280]{1,0:T(8,128)(2,1)} %bitcast.2.own_ref), channel_id=1, source_target_pairs={{0,16},{4,20},{8,24},{12,28},{16,0},{20,4},{24,8},{28,12},{1,17},{... | collective-permute-start | bytes 3932168 | tf_op jit(solution)/shard_map/ppermute | solution.py:187
  6.6 0.1 copy.19
  6.7 0.7 reshape.192.slots_ref
  7.3 5.8 %shard_map.64 = (bf16[2,4,96,640]{3,2,1,0:T(8,128)(2,1)}, bf16[2,4,96,640]{3,2,1,0:T(8,128)(2,1)}, bf16[2,4,96,640]{3,2,1,0:T(8,128)(2,1)}, bf16[2,4,96,640]{3,2,1,0:T(8,128)(2,1)}) custom-call(s32[1]{0:T(128)} %bitcast.4.place_ref, s32[16]{0:T(128)} %reshape.192.slots_ref, bf16[2,8,96,1280]{3,2,1,0:T(8,128)(2,1)} %refs_3_.3, ...), custom_call_target="tpu_custom_call" | custom-call | bytes 7864320 | tf_op jit(solution)/shard_map/pallas_call | solution.py:157
  13.2 1.5 collective-permute-start.1
  14.7 1.6 collective-permute-start.2
  16.3 0.4 collective-permute-start.3
  16.7 2.3 copy.20
  18.9 18.1 %collective-permute-done.1.refs_1_ = bf16[2,4,96,640]{3,2,1,0:T(8,128)(2,1)S(1)} collective-permute-done((bf16[2,4,96,640]{3,2,1,0:T(8,128)(2,1)}, bf16[2,4,96,640]{3,2,1,0:T(8,128)(2,1)S(1)}, u32[]{:S(2)}, u32[]{:S(2)}) %collective-permute-start.1) | collective-permute-done | bytes 983072 | tf_op jit(solution)/shard_map/ppermute | solution.py:187
  37.0 29.5 %collective-permute-done.2.refs_2_ = bf16[2,4,96,640]{3,2,1,0:T(8,128)(2,1)S(1)} collective-permute-done((bf16[2,4,96,640]{3,2,1,0:T(8,128)(2,1)}, bf16[2,4,96,640]{3,2,1,0:T(8,128)(2,1)S(1)}, u32[]{:S(2)}, u32[]{:S(2)}) %collective-permute-start.2) | collective-permute-done | bytes 983072 | tf_op jit(solution)/shard_map/ppermute | solution.py:187
  66.5 19.3 %collective-permute-done.3.refs_3_ = bf16[2,4,96,640]{3,2,1,0:T(8,128)(2,1)S(1)} collective-permute-done((bf16[2,4,96,640]{3,2,1,0:T(8,128)(2,1)}, bf16[2,4,96,640]{3,2,1,0:T(8,128)(2,1)S(1)}, u32[]{:S(2)}, u32[]{:S(2)}) %collective-permute-start.3) | collective-permute-done | bytes 983072 | tf_op jit(solution)/shard_map/ppermute | solution.py:187
  85.8 0.9 copy-done.13
  86.8 4.8 %all-to-all-start = ((bf16[8,3,2,32,1280]{4,3,2,1,0:T(8,128)(2,1)}), bf16[8,3,2,32,1280]{4,3,2,1,0:T(8,128)(2,1)}, u32[]{:S(2)}, u32[]{:S(2)}) async-start(bf16[8,3,2,32,1280]{4,3,2,1,0:T(8,128)(2,1)} %bitcast.159), calls=%async_computation | async-start | bytes 7864320 | tf_op jit(solution)/shard_map/all_to_all | solution.py:208
  91.6 0.1 constant_dynamic-slice_fusion.1
  91.7 0.1 copy.28
  91.8 0.1 copy.27
  91.8 0.6 pad_add_fusion.live_ref
  92.4 10.6 %shard_map.65 = (bf16[2,640,256]{2,1,0:T(8,128)(2,1)}, f32[2,5,256]{2,1,0:T(8,128)}, bf16[2,640,256]{2,1,0:T(8,128)(2,1)}, f32[2,5,256]{2,1,0:T(8,128)}) custom-call(s32[2,2]{1,0:T(2,128)} %pad_add_fusion.live_ref, bf16[512,1280]{1,0:T(8,128)(2,1)} %bitcast.2.own_ref, bf16[512,1280]{1,0:T(8,128)(2,1)} %collective-permute-done.far_ref, ...), custom_call_target="tpu_custom_call" | custom-call | flops 8053063680 | bytes 6553600 | tf_op jit(solution)/shard_map/pallas_call | solution.py:83
  103.0 0.1 copy.21
  103.1 0.6 reshape.195.slots_ref
  103.7 5.5 %shard_map.67 = (bf16[2,4,96,640]{3,2,1,0:T(8,128)(2,1)}, bf16[2,4,96,640]{3,2,1,0:T(8,128)(2,1)}, bf16[2,4,96,640]{3,2,1,0:T(8,128)(2,1)}, bf16[2,4,96,640]{3,2,1,0:T(8,128)(2,1)}) custom-call(s32[1]{0:T(128)} %bitcast.4.place_ref, s32[16]{0:T(128)} %reshape.195.slots_ref, bf16[2,8,96,1280]{3,2,1,0:T(8,128)(2,1)} %refs_3_.3, ...), custom_call_target="tpu_custom_call" | custom-call | bytes 7864320 | tf_op jit(solution)/shard_map/pallas_call | solution.py:157
  109.2 2.0 collective-permute-start.5
  111.3 1.5 collective-permute-start.6
  112.7 0.1 collective-permute-start.7
  112.8 65.1 %all-to-all-done.token_ref = bf16[8,3,2,32,1280]{4,3,2,1,0:T(8,128)(2,1)} async-done(((bf16[8,3,2,32,1280]{4,3,2,1,0:T(8,128)(2,1)}), bf16[8,3,2,32,1280]{4,3,2,1,0:T(8,128)(2,1)}, u32[]{:S(2)}, u32[]{:S(2)}) %all-to-all-start) | async-done | bytes 3932192 | tf_op jit(solution)/shard_map/all_to_all | solution.py:208
  177.9 10.2 %shard_map.66 = bf16[8,2,32,1280]{3,2,1,0:T(8,128)(2,1)} custom-call(bf16[8,3,2,32,1280]{4,3,2,1,0:T(8,128)(2,1)} %all-to-all-done.token_ref), custom_call_target="tpu_custom_call" | custom-call | flops 2684354560 | bytes 5242880 | tf_op jit(solution)/shard_map/pallas_call | solution.py:125
  188.1 3.8 %all-to-all-start.1 = ((bf16[8,2,32,1280]{3,2,1,0:T(8,128)(2,1)}), bf16[8,2,32,1280]{3,2,1,0:T(8,128)(2,1)S(1)}, u32[]{:S(2)}, u32[]{:S(2)}) async-start(bf16[8,2,32,1280]{3,2,1,0:T(8,128)(2,1)} %shard_map.66), calls=%async_computation.1 | async-start | bytes 2621440 | tf_op jit(solution)/shard_map/all_to_all | solution.py:237
  191.9 3.0 collective-permute-start.4
  194.9 58.5 %collective-permute-done.4 = bf16[2,656,256]{2,1,0:T(8,128)(2,1)S(1)} collective-permute-done((bf16[2,656,256]{2,1,0:T(8,128)(2,1)S(1)}, bf16[2,656,256]{2,1,0:T(8,128)(2,1)S(1)}, u32[]{:S(2)}, u32[]{:S(2)}) %collective-permute-start.4) | collective-permute-done | bytes 671776 | tf_op jit(solution)/shard_map/ppermute | solution.py:187
  253.4 10.8 %shard_map.68 = (bf16[2,640,256]{2,1,0:T(8,128)(2,1)}, f32[2,5,256]{2,1,0:T(8,128)}, bf16[2,640,256]{2,1,0:T(8,128)(2,1)}, f32[2,5,256]{2,1,0:T(8,128)}) custom-call(s32[2,2]{1,0:T(2,128)} %pad_add_fusion.live_ref, bf16[512,1280]{1,0:T(8,128)(2,1)} %bitcast.2.own_ref, bf16[512,1280]{1,0:T(8,128)(2,1)} %collective-permute-done.far_ref, ...), custom_call_target="tpu_custom_call" | custom-call | flops 8053063680 | bytes 6553600 | tf_op jit(solution)/shard_map/pallas_call | solution.py:83
  264.2 0.7 reduce-precision_convert_fusion.1
  264.9 1.1 fusion.25
  266.1 0.9 slice_bitcast_fusion.1
  267.1 0.1 fusion.50
  267.2 0.1 fusion.51
  267.2 0.2 copy.29
  267.4 0.1 fusion.52
  267.5 0.2 copy.30
  267.7 0.2 copy.31
  267.9 0.6 copy-done.5
  268.5 1.4 fusion.37
  269.9 7.6 %fusion.4 = f32[256,5120]{1,0:T(8,128)} fusion(bf16[640,256]{1,0:T(8,128)(2,1)S(1)} %get-tuple-element.58, bf16[1280,5120]{1,0:T(8,128)(2,1)} %param.11), kind=kOutput, calls=%fused_computation.6 | convolution fusion | flops 1677721600 | bytes 12124160 | tf_op jit(solution)/shard_map/dot_general | solution.py:269
  277.5 5.3 %fusion.6 = f32[256,5120]{1,0:T(8,128)S(1)} fusion(bf16[640,256]{1,0:T(8,128)(2,1)S(1)} %get-tuple-element.57, bf16[1280,5120]{1,0:T(8,128)(2,1)} %param.11), kind=kOutput, calls=%fused_computation.8 | convolution fusion | flops 1677721600 | bytes 12124160 | tf_op jit(solution)/shard_map/dot_general | solution.py:269
  282.9 0.2 fusion.34
  283.1 2.5 fusion
  285.6 1.2 dynamic-slice_bitcast_fusion.1
  286.8 2.9 collective-permute-start.11
  289.7 0.2 copy.32
  289.9 15.9 %collective-permute-done.11 = bf16[656,256]{1,0:T(8,128)(2,1)} collective-permute-done((bf16[656,256]{1,0:T(8,128)(2,1)}, bf16[656,256]{1,0:T(8,128)(2,1)}, u32[]{:S(2)}, u32[]{:S(2)}) %collective-permute-start.11) | collective-permute-done | bytes 335904 | tf_op jit(solution)/shard_map/ppermute | solution.py:187
  305.8 0.8 add_divide_fusion.1
  306.5 1.2 fusion.28
  307.8 1.6 fusion.9
  309.5 7.1 %fusion.1 = bf16[256,5120]{1,0:T(8,128)(2,1)S(1)} fusion(f32[256,5120]{1,0:T(8,128)} %fusion.4, bf16[640,256]{1,0:T(8,128)(2,1)S(1)} %fusion.28, bf16[1280,5120]{1,0:T(8,128)(2,1)} %param.11), kind=kOutput, calls=%fused_computation.3 | convolution fusion | flops 1680343040 | bytes 14745600 | tf_op jit(solution)/shard_map/dot_general | solution.py:269
  316.6 0.9 dynamic-slice_bitcast_fusion.3
  317.5 1.5 collective-permute-start.10
  319.0 1.1 dynamic-slice_bitcast_fusion
  320.1 14.1 %collective-permute-done.10 = bf16[64,5120]{1,0:T(8,128)(2,1)S(1)} collective-permute-done((bf16[64,5120]{1,0:T(8,128)(2,1)}, bf16[64,5120]{1,0:T(8,128)(2,1)S(1)}, u32[]{:S(2)}, u32[]{:S(2)}) %collective-permute-start.10) | collective-permute-done | bytes 655392 | tf_op jit(solution)/shard_map/ppermute | solution.py:225
  334.2 1.2 fusion.19
  335.5 1.6 fusion.8
  337.2 1.6 collective-permute-start.13
  338.8 14.2 %collective-permute-done.13 = bf16[64,5120]{1,0:T(8,128)(2,1)S(1)} collective-permute-done((bf16[64,5120]{1,0:T(8,128)(2,1)S(1)}, bf16[64,5120]{1,0:T(8,128)(2,1)S(1)}, u32[]{:S(2)}, u32[]{:S(2)}) %collective-permute-start.13) | collective-permute-done | bytes 655392 | tf_op jit(solution)/shard_map/ppermute | solution.py:225
  353.0 0.2 fusion.18
  353.1 1.2 maximum_bitcast_fusion
  (51 shorter events, 0.3 us)
Async XLA Ops:
  0.0 6.6 %copy-start.9 = (s32[8,2]{0,1:T(2,128)S(1)}, s32[8,2]{0,1:T(2,128)}, u32[]{:S(2)}) copy-start(s32[8,2]{0,1:T(2,128)} %param.8) | copy-start | bytes 196
  2.6 83.3 %collective-permute-start = (bf16[512,1280]{1,0:T(8,128)(2,1)}, bf16[512,1280]{1,0:T(8,128)(2,1)}, u32[]{:S(2)}, u32[]{:S(2)}) collective-permute-start(bf16[512,1280]{1,0:T(8,128)(2,1)} %bitcast.2.own_ref), channel_id=1, source_target_pairs={{0,16},{4,20},{8,24},{12,28},{16,0},{20,4},{24,8},{28,12},{1,17},{... | collective-permute-start | bytes 3932168 | tf_op jit(solution)/shard_map/ppermute | solution.py:187
  7.3 9.3 %copy-start.1 = (bf16[3,64,8,1280]{3,2,1,0:T(8,128)(2,1)S(1)}, bf16[3,64,8,1280]{3,2,1,0:T(8,128)(2,1)}, u32[]{:S(2)}) copy-start(bf16[3,64,8,1280]{3,2,1,0:T(8,128)(2,1)} %param.10) | copy-start | bytes 11796484
  13.2 23.8 %collective-permute-start.1 = (bf16[2,4,96,640]{3,2,1,0:T(8,128)(2,1)}, bf16[2,4,96,640]{3,2,1,0:T(8,128)(2,1)S(1)}, u32[]{:S(2)}, u32[]{:S(2)}) collective-permute-start(bf16[2,4,96,640]{3,2,1,0:T(8,128)(2,1)} %get-tuple-element.32), channel_id=1, source_target_pairs={{0,4},{4,0},{8,12},{12,8},{16,20},{20,16},{24,28},{28,24},{1,5},{5... | collective-permute-start | bytes 2949128 | tf_op jit(solution)/shard_map/ppermute | solution.py:187
  14.7 51.8 %collective-permute-start.2 = (bf16[2,4,96,640]{3,2,1,0:T(8,128)(2,1)}, bf16[2,4,96,640]{3,2,1,0:T(8,128)(2,1)S(1)}, u32[]{:S(2)}, u32[]{:S(2)}) collective-permute-start(bf16[2,4,96,640]{3,2,1,0:T(8,128)(2,1)} %get-tuple-element.33), channel_id=1, source_target_pairs={{0,8},{4,12},{8,0},{12,4},{16,24},{20,28},{24,16},{28,20},{1,9},{5... | collective-permute-start | bytes 2949128 | tf_op jit(solution)/shard_map/ppermute | solution.py:187
  16.3 69.6 %collective-permute-start.3 = (bf16[2,4,96,640]{3,2,1,0:T(8,128)(2,1)}, bf16[2,4,96,640]{3,2,1,0:T(8,128)(2,1)S(1)}, u32[]{:S(2)}, u32[]{:S(2)}) collective-permute-start(bf16[2,4,96,640]{3,2,1,0:T(8,128)(2,1)} %get-tuple-element.34), channel_id=1, source_target_pairs={{0,12},{4,8},{8,4},{12,0},{16,28},{20,24},{24,20},{28,16},{1,13},{... | collective-permute-start | bytes 2949128 | tf_op jit(solution)/shard_map/ppermute | solution.py:187
  37.0 48.8 %copy-start.11 = (bf16[2,4,96,640]{3,2,1,0:T(8,128)(2,1)}, bf16[2,4,96,640]{3,2,1,0:T(8,128)(2,1)S(1)}, u32[]{:S(2)}) copy-start(bf16[2,4,96,640]{3,2,1,0:T(8,128)(2,1)S(1)} %collective-permute-done.1.refs_1_) | copy-start | bytes 2949124
  66.5 19.3 %copy-start.12 = (bf16[2,4,96,640]{3,2,1,0:T(8,128)(2,1)}, bf16[2,4,96,640]{3,2,1,0:T(8,128)(2,1)S(1)}, u32[]{:S(2)}) copy-start(bf16[2,4,96,640]{3,2,1,0:T(8,128)(2,1)S(1)} %collective-permute-done.2.refs_2_) | copy-start | bytes 2949124
  85.8 1.0 copy-start.13
  86.8 4.8 %copy-start.10 = (s32[8,2]{0,1:T(2,128)S(1)}, s32[8,2]{0,1:T(2,128)}, u32[]{:S(2)}) copy-start(s32[8,2]{0,1:T(2,128)} %param.9) | copy-start | bytes 196
  86.8 91.1 %all-to-all-start = ((bf16[8,3,2,32,1280]{4,3,2,1,0:T(8,128)(2,1)}), bf16[8,3,2,32,1280]{4,3,2,1,0:T(8,128)(2,1)}, u32[]{:S(2)}, u32[]{:S(2)}) async-start(bf16[8,3,2,32,1280]{4,3,2,1,0:T(8,128)(2,1)} %bitcast.159), calls=%async_computation | async-start | bytes 7864320 | tf_op jit(solution)/shard_map/all_to_all | solution.py:208
  103.7 9.1 %copy-start.6 = (f32[2,5,256]{2,1,0:T(8,128)S(1)}, f32[2,5,256]{2,1,0:T(8,128)}, u32[]{:S(2)}) copy-start(f32[2,5,256]{2,1,0:T(8,128)} %get-tuple-element.38) | copy-start | bytes 30724
  109.2 144.1 %collective-permute-start.5 = (bf16[2,4,96,640]{3,2,1,0:T(8,128)(2,1)}, bf16[2,4,96,640]{3,2,1,0:T(8,128)(2,1)}, u32[]{:S(2)}, u32[]{:S(2)}) collective-permute-start(bf16[2,4,96,640]{3,2,1,0:T(8,128)(2,1)} %get-tuple-element.45), channel_id=1, source_target_pairs={{0,4},{4,0},{8,12},{12,8},{16,20},{20,16},{24,28},{28,24},{1,5},{5... | collective-permute-start | bytes 2949128 | tf_op jit(solution)/shard_map/ppermute | solution.py:187
  111.3 142.1 %collective-permute-start.6 = (bf16[2,4,96,640]{3,2,1,0:T(8,128)(2,1)}, bf16[2,4,96,640]{3,2,1,0:T(8,128)(2,1)}, u32[]{:S(2)}, u32[]{:S(2)}) collective-permute-start(bf16[2,4,96,640]{3,2,1,0:T(8,128)(2,1)} %get-tuple-element.46), channel_id=1, source_target_pairs={{0,8},{4,12},{8,0},{12,4},{16,24},{20,28},{24,16},{28,20},{1,9},{5... | collective-permute-start | bytes 2949128 | tf_op jit(solution)/shard_map/ppermute | solution.py:187
  112.7 140.6 %collective-permute-start.7 = (bf16[2,4,96,640]{3,2,1,0:T(8,128)(2,1)}, bf16[2,4,96,640]{3,2,1,0:T(8,128)(2,1)}, u32[]{:S(2)}, u32[]{:S(2)}) collective-permute-start(bf16[2,4,96,640]{3,2,1,0:T(8,128)(2,1)} %get-tuple-element.47), channel_id=1, source_target_pairs={{0,12},{4,8},{8,4},{12,0},{16,28},{20,24},{24,20},{28,16},{1,13},{... | collective-permute-start | bytes 2949128 | tf_op jit(solution)/shard_map/ppermute | solution.py:187
  188.1 3.8 %copy-start.3 = (bf16[2,640,256]{2,1,0:T(8,128)(2,1)S(1)}, bf16[2,640,256]{2,1,0:T(8,128)(2,1)}, u32[]{:S(2)}) copy-start(bf16[2,640,256]{2,1,0:T(8,128)(2,1)} %get-tuple-element.37) | copy-start | bytes 1966084
  188.1 79.0 %all-to-all-start.1 = ((bf16[8,2,32,1280]{3,2,1,0:T(8,128)(2,1)}), bf16[8,2,32,1280]{3,2,1,0:T(8,128)(2,1)S(1)}, u32[]{:S(2)}, u32[]{:S(2)}) async-start(bf16[8,2,32,1280]{3,2,1,0:T(8,128)(2,1)} %shard_map.66), calls=%async_computation.1 | async-start | bytes 2621440 | tf_op jit(solution)/shard_map/all_to_all | solution.py:237
  191.9 61.5 %collective-permute-start.4 = (bf16[2,656,256]{2,1,0:T(8,128)(2,1)S(1)}, bf16[2,656,256]{2,1,0:T(8,128)(2,1)S(1)}, u32[]{:S(2)}, u32[]{:S(2)}) collective-permute-start(bf16[2,656,256]{2,1,0:T(8,128)(2,1)S(1)} %fusion.22), channel_id=1, source_target_pairs={{0,16},{4,20},{8,24},{12,28},{16,0},{20,4},{24,8},{28,12},{1,17},{... | collective-permute-start | bytes 2015240 | tf_op jit(solution)/shard_map/ppermute | solution.py:187
  253.4 13.6 %copy-start.2 = (bf16[2,656,256]{2,1,0:T(8,128)(2,1)}, bf16[2,656,256]{2,1,0:T(8,128)(2,1)S(1)}, u32[]{:S(2)}) copy-start(bf16[2,656,256]{2,1,0:T(8,128)(2,1)S(1)} %collective-permute-done.4) | copy-start | bytes 2015236
  264.9 2.1 copy-start.8
  267.0 15.8 %collective-permute-start.8 = (bf16[656,256]{1,0:T(8,128)(2,1)}, bf16[656,256]{1,0:T(8,128)(2,1)S(1)}, u32[]{:S(2)}, u32[]{:S(2)}) collective-permute-start(bf16[656,256]{1,0:T(8,128)(2,1)} %get-tuple-element.65), channel_id=1, source_target_pairs={{0,16},{4,20},{8,24},{12,28},{16,0},{20,4},{24,8},{28,12},{1,17},{... | collective-permute-start | bytes 1007624 | tf_op jit(solution)/shard_map/ppermute | solution.py:187
  267.4 1.1 copy-start.5
  269.9 13.2 %slice-start = ((s8[13107200]{0:T(1024)(128)(4,1)}), s8[4194304]{0:T(1024)(128)(4,1)S(1)}, s32[]{:S(2)}) async-start(s8[13107200]{0:T(1024)(128)(4,1)} %bitcast.157), calls=%async_computation.2 | async-start | bytes 8388608
  269.9 13.2 %slice-start.1 = ((s8[13107200]{0:T(1024)(128)(4,1)}), s8[4194304]{0:T(1024)(128)(4,1)S(1)}, s32[]{:S(2)}) async-start(s8[13107200]{0:T(1024)(128)(4,1)} %bitcast.157), calls=%async_computation.3 | async-start | bytes 8388608
  277.5 5.4 %copy-start.7 = (f32[2,5,256]{2,1,0:T(8,128)S(1)}, f32[2,5,256]{2,1,0:T(8,128)}, u32[]{:S(2)}) copy-start(f32[2,5,256]{2,1,0:T(8,128)} %get-tuple-element.48) | copy-start | bytes 30724
  277.5 5.4 %copy-start.4 = (bf16[2,640,256]{2,1,0:T(8,128)(2,1)S(1)}, bf16[2,640,256]{2,1,0:T(8,128)(2,1)}, u32[]{:S(2)}) copy-start(bf16[2,640,256]{2,1,0:T(8,128)(2,1)} %get-tuple-element.50) | copy-start | bytes 1966084
  277.5 5.6 %slice-start.2 = ((s8[13107200]{0:T(1024)(128)(4,1)}), s8[4194304]{0:T(1024)(128)(4,1)S(1)}, s32[]{:S(2)}) async-start(s8[13107200]{0:T(1024)(128)(4,1)} %bitcast.157), calls=%async_computation.4 | async-start | bytes 8388608
  277.5 5.6 %slice-start.3 = ((s8[13107200]{0:T(1024)(128)(4,1)}), s8[524288]{0:T(1024)(128)(4,1)S(1)}, s32[]{:S(2)}) async-start(s8[13107200]{0:T(1024)(128)(4,1)} %bitcast.157), calls=%async_computation.5 | async-start | bytes 1048576
  286.8 21.0 %collective-permute-start.9 = (bf16[2,64,5120]{2,1,0:T(8,128)(2,1)}, bf16[2,64,5120]{2,1,0:T(8,128)(2,1)}, u32[]{:S(2)}, u32[]{:S(2)}) collective-permute-start(bf16[2,64,5120]{2,1,0:T(8,128)(2,1)} %dynamic-slice_bitcast_fusion.1), channel_id=1, source_target_pairs={{0,1},{1,0},{2,3},{3,2},{4,5},{5,4},{6,7},{7,6},{8,9},{9,8},{10,11... | collective-permute-start | bytes 3932168 | tf_op jit(solution)/shard_map/ppermute | solution.py:218
  286.8 19.0 %collective-permute-start.11 = (bf16[656,256]{1,0:T(8,128)(2,1)}, bf16[656,256]{1,0:T(8,128)(2,1)}, u32[]{:S(2)}, u32[]{:S(2)}) collective-permute-start(bf16[656,256]{1,0:T(8,128)(2,1)} %get-tuple-element.66), channel_id=1, source_target_pairs={{0,16},{4,20},{8,24},{12,28},{16,0},{20,4},{24,8},{28,12},{1,17},{... | collective-permute-start | bytes 1007624 | tf_op jit(solution)/shard_map/ppermute | solution.py:187
  309.5 7.1 %copy-start = (bf16[2,64,5120]{2,1,0:T(8,128)(2,1)}, bf16[2,64,5120]{2,1,0:T(8,128)(2,1)S(1)}, u32[]{:S(2)}) copy-start(bf16[2,64,5120]{2,1,0:T(8,128)(2,1)S(1)} %fusion.9) | copy-start | bytes 3932164
  317.5 16.8 %collective-permute-start.10 = (bf16[64,5120]{1,0:T(8,128)(2,1)}, bf16[64,5120]{1,0:T(8,128)(2,1)S(1)}, u32[]{:S(2)}, u32[]{:S(2)}) collective-permute-start(bf16[64,5120]{1,0:T(8,128)(2,1)} %dynamic-slice_bitcast_fusion.3), channel_id=1, source_target_pairs={{0,2},{1,3},{2,0},{3,1},{4,6},{5,7},{6,4},{7,5},{8,10},{9,11},{10,... | collective-permute-start | bytes 1966088 | tf_op jit(solution)/shard_map/ppermute | solution.py:225
  320.1 15.4 %collective-permute-start.12 = (bf16[2,64,5120]{2,1,0:T(8,128)(2,1)}, bf16[2,64,5120]{2,1,0:T(8,128)(2,1)}, u32[]{:S(2)}, u32[]{:S(2)}) collective-permute-start(bf16[2,64,5120]{2,1,0:T(8,128)(2,1)} %dynamic-slice_bitcast_fusion), channel_id=1, source_target_pairs={{0,1},{1,0},{2,3},{3,2},{4,5},{5,4},{6,7},{7,6},{8,9},{9,8},{10,11... | collective-permute-start | bytes 3932168 | tf_op jit(solution)/shard_map/ppermute | solution.py:218
  337.2 15.8 %collective-permute-start.13 = (bf16[64,5120]{1,0:T(8,128)(2,1)S(1)}, bf16[64,5120]{1,0:T(8,128)(2,1)S(1)}, u32[]{:S(2)}, u32[]{:S(2)}) collective-permute-start(bf16[64,5120]{1,0:T(8,128)(2,1)S(1)} %dynamic-slice_bitcast_fusion.2), channel_id=1, source_target_pairs={{0,2},{1,3},{2,0},{3,1},{4,6},{5,7},{6,4},{7,5},{8,10},{9,11},{10,... | collective-permute-start | bytes 1966088 | tf_op jit(solution)/shard_map/ppermute | solution.py:225

commit v10 on v5

--- a/solution.py
+++ b/solution.py
@@ -10,6 +10,7 @@
 HEAD_DIM = 128
 TILE_ROWS = 16
 PART_TILE = 32
+COLUMN_CUTS = 2
 HEAD_GROUPS = 2
 VMEM_BYTES = 60 * 1024 * 1024
 
@@ -261,22 +262,26 @@
             + wide(got[: width // groups].reshape(split)) * (got_share / total)[:, None, :]
         )
 
-    projected, summed = [], []
+    projected, summed, pieces = [], [], []
+    cut = out_weight.shape[1] // COLUMN_CUTS
     for part in range(parts):
-        shares = [share_of(group, part, *projected[-1:]) for group in range(groups)]
+        shares = [share_of(group, part, *projected[-1:], *summed[-2:-1]) for group in range(groups)]
         ref_out = jnp.concatenate(shares, axis=0).reshape(width, rows)
         frame_out = back[:, part].reshape(rows, width)
         combined = (ref_out + wide(frame_out.T)).astype(jnp.bfloat16)
-        projected.append(
-            lax.dot_general(
-                after(combined, *summed[-1:]), out_weight, (((0,), (0,)), ((), ())),
-                preferred_element_type=jnp.float32,
-            ).astype(jnp.bfloat16)
-        )
-        summed.append(scatter_cores(projected[-1]))
-    pieces = []
+        for low in range(0, cut * COLUMN_CUTS, cut):
+            projected.append(
+                lax.dot_general(
+                    after(combined, *summed[-2:-1]), out_weight[:, low : low + cut], (((0,), (0,)), ((), ())),
+                    preferred_element_type=jnp.float32,
+                ).astype(jnp.bfloat16)
+            )
+            summed.append(scatter_cores(projected[-1]))
     for block in summed:
-        pieces.append(scatter_chips(after(block, *pieces[-1:])))
+        pieces.append(scatter_chips(after(block, *pieces[-2:-1])))
+    pieces = [
+        jnp.concatenate(pieces[low : low + COLUMN_CUTS], axis=1) for low in range(0, len(pieces), COLUMN_CUTS)
+    ]
     return jnp.concatenate(pieces, axis=0).reshape(spatial // head_groups, frames_here, -1)
 
 

time: 320 us -> 319 us (level)
  local copies, waits for them, and re-layouts: 19.3 us -> 15.3 us
    dot_general x2 -> x4, matrix products: 17.4 us -> 18.8 us  [local(): lax.dot_general(after(combined, *summed[-2:-1]), out_weight[:, low:low +...]
    ppermute x2 -> x4, waiting for transfers between devices: 19.7 us -> 18.6 us  [scatter_chips(): lax.ppermute(give, 'heads', [(h, (h + 2 * step) % head_groups) for h in r...]
  transfers between devices with their start and end apart: 16 -> 20, of which waited for: 9 -> 9; matrix products, arithmetic and copies ran while one was open for 10% -> 12% of each run, Pallas kernels for 13% -> 14%
where the time goes in v10:
time: 319 us; the launch traced here: 317 us
  waiting for transfers between devices  199 us (62%)
  Pallas kernels  42.9 us (13%)
  starting transfers between devices  30.3 us (9%)
  matrix products  18.8 us (6%)
  local copies, waits for them, and re-layouts  15.3 us (5%)
  other arithmetic  10.2 us (3%)
    ppermute x10, waiting for transfers between devices, swap(): return lax.ppermute(block, 'frames', [(a, a ^ step) for a in range(shards)])  116 us
    all_to_all x1, waiting for transfers between devices, local(): lax.all_to_all(after(tokens, far, *banks[0]), 'frames', 0, 0, tiled=True)  64.8 us
    pallas_call x2, Pallas kernels, attend_bank(): pl.pallas_call(functools.partial(bank_kernel, len(banks)), grid=(heads,),...  21.2 us
    dot_general x4, matrix products, local(): lax.dot_general(after(combined, *summed[-2:-1]), out_weight[:, low:low +...  18.8 us
    ppermute x4, waiting for transfers between devices, scatter_chips(): lax.ppermute(give, 'heads', [(h, (h + 2 * step) % head_groups) for h in r...  18.6 us
    ppermute x10, starting transfers between devices, swap(): return lax.ppermute(block, 'frames', [(a, a ^ step) for a in range(shards)])  16.7 us
    pallas_call x2, Pallas kernels, listed_banks(): pl.pallas_call(listed_kernel, grid_spec=pltpu.PrefetchScalarGridSpec(num_...  11.5 us
    pallas_call x1, Pallas kernels, attend_frames(): pl.pallas_call(functools.partial(frame_kernel, frames_here), grid=(width...  10.2 us
  transfers between devices with their start and end apart: 20, of which 9 were waited for; matrix products, arithmetic and copies ran while one was open for 12% of the time, Pallas kernels for 14%

profile of v10, /device:TPU:0, one launch (start us, length us, event | category | flops | bytes accessed | tf_op | source)
XLA Modules:
  0.0 317.4 jit_solution(7248558420408148049)
XLA Ops:
  0.0 2.5 copy.20
  2.5 4.0 %collective-permute-start = (bf16[512,1280]{1,0:T(8,128)(2,1)}, bf16[512,1280]{1,0:T(8,128)(2,1)}, u32[]{:S(2)}, u32[]{:S(2)}) collective-permute-start(bf16[512,1280]{1,0:T(8,128)(2,1)} %bitcast.2.own_ref), channel_id=1, source_target_pairs={{0,16},{4,20},{8,24},{12,28},{16,0},{20,4},{24,8},{28,12},{1,17},{... | collective-permute-start | bytes 3932168 | tf_op jit(solution)/shard_map/ppermute | solution.py:188
  6.6 0.7 reshape.202.slots_ref
  7.3 5.9 %shard_map.64 = (bf16[2,4,96,640]{3,2,1,0:T(8,128)(2,1)}, bf16[2,4,96,640]{3,2,1,0:T(8,128)(2,1)}, bf16[2,4,96,640]{3,2,1,0:T(8,128)(2,1)}, bf16[2,4,96,640]{3,2,1,0:T(8,128)(2,1)}) custom-call(s32[1]{0:T(128)} %bitcast.4.place_ref, s32[16]{0:T(128)} %reshape.202.slots_ref, bf16[2,8,96,1280]{3,2,1,0:T(8,128)(2,1)} %refs_3_.3, ...), custom_call_target="tpu_custom_call" | custom-call | bytes 7864320 | tf_op jit(solution)/shard_map/pallas_call | solution.py:158
  13.2 1.5 collective-permute-start.1
  14.7 1.6 collective-permute-start.2
  16.3 0.4 collective-permute-start.3
  16.7 2.3 copy.22
  18.9 18.1 %collective-permute-done.1.refs_1_ = bf16[2,4,96,640]{3,2,1,0:T(8,128)(2,1)S(1)} collective-permute-done((bf16[2,4,96,640]{3,2,1,0:T(8,128)(2,1)}, bf16[2,4,96,640]{3,2,1,0:T(8,128)(2,1)S(1)}, u32[]{:S(2)}, u32[]{:S(2)}) %collective-permute-start.1) | collective-permute-done | bytes 983072 | tf_op jit(solution)/shard_map/ppermute | solution.py:188
  37.0 29.5 %collective-permute-done.2.refs_2_ = bf16[2,4,96,640]{3,2,1,0:T(8,128)(2,1)S(1)} collective-permute-done((bf16[2,4,96,640]{3,2,1,0:T(8,128)(2,1)}, bf16[2,4,96,640]{3,2,1,0:T(8,128)(2,1)S(1)}, u32[]{:S(2)}, u32[]{:S(2)}) %collective-permute-start.2) | collective-permute-done | bytes 983072 | tf_op jit(solution)/shard_map/ppermute | solution.py:188
  66.5 19.3 %collective-permute-done.3.refs_3_ = bf16[2,4,96,640]{3,2,1,0:T(8,128)(2,1)S(1)} collective-permute-done((bf16[2,4,96,640]{3,2,1,0:T(8,128)(2,1)}, bf16[2,4,96,640]{3,2,1,0:T(8,128)(2,1)S(1)}, u32[]{:S(2)}, u32[]{:S(2)}) %collective-permute-start.3) | collective-permute-done | bytes 983072 | tf_op jit(solution)/shard_map/ppermute | solution.py:188
  85.9 1.0 copy-done.16
  86.8 4.7 %all-to-all-start = ((bf16[8,3,2,32,1280]{4,3,2,1,0:T(8,128)(2,1)}), bf16[8,3,2,32,1280]{4,3,2,1,0:T(8,128)(2,1)}, u32[]{:S(2)}, u32[]{:S(2)}) async-start(bf16[8,3,2,32,1280]{4,3,2,1,0:T(8,128)(2,1)} %bitcast.171), calls=%async_computation | async-start | bytes 7864320 | tf_op jit(solution)/shard_map/all_to_all | solution.py:209
  91.7 0.1 copy.29
  91.8 0.6 pad_add_fusion.live_ref
  92.4 10.6 %shard_map.65 = (bf16[2,640,256]{2,1,0:T(8,128)(2,1)}, f32[2,5,256]{2,1,0:T(8,128)}, bf16[2,640,256]{2,1,0:T(8,128)(2,1)}, f32[2,5,256]{2,1,0:T(8,128)}) custom-call(s32[2,2]{1,0:T(2,128)} %pad_add_fusion.live_ref, bf16[512,1280]{1,0:T(8,128)(2,1)} %bitcast.2.own_ref, bf16[512,1280]{1,0:T(8,128)(2,1)} %collective-permute-done.far_ref, ...), custom_call_target="tpu_custom_call" | custom-call | flops 8053063680 | bytes 6553600 | tf_op jit(solution)/shard_map/pallas_call | solution.py:84
  103.1 0.6 reshape.205.slots_ref
  103.7 5.6 %shard_map.67 = (bf16[2,4,96,640]{3,2,1,0:T(8,128)(2,1)}, bf16[2,4,96,640]{3,2,1,0:T(8,128)(2,1)}, bf16[2,4,96,640]{3,2,1,0:T(8,128)(2,1)}, bf16[2,4,96,640]{3,2,1,0:T(8,128)(2,1)}) custom-call(s32[1]{0:T(128)} %bitcast.4.place_ref, s32[16]{0:T(128)} %reshape.205.slots_ref, bf16[2,8,96,1280]{3,2,1,0:T(8,128)(2,1)} %refs_3_.3, ...), custom_call_target="tpu_custom_call" | custom-call | bytes 7864320 | tf_op jit(solution)/shard_map/pallas_call | solution.py:158
  109.3 2.1 collective-permute-start.5
  111.4 1.5 collective-permute-start.6
  113.0 2.9 collective-permute-start.4
  116.0 64.8 %all-to-all-done.token_ref = bf16[8,3,2,32,1280]{4,3,2,1,0:T(8,128)(2,1)} async-done(((bf16[8,3,2,32,1280]{4,3,2,1,0:T(8,128)(2,1)}), bf16[8,3,2,32,1280]{4,3,2,1,0:T(8,128)(2,1)}, u32[]{:S(2)}, u32[]{:S(2)}) %all-to-all-start) | async-done | bytes 3932192 | tf_op jit(solution)/shard_map/all_to_all | solution.py:209
  180.8 10.2 %shard_map.66 = bf16[8,2,32,1280]{3,2,1,0:T(8,128)(2,1)} custom-call(bf16[8,3,2,32,1280]{4,3,2,1,0:T(8,128)(2,1)} %all-to-all-done.token_ref), custom_call_target="tpu_custom_call" | custom-call | flops 2684354560 | bytes 5242880 | tf_op jit(solution)/shard_map/pallas_call | solution.py:126
  191.0 3.7 %all-to-all-start.1 = ((bf16[8,2,32,1280]{3,2,1,0:T(8,128)(2,1)}), bf16[8,2,32,1280]{3,2,1,0:T(8,128)(2,1)S(1)}, u32[]{:S(2)}, u32[]{:S(2)}) async-start(bf16[8,2,32,1280]{3,2,1,0:T(8,128)(2,1)} %shard_map.66), calls=%async_computation.1 | async-start | bytes 2621440 | tf_op jit(solution)/shard_map/all_to_all | solution.py:238
  194.7 23.7 %collective-permute-done.7.refs_3_ = bf16[2,4,96,640]{3,2,1,0:T(8,128)(2,1)} collective-permute-done((bf16[2,4,96,640]{3,2,1,0:T(8,128)(2,1)}, bf16[2,4,96,640]{3,2,1,0:T(8,128)(2,1)}, u32[]{:S(2)}, u32[]{:S(2)}) %collective-permute-start.7) | collective-permute-done | bytes 983072 | tf_op jit(solution)/shard_map/ppermute | solution.py:188
  218.5 10.6 %shard_map.68 = (bf16[2,640,256]{2,1,0:T(8,128)(2,1)}, f32[2,5,256]{2,1,0:T(8,128)}, bf16[2,640,256]{2,1,0:T(8,128)(2,1)}, f32[2,5,256]{2,1,0:T(8,128)}) custom-call(s32[2,2]{1,0:T(2,128)} %pad_add_fusion.live_ref, bf16[512,1280]{1,0:T(8,128)(2,1)} %bitcast.2.own_ref, bf16[512,1280]{1,0:T(8,128)(2,1)} %collective-permute-done.far_ref, ...), custom_call_target="tpu_custom_call" | custom-call | flops 8053063680 | bytes 6553600 | tf_op jit(solution)/shard_map/pallas_call | solution.py:84
  229.1 0.7 reduce-precision_convert_fusion.1
  229.8 1.1 fusion.41
  231.0 0.8 slice_bitcast_fusion.1
  231.8 0.4 copy-done.8
  232.2 0.8 fusion.65
  233.0 2.6 collective-permute-start.13
  235.6 1.1 fusion.45
  236.7 25.3 %collective-permute-done.8 = bf16[656,256]{1,0:T(8,128)(2,1)S(1)} collective-permute-done((bf16[656,256]{1,0:T(8,128)(2,1)S(1)}, bf16[656,256]{1,0:T(8,128)(2,1)S(1)}, u32[]{:S(2)}, u32[]{:S(2)}) %collective-permute-start.8) | collective-permute-done | bytes 335904 | tf_op jit(solution)/shard_map/ppermute | solution.py:188
  262.1 0.1 fusion.48
  262.2 1.2 pad_maximum_fusion
  263.3 1.7 copy.24
  265.2 0.2 fusion.35
  265.3 4.7 %fusion.8 = bf16[256,2560]{1,0:T(8,128)(2,1)S(1)} fusion(bf16[1280,256]{0,1:T(8,128)(2,1)S(1)} %fusion.35, bf16[1280,5120]{1,0:T(8,128)(2,1)} %param.11), kind=kOutput, calls=%fused_computation.8 | convolution fusion | flops 1678376960 | bytes 8519680 | tf_op jit(solution)/shard_map/dot_general | solution.py:274
  270.2 4.7 %fusion.14 = bf16[256,2560]{1,0:T(8,128)(2,1)S(1)} fusion(bf16[1280,256]{0,1:T(8,128)(2,1)S(1)} %fusion.35, bf16[1280,5120]{1,0:T(8,128)(2,1)} %param.11), kind=kOutput, calls=%fused_computation.10 | convolution fusion | flops 1678376960 | bytes 8519680 | tf_op jit(solution)/shard_map/dot_general | solution.py:274
  274.9 1.0 dynamic-slice_bitcast_fusion.2
  275.9 0.5 collective-permute-start.11
  276.4 1.0 fusion.33
  277.4 0.8 add_divide_fusion.1
  278.2 1.0 slice.142
  279.2 0.1 fusion.44
  279.4 0.4 copy.26
  279.9 0.2 fusion.31
  280.0 0.9 copy-done.2
  281.0 0.4 copy-done.4
  281.4 1.2 fusion.32
  282.6 1.6 collective-permute-start.10
  284.2 4.7 %fusion.11 = bf16[256,2560]{1,0:T(8,128)(2,1)S(1)} fusion(bf16[1280,256]{0,1:T(8,128)(2,1)S(1)} %fusion.31, bf16[1280,5120]{1,0:T(8,128)(2,1)} %param.11), kind=kOutput, calls=%fused_computation.9 | convolution fusion | flops 1678376960 | bytes 8519680 | tf_op jit(solution)/shard_map/dot_general | solution.py:274
  289.1 0.6 collective-permute-start.12
  289.7 4.7 %fusion.17 = bf16[256,2560]{1,0:T(8,128)(2,1)S(1)} fusion(bf16[1280,256]{0,1:T(8,128)(2,1)S(1)} %fusion.31, bf16[1280,5120]{1,0:T(8,128)(2,1)} %param.11), kind=kOutput, calls=%fused_computation.11 | convolution fusion | flops 1678376960 | bytes 8519680 | tf_op jit(solution)/shard_map/dot_general | solution.py:274
  294.4 0.2 collective-permute-start.16
  294.8 4.6 %collective-permute-done.12 = bf16[64,2560]{1,0:T(8,128)(2,1)S(1)} collective-permute-done((bf16[64,2560]{1,0:T(8,128)(2,1)S(1)}, bf16[64,2560]{1,0:T(8,128)(2,1)S(1)}, u32[]{:S(2)}, u32[]{:S(2)}) %collective-permute-start.12) | collective-permute-done | bytes 327712 | tf_op jit(solution)/shard_map/ppermute | solution.py:226
  299.5 0.2 fusion.29
  299.7 1.6 collective-permute-start.15
  301.2 0.2 fusion.28
  301.4 0.6 collective-permute-start.17
  302.0 8.3 %collective-permute-done.15 = bf16[64,2560]{1,0:T(8,128)(2,1)S(1)} collective-permute-done((bf16[64,2560]{1,0:T(8,128)(2,1)S(1)}, bf16[64,2560]{1,0:T(8,128)(2,1)S(1)}, u32[]{:S(2)}, u32[]{:S(2)}) %collective-permute-start.15) | collective-permute-done | bytes 327712 | tf_op jit(solution)/shard_map/ppermute | solution.py:226
  310.4 5.7 %collective-permute-done.17 = bf16[64,2560]{1,0:T(8,128)(2,1)S(1)} collective-permute-done((bf16[64,2560]{1,0:T(8,128)(2,1)S(1)}, bf16[64,2560]{1,0:T(8,128)(2,1)S(1)}, u32[]{:S(2)}, u32[]{:S(2)}) %collective-permute-start.17) | collective-permute-done | bytes 327712 | tf_op jit(solution)/shard_map/ppermute | solution.py:226
  316.2 1.2 maximum_bitcast_fusion
  (69 shorter events, 1.6 us)
Async XLA Ops:
  0.0 6.5 %copy-start.12 = (s32[8,2]{0,1:T(2,128)S(1)}, s32[8,2]{0,1:T(2,128)}, u32[]{:S(2)}) copy-start(s32[8,2]{0,1:T(2,128)} %param.8) | copy-start | bytes 196
  2.5 83.4 %collective-permute-start = (bf16[512,1280]{1,0:T(8,128)(2,1)}, bf16[512,1280]{1,0:T(8,128)(2,1)}, u32[]{:S(2)}, u32[]{:S(2)}) collective-permute-start(bf16[512,1280]{1,0:T(8,128)(2,1)} %bitcast.2.own_ref), channel_id=1, source_target_pairs={{0,16},{4,20},{8,24},{12,28},{16,0},{20,4},{24,8},{28,12},{1,17},{... | collective-permute-start | bytes 3932168 | tf_op jit(solution)/shard_map/ppermute | solution.py:188
  7.3 9.4 %copy-start = (bf16[3,64,8,1280]{3,2,1,0:T(8,128)(2,1)S(1)}, bf16[3,64,8,1280]{3,2,1,0:T(8,128)(2,1)}, u32[]{:S(2)}) copy-start(bf16[3,64,8,1280]{3,2,1,0:T(8,128)(2,1)} %param.10) | copy-start | bytes 11796484
  13.2 23.8 %collective-permute-start.1 = (bf16[2,4,96,640]{3,2,1,0:T(8,128)(2,1)}, bf16[2,4,96,640]{3,2,1,0:T(8,128)(2,1)S(1)}, u32[]{:S(2)}, u32[]{:S(2)}) collective-permute-start(bf16[2,4,96,640]{3,2,1,0:T(8,128)(2,1)} %get-tuple-element.32), channel_id=1, source_target_pairs={{0,4},{4,0},{8,12},{12,8},{16,20},{20,16},{24,28},{28,24},{1,5},{5... | collective-permute-start | bytes 2949128 | tf_op jit(solution)/shard_map/ppermute | solution.py:188
  14.7 51.8 %collective-permute-start.2 = (bf16[2,4,96,640]{3,2,1,0:T(8,128)(2,1)}, bf16[2,4,96,640]{3,2,1,0:T(8,128)(2,1)S(1)}, u32[]{:S(2)}, u32[]{:S(2)}) collective-permute-start(bf16[2,4,96,640]{3,2,1,0:T(8,128)(2,1)} %get-tuple-element.33), channel_id=1, source_target_pairs={{0,8},{4,12},{8,0},{12,4},{16,24},{20,28},{24,16},{28,20},{1,9},{5... | collective-permute-start | bytes 2949128 | tf_op jit(solution)/shard_map/ppermute | solution.py:188
  16.3 69.6 %collective-permute-start.3 = (bf16[2,4,96,640]{3,2,1,0:T(8,128)(2,1)}, bf16[2,4,96,640]{3,2,1,0:T(8,128)(2,1)S(1)}, u32[]{:S(2)}, u32[]{:S(2)}) collective-permute-start(bf16[2,4,96,640]{3,2,1,0:T(8,128)(2,1)} %get-tuple-element.34), channel_id=1, source_target_pairs={{0,12},{4,8},{8,4},{12,0},{16,28},{20,24},{24,20},{28,16},{1,13},{... | collective-permute-start | bytes 2949128 | tf_op jit(solution)/shard_map/ppermute | solution.py:188
  37.0 48.9 %copy-start.14 = (bf16[2,4,96,640]{3,2,1,0:T(8,128)(2,1)}, bf16[2,4,96,640]{3,2,1,0:T(8,128)(2,1)S(1)}, u32[]{:S(2)}) copy-start(bf16[2,4,96,640]{3,2,1,0:T(8,128)(2,1)S(1)} %collective-permute-done.1.refs_1_) | copy-start | bytes 2949124
  66.5 19.3 %copy-start.15 = (bf16[2,4,96,640]{3,2,1,0:T(8,128)(2,1)}, bf16[2,4,96,640]{3,2,1,0:T(8,128)(2,1)S(1)}, u32[]{:S(2)}) copy-start(bf16[2,4,96,640]{3,2,1,0:T(8,128)(2,1)S(1)} %collective-permute-done.2.refs_2_) | copy-start | bytes 2949124
  85.8 1.0 copy-start.16
  86.8 4.7 %copy-start.13 = (s32[8,2]{0,1:T(2,128)S(1)}, s32[8,2]{0,1:T(2,128)}, u32[]{:S(2)}) copy-start(s32[8,2]{0,1:T(2,128)} %param.9) | copy-start | bytes 196
  86.8 93.9 %all-to-all-start = ((bf16[8,3,2,32,1280]{4,3,2,1,0:T(8,128)(2,1)}), bf16[8,3,2,32,1280]{4,3,2,1,0:T(8,128)(2,1)}, u32[]{:S(2)}, u32[]{:S(2)}) async-start(bf16[8,3,2,32,1280]{4,3,2,1,0:T(8,128)(2,1)} %bitcast.171), calls=%async_computation | async-start | bytes 7864320 | tf_op jit(solution)/shard_map/all_to_all | solution.py:209
  103.7 9.2 %copy-start.9 = (f32[2,5,256]{2,1,0:T(8,128)S(1)}, f32[2,5,256]{2,1,0:T(8,128)}, u32[]{:S(2)}) copy-start(f32[2,5,256]{2,1,0:T(8,128)} %get-tuple-element.38) | copy-start | bytes 30724
  103.7 9.2 %copy-start.7 = (bf16[2,640,256]{2,1,0:T(8,128)(2,1)S(1)}, bf16[2,640,256]{2,1,0:T(8,128)(2,1)}, u32[]{:S(2)}) copy-start(bf16[2,640,256]{2,1,0:T(8,128)(2,1)} %get-tuple-element.37) | copy-start | bytes 1966084
  109.3 6.6 %copy-start.6 = (bf16[2,640,256]{2,1,0:T(8,128)(2,1)S(1)}, bf16[2,640,256]{2,1,0:T(8,128)(2,1)}, u32[]{:S(2)}) copy-start(bf16[2,640,256]{2,1,0:T(8,128)(2,1)} %get-tuple-element.35) | copy-start | bytes 1966084
  109.3 85.4 %collective-permute-start.5 = (bf16[2,4,96,640]{3,2,1,0:T(8,128)(2,1)}, bf16[2,4,96,640]{3,2,1,0:T(8,128)(2,1)}, u32[]{:S(2)}, u32[]{:S(2)}) collective-permute-start(bf16[2,4,96,640]{3,2,1,0:T(8,128)(2,1)} %get-tuple-element.44), channel_id=1, source_target_pairs={{0,4},{4,0},{8,12},{12,8},{16,20},{20,16},{24,28},{28,24},{1,5},{5... | collective-permute-start | bytes 2949128 | tf_op jit(solution)/shard_map/ppermute | solution.py:188
  111.4 83.3 %collective-permute-start.6 = (bf16[2,4,96,640]{3,2,1,0:T(8,128)(2,1)}, bf16[2,4,96,640]{3,2,1,0:T(8,128)(2,1)}, u32[]{:S(2)}, u32[]{:S(2)}) collective-permute-start(bf16[2,4,96,640]{3,2,1,0:T(8,128)(2,1)} %get-tuple-element.45), channel_id=1, source_target_pairs={{0,8},{4,12},{8,0},{12,4},{16,24},{20,28},{24,16},{28,20},{1,9},{5... | collective-permute-start | bytes 2949128 | tf_op jit(solution)/shard_map/ppermute | solution.py:188
  112.9 105.6 %collective-permute-start.7 = (bf16[2,4,96,640]{3,2,1,0:T(8,128)(2,1)}, bf16[2,4,96,640]{3,2,1,0:T(8,128)(2,1)}, u32[]{:S(2)}, u32[]{:S(2)}) collective-permute-start(bf16[2,4,96,640]{3,2,1,0:T(8,128)(2,1)} %get-tuple-element.46), channel_id=1, source_target_pairs={{0,12},{4,8},{8,4},{12,0},{16,28},{20,24},{24,20},{28,16},{1,13},{... | collective-permute-start | bytes 2949128 | tf_op jit(solution)/shard_map/ppermute | solution.py:188
  113.0 116.1 %collective-permute-start.4 = (bf16[2,656,256]{2,1,0:T(8,128)(2,1)S(1)}, bf16[2,656,256]{2,1,0:T(8,128)(2,1)S(1)}, u32[]{:S(2)}, u32[]{:S(2)}) collective-permute-start(bf16[2,656,256]{2,1,0:T(8,128)(2,1)S(1)} %fusion.38), channel_id=1, source_target_pairs={{0,16},{4,20},{8,24},{12,28},{16,0},{20,4},{24,8},{28,12},{1,17},{... | collective-permute-start | bytes 2015240 | tf_op jit(solution)/shard_map/ppermute | solution.py:188
  191.0 74.1 %all-to-all-start.1 = ((bf16[8,2,32,1280]{3,2,1,0:T(8,128)(2,1)}), bf16[8,2,32,1280]{3,2,1,0:T(8,128)(2,1)S(1)}, u32[]{:S(2)}, u32[]{:S(2)}) async-start(bf16[8,2,32,1280]{3,2,1,0:T(8,128)(2,1)} %shard_map.66), calls=%async_computation.1 | async-start | bytes 2621440 | tf_op jit(solution)/shard_map/all_to_all | solution.py:238
  230.9 1.2 copy-start.8
  231.7 1.2 copy-start.10
  231.7 30.3 %collective-permute-start.8 = (bf16[656,256]{1,0:T(8,128)(2,1)S(1)}, bf16[656,256]{1,0:T(8,128)(2,1)S(1)}, u32[]{:S(2)}, u32[]{:S(2)}) collective-permute-start(bf16[656,256]{1,0:T(8,128)(2,1)S(1)} %get-tuple-element.65), channel_id=1, source_target_pairs={{0,16},{4,20},{8,24},{12,28},{16,0},{20,4},{24,8},{28,12},{1,17},{... | collective-permute-start | bytes 1007624 | tf_op jit(solution)/shard_map/ppermute | solution.py:188
  233.0 44.4 %collective-permute-start.13 = (bf16[656,256]{1,0:T(8,128)(2,1)}, bf16[656,256]{1,0:T(8,128)(2,1)}, u32[]{:S(2)}, u32[]{:S(2)}) collective-permute-start(bf16[656,256]{1,0:T(8,128)(2,1)} %get-tuple-element.66), channel_id=1, source_target_pairs={{0,16},{4,20},{8,24},{12,28},{16,0},{20,4},{24,8},{28,12},{1,17},{... | collective-permute-start | bytes 1007624 | tf_op jit(solution)/shard_map/ppermute | solution.py:188
  235.6 26.4 %copy-start.11 = (f32[2,5,256]{2,1,0:T(8,128)S(1)}, f32[2,5,256]{2,1,0:T(8,128)}, u32[]{:S(2)}) copy-start(f32[2,5,256]{2,1,0:T(8,128)} %get-tuple-element.47) | copy-start | bytes 30724
  270.1 6.3 %collective-permute-start.9 = (bf16[2,64,2560]{2,1,0:T(8,128)(2,1)S(1)}, bf16[2,64,2560]{2,1,0:T(8,128)(2,1)S(1)}, u32[]{:S(2)}, u32[]{:S(2)}) collective-permute-start(bf16[2,64,2560]{2,1,0:T(8,128)(2,1)S(1)} %dynamic-slice_bitcast_fusion.3), channel_id=1, source_target_pairs={{0,1},{1,0},{2,3},{3,2},{4,5},{5,4},{6,7},{7,6},{8,9},{9,8},{10,11... | collective-permute-start | bytes 1966088 | tf_op jit(solution)/shard_map/ppermute | solution.py:219
  274.9 2.5 copy-start.3
  275.9 3.3 %copy-start.5 = (bf16[1,640,256]{2,1,0:T(8,128)(2,1)S(1)}, bf16[1,640,256]{2,1,0:T(8,128)(2,1)}, u32[]{:S(2)}) copy-start(bf16[1,640,256]{2,1,0:T(8,128)(2,1)} %get-tuple-element.69) | copy-start | bytes 983044
  275.9 5.1 %collective-permute-start.11 = (bf16[2,64,2560]{2,1,0:T(8,128)(2,1)}, bf16[2,64,2560]{2,1,0:T(8,128)(2,1)}, u32[]{:S(2)}, u32[]{:S(2)}) collective-permute-start(bf16[2,64,2560]{2,1,0:T(8,128)(2,1)} %dynamic-slice_bitcast_fusion.2), channel_id=1, source_target_pairs={{0,1},{1,0},{2,3},{3,2},{4,5},{5,4},{6,7},{7,6},{8,9},{9,8},{10,11... | collective-permute-start | bytes 1966088 | tf_op jit(solution)/shard_map/ppermute | solution.py:219
  277.4 1.9 copy-start.1
  279.8 1.1 copy-start.2
  279.8 1.5 copy-start.4
  282.6 12.0 %collective-permute-start.10 = (bf16[64,2560]{1,0:T(8,128)(2,1)S(1)}, bf16[64,2560]{1,0:T(8,128)(2,1)S(1)}, u32[]{:S(2)}, u32[]{:S(2)}) collective-permute-start(bf16[64,2560]{1,0:T(8,128)(2,1)S(1)} %dynamic-slice_bitcast_fusion.7), channel_id=1, source_target_pairs={{0,2},{1,3},{2,0},{3,1},{4,6},{5,7},{6,4},{7,5},{8,10},{9,11},{10,... | collective-permute-start | bytes 983048 | tf_op jit(solution)/shard_map/ppermute | solution.py:226
  289.0 10.5 %collective-permute-start.14 = (bf16[2,64,2560]{2,1,0:T(8,128)(2,1)S(1)}, bf16[2,64,2560]{2,1,0:T(8,128)(2,1)S(1)}, u32[]{:S(2)}, u32[]{:S(2)}) collective-permute-start(bf16[2,64,2560]{2,1,0:T(8,128)(2,1)S(1)} %dynamic-slice_bitcast_fusion.1), channel_id=1, source_target_pairs={{0,1},{1,0},{2,3},{3,2},{4,5},{5,4},{6,7},{7,6},{8,9},{9,8},{10,11... | collective-permute-start | bytes 1966088 | tf_op jit(solution)/shard_map/ppermute | solution.py:219
  289.1 10.3 %collective-permute-start.12 = (bf16[64,2560]{1,0:T(8,128)(2,1)S(1)}, bf16[64,2560]{1,0:T(8,128)(2,1)S(1)}, u32[]{:S(2)}, u32[]{:S(2)}) collective-permute-start(bf16[64,2560]{1,0:T(8,128)(2,1)S(1)} %dynamic-slice_bitcast_fusion.6), channel_id=1, source_target_pairs={{0,2},{1,3},{2,0},{3,1},{4,6},{5,7},{6,4},{7,5},{8,10},{9,11},{10,... | collective-permute-start | bytes 983048 | tf_op jit(solution)/shard_map/ppermute | solution.py:226
  294.4 6.8 %collective-permute-start.16 = (bf16[2,64,2560]{2,1,0:T(8,128)(2,1)S(1)}, bf16[2,64,2560]{2,1,0:T(8,128)(2,1)S(1)}, u32[]{:S(2)}, u32[]{:S(2)}) collective-permute-start(bf16[2,64,2560]{2,1,0:T(8,128)(2,1)S(1)} %dynamic-slice_bitcast_fusion), channel_id=1, source_target_pairs={{0,1},{1,0},{2,3},{3,2},{4,5},{5,4},{6,7},{7,6},{8,9},{9,8},{10,11... | collective-permute-start | bytes 1966088 | tf_op jit(solution)/shard_map/ppermute | solution.py:219
  299.7 10.7 %collective-permute-start.15 = (bf16[64,2560]{1,0:T(8,128)(2,1)S(1)}, bf16[64,2560]{1,0:T(8,128)(2,1)S(1)}, u32[]{:S(2)}, u32[]{:S(2)}) collective-permute-start(bf16[64,2560]{1,0:T(8,128)(2,1)S(1)} %dynamic-slice_bitcast_fusion.5), channel_id=1, source_target_pairs={{0,2},{1,3},{2,0},{3,1},{4,6},{5,7},{6,4},{7,5},{8,10},{9,11},{10,... | collective-permute-start | bytes 983048 | tf_op jit(solution)/shard_map/ppermute | solution.py:226
  301.4 14.7 %collective-permute-start.17 = (bf16[64,2560]{1,0:T(8,128)(2,1)S(1)}, bf16[64,2560]{1,0:T(8,128)(2,1)S(1)}, u32[]{:S(2)}, u32[]{:S(2)}) collective-permute-start(bf16[64,2560]{1,0:T(8,128)(2,1)S(1)} %dynamic-slice_bitcast_fusion.4), channel_id=1, source_target_pairs={{0,2},{1,3},{2,0},{3,1},{4,6},{5,7},{6,4},{7,5},{8,10},{9,11},{10,... | collective-permute-start | bytes 983048 | tf_op jit(solution)/shard_map/ppermute | solution.py:226

commit v11 on v10

--- a/solution.py
+++ b/solution.py
@@ -278,7 +278,8 @@
             )
             summed.append(scatter_cores(projected[-1]))
     for block in summed:
-        pieces.append(scatter_chips(after(block, *pieces[-2:-1])))
+        before = pieces if len(pieces) == 1 else pieces[-2:-1]
+        pieces.append(scatter_chips(after(block, *before)))
     pieces = [
         jnp.concatenate(pieces[low : low + COLUMN_CUTS], axis=1) for low in range(0, len(pieces), COLUMN_CUTS)
     ]

time: 319 us -> 321 us (level)
  transfers between devices with their start and end apart: 20 -> 20, of which waited for: 9 -> 10; matrix products, arithmetic and copies ran while one was open for 12% -> 12% of each run, Pallas kernels for 14% -> 13%
where the time goes in v11:
time: 321 us; the launch traced here: 320 us
  waiting for transfers between devices  201 us (63%)
  Pallas kernels  42.9 us (13%)
  starting transfers between devices  31.1 us (10%)
  matrix products  18.9 us (6%)
  local copies, waits for them, and re-layouts  14.9 us (5%)
  other arithmetic  10.2 us (3%)
    ppermute x10, waiting for transfers between devices, swap(): return lax.ppermute(block, 'frames', [(a, a ^ step) for a in range(shards)])  116 us
    all_to_all x1, waiting for transfers between devices, local(): lax.all_to_all(after(tokens, far, *banks[0]), 'frames', 0, 0, tiled=True)  64.8 us
    pallas_call x2, Pallas kernels, attend_bank(): pl.pallas_call(functools.partial(bank_kernel, len(banks)), grid=(heads,),...  21.2 us
    ppermute x4, waiting for transfers between devices, scatter_chips(): lax.ppermute(give, 'heads', [(h, (h + 2 * step) % head_groups) for h in r...  20.6 us
    dot_general x4, matrix products, local(): lax.dot_general(after(combined, *summed[-2:-1]), out_weight[:, low:low +...  18.9 us
    ppermute x10, starting transfers between devices, swap(): return lax.ppermute(block, 'frames', [(a, a ^ step) for a in range(shards)])  16.7 us
    pallas_call x2, Pallas kernels, listed_banks(): pl.pallas_call(listed_kernel, grid_spec=pltpu.PrefetchScalarGridSpec(num_...  11.5 us
    pallas_call x1, Pallas kernels, attend_frames(): pl.pallas_call(functools.partial(frame_kernel, frames_here), grid=(width...  10.2 us
  transfers between devices with their start and end apart: 20, of which 10 were waited for; matrix products, arithmetic and copies ran while one was open for 12% of the time, Pallas kernels for 13%

profile of v11, /device:TPU:0, one launch (start us, length us, event | category | flops | bytes accessed | tf_op | source)
XLA Modules:
  0.0 319.8 jit_solution(6699539381629693592)
XLA Ops:
  0.0 2.5 copy.20
  2.5 4.0 %collective-permute-start = (bf16[512,1280]{1,0:T(8,128)(2,1)}, bf16[512,1280]{1,0:T(8,128)(2,1)}, u32[]{:S(2)}, u32[]{:S(2)}) collective-permute-start(bf16[512,1280]{1,0:T(8,128)(2,1)} %bitcast.2.own_ref), channel_id=1, source_target_pairs={{0,16},{4,20},{8,24},{12,28},{16,0},{20,4},{24,8},{28,12},{1,17},{... | collective-permute-start | bytes 3932168 | tf_op jit(solution)/shard_map/ppermute | solution.py:188
  6.6 0.7 reshape.202.slots_ref
  7.3 5.9 %shard_map.64 = (bf16[2,4,96,640]{3,2,1,0:T(8,128)(2,1)}, bf16[2,4,96,640]{3,2,1,0:T(8,128)(2,1)}, bf16[2,4,96,640]{3,2,1,0:T(8,128)(2,1)}, bf16[2,4,96,640]{3,2,1,0:T(8,128)(2,1)}) custom-call(s32[1]{0:T(128)} %bitcast.4.place_ref, s32[16]{0:T(128)} %reshape.202.slots_ref, bf16[2,8,96,1280]{3,2,1,0:T(8,128)(2,1)} %refs_3_.3, ...), custom_call_target="tpu_custom_call" | custom-call | bytes 7864320 | tf_op jit(solution)/shard_map/pallas_call | solution.py:158
  13.2 1.5 collective-permute-start.1
  14.7 1.6 collective-permute-start.2
  16.3 0.4 collective-permute-start.3
  16.7 2.3 copy.22
  18.9 18.1 %collective-permute-done.1.refs_1_ = bf16[2,4,96,640]{3,2,1,0:T(8,128)(2,1)S(1)} collective-permute-done((bf16[2,4,96,640]{3,2,1,0:T(8,128)(2,1)}, bf16[2,4,96,640]{3,2,1,0:T(8,128)(2,1)S(1)}, u32[]{:S(2)}, u32[]{:S(2)}) %collective-permute-start.1) | collective-permute-done | bytes 983072 | tf_op jit(solution)/shard_map/ppermute | solution.py:188
  37.0 29.5 %collective-permute-done.2.refs_2_ = bf16[2,4,96,640]{3,2,1,0:T(8,128)(2,1)S(1)} collective-permute-done((bf16[2,4,96,640]{3,2,1,0:T(8,128)(2,1)}, bf16[2,4,96,640]{3,2,1,0:T(8,128)(2,1)S(1)}, u32[]{:S(2)}, u32[]{:S(2)}) %collective-permute-start.2) | collective-permute-done | bytes 983072 | tf_op jit(solution)/shard_map/ppermute | solution.py:188
  66.5 19.3 %collective-permute-done.3.refs_3_ = bf16[2,4,96,640]{3,2,1,0:T(8,128)(2,1)S(1)} collective-permute-done((bf16[2,4,96,640]{3,2,1,0:T(8,128)(2,1)}, bf16[2,4,96,640]{3,2,1,0:T(8,128)(2,1)S(1)}, u32[]{:S(2)}, u32[]{:S(2)}) %collective-permute-start.3) | collective-permute-done | bytes 983072 | tf_op jit(solution)/shard_map/ppermute | solution.py:188
  85.9 1.0 copy-done.16
  86.8 4.7 %all-to-all-start = ((bf16[8,3,2,32,1280]{4,3,2,1,0:T(8,128)(2,1)}), bf16[8,3,2,32,1280]{4,3,2,1,0:T(8,128)(2,1)}, u32[]{:S(2)}, u32[]{:S(2)}) async-start(bf16[8,3,2,32,1280]{4,3,2,1,0:T(8,128)(2,1)} %bitcast.171), calls=%async_computation | async-start | bytes 7864320 | tf_op jit(solution)/shard_map/all_to_all | solution.py:209
  91.7 0.1 copy.29
  91.8 0.1 copy.30
  91.8 0.6 pad_add_fusion.live_ref
  92.4 10.6 %shard_map.65 = (bf16[2,640,256]{2,1,0:T(8,128)(2,1)}, f32[2,5,256]{2,1,0:T(8,128)}, bf16[2,640,256]{2,1,0:T(8,128)(2,1)}, f32[2,5,256]{2,1,0:T(8,128)}) custom-call(s32[2,2]{1,0:T(2,128)} %pad_add_fusion.live_ref, bf16[512,1280]{1,0:T(8,128)(2,1)} %bitcast.2.own_ref, bf16[512,1280]{1,0:T(8,128)(2,1)} %collective-permute-done.far_ref, ...), custom_call_target="tpu_custom_call" | custom-call | flops 8053063680 | bytes 6553600 | tf_op jit(solution)/shard_map/pallas_call | solution.py:84
  103.1 0.6 reshape.205.slots_ref
  103.7 5.6 %shard_map.67 = (bf16[2,4,96,640]{3,2,1,0:T(8,128)(2,1)}, bf16[2,4,96,640]{3,2,1,0:T(8,128)(2,1)}, bf16[2,4,96,640]{3,2,1,0:T(8,128)(2,1)}, bf16[2,4,96,640]{3,2,1,0:T(8,128)(2,1)}) custom-call(s32[1]{0:T(128)} %bitcast.4.place_ref, s32[16]{0:T(128)} %reshape.205.slots_ref, bf16[2,8,96,1280]{3,2,1,0:T(8,128)(2,1)} %refs_3_.3, ...), custom_call_target="tpu_custom_call" | custom-call | bytes 7864320 | tf_op jit(solution)/shard_map/pallas_call | solution.py:158
  109.3 2.1 collective-permute-start.5
  111.4 1.5 collective-permute-start.6
  113.0 2.9 collective-permute-start.4
  116.0 64.8 %all-to-all-done.token_ref = bf16[8,3,2,32,1280]{4,3,2,1,0:T(8,128)(2,1)} async-done(((bf16[8,3,2,32,1280]{4,3,2,1,0:T(8,128)(2,1)}), bf16[8,3,2,32,1280]{4,3,2,1,0:T(8,128)(2,1)}, u32[]{:S(2)}, u32[]{:S(2)}) %all-to-all-start) | async-done | bytes 3932192 | tf_op jit(solution)/shard_map/all_to_all | solution.py:209
  180.8 10.2 %shard_map.66 = bf16[8,2,32,1280]{3,2,1,0:T(8,128)(2,1)} custom-call(bf16[8,3,2,32,1280]{4,3,2,1,0:T(8,128)(2,1)} %all-to-all-done.token_ref), custom_call_target="tpu_custom_call" | custom-call | flops 2684354560 | bytes 5242880 | tf_op jit(solution)/shard_map/pallas_call | solution.py:126
  191.0 3.7 %all-to-all-start.1 = ((bf16[8,2,32,1280]{3,2,1,0:T(8,128)(2,1)}), bf16[8,2,32,1280]{3,2,1,0:T(8,128)(2,1)S(1)}, u32[]{:S(2)}, u32[]{:S(2)}) async-start(bf16[8,2,32,1280]{3,2,1,0:T(8,128)(2,1)} %shard_map.66), calls=%async_computation.1 | async-start | bytes 2621440 | tf_op jit(solution)/shard_map/all_to_all | solution.py:238
  194.7 23.7 %collective-permute-done.7.refs_3_ = bf16[2,4,96,640]{3,2,1,0:T(8,128)(2,1)} collective-permute-done((bf16[2,4,96,640]{3,2,1,0:T(8,128)(2,1)}, bf16[2,4,96,640]{3,2,1,0:T(8,128)(2,1)}, u32[]{:S(2)}, u32[]{:S(2)}) %collective-permute-start.7) | collective-permute-done | bytes 983072 | tf_op jit(solution)/shard_map/ppermute | solution.py:188
  218.5 10.6 %shard_map.68 = (bf16[2,640,256]{2,1,0:T(8,128)(2,1)}, f32[2,5,256]{2,1,0:T(8,128)}, bf16[2,640,256]{2,1,0:T(8,128)(2,1)}, f32[2,5,256]{2,1,0:T(8,128)}) custom-call(s32[2,2]{1,0:T(2,128)} %pad_add_fusion.live_ref, bf16[512,1280]{1,0:T(8,128)(2,1)} %bitcast.2.own_ref, bf16[512,1280]{1,0:T(8,128)(2,1)} %collective-permute-done.far_ref, ...), custom_call_target="tpu_custom_call" | custom-call | flops 8053063680 | bytes 6553600 | tf_op jit(solution)/shard_map/pallas_call | solution.py:84
  229.1 0.7 reduce-precision_convert_fusion.1
  229.8 1.1 fusion.41
  231.0 0.8 slice_bitcast_fusion.1
  231.8 0.4 copy-done.8
  232.2 0.8 fusion.65
  233.0 2.6 collective-permute-start.13
  235.6 1.1 fusion.45
  236.7 25.3 %collective-permute-done.8 = bf16[656,256]{1,0:T(8,128)(2,1)S(1)} collective-permute-done((bf16[656,256]{1,0:T(8,128)(2,1)S(1)}, bf16[656,256]{1,0:T(8,128)(2,1)S(1)}, u32[]{:S(2)}, u32[]{:S(2)}) %collective-permute-start.8) | collective-permute-done | bytes 335904 | tf_op jit(solution)/shard_map/ppermute | solution.py:188
  262.1 0.1 fusion.48
  262.2 1.2 pad_maximum_fusion
  263.3 1.7 copy.24
  265.2 0.2 fusion.35
  265.3 4.7 %fusion.8 = bf16[256,2560]{1,0:T(8,128)(2,1)S(1)} fusion(bf16[1280,256]{0,1:T(8,128)(2,1)S(1)} %fusion.35, bf16[1280,5120]{1,0:T(8,128)(2,1)} %param.11), kind=kOutput, calls=%fused_computation.8 | convolution fusion | flops 1678376960 | bytes 8519680 | tf_op jit(solution)/shard_map/dot_general | solution.py:274
  270.2 4.7 %fusion.14 = bf16[256,2560]{1,0:T(8,128)(2,1)S(1)} fusion(bf16[1280,256]{0,1:T(8,128)(2,1)S(1)} %fusion.35, bf16[1280,5120]{1,0:T(8,128)(2,1)} %param.11), kind=kOutput, calls=%fused_computation.10 | convolution fusion | flops 1678376960 | bytes 8519680 | tf_op jit(solution)/shard_map/dot_general | solution.py:274
  274.9 1.0 dynamic-slice_bitcast_fusion.2
  275.9 0.5 collective-permute-start.11
  276.4 1.0 fusion.33
  277.4 0.8 add_divide_fusion.1
  278.2 1.0 slice.142
  279.2 0.1 fusion.44
  279.4 0.4 copy.26
  279.8 0.2 fusion.31
  280.0 4.7 %fusion.11 = bf16[256,2560]{1,0:T(8,128)(2,1)S(1)} fusion(bf16[1280,256]{0,1:T(8,128)(2,1)S(1)} %fusion.31, bf16[1280,5120]{1,0:T(8,128)(2,1)} %param.11), kind=kOutput, calls=%fused_computation.9 | convolution fusion | flops 1678376960 | bytes 8519680 | tf_op jit(solution)/shard_map/dot_general | solution.py:274
  284.9 0.9 copy-done.2
  285.8 1.6 collective-permute-start.10
  287.4 1.2 fusion.32
  288.6 4.7 %fusion.17 = bf16[256,2560]{1,0:T(8,128)(2,1)S(1)} fusion(bf16[1280,256]{0,1:T(8,128)(2,1)S(1)} %fusion.31, bf16[1280,5120]{1,0:T(8,128)(2,1)} %param.11), kind=kOutput, calls=%fused_computation.11 | convolution fusion | flops 1678376960 | bytes 8519680 | tf_op jit(solution)/shard_map/dot_general | solution.py:274
  293.5 2.0 collective-permute-done.10
  295.7 1.6 collective-permute-start.12
  297.2 0.2 fusion.29
  297.4 0.6 collective-permute-start.15
  298.0 8.4 %collective-permute-done.12 = bf16[64,2560]{1,0:T(8,128)(2,1)S(1)} collective-permute-done((bf16[64,2560]{1,0:T(8,128)(2,1)S(1)}, bf16[64,2560]{1,0:T(8,128)(2,1)S(1)}, u32[]{:S(2)}, u32[]{:S(2)}) %collective-permute-start.12) | collective-permute-done | bytes 327712 | tf_op jit(solution)/shard_map/ppermute | solution.py:226
  306.5 0.2 fusion.28
  306.7 1.6 collective-permute-start.17
  308.2 5.2 %collective-permute-done.15 = bf16[64,2560]{1,0:T(8,128)(2,1)S(1)} collective-permute-done((bf16[64,2560]{1,0:T(8,128)(2,1)S(1)}, bf16[64,2560]{1,0:T(8,128)(2,1)S(1)}, u32[]{:S(2)}, u32[]{:S(2)}) %collective-permute-start.15) | collective-permute-done | bytes 327712 | tf_op jit(solution)/shard_map/ppermute | solution.py:226
  313.5 5.1 %collective-permute-done.17 = bf16[64,2560]{1,0:T(8,128)(2,1)S(1)} collective-permute-done((bf16[64,2560]{1,0:T(8,128)(2,1)S(1)}, bf16[64,2560]{1,0:T(8,128)(2,1)S(1)}, u32[]{:S(2)}, u32[]{:S(2)}) %collective-permute-start.17) | collective-permute-done | bytes 327712 | tf_op jit(solution)/shard_map/ppermute | solution.py:226
  318.6 1.2 maximum_bitcast_fusion
  (69 shorter events, 1.6 us)
Async XLA Ops:
  0.0 6.5 %copy-start.12 = (s32[8,2]{0,1:T(2,128)S(1)}, s32[8,2]{0,1:T(2,128)}, u32[]{:S(2)}) copy-start(s32[8,2]{0,1:T(2,128)} %param.8) | copy-start | bytes 196
  2.5 83.4 %collective-permute-start = (bf16[512,1280]{1,0:T(8,128)(2,1)}, bf16[512,1280]{1,0:T(8,128)(2,1)}, u32[]{:S(2)}, u32[]{:S(2)}) collective-permute-start(bf16[512,1280]{1,0:T(8,128)(2,1)} %bitcast.2.own_ref), channel_id=1, source_target_pairs={{0,16},{4,20},{8,24},{12,28},{16,0},{20,4},{24,8},{28,12},{1,17},{... | collective-permute-start | bytes 3932168 | tf_op jit(solution)/shard_map/ppermute | solution.py:188
  7.3 9.4 %copy-start = (bf16[3,64,8,1280]{3,2,1,0:T(8,128)(2,1)S(1)}, bf16[3,64,8,1280]{3,2,1,0:T(8,128)(2,1)}, u32[]{:S(2)}) copy-start(bf16[3,64,8,1280]{3,2,1,0:T(8,128)(2,1)} %param.10) | copy-start | bytes 11796484
  13.2 23.8 %collective-permute-start.1 = (bf16[2,4,96,640]{3,2,1,0:T(8,128)(2,1)}, bf16[2,4,96,640]{3,2,1,0:T(8,128)(2,1)S(1)}, u32[]{:S(2)}, u32[]{:S(2)}) collective-permute-start(bf16[2,4,96,640]{3,2,1,0:T(8,128)(2,1)} %get-tuple-element.33), channel_id=1, source_target_pairs={{0,4},{4,0},{8,12},{12,8},{16,20},{20,16},{24,28},{28,24},{1,5},{5... | collective-permute-start | bytes 2949128 | tf_op jit(solution)/shard_map/ppermute | solution.py:188
  14.7 51.8 %collective-permute-start.2 = (bf16[2,4,96,640]{3,2,1,0:T(8,128)(2,1)}, bf16[2,4,96,640]{3,2,1,0:T(8,128)(2,1)S(1)}, u32[]{:S(2)}, u32[]{:S(2)}) collective-permute-start(bf16[2,4,96,640]{3,2,1,0:T(8,128)(2,1)} %get-tuple-element.34), channel_id=1, source_target_pairs={{0,8},{4,12},{8,0},{12,4},{16,24},{20,28},{24,16},{28,20},{1,9},{5... | collective-permute-start | bytes 2949128 | tf_op jit(solution)/shard_map/ppermute | solution.py:188
  16.3 69.6 %collective-permute-start.3 = (bf16[2,4,96,640]{3,2,1,0:T(8,128)(2,1)}, bf16[2,4,96,640]{3,2,1,0:T(8,128)(2,1)S(1)}, u32[]{:S(2)}, u32[]{:S(2)}) collective-permute-start(bf16[2,4,96,640]{3,2,1,0:T(8,128)(2,1)} %get-tuple-element.35), channel_id=1, source_target_pairs={{0,12},{4,8},{8,4},{12,0},{16,28},{20,24},{24,20},{28,16},{1,13},{... | collective-permute-start | bytes 2949128 | tf_op jit(solution)/shard_map/ppermute | solution.py:188
  37.0 48.9 %copy-start.14 = (bf16[2,4,96,640]{3,2,1,0:T(8,128)(2,1)}, bf16[2,4,96,640]{3,2,1,0:T(8,128)(2,1)S(1)}, u32[]{:S(2)}) copy-start(bf16[2,4,96,640]{3,2,1,0:T(8,128)(2,1)S(1)} %collective-permute-done.1.refs_1_) | copy-start | bytes 2949124
  66.5 19.3 %copy-start.15 = (bf16[2,4,96,640]{3,2,1,0:T(8,128)(2,1)}, bf16[2,4,96,640]{3,2,1,0:T(8,128)(2,1)S(1)}, u32[]{:S(2)}) copy-start(bf16[2,4,96,640]{3,2,1,0:T(8,128)(2,1)S(1)} %collective-permute-done.2.refs_2_) | copy-start | bytes 2949124
  85.8 1.0 copy-start.16
  86.8 4.7 %copy-start.13 = (s32[8,2]{0,1:T(2,128)S(1)}, s32[8,2]{0,1:T(2,128)}, u32[]{:S(2)}) copy-start(s32[8,2]{0,1:T(2,128)} %param.9) | copy-start | bytes 196
  86.8 93.9 %all-to-all-start = ((bf16[8,3,2,32,1280]{4,3,2,1,0:T(8,128)(2,1)}), bf16[8,3,2,32,1280]{4,3,2,1,0:T(8,128)(2,1)}, u32[]{:S(2)}, u32[]{:S(2)}) async-start(bf16[8,3,2,32,1280]{4,3,2,1,0:T(8,128)(2,1)} %bitcast.171), calls=%async_computation | async-start | bytes 7864320 | tf_op jit(solution)/shard_map/all_to_all | solution.py:209
  103.7 9.2 %copy-start.9 = (f32[2,5,256]{2,1,0:T(8,128)S(1)}, f32[2,5,256]{2,1,0:T(8,128)}, u32[]{:S(2)}) copy-start(f32[2,5,256]{2,1,0:T(8,128)} %get-tuple-element.39) | copy-start | bytes 30724
  103.7 9.2 %copy-start.7 = (bf16[2,640,256]{2,1,0:T(8,128)(2,1)S(1)}, bf16[2,640,256]{2,1,0:T(8,128)(2,1)}, u32[]{:S(2)}) copy-start(bf16[2,640,256]{2,1,0:T(8,128)(2,1)} %get-tuple-element.38) | copy-start | bytes 1966084
  109.3 6.6 %copy-start.6 = (bf16[2,640,256]{2,1,0:T(8,128)(2,1)S(1)}, bf16[2,640,256]{2,1,0:T(8,128)(2,1)}, u32[]{:S(2)}) copy-start(bf16[2,640,256]{2,1,0:T(8,128)(2,1)} %get-tuple-element.36) | copy-start | bytes 1966084
  109.3 85.4 %collective-permute-start.5 = (bf16[2,4,96,640]{3,2,1,0:T(8,128)(2,1)}, bf16[2,4,96,640]{3,2,1,0:T(8,128)(2,1)}, u32[]{:S(2)}, u32[]{:S(2)}) collective-permute-start(bf16[2,4,96,640]{3,2,1,0:T(8,128)(2,1)} %get-tuple-element.45), channel_id=1, source_target_pairs={{0,4},{4,0},{8,12},{12,8},{16,20},{20,16},{24,28},{28,24},{1,5},{5... | collective-permute-start | bytes 2949128 | tf_op jit(solution)/shard_map/ppermute | solution.py:188
  111.4 83.3 %collective-permute-start.6 = (bf16[2,4,96,640]{3,2,1,0:T(8,128)(2,1)}, bf16[2,4,96,640]{3,2,1,0:T(8,128)(2,1)}, u32[]{:S(2)}, u32[]{:S(2)}) collective-permute-start(bf16[2,4,96,640]{3,2,1,0:T(8,128)(2,1)} %get-tuple-element.46), channel_id=1, source_target_pairs={{0,8},{4,12},{8,0},{12,4},{16,24},{20,28},{24,16},{28,20},{1,9},{5... | collective-permute-start | bytes 2949128 | tf_op jit(solution)/shard_map/ppermute | solution.py:188
  112.9 105.6 %collective-permute-start.7 = (bf16[2,4,96,640]{3,2,1,0:T(8,128)(2,1)}, bf16[2,4,96,640]{3,2,1,0:T(8,128)(2,1)}, u32[]{:S(2)}, u32[]{:S(2)}) collective-permute-start(bf16[2,4,96,640]{3,2,1,0:T(8,128)(2,1)} %get-tuple-element.47), channel_id=1, source_target_pairs={{0,12},{4,8},{8,4},{12,0},{16,28},{20,24},{24,20},{28,16},{1,13},{... | collective-permute-start | bytes 2949128 | tf_op jit(solution)/shard_map/ppermute | solution.py:188
  113.0 116.1 %collective-permute-start.4 = (bf16[2,656,256]{2,1,0:T(8,128)(2,1)S(1)}, bf16[2,656,256]{2,1,0:T(8,128)(2,1)S(1)}, u32[]{:S(2)}, u32[]{:S(2)}) collective-permute-start(bf16[2,656,256]{2,1,0:T(8,128)(2,1)S(1)} %fusion.38), channel_id=1, source_target_pairs={{0,16},{4,20},{8,24},{12,28},{16,0},{20,4},{24,8},{28,12},{1,17},{... | collective-permute-start | bytes 2015240 | tf_op jit(solution)/shard_map/ppermute | solution.py:188
  191.0 74.1 %all-to-all-start.1 = ((bf16[8,2,32,1280]{3,2,1,0:T(8,128)(2,1)}), bf16[8,2,32,1280]{3,2,1,0:T(8,128)(2,1)S(1)}, u32[]{:S(2)}, u32[]{:S(2)}) async-start(bf16[8,2,32,1280]{3,2,1,0:T(8,128)(2,1)} %shard_map.66), calls=%async_computation.1 | async-start | bytes 2621440 | tf_op jit(solution)/shard_map/all_to_all | solution.py:238
  230.9 1.2 copy-start.8
  231.7 1.2 copy-start.10
  231.7 30.3 %collective-permute-start.8 = (bf16[656,256]{1,0:T(8,128)(2,1)S(1)}, bf16[656,256]{1,0:T(8,128)(2,1)S(1)}, u32[]{:S(2)}, u32[]{:S(2)}) collective-permute-start(bf16[656,256]{1,0:T(8,128)(2,1)S(1)} %get-tuple-element.67), channel_id=1, source_target_pairs={{0,16},{4,20},{8,24},{12,28},{16,0},{20,4},{24,8},{28,12},{1,17},{... | collective-permute-start | bytes 1007624 | tf_op jit(solution)/shard_map/ppermute | solution.py:188
  233.0 44.4 %collective-permute-start.13 = (bf16[656,256]{1,0:T(8,128)(2,1)}, bf16[656,256]{1,0:T(8,128)(2,1)}, u32[]{:S(2)}, u32[]{:S(2)}) collective-permute-start(bf16[656,256]{1,0:T(8,128)(2,1)} %get-tuple-element.68), channel_id=1, source_target_pairs={{0,16},{4,20},{8,24},{12,28},{16,0},{20,4},{24,8},{28,12},{1,17},{... | collective-permute-start | bytes 1007624 | tf_op jit(solution)/shard_map/ppermute | solution.py:188
  235.6 26.4 %copy-start.11 = (f32[2,5,256]{2,1,0:T(8,128)S(1)}, f32[2,5,256]{2,1,0:T(8,128)}, u32[]{:S(2)}) copy-start(f32[2,5,256]{2,1,0:T(8,128)} %get-tuple-element.48) | copy-start | bytes 30724
  270.1 6.3 %collective-permute-start.9 = (bf16[2,64,2560]{2,1,0:T(8,128)(2,1)S(1)}, bf16[2,64,2560]{2,1,0:T(8,128)(2,1)S(1)}, u32[]{:S(2)}, u32[]{:S(2)}) collective-permute-start(bf16[2,64,2560]{2,1,0:T(8,128)(2,1)S(1)} %dynamic-slice_bitcast_fusion.3), channel_id=1, source_target_pairs={{0,1},{1,0},{2,3},{3,2},{4,5},{5,4},{6,7},{7,6},{8,9},{9,8},{10,11... | collective-permute-start | bytes 1966088 | tf_op jit(solution)/shard_map/ppermute | solution.py:219
  274.9 2.5 copy-start.3
  275.9 3.3 %copy-start.5 = (bf16[1,640,256]{2,1,0:T(8,128)(2,1)S(1)}, bf16[1,640,256]{2,1,0:T(8,128)(2,1)}, u32[]{:S(2)}) copy-start(bf16[1,640,256]{2,1,0:T(8,128)(2,1)} %get-tuple-element.71) | copy-start | bytes 983044
  275.9 11.5 %collective-permute-start.11 = (bf16[2,64,2560]{2,1,0:T(8,128)(2,1)}, bf16[2,64,2560]{2,1,0:T(8,128)(2,1)}, u32[]{:S(2)}, u32[]{:S(2)}) collective-permute-start(bf16[2,64,2560]{2,1,0:T(8,128)(2,1)} %dynamic-slice_bitcast_fusion.2), channel_id=1, source_target_pairs={{0,1},{1,0},{2,3},{3,2},{4,5},{5,4},{6,7},{7,6},{8,9},{9,8},{10,11... | collective-permute-start | bytes 1966088 | tf_op jit(solution)/shard_map/ppermute | solution.py:219
  277.4 1.9 copy-start.1
  284.7 1.1 copy-start.2
  284.7 2.7 copy-start.4
  284.8 12.4 %collective-permute-start.14 = (bf16[2,64,2560]{2,1,0:T(8,128)(2,1)S(1)}, bf16[2,64,2560]{2,1,0:T(8,128)(2,1)S(1)}, u32[]{:S(2)}, u32[]{:S(2)}) collective-permute-start(bf16[2,64,2560]{2,1,0:T(8,128)(2,1)S(1)} %dynamic-slice_bitcast_fusion.1), channel_id=1, source_target_pairs={{0,1},{1,0},{2,3},{3,2},{4,5},{5,4},{6,7},{7,6},{8,9},{9,8},{10,11... | collective-permute-start | bytes 1966088 | tf_op jit(solution)/shard_map/ppermute | solution.py:219
  285.8 9.7 %collective-permute-start.10 = (bf16[64,2560]{1,0:T(8,128)(2,1)S(1)}, bf16[64,2560]{1,0:T(8,128)(2,1)S(1)}, u32[]{:S(2)}, u32[]{:S(2)}) collective-permute-start(bf16[64,2560]{1,0:T(8,128)(2,1)S(1)} %dynamic-slice_bitcast_fusion.7), channel_id=1, source_target_pairs={{0,2},{1,3},{2,0},{3,1},{4,6},{5,7},{6,4},{7,5},{8,10},{9,11},{10,... | collective-permute-start | bytes 983048 | tf_op jit(solution)/shard_map/ppermute | solution.py:226
  293.4 13.0 %collective-permute-start.16 = (bf16[2,64,2560]{2,1,0:T(8,128)(2,1)S(1)}, bf16[2,64,2560]{2,1,0:T(8,128)(2,1)S(1)}, u32[]{:S(2)}, u32[]{:S(2)}) collective-permute-start(bf16[2,64,2560]{2,1,0:T(8,128)(2,1)S(1)} %dynamic-slice_bitcast_fusion), channel_id=1, source_target_pairs={{0,1},{1,0},{2,3},{3,2},{4,5},{5,4},{6,7},{7,6},{8,9},{9,8},{10,11... | collective-permute-start | bytes 1966088 | tf_op jit(solution)/shard_map/ppermute | solution.py:219
  295.7 10.7 %collective-permute-start.12 = (bf16[64,2560]{1,0:T(8,128)(2,1)S(1)}, bf16[64,2560]{1,0:T(8,128)(2,1)S(1)}, u32[]{:S(2)}, u32[]{:S(2)}) collective-permute-start(bf16[64,2560]{1,0:T(8,128)(2,1)S(1)} %dynamic-slice_bitcast_fusion.6), channel_id=1, source_target_pairs={{0,2},{1,3},{2,0},{3,1},{4,6},{5,7},{6,4},{7,5},{8,10},{9,11},{10,... | collective-permute-start | bytes 983048 | tf_op jit(solution)/shard_map/ppermute | solution.py:226
  297.4 16.0 %collective-permute-start.15 = (bf16[64,2560]{1,0:T(8,128)(2,1)S(1)}, bf16[64,2560]{1,0:T(8,128)(2,1)S(1)}, u32[]{:S(2)}, u32[]{:S(2)}) collective-permute-start(bf16[64,2560]{1,0:T(8,128)(2,1)S(1)} %dynamic-slice_bitcast_fusion.5), channel_id=1, source_target_pairs={{0,2},{1,3},{2,0},{3,1},{4,6},{5,7},{6,4},{7,5},{8,10},{9,11},{10,... | collective-permute-start | bytes 983048 | tf_op jit(solution)/shard_map/ppermute | solution.py:226
  306.7 11.9 %collective-permute-start.17 = (bf16[64,2560]{1,0:T(8,128)(2,1)S(1)}, bf16[64,2560]{1,0:T(8,128)(2,1)S(1)}, u32[]{:S(2)}, u32[]{:S(2)}) collective-permute-start(bf16[64,2560]{1,0:T(8,128)(2,1)S(1)} %dynamic-slice_bitcast_fusion.4), channel_id=1, source_target_pairs={{0,2},{1,3},{2,0},{3,1},{4,6},{5,7},{6,4},{7,5},{8,10},{9,11},{10,... | collective-permute-start | bytes 983048 | tf_op jit(solution)/shard_map/ppermute | solution.py:226

commit v12 on v10

--- a/solution.py
+++ b/solution.py
@@ -196,17 +196,18 @@
 
     groups = HEAD_GROUPS if heads_here % HEAD_GROUPS == 0 else 1
 
-    def banks_of(group, *before):
-        blocks = listed_banks(
-            place, after(char_slots, *before), char_bank, half, group, width // groups
-        )
-        blocks = [blocks[0]] + [swap(blocks[step], step) for step in range(1, half)]
+    def listed_of(group):
+        return listed_banks(place, char_slots, char_bank, half, group, width // groups)
+
+    def banks_of(blocks, *before):
+        blocks = [blocks[0]] + [swap(after(blocks[step], *before), step) for step in range(1, half)]
         return blocks if char_bank.shape[2] % TILE_ROWS == 0 else [jnp.concatenate(blocks, axis=2)]
 
-    banks = [banks_of(0)]
+    listed = [listed_of(group) for group in range(groups)]
+    banks = [banks_of(listed[0])]
     tokens = frame_tokens.reshape(3, head_groups, parts, across, spots, frames_here, width)
     tokens = tokens.transpose(1, 3, 0, 2, 4, 5, 6).reshape(shards, 3, parts, tile, width)
-    tokens = lax.all_to_all(after(tokens, far, *banks[0]), "frames", 0, 0, tiled=True)
+    tokens = lax.all_to_all(after(tokens, far, *banks[0], *[blocks[0] for blocks in listed[1:]]), "frames", 0, 0, tiled=True)
     live = jnp.stack([slot_live[place], slot_live[place ^ half]])
 
     place_heads = lax.axis_index("heads")
@@ -232,7 +233,7 @@
     for group in range(groups):
         near_out, near_level, far_out, far_level = attend_bank(group, parts, rows, live, own, far, banks[group])
         if group < groups - 1:
-            banks.append(banks_of(group + 1, far_level))
+            banks.append(banks_of(listed[group + 1], far_level))
         if group == 0:
             frame_parts = attend_frames(frames_here, after(tokens, far_level))
             back = lax.all_to_all(frame_parts, "frames", 0, 0, tiled=True)

time: 319 us -> 320 us (level)
    ppermute x10, waiting for transfers between devices: 116 us -> 109 us  [swap(): return lax.ppermute(block, 'frames', [(a, a ^ step) for a in range(shards)])]
    all_to_all x1, waiting for transfers between devices: 64.8 us -> 69.3 us  [local(): lax.all_to_all(after(tokens, far, *banks[0], *[blocks[0] for blocks in li...]
  transfers between devices with their start and end apart: 20 -> 20, of which waited for: 9 -> 9; matrix products, arithmetic and copies ran while one was open for 12% -> 12% of each run, Pallas kernels for 14% -> 13%
where the time goes in v12:
time: 320 us; the launch traced here: 318 us
  waiting for transfers between devices  197 us (62%)
  Pallas kernels  42.7 us (13%)
  starting transfers between devices  33.4 us (10%)
  matrix products  18.8 us (6%)
  local copies, waits for them, and re-layouts  13.4 us (4%)
  other arithmetic  12 us (4%)
    ppermute x10, waiting for transfers between devices, swap(): return lax.ppermute(block, 'frames', [(a, a ^ step) for a in range(shards)])  109 us
    all_to_all x1, waiting for transfers between devices, local(): lax.all_to_all(after(tokens, far, *banks[0], *[blocks[0] for blocks in li...  69.3 us
    pallas_call x2, Pallas kernels, attend_bank(): pl.pallas_call(functools.partial(bank_kernel, len(banks)), grid=(heads,),...  21.2 us
    dot_general x4, matrix products, local(): lax.dot_general(after(combined, *summed[-2:-1]), out_weight[:, low:low +...  18.8 us
    ppermute x4, waiting for transfers between devices, scatter_chips(): lax.ppermute(give, 'heads', [(h, (h + 2 * step) % head_groups) for h in r...  18.6 us
    ppermute x10, starting transfers between devices, swap(): return lax.ppermute(block, 'frames', [(a, a ^ step) for a in range(shards)])  16.7 us
    pallas_call x2, Pallas kernels, listed_banks(): pl.pallas_call(listed_kernel, grid_spec=pltpu.PrefetchScalarGridSpec(num_...  11.4 us
    pallas_call x1, Pallas kernels, attend_frames(): pl.pallas_call(functools.partial(frame_kernel, frames_here), grid=(width...  10.2 us
  transfers between devices with their start and end apart: 20, of which 9 were waited for; matrix products, arithmetic and copies ran while one was open for 12% of the time, Pallas kernels for 13%

profile of v12, /device:TPU:0, one launch (start us, length us, event | category | flops | bytes accessed | tf_op | source)
XLA Modules:
  0.0 317.9 jit_solution(413931148642064865)
XLA Ops:
  0.0 2.5 copy.19
  2.5 4.0 %collective-permute-start = (bf16[512,1280]{1,0:T(8,128)(2,1)}, bf16[512,1280]{1,0:T(8,128)(2,1)}, u32[]{:S(2)}, u32[]{:S(2)}) collective-permute-start(bf16[512,1280]{1,0:T(8,128)(2,1)} %bitcast.2.own_ref), channel_id=1, source_target_pairs={{0,16},{4,20},{8,24},{12,28},{16,0},{20,4},{24,8},{28,12},{1,17},{... | collective-permute-start | bytes 3932168 | tf_op jit(solution)/shard_map/ppermute | solution.py:188
  6.6 0.6 reshape.200.slots_ref
  7.2 5.4 %shard_map.64 = (bf16[2,4,96,640]{3,2,1,0:T(8,128)(2,1)}, bf16[2,4,96,640]{3,2,1,0:T(8,128)(2,1)}, bf16[2,4,96,640]{3,2,1,0:T(8,128)(2,1)}, bf16[2,4,96,640]{3,2,1,0:T(8,128)(2,1)}) custom-call(s32[1]{0:T(128)} %bitcast.4.place_ref, s32[16]{0:T(128)} %reshape.200.slots_ref, bf16[2,8,96,1280]{3,2,1,0:T(8,128)(2,1)} %refs_3_.3, ...), custom_call_target="tpu_custom_call" | custom-call | bytes 7864320 | tf_op jit(solution)/shard_map/pallas_call | solution.py:158
  12.6 1.5 collective-permute-start.1
  14.2 1.6 collective-permute-start.2
  15.7 0.4 collective-permute-start.3
  16.1 5.9 %shard_map.66 = (bf16[2,4,96,640]{3,2,1,0:T(8,128)(2,1)}, bf16[2,4,96,640]{3,2,1,0:T(8,128)(2,1)}, bf16[2,4,96,640]{3,2,1,0:T(8,128)(2,1)}, bf16[2,4,96,640]{3,2,1,0:T(8,128)(2,1)}) custom-call(s32[1]{0:T(128)} %bitcast.4.place_ref, s32[16]{0:T(128)} %reshape.200.slots_ref, bf16[2,8,96,1280]{3,2,1,0:T(8,128)(2,1)} %refs_3_.3, ...), custom_call_target="tpu_custom_call" | custom-call | bytes 7864320 | tf_op jit(solution)/shard_map/pallas_call | solution.py:158
  22.1 2.2 copy.21
  24.3 12.4 %collective-permute-done.1.refs_1_ = bf16[2,4,96,640]{3,2,1,0:T(8,128)(2,1)} collective-permute-done((bf16[2,4,96,640]{3,2,1,0:T(8,128)(2,1)}, bf16[2,4,96,640]{3,2,1,0:T(8,128)(2,1)}, u32[]{:S(2)}, u32[]{:S(2)}) %collective-permute-start.1) | collective-permute-done | bytes 983072 | tf_op jit(solution)/shard_map/ppermute | solution.py:188
  36.7 29.4 %collective-permute-done.2.refs_2_ = bf16[2,4,96,640]{3,2,1,0:T(8,128)(2,1)} collective-permute-done((bf16[2,4,96,640]{3,2,1,0:T(8,128)(2,1)}, bf16[2,4,96,640]{3,2,1,0:T(8,128)(2,1)}, u32[]{:S(2)}, u32[]{:S(2)}) %collective-permute-start.2) | collective-permute-done | bytes 983072 | tf_op jit(solution)/shard_map/ppermute | solution.py:188
  66.1 19.3 %collective-permute-done.3.refs_3_ = bf16[2,4,96,640]{3,2,1,0:T(8,128)(2,1)} collective-permute-done((bf16[2,4,96,640]{3,2,1,0:T(8,128)(2,1)}, bf16[2,4,96,640]{3,2,1,0:T(8,128)(2,1)}, u32[]{:S(2)}, u32[]{:S(2)}) %collective-permute-start.3) | collective-permute-done | bytes 983072 | tf_op jit(solution)/shard_map/ppermute | solution.py:188
  85.4 4.7 %all-to-all-start = ((bf16[8,3,2,32,1280]{4,3,2,1,0:T(8,128)(2,1)}), bf16[8,3,2,32,1280]{4,3,2,1,0:T(8,128)(2,1)}, u32[]{:S(2)}, u32[]{:S(2)}) async-start(bf16[8,3,2,32,1280]{4,3,2,1,0:T(8,128)(2,1)} %bitcast.171), calls=%async_computation | async-start | bytes 7864320 | tf_op jit(solution)/shard_map/all_to_all | solution.py:210
  90.2 0.1 copy.27
  90.4 0.6 pad_add_fusion.live_ref
  91.0 10.6 %shard_map.65 = (bf16[2,640,256]{2,1,0:T(8,128)(2,1)}, f32[2,5,256]{2,1,0:T(8,128)}, bf16[2,640,256]{2,1,0:T(8,128)(2,1)}, f32[2,5,256]{2,1,0:T(8,128)}) custom-call(s32[2,2]{1,0:T(2,128)} %pad_add_fusion.live_ref, bf16[512,1280]{1,0:T(8,128)(2,1)} %bitcast.2.own_ref, bf16[512,1280]{1,0:T(8,128)(2,1)} %collective-permute-done.far_ref, ...), custom_call_target="tpu_custom_call" | custom-call | flops 8053063680 | bytes 6553600 | tf_op jit(solution)/shard_map/pallas_call | solution.py:84
  101.5 2.9 collective-permute-start.7
  104.5 0.6 collective-permute-start.6
  105.1 0.7 reduce-precision_convert_fusion.3
  105.9 1.1 fusion.38
  107.0 2.9 collective-permute-start.4
  110.0 69.3 %all-to-all-done.token_ref = bf16[8,3,2,32,1280]{4,3,2,1,0:T(8,128)(2,1)} async-done(((bf16[8,3,2,32,1280]{4,3,2,1,0:T(8,128)(2,1)}), bf16[8,3,2,32,1280]{4,3,2,1,0:T(8,128)(2,1)}, u32[]{:S(2)}, u32[]{:S(2)}) %all-to-all-start) | async-done | bytes 3932192 | tf_op jit(solution)/shard_map/all_to_all | solution.py:210
  179.3 10.2 %shard_map.67 = bf16[8,2,32,1280]{3,2,1,0:T(8,128)(2,1)} custom-call(bf16[8,3,2,32,1280]{4,3,2,1,0:T(8,128)(2,1)} %all-to-all-done.token_ref), custom_call_target="tpu_custom_call" | custom-call | flops 2684354560 | bytes 5242880 | tf_op jit(solution)/shard_map/pallas_call | solution.py:126
  189.4 6.9 %all-to-all-start.1 = ((bf16[8,2,32,1280]{3,2,1,0:T(8,128)(2,1)}), bf16[8,2,32,1280]{3,2,1,0:T(8,128)(2,1)S(1)}, u32[]{:S(2)}, u32[]{:S(2)}) async-start(bf16[8,2,32,1280]{3,2,1,0:T(8,128)(2,1)} %shard_map.67), calls=%async_computation.1 | async-start | bytes 2621440 | tf_op jit(solution)/shard_map/all_to_all | solution.py:239
  196.4 17.4 %collective-permute-done.6.refs_2_ = bf16[2,4,96,640]{3,2,1,0:T(8,128)(2,1)} collective-permute-done((bf16[2,4,96,640]{3,2,1,0:T(8,128)(2,1)}, bf16[2,4,96,640]{3,2,1,0:T(8,128)(2,1)}, u32[]{:S(2)}, u32[]{:S(2)}) %collective-permute-start.6) | collective-permute-done | bytes 983072 | tf_op jit(solution)/shard_map/ppermute | solution.py:188
  213.8 10.6 %shard_map.68 = (bf16[2,640,256]{2,1,0:T(8,128)(2,1)}, f32[2,5,256]{2,1,0:T(8,128)}, bf16[2,640,256]{2,1,0:T(8,128)(2,1)}, f32[2,5,256]{2,1,0:T(8,128)}) custom-call(s32[2,2]{1,0:T(2,128)} %pad_add_fusion.live_ref, bf16[512,1280]{1,0:T(8,128)(2,1)} %bitcast.2.own_ref, bf16[512,1280]{1,0:T(8,128)(2,1)} %collective-permute-done.far_ref, ...), custom_call_target="tpu_custom_call" | custom-call | flops 8053063680 | bytes 6553600 | tf_op jit(solution)/shard_map/pallas_call | solution.py:84
  224.4 0.7 reduce-precision_convert_fusion.1
  225.1 1.1 fusion.41
  226.3 0.8 slice_bitcast_fusion.1
  227.1 0.4 copy-done.7
  227.5 0.7 fusion.65
  228.2 2.6 collective-permute-start.13
  230.9 1.1 fusion.45
  231.9 30.6 %collective-permute-done.8 = bf16[656,256]{1,0:T(8,128)(2,1)S(1)} collective-permute-done((bf16[656,256]{1,0:T(8,128)(2,1)S(1)}, bf16[656,256]{1,0:T(8,128)(2,1)S(1)}, u32[]{:S(2)}, u32[]{:S(2)}) %collective-permute-start.8) | collective-permute-done | bytes 335904 | tf_op jit(solution)/shard_map/ppermute | solution.py:188
  262.6 0.1 fusion.48
  262.7 1.2 pad_maximum_fusion
  263.9 1.7 copy.22
  265.7 0.2 fusion.35
  265.8 4.7 %fusion.8 = bf16[256,2560]{1,0:T(8,128)(2,1)S(1)} fusion(bf16[1280,256]{0,1:T(8,128)(2,1)S(1)} %fusion.35, bf16[1280,5120]{1,0:T(8,128)(2,1)} %param.11), kind=kOutput, calls=%fused_computation.8 | convolution fusion | flops 1678376960 | bytes 8519680 | tf_op jit(solution)/shard_map/dot_general | solution.py:275
  270.7 4.7 %fusion.14 = bf16[256,2560]{1,0:T(8,128)(2,1)S(1)} fusion(bf16[1280,256]{0,1:T(8,128)(2,1)S(1)} %fusion.35, bf16[1280,5120]{1,0:T(8,128)(2,1)} %param.11), kind=kOutput, calls=%fused_computation.10 | convolution fusion | flops 1678376960 | bytes 8519680 | tf_op jit(solution)/shard_map/dot_general | solution.py:275
  275.4 1.0 dynamic-slice_bitcast_fusion.2
  276.4 0.5 collective-permute-start.11
  276.9 1.0 fusion.33
  277.9 0.8 add_divide_fusion.1
  278.7 1.0 slice.142
  279.7 0.1 fusion.44
  279.9 0.4 copy.24
  280.4 0.2 fusion.31
  280.5 0.9 copy-done.2
  281.5 0.4 copy-done.4
  281.9 1.2 fusion.32
  283.1 1.6 collective-permute-start.10
  284.7 4.7 %fusion.11 = bf16[256,2560]{1,0:T(8,128)(2,1)S(1)} fusion(bf16[1280,256]{0,1:T(8,128)(2,1)S(1)} %fusion.31, bf16[1280,5120]{1,0:T(8,128)(2,1)} %param.11), kind=kOutput, calls=%fused_computation.9 | convolution fusion | flops 1678376960 | bytes 8519680 | tf_op jit(solution)/shard_map/dot_general | solution.py:275
  289.6 0.6 collective-permute-start.12
  290.2 4.7 %fusion.17 = bf16[256,2560]{1,0:T(8,128)(2,1)S(1)} fusion(bf16[1280,256]{0,1:T(8,128)(2,1)S(1)} %fusion.31, bf16[1280,5120]{1,0:T(8,128)(2,1)} %param.11), kind=kOutput, calls=%fused_computation.11 | convolution fusion | flops 1678376960 | bytes 8519680 | tf_op jit(solution)/shard_map/dot_general | solution.py:275
  294.9 0.2 collective-permute-start.16
  295.3 4.6 %collective-permute-done.12 = bf16[64,2560]{1,0:T(8,128)(2,1)S(1)} collective-permute-done((bf16[64,2560]{1,0:T(8,128)(2,1)S(1)}, bf16[64,2560]{1,0:T(8,128)(2,1)S(1)}, u32[]{:S(2)}, u32[]{:S(2)}) %collective-permute-start.12) | collective-permute-done | bytes 327712 | tf_op jit(solution)/shard_map/ppermute | solution.py:227
  300.0 0.2 fusion.29
  300.2 1.6 collective-permute-start.15
  301.7 0.2 fusion.28
  301.9 0.6 collective-permute-start.17
  302.5 8.3 %collective-permute-done.15 = bf16[64,2560]{1,0:T(8,128)(2,1)S(1)} collective-permute-done((bf16[64,2560]{1,0:T(8,128)(2,1)S(1)}, bf16[64,2560]{1,0:T(8,128)(2,1)S(1)}, u32[]{:S(2)}, u32[]{:S(2)}) %collective-permute-start.15) | collective-permute-done | bytes 327712 | tf_op jit(solution)/shard_map/ppermute | solution.py:227
  310.9 5.7 %collective-permute-done.17 = bf16[64,2560]{1,0:T(8,128)(2,1)S(1)} collective-permute-done((bf16[64,2560]{1,0:T(8,128)(2,1)S(1)}, bf16[64,2560]{1,0:T(8,128)(2,1)S(1)}, u32[]{:S(2)}, u32[]{:S(2)}) %collective-permute-start.17) | collective-permute-done | bytes 327712 | tf_op jit(solution)/shard_map/ppermute | solution.py:227
  316.7 1.2 maximum_bitcast_fusion
  (57 shorter events, 1.5 us)
Async XLA Ops:
  0.0 6.5 %copy-start.11 = (s32[8,2]{0,1:T(2,128)S(1)}, s32[8,2]{0,1:T(2,128)}, u32[]{:S(2)}) copy-start(s32[8,2]{0,1:T(2,128)} %param.8) | copy-start | bytes 196
  2.5 82.9 %collective-permute-start = (bf16[512,1280]{1,0:T(8,128)(2,1)}, bf16[512,1280]{1,0:T(8,128)(2,1)}, u32[]{:S(2)}, u32[]{:S(2)}) collective-permute-start(bf16[512,1280]{1,0:T(8,128)(2,1)} %bitcast.2.own_ref), channel_id=1, source_target_pairs={{0,16},{4,20},{8,24},{12,28},{16,0},{20,4},{24,8},{28,12},{1,17},{... | collective-permute-start | bytes 3932168 | tf_op jit(solution)/shard_map/ppermute | solution.py:188
  12.6 24.1 %collective-permute-start.1 = (bf16[2,4,96,640]{3,2,1,0:T(8,128)(2,1)}, bf16[2,4,96,640]{3,2,1,0:T(8,128)(2,1)}, u32[]{:S(2)}, u32[]{:S(2)}) collective-permute-start(bf16[2,4,96,640]{3,2,1,0:T(8,128)(2,1)} %get-tuple-element.34), channel_id=1, source_target_pairs={{0,4},{4,0},{8,12},{12,8},{16,20},{20,16},{24,28},{28,24},{1,5},{5... | collective-permute-start | bytes 2949128 | tf_op jit(solution)/shard_map/ppermute | solution.py:188
  14.2 51.9 %collective-permute-start.2 = (bf16[2,4,96,640]{3,2,1,0:T(8,128)(2,1)}, bf16[2,4,96,640]{3,2,1,0:T(8,128)(2,1)}, u32[]{:S(2)}, u32[]{:S(2)}) collective-permute-start(bf16[2,4,96,640]{3,2,1,0:T(8,128)(2,1)} %get-tuple-element.35), channel_id=1, source_target_pairs={{0,8},{4,12},{8,0},{12,4},{16,24},{20,28},{24,16},{28,20},{1,9},{5... | collective-permute-start | bytes 2949128 | tf_op jit(solution)/shard_map/ppermute | solution.py:188
  15.7 69.7 %collective-permute-start.3 = (bf16[2,4,96,640]{3,2,1,0:T(8,128)(2,1)}, bf16[2,4,96,640]{3,2,1,0:T(8,128)(2,1)}, u32[]{:S(2)}, u32[]{:S(2)}) collective-permute-start(bf16[2,4,96,640]{3,2,1,0:T(8,128)(2,1)} %get-tuple-element.36), channel_id=1, source_target_pairs={{0,12},{4,8},{8,4},{12,0},{16,28},{20,24},{24,20},{28,16},{1,13},{... | collective-permute-start | bytes 2949128 | tf_op jit(solution)/shard_map/ppermute | solution.py:188
  16.1 5.9 %copy-start = (bf16[3,64,8,1280]{3,2,1,0:T(8,128)(2,1)S(1)}, bf16[3,64,8,1280]{3,2,1,0:T(8,128)(2,1)}, u32[]{:S(2)}) copy-start(bf16[3,64,8,1280]{3,2,1,0:T(8,128)(2,1)} %param.10) | copy-start | bytes 11796484
  85.4 4.7 %copy-start.10 = (s32[8,2]{0,1:T(2,128)S(1)}, s32[8,2]{0,1:T(2,128)}, u32[]{:S(2)}) copy-start(s32[8,2]{0,1:T(2,128)} %param.9) | copy-start | bytes 196
  85.4 93.9 %all-to-all-start = ((bf16[8,3,2,32,1280]{4,3,2,1,0:T(8,128)(2,1)}), bf16[8,3,2,32,1280]{4,3,2,1,0:T(8,128)(2,1)}, u32[]{:S(2)}, u32[]{:S(2)}) async-start(bf16[8,3,2,32,1280]{4,3,2,1,0:T(8,128)(2,1)} %bitcast.171), calls=%async_computation | async-start | bytes 7864320 | tf_op jit(solution)/shard_map/all_to_all | solution.py:210
  101.5 8.4 %copy-start.6 = (bf16[2,640,256]{2,1,0:T(8,128)(2,1)S(1)}, bf16[2,640,256]{2,1,0:T(8,128)(2,1)}, u32[]{:S(2)}) copy-start(bf16[2,640,256]{2,1,0:T(8,128)(2,1)} %get-tuple-element.37) | copy-start | bytes 1966084
  101.5 94.8 %collective-permute-start.7 = (bf16[2,4,96,640]{3,2,1,0:T(8,128)(2,1)}, bf16[2,4,96,640]{3,2,1,0:T(8,128)(2,1)}, u32[]{:S(2)}, u32[]{:S(2)}) collective-permute-start(bf16[2,4,96,640]{3,2,1,0:T(8,128)(2,1)} %get-tuple-element.50), channel_id=1, source_target_pairs={{0,12},{4,8},{8,4},{12,0},{16,28},{20,24},{24,20},{28,16},{1,13},{... | collective-permute-start | bytes 2949128 | tf_op jit(solution)/shard_map/ppermute | solution.py:188
  104.5 109.3 %collective-permute-start.6 = (bf16[2,4,96,640]{3,2,1,0:T(8,128)(2,1)}, bf16[2,4,96,640]{3,2,1,0:T(8,128)(2,1)}, u32[]{:S(2)}, u32[]{:S(2)}) collective-permute-start(bf16[2,4,96,640]{3,2,1,0:T(8,128)(2,1)} %get-tuple-element.48), channel_id=1, source_target_pairs={{0,8},{4,12},{8,0},{12,4},{16,24},{20,28},{24,16},{28,20},{1,9},{5... | collective-permute-start | bytes 2949128 | tf_op jit(solution)/shard_map/ppermute | solution.py:188
  105.0 108.7 %collective-permute-start.5 = (bf16[2,4,96,640]{3,2,1,0:T(8,128)(2,1)}, bf16[2,4,96,640]{3,2,1,0:T(8,128)(2,1)}, u32[]{:S(2)}, u32[]{:S(2)}) collective-permute-start(bf16[2,4,96,640]{3,2,1,0:T(8,128)(2,1)} %get-tuple-element.46), channel_id=1, source_target_pairs={{0,4},{4,0},{8,12},{12,8},{16,20},{20,16},{24,28},{28,24},{1,5},{5... | collective-permute-start | bytes 2949128 | tf_op jit(solution)/shard_map/ppermute | solution.py:188
  107.0 117.4 %collective-permute-start.4 = (bf16[2,656,256]{2,1,0:T(8,128)(2,1)S(1)}, bf16[2,656,256]{2,1,0:T(8,128)(2,1)S(1)}, u32[]{:S(2)}, u32[]{:S(2)}) collective-permute-start(bf16[2,656,256]{2,1,0:T(8,128)(2,1)S(1)} %fusion.38), channel_id=1, source_target_pairs={{0,16},{4,20},{8,24},{12,28},{16,0},{20,4},{24,8},{28,12},{1,17},{... | collective-permute-start | bytes 2015240 | tf_op jit(solution)/shard_map/ppermute | solution.py:188
  189.4 76.1 %all-to-all-start.1 = ((bf16[8,2,32,1280]{3,2,1,0:T(8,128)(2,1)}), bf16[8,2,32,1280]{3,2,1,0:T(8,128)(2,1)S(1)}, u32[]{:S(2)}, u32[]{:S(2)}) async-start(bf16[8,2,32,1280]{3,2,1,0:T(8,128)(2,1)} %shard_map.67), calls=%async_computation.1 | async-start | bytes 2621440 | tf_op jit(solution)/shard_map/all_to_all | solution.py:239
  226.2 1.2 copy-start.7
  227.0 1.2 copy-start.8
  227.0 35.5 %collective-permute-start.8 = (bf16[656,256]{1,0:T(8,128)(2,1)S(1)}, bf16[656,256]{1,0:T(8,128)(2,1)S(1)}, u32[]{:S(2)}, u32[]{:S(2)}) collective-permute-start(bf16[656,256]{1,0:T(8,128)(2,1)S(1)} %get-tuple-element.69), channel_id=1, source_target_pairs={{0,16},{4,20},{8,24},{12,28},{16,0},{20,4},{24,8},{28,12},{1,17},{... | collective-permute-start | bytes 1007624 | tf_op jit(solution)/shard_map/ppermute | solution.py:188
  228.2 49.7 %collective-permute-start.13 = (bf16[656,256]{1,0:T(8,128)(2,1)}, bf16[656,256]{1,0:T(8,128)(2,1)}, u32[]{:S(2)}, u32[]{:S(2)}) collective-permute-start(bf16[656,256]{1,0:T(8,128)(2,1)} %get-tuple-element.70), channel_id=1, source_target_pairs={{0,16},{4,20},{8,24},{12,28},{16,0},{20,4},{24,8},{28,12},{1,17},{... | collective-permute-start | bytes 1007624 | tf_op jit(solution)/shard_map/ppermute | solution.py:188
  230.9 31.7 %copy-start.9 = (f32[2,5,256]{2,1,0:T(8,128)S(1)}, f32[2,5,256]{2,1,0:T(8,128)}, u32[]{:S(2)}) copy-start(f32[2,5,256]{2,1,0:T(8,128)} %get-tuple-element.51) | copy-start | bytes 30724
  270.6 6.3 %collective-permute-start.9 = (bf16[2,64,2560]{2,1,0:T(8,128)(2,1)S(1)}, bf16[2,64,2560]{2,1,0:T(8,128)(2,1)S(1)}, u32[]{:S(2)}, u32[]{:S(2)}) collective-permute-start(bf16[2,64,2560]{2,1,0:T(8,128)(2,1)S(1)} %dynamic-slice_bitcast_fusion.3), channel_id=1, source_target_pairs={{0,1},{1,0},{2,3},{3,2},{4,5},{5,4},{6,7},{7,6},{8,9},{9,8},{10,11... | collective-permute-start | bytes 1966088 | tf_op jit(solution)/shard_map/ppermute | solution.py:220
  275.4 2.5 copy-start.3
  276.4 3.3 %copy-start.5 = (bf16[1,640,256]{2,1,0:T(8,128)(2,1)S(1)}, bf16[1,640,256]{2,1,0:T(8,128)(2,1)}, u32[]{:S(2)}) copy-start(bf16[1,640,256]{2,1,0:T(8,128)(2,1)} %get-tuple-element.73) | copy-start | bytes 983044
  276.4 5.0 %collective-permute-start.11 = (bf16[2,64,2560]{2,1,0:T(8,128)(2,1)}, bf16[2,64,2560]{2,1,0:T(8,128)(2,1)}, u32[]{:S(2)}, u32[]{:S(2)}) collective-permute-start(bf16[2,64,2560]{2,1,0:T(8,128)(2,1)} %dynamic-slice_bitcast_fusion.2), channel_id=1, source_target_pairs={{0,1},{1,0},{2,3},{3,2},{4,5},{5,4},{6,7},{7,6},{8,9},{9,8},{10,11... | collective-permute-start | bytes 1966088 | tf_op jit(solution)/shard_map/ppermute | solution.py:220
  277.9 1.9 copy-start.1
  280.3 1.1 copy-start.2
  280.3 1.5 copy-start.4
  283.1 12.0 %collective-permute-start.10 = (bf16[64,2560]{1,0:T(8,128)(2,1)S(1)}, bf16[64,2560]{1,0:T(8,128)(2,1)S(1)}, u32[]{:S(2)}, u32[]{:S(2)}) collective-permute-start(bf16[64,2560]{1,0:T(8,128)(2,1)S(1)} %dynamic-slice_bitcast_fusion.7), channel_id=1, source_target_pairs={{0,2},{1,3},{2,0},{3,1},{4,6},{5,7},{6,4},{7,5},{8,10},{9,11},{10,... | collective-permute-start | bytes 983048 | tf_op jit(solution)/shard_map/ppermute | solution.py:227
  289.5 10.5 %collective-permute-start.14 = (bf16[2,64,2560]{2,1,0:T(8,128)(2,1)S(1)}, bf16[2,64,2560]{2,1,0:T(8,128)(2,1)S(1)}, u32[]{:S(2)}, u32[]{:S(2)}) collective-permute-start(bf16[2,64,2560]{2,1,0:T(8,128)(2,1)S(1)} %dynamic-slice_bitcast_fusion.1), channel_id=1, source_target_pairs={{0,1},{1,0},{2,3},{3,2},{4,5},{5,4},{6,7},{7,6},{8,9},{9,8},{10,11... | collective-permute-start | bytes 1966088 | tf_op jit(solution)/shard_map/ppermute | solution.py:220
  289.6 10.3 %collective-permute-start.12 = (bf16[64,2560]{1,0:T(8,128)(2,1)S(1)}, bf16[64,2560]{1,0:T(8,128)(2,1)S(1)}, u32[]{:S(2)}, u32[]{:S(2)}) collective-permute-start(bf16[64,2560]{1,0:T(8,128)(2,1)S(1)} %dynamic-slice_bitcast_fusion.6), channel_id=1, source_target_pairs={{0,2},{1,3},{2,0},{3,1},{4,6},{5,7},{6,4},{7,5},{8,10},{9,11},{10,... | collective-permute-start | bytes 983048 | tf_op jit(solution)/shard_map/ppermute | solution.py:227
  294.9 6.8 %collective-permute-start.16 = (bf16[2,64,2560]{2,1,0:T(8,128)(2,1)S(1)}, bf16[2,64,2560]{2,1,0:T(8,128)(2,1)S(1)}, u32[]{:S(2)}, u32[]{:S(2)}) collective-permute-start(bf16[2,64,2560]{2,1,0:T(8,128)(2,1)S(1)} %dynamic-slice_bitcast_fusion), channel_id=1, source_target_pairs={{0,1},{1,0},{2,3},{3,2},{4,5},{5,4},{6,7},{7,6},{8,9},{9,8},{10,11... | collective-permute-start | bytes 1966088 | tf_op jit(solution)/shard_map/ppermute | solution.py:220
  300.2 10.7 %collective-permute-start.15 = (bf16[64,2560]{1,0:T(8,128)(2,1)S(1)}, bf16[64,2560]{1,0:T(8,128)(2,1)S(1)}, u32[]{:S(2)}, u32[]{:S(2)}) collective-permute-start(bf16[64,2560]{1,0:T(8,128)(2,1)S(1)} %dynamic-slice_bitcast_fusion.5), channel_id=1, source_target_pairs={{0,2},{1,3},{2,0},{3,1},{4,6},{5,7},{6,4},{7,5},{8,10},{9,11},{10,... | collective-permute-start | bytes 983048 | tf_op jit(solution)/shard_map/ppermute | solution.py:227
  301.9 14.7 %collective-permute-start.17 = (bf16[64,2560]{1,0:T(8,128)(2,1)S(1)}, bf16[64,2560]{1,0:T(8,128)(2,1)S(1)}, u32[]{:S(2)}, u32[]{:S(2)}) collective-permute-start(bf16[64,2560]{1,0:T(8,128)(2,1)S(1)} %dynamic-slice_bitcast_fusion.4), channel_id=1, source_target_pairs={{0,2},{1,3},{2,0},{3,1},{4,6},{5,7},{6,4},{7,5},{8,10},{9,11},{10,... | collective-permute-start | bytes 983048 | tf_op jit(solution)/shard_map/ppermute | solution.py:227
